TPU v7x, 32 devices: a whole 2x2x4 slice. The times are simulated.
32 devices in a mesh: dp: 4 (over z), seq: 8 (over y, x, core).
Axes of the slice: x: 2, y: 2, z: 4, core: 2. Of those that a mesh axis runs over, the one named last changes fastest.
Arguments:
- tokens: bfloat16 [8, 1024, 2048], P('dp', 'seq'), may hold values from -6 to 6
- lengths: int32 [8], P('dp'), may hold values from 256 to 1024, as said below
- second_queries: bfloat16 [8, 1024, 2048], P('dp', 'seq'), may hold values from -0.75 to 0.75
- cotangent: bfloat16 [8, 1024, 2048], P('dp', 'seq'), may hold values from -6 to 6
- second_cotangent: bfloat16 [8, 1024, 2048], P('dp', 'seq'), may hold values from -6 to 6
- gain_attn: bfloat16 [2048], P('seq'), may hold values from 0.5 to 1.5
- w_query: bfloat16 [2048, 2048], P('seq'), may hold values from -0.125 to 0.125
- w_key: bfloat16 [2048, 128], P('seq'), may hold values from -0.125 to 0.125
- w_value: bfloat16 [2048, 128], P('seq'), may hold values from -0.125 to 0.125
- w_out: bfloat16 [2048, 2048], P('seq'), may hold values from -0.5 to 0.5
- gain_mlp: bfloat16 [2048], P('seq'), may hold values from 0.5 to 1.5
- w_gate: bfloat16 [2048, 5632], P('seq'), may hold values from -0.125 to 0.125
- w_up: bfloat16 [2048, 5632], P('seq'), may hold values from -0.125 to 0.125
- w_down: bfloat16 [5632, 2048], P('seq'), may hold values from -0.078125 to 0.078125
Outputs:
- out: bfloat16 [8, 1024, 2048], P('dp', 'seq')
- grad_tokens: float32 [8, 1024, 2048], P('dp', 'seq')
- grad_second_queries: bfloat16 [8, 1024, 2048], P('dp', 'seq')
- grad_gain_attn: float32 [2048], P('seq')
- grad_w_query: float32 [2048, 2048], P('seq')
- grad_w_key: float32 [2048, 128], P('seq')
- grad_w_value: float32 [2048, 128], P('seq')
- grad_w_out: float32 [2048, 2048], P('seq')
- grad_gain_mlp: float32 [2048], P('seq')
- grad_w_gate: float32 [2048, 5632], P('seq')
- grad_w_up: float32 [2048, 5632], P('seq')
- grad_w_down: float32 [5632, 2048], P('seq')
Inputs may be any that keep to these rules, and one draw needn't show every extreme that they name: `lengths`: in each group of 2 sequences of one index of dp, one is exactly 1024 long; in the first group another is exactly 256 long; positions at or past a sequence's length are padding.
All inputs are finite; a program needn't handle non-finite values.
Results may differ from a plain program's by a relative error of at most 0.023.
Values may be sent and summed in bfloat16 or wider, within the bound.
No kernel may reach another device: no remote copies, remote signals or barrier semaphores. Data moves between devices by JAX's collectives and lax.ppermute only.
A program may use at most 448 MiB of HBM per device.

v0:
```python
import math

import jax
import jax.numpy as jnp
from jax import lax
from jax.sharding import PartitionSpec as P

EPSILON = 1e-05


def rope_tables(positions, head_width):
    half_width = head_width // 2
    spacing = jnp.exp(
        jnp.arange(half_width).astype(jnp.float32) * (-2.0 * math.log(10000.0) / head_width)
    )
    angles = positions.astype(jnp.float32)[:, None] * spacing[None, :]
    angles = jnp.concatenate([angles, angles], 1)
    return (jnp.cos(angles), jnp.sin(angles))


def rotate(vector, cosine, sine_table):
    half_width = vector.shape[-1] // 2
    turned = jnp.concatenate([-vector[..., half_width:], vector[..., :half_width]], -1)
    return vector * cosine + turned * sine_table


def rotate_back(gradient, cosine, sine_table):
    half_width = gradient.shape[-1] // 2
    scaled = gradient * sine_table
    turned = jnp.concatenate([scaled[..., half_width:], -scaled[..., :half_width]], -1)
    return gradient * cosine + turned


def rms_scale(values_in):
    return lax.rsqrt(jnp.mean(values_in * values_in, -1, keepdims=True) + EPSILON)


def norm_back(grad_normed, inputs, scale_rows, gain):
    weighted = grad_normed * gain
    cubed = scale_rows * scale_rows * scale_rows
    return scale_rows * weighted - inputs * cubed * jnp.mean(weighted * inputs, -1, keepdims=True)


def outer_sum(left, right):
    return lax.dot_general(
        left, right, (((0,), (0,)), ((), ())), preferred_element_type=jnp.float32
    )


def through(grad_rows, matrix):
    return lax.dot_general(
        grad_rows, matrix, (((1,), (1,)), ((), ())), preferred_element_type=jnp.float32
    )


def split_blocks(array):
    seq_len = array.shape[0]
    block_rows = min(512, seq_len)
    block_count = seq_len // block_rows
    return (
        array.reshape((block_count, block_rows) + array.shape[1:]),
        jnp.arange(block_count, dtype=jnp.int32) * block_rows,
    )


def masked_probs(query_block, key_rows, offset, length):
    scores = jnp.einsum("qhd,kd->hqk", query_block, key_rows, preferred_element_type=jnp.float32)
    query_pos = offset + jnp.arange(query_block.shape[0], dtype=jnp.int32)
    key_pos = jnp.arange(key_rows.shape[0], dtype=jnp.int32)
    allowed = (key_pos[None, :] <= query_pos[:, None]) & (key_pos[None, :] < length)
    scores = jnp.where(allowed[None], scores, -jnp.inf)
    shifted = jnp.exp(scores - jnp.max(scores, -1, keepdims=True))
    return shifted / jnp.sum(shifted, -1, keepdims=True)


def attend_forward(inputs):
    queries, key_rows, value_rows, length = inputs
    query_blocks, offsets = split_blocks(queries)

    def one_block(block_inputs):
        query_block, offset = block_inputs
        probabilities = masked_probs(query_block, key_rows, offset, length)
        return jnp.einsum(
            "hqk,kd->qhd",
            probabilities.astype(jnp.bfloat16),
            value_rows,
            preferred_element_type=jnp.float32,
        )

    return lax.map(one_block, (query_blocks, offsets)).reshape(queries.shape).astype(jnp.bfloat16)


def attend_backward(inputs):
    queries, upstream, key_rows, value_rows, length = inputs
    query_blocks, offsets = split_blocks(queries)
    upstream_blocks = split_blocks(upstream)[0]

    def one_block(totals, block_inputs):
        query_block, upstream_block, offset = block_inputs
        probabilities = masked_probs(query_block, key_rows, offset, length)
        grad_probs = jnp.einsum(
            "qhd,kd->hqk", upstream_block, value_rows, preferred_element_type=jnp.float32
        )
        centre = jnp.sum(probabilities * grad_probs, -1, keepdims=True)
        grad_scores = (probabilities * (grad_probs - centre)).astype(jnp.bfloat16)
        grad_query = jnp.einsum(
            "hqk,kd->qhd", grad_scores, key_rows, preferred_element_type=jnp.float32
        ).astype(jnp.bfloat16)
        key_total = totals[0] + jnp.einsum(
            "hqk,qhd->kd", grad_scores, query_block, preferred_element_type=jnp.float32
        )
        value_total = totals[1] + jnp.einsum(
            "hqk,qhd->kd",
            probabilities.astype(jnp.bfloat16),
            upstream_block,
            preferred_element_type=jnp.float32,
        )
        return ((key_total, value_total), grad_query)

    zero_rows = jnp.zeros(key_rows.shape, jnp.float32)
    totals, grad_queries = lax.scan(
        one_block, (zero_rows, zero_rows), (query_blocks, upstream_blocks, offsets)
    )
    return (totals[0], totals[1], grad_queries.reshape(queries.shape))


def body(
    tokens,
    lengths,
    second_queries,
    cotangent,
    second_cotangent,
    gain_attn,
    w_query,
    w_key,
    w_value,
    w_out,
    gain_mlp,
    w_gate,
    w_up,
    w_down,
):
    seq_rank = lax.axis_index("seq")
    gathered = (
        lax.all_gather(gain_attn, "seq", axis=0, tiled=True),
        lax.all_gather(w_query, "seq", axis=0, tiled=True),
        lax.all_gather(w_key, "seq", axis=0, tiled=True),
        lax.all_gather(w_value, "seq", axis=0, tiled=True),
        lax.all_gather(w_out, "seq", axis=0, tiled=True),
        lax.all_gather(gain_mlp, "seq", axis=0, tiled=True),
        lax.all_gather(w_gate, "seq", axis=0, tiled=True),
        lax.all_gather(w_up, "seq", axis=0, tiled=True),
        lax.all_gather(w_down, "seq", axis=0, tiled=True),
    )
    gain_one, query_mat, key_mat, value_mat, out_mat, gain_two, gate_mat, up_mat, down_mat = (
        gathered
    )
    seq_count, local_len, model_width = tokens.shape
    head_width = key_mat.shape[1]
    head_total = query_mat.shape[1] // head_width
    token_rows = seq_count * local_len
    positions = seq_rank * local_len + jnp.arange(local_len, dtype=jnp.int32)
    valid = (positions[None, :] < lengths[:, None]).astype(jnp.float32)
    cosine, sine_table = rope_tables(positions, head_width)
    cosine_heads = cosine[None, :, None, :]
    sine_heads = sine_table[None, :, None, :]
    scale = 1.0 / math.sqrt(head_width)
    gain_one_f = gain_one.astype(jnp.float32)
    gain_two_f = gain_two.astype(jnp.float32)
    inputs_f = tokens.reshape(token_rows, model_width).astype(jnp.float32)
    scale_one = rms_scale(inputs_f)
    normed_one = (inputs_f * scale_one * gain_one_f).astype(jnp.bfloat16)
    q_linear = jnp.dot(normed_one, query_mat, preferred_element_type=jnp.float32).reshape(
        seq_count, local_len, head_total, head_width
    )
    queries = (rotate(q_linear, cosine_heads, sine_heads) * scale).astype(jnp.bfloat16)
    k_linear = jnp.dot(normed_one, key_mat, preferred_element_type=jnp.float32).reshape(
        seq_count, local_len, head_width
    )
    key_local = rotate(k_linear, cosine[None], sine_table[None]).astype(jnp.bfloat16)
    value_local = (
        jnp.dot(normed_one, value_mat, preferred_element_type=jnp.float32)
        .reshape(seq_count, local_len, head_width)
        .astype(jnp.bfloat16)
    )
    second_split = second_queries.reshape(seq_count, local_len, head_total, head_width)
    second_masked = (second_cotangent * valid[:, :, None].astype(jnp.bfloat16)).reshape(
        seq_count, local_len, head_total, head_width
    )
    head_queries, head_second, head_upstream = (
        lax.all_to_all(queries, "seq", split_axis=2, concat_axis=1, tiled=True),
        lax.all_to_all(second_split, "seq", split_axis=2, concat_axis=1, tiled=True),
        lax.all_to_all(second_masked, "seq", split_axis=2, concat_axis=1, tiled=True),
    )
    key_rows, value_rows = (
        lax.all_gather(key_local, "seq", axis=1, tiled=True),
        lax.all_gather(value_local, "seq", axis=1, tiled=True),
    )
    attn_heads = lax.map(attend_forward, (head_queries, key_rows, value_rows, lengths))
    attn_seq = lax.all_to_all(attn_heads, "seq", split_axis=1, concat_axis=2, tiled=True).reshape(
        token_rows, head_total * head_width
    )
    middle = inputs_f + jnp.dot(attn_seq, out_mat, preferred_element_type=jnp.float32)
    scale_two = rms_scale(middle)
    normed_two = (middle * scale_two * gain_two_f).astype(jnp.bfloat16)
    gate_pre = jnp.dot(normed_two, gate_mat, preferred_element_type=jnp.float32)
    up_pre = jnp.dot(normed_two, up_mat, preferred_element_type=jnp.float32)
    sigma = jax.nn.sigmoid(gate_pre)
    silu_gate = gate_pre * sigma
    hidden = (silu_gate * up_pre).astype(jnp.bfloat16)
    out_rows = middle + jnp.dot(hidden, down_mat, preferred_element_type=jnp.float32)
    out = out_rows.astype(jnp.bfloat16).reshape(seq_count, local_len, model_width)
    grad_out = cotangent.reshape(token_rows, model_width).astype(jnp.float32) * valid.reshape(
        token_rows, 1
    )
    grad_branch = grad_out.astype(jnp.bfloat16)
    grad_hidden = through(grad_branch, down_mat)
    grad_gate_pre = (grad_hidden * up_pre * (sigma * (1.0 + gate_pre * (1.0 - sigma)))).astype(
        jnp.bfloat16
    )
    grad_up_pre = (grad_hidden * silu_gate).astype(jnp.bfloat16)
    grad_normed_two = through(grad_gate_pre, gate_mat) + through(grad_up_pre, up_mat)
    grad_gain_two = jnp.sum(grad_normed_two * (middle * scale_two), 0)
    grad_middle = grad_out + norm_back(grad_normed_two, middle, scale_two, gain_two_f)
    feed_shares = (
        lax.psum_scatter(
            grad_gain_two.astype(jnp.bfloat16), "seq", scatter_dimension=0, tiled=True
        ).astype(jnp.float32),
        lax.psum_scatter(
            outer_sum(normed_two, grad_gate_pre).astype(jnp.bfloat16),
            "seq",
            scatter_dimension=0,
            tiled=True,
        ).astype(jnp.float32),
        lax.psum_scatter(
            outer_sum(normed_two, grad_up_pre).astype(jnp.bfloat16),
            "seq",
            scatter_dimension=0,
            tiled=True,
        ).astype(jnp.float32),
        lax.psum_scatter(
            outer_sum(hidden, grad_branch).astype(jnp.bfloat16),
            "seq",
            scatter_dimension=0,
            tiled=True,
        ).astype(jnp.float32),
    )
    grad_proj = grad_middle.astype(jnp.bfloat16)
    grad_attn = (
        through(grad_proj, out_mat)
        .astype(jnp.bfloat16)
        .reshape(seq_count, local_len, head_total, head_width)
    )
    head_grad = lax.all_to_all(grad_attn, "seq", split_axis=2, concat_axis=1, tiled=True)
    local_heads = head_queries.shape[2]
    both_queries = jnp.concatenate([head_queries, head_second], 2)
    both_upstream = jnp.concatenate([head_grad, head_upstream], 2)
    key_sums, value_sums, both_grads = lax.map(
        attend_backward, (both_queries, both_upstream, key_rows, value_rows, lengths)
    )
    grad_q_first = both_grads[:, :, :local_heads]
    grad_q_second = both_grads[:, :, local_heads:]
    back_first, back_second = (
        lax.all_to_all(grad_q_first, "seq", split_axis=1, concat_axis=2, tiled=True),
        lax.all_to_all(grad_q_second, "seq", split_axis=1, concat_axis=2, tiled=True),
    )
    key_owner, value_owner = (
        lax.psum_scatter(
            key_sums.astype(jnp.bfloat16), "seq", scatter_dimension=1, tiled=True
        ).astype(jnp.float32),
        lax.psum_scatter(
            value_sums.astype(jnp.bfloat16), "seq", scatter_dimension=1, tiled=True
        ).astype(jnp.float32),
    )
    key_rounded = lax.optimization_barrier(key_owner.astype(jnp.bfloat16)).astype(jnp.float32)
    grad_k_linear = (
        rotate_back(key_rounded, cosine[None], sine_table[None])
        .astype(jnp.bfloat16)
        .reshape(token_rows, head_width)
    )
    grad_value_rows = value_owner.astype(jnp.bfloat16).reshape(token_rows, head_width)
    grad_q_linear = (
        rotate_back(back_first.astype(jnp.float32) * scale, cosine_heads, sine_heads)
        .astype(jnp.bfloat16)
        .reshape(token_rows, head_total * head_width)
    )
    grad_normed_one = (
        through(grad_q_linear, query_mat)
        + through(grad_k_linear, key_mat)
        + through(grad_value_rows, value_mat)
    )
    grad_gain_one = jnp.sum(grad_normed_one * (inputs_f * scale_one), 0)
    grad_tokens = grad_middle + norm_back(grad_normed_one, inputs_f, scale_one, gain_one_f)
    attn_shares = (
        lax.psum_scatter(
            grad_gain_one.astype(jnp.bfloat16), "seq", scatter_dimension=0, tiled=True
        ).astype(jnp.float32),
        lax.psum_scatter(
            outer_sum(normed_one, grad_q_linear).astype(jnp.bfloat16),
            "seq",
            scatter_dimension=0,
            tiled=True,
        ).astype(jnp.float32),
        lax.psum_scatter(
            outer_sum(normed_one, grad_k_linear).astype(jnp.bfloat16),
            "seq",
            scatter_dimension=0,
            tiled=True,
        ).astype(jnp.float32),
        lax.psum_scatter(
            outer_sum(normed_one, grad_value_rows).astype(jnp.bfloat16),
            "seq",
            scatter_dimension=0,
            tiled=True,
        ).astype(jnp.float32),
        lax.psum_scatter(
            outer_sum(attn_seq, grad_proj).astype(jnp.bfloat16),
            "seq",
            scatter_dimension=0,
            tiled=True,
        ).astype(jnp.float32),
    )
    summed = (
        lax.psum(feed_shares[0].astype(jnp.bfloat16), "dp").astype(jnp.float32),
        lax.psum(feed_shares[1].astype(jnp.bfloat16), "dp").astype(jnp.float32),
        lax.psum(feed_shares[2].astype(jnp.bfloat16), "dp").astype(jnp.float32),
        lax.psum(feed_shares[3].astype(jnp.bfloat16), "dp").astype(jnp.float32),
        lax.psum(attn_shares[0].astype(jnp.bfloat16), "dp").astype(jnp.float32),
        lax.psum(attn_shares[1].astype(jnp.bfloat16), "dp").astype(jnp.float32),
        lax.psum(attn_shares[2].astype(jnp.bfloat16), "dp").astype(jnp.float32),
        lax.psum(attn_shares[3].astype(jnp.bfloat16), "dp").astype(jnp.float32),
        lax.psum(attn_shares[4].astype(jnp.bfloat16), "dp").astype(jnp.float32),
    )
    grad_tokens_out = grad_tokens.reshape(seq_count, local_len, model_width)
    grad_second_out = back_second.reshape(seq_count, local_len, head_total * head_width)
    return (
        out,
        grad_tokens_out,
        grad_second_out,
        summed[4],
        summed[5],
        summed[6],
        summed[7],
        summed[8],
        summed[0],
        summed[1],
        summed[2],
        summed[3],
    )


def solution(mesh):
    return jax.shard_map(
        body,
        mesh=mesh,
        in_specs=(
            P("dp", "seq", None),
            P("dp"),
            P("dp", "seq", None),
            P("dp", "seq", None),
            P("dp", "seq", None),
            P("seq"),
            P("seq", None),
            P("seq", None),
            P("seq", None),
            P("seq", None),
            P("seq"),
            P("seq", None),
            P("seq", None),
            P("seq", None),
        ),
        out_specs=(
            P("dp", "seq", None),
            P("dp", "seq", None),
            P("dp", "seq", None),
            P("seq"),
            P("seq", None),
            P("seq", None),
            P("seq", None),
            P("seq", None),
            P("seq"),
            P("seq", None),
            P("seq", None),
            P("seq", None),
        ),
        check_vma=False,
    )
```

profile of v0, /device:TPU:0, one launch (start us, length us, event | category | flops | bytes accessed | tf_op | source)
XLA Modules:
  0.0 1886.1 jit_solution(3979871306918459586)
XLA Ops:
  10.6 10.3 all-gather
  21.1 16.5 all_gather.35
  40.3 29.0 %all-gather.8.cloned.1.call-done = bf16[2048,2048]{1,0:T(8,128)(2,1)} async-done(((bf16[256,2048]{1,0:T(8,128)(2,1)}), bf16[2048,2048]{1,0:T(8,128)(2,1)}) %all-gather.8.cloned.1.call-update) | async-done | bytes 8388624 | tf_op jit(solution)/shard_map/all_gather | solution.py:146
  69.3 12.4 copy.109
  81.7 4.8 fusion.115
  92.1 27.5 %all_gather.36 = bf16[2,1024,128]{1,2,0:T(8,128)(2,1)S(1)} all-gather(bf16[2,128,128]{1,2,0:T(8,128)(2,1)S(1)} %fusion.125), channel_id=1, replica_groups=mesh['dp'=4,'seq'=8] {'seq'}, dimensions={1}, use_global_device_ids=true | all-gather | bytes 589824 | tf_op jit(solution)/shard_map/all_gather | solution.py:196
  120.6 7.9 all-gather.1
  131.4 9.8 all_gather.37
  142.0 11.9 all_gather.38
  155.2 42.8 %while.50 = (s32[]{:T(128)}, bf16[2,1024,2,128]{3,2,0,1:T(2,128)(2,1)}, bf16[2,1024,2,128]{3,1,2,0:T(8,128)(2,1)S(1)}, bf16[2,1024,128]{2,1,0:T(8,128)(2,1)}, s3...) while((s32[]{:T(128)}, bf16[2,1024,2,128]{3,2,0,1:T(2,128)(2,1)}, ...), condition=%wide.region_6.7_spmd, body=%wide.region_1.6_spmd.sunk | while | flops 543164928 | bytes 14957362 | solution.py:199
  156.9 17.8 while.53
  178.2 18.1 while.53
  198.0 4.6 all-to-all-start.1
  208.2 21.3 %all-to-all-done.1 = bf16[2,1024,2,128]{3,2,0,1:T(2,128)(2,1)} async-done(((bf16[2,1024,2,128]{3,2,0,1:T(2,128)(2,1)}), bf16[2,1024,2,128]{3,2,0,1:T(2,128)(2,1)}, u32[]{:S(2)}, u32[]{:S(2)}) %all-to-all-start.1) | async-done | bytes 1048608 | tf_op jit(solution)/shard_map/all_to_all | solution.py:200
  229.5 4.2 all-to-all-start.4
  239.4 6.3 multiply_reduce_fusion.2
  247.3 28.0 %all-gather.12.cloned.1.call-done = bf16[2048,5632]{1,0:T(8,128)(2,1)} async-done(((bf16[256,5632]{1,0:T(8,128)(2,1)}), bf16[2048,5632]{1,0:T(8,128)(2,1)}) %all-gather.12.cloned.1.call-update) | async-done | bytes 23068688 | tf_op jit(solution)/shard_map/all_gather | solution.py:151
  275.3 13.5 fusion.153
  288.7 104.8 %all-gather.14.cloned.1.call-done = bf16[2048,5632]{1,0:T(8,128)(2,1)} async-done(((bf16[256,5632]{1,0:T(8,128)(2,1)}), bf16[2048,5632]{1,0:T(8,128)(2,1)}) %all-gather.14.cloned.1.call-update) | async-done | bytes 23068688 | tf_op jit(solution)/shard_map/all_gather | solution.py:152
  393.5 13.5 fusion.154
  407.0 104.7 %all-gather.16.cloned.1.call-done = bf16[5632,2048]{1,0:T(8,128)(2,1)} async-done(((bf16[704,2048]{1,0:T(8,128)(2,1)}), bf16[5632,2048]{1,0:T(8,128)(2,1)}) %all-gather.16.cloned.1.call-update) | async-done | bytes 23068688 | tf_op jit(solution)/shard_map/all_gather | solution.py:153
  511.7 18.4 multiply_convert_fusion
  530.1 13.0 fusion.155
  543.1 14.5 multiply_reduce_fusion
  564.4 6.5 fusion.110
  587.3 8.9 all-to-all-done.3
  599.0 134.1 %while.52 = (s32[]{:T(128)}, bf16[2,1024,128]{1,2,0:T(8,128)(2,1)}, bf16[2,1024,128]{2,1,0:T(8,128)(2,1)}, bf16[2,1024,4,128]{3,2,0,1:T(4,128)(2,1)}, bf16[2,102...) while((s32[]{:T(128)}, bf16[2,1024,128]{1,2,0:T(8,128)(2,1)}, ...), condition=%wide.region_15.16_spmd, body=%wide.region_9.15_spmd.sunk | while | flops 2711355904 | bytes 137944944 | solution.py:258
  603.2 59.0 %while.54 = (s32[]{:T(128)}, f32[1024,128]{1,0:T(8,128)S(1)}, f32[1024,128]{1,0:T(8,128)}, bf16[2,512,4,128]{3,2,1,0:T(4,128)(2,1)}, s32[2]{0:T(128)S(1)}, /*ind...) while((s32[]{:T(128)}, f32[1024,128]{1,0:T(8,128)S(1)}, ...), condition=%wide.region_14.14_spmd.clone, body=%wide.region_10.13_spmd.clone.sunk | while | flops 2711355904 | bytes 117758800 | solution.py:121
  605.5 7.1 fusion.223
  612.5 4.4 fusion.224
  626.7 5.2 fusion.227
  635.0 7.1 fusion.223
  642.0 4.4 fusion.224
  656.2 5.2 fusion.227
  670.2 59.0 %while.54 = (s32[]{:T(128)}, f32[1024,128]{1,0:T(8,128)S(1)}, f32[1024,128]{1,0:T(8,128)}, bf16[2,512,4,128]{3,2,1,0:T(4,128)(2,1)}, s32[2]{0:T(128)S(1)}, /*ind...) while((s32[]{:T(128)}, f32[1024,128]{1,0:T(8,128)S(1)}, ...), condition=%wide.region_14.14_spmd.clone, body=%wide.region_10.13_spmd.clone.sunk | while | flops 2711355904 | bytes 117758800 | solution.py:121
  672.5 7.1 fusion.223
  679.6 4.4 fusion.224
  693.7 5.2 fusion.227
  702.0 7.1 fusion.223
  709.1 4.4 fusion.224
  723.2 5.2 fusion.227
  736.4 32.4 %reduce-scatter.28.cloned.1.call-done = bf16[128,256]{1,0:T(8,128)(2,1)} async-done(((bf16[1024,256]{1,0:T(8,128)(2,1)}), bf16[128,256]{1,0:T(8,128)(2,1)}) %reduce-scatter.28.cloned.1.call-update) | async-done | bytes 65552
  771.3 35.1 %reduce-scatter.12.cloned.1.call-done = bf16[2,128,128]{2,1,0:T(8,128)(2,1)} async-done(((bf16[2,1024,128]{2,1,0:T(8,128)(2,1)}), bf16[2,128,128]{2,1,0:T(8,128)(2,1)}) %reduce-scatter.12.cloned.1.call-update) | async-done | bytes 65552 | tf_op jit(solution)/shard_map/reduce_scatter | solution.py:271
  808.6 6.9 convolution_convert_fusion.4
  815.5 5.0 fusion.150
  820.5 4.4 all-to-all-start.5
  825.2 16.5 all-to-all-done.5
  848.3 5.7 convolution_convert_fusion.5
  855.2 12.7 convolution_convert_fusion.3
  868.1 12.7 convolution_convert_fusion.2
  882.0 12.8 convolution_convert_fusion.1
  894.9 66.0 %reduce-scatter.20.cloned.1.call-done = bf16[256,2048]{1,0:T(8,128)(2,1)} async-done(((bf16[2048,2048]{1,0:T(8,128)(2,1)}), bf16[256,2048]{1,0:T(8,128)(2,1)}) %reduce-scatter.20.cloned.1.call-update) | async-done | bytes 1048592 | tf_op jit(solution)/shard_map/reduce_scatter | solution.py:316
  960.9 75.2 %reduce-scatter.14.cloned.1.call-done = bf16[256,2048]{1,0:T(8,128)(2,1)} async-done(((bf16[2048,2048]{1,0:T(8,128)(2,1)}), bf16[256,2048]{1,0:T(8,128)(2,1)}) %reduce-scatter.14.cloned.1.call-update) | async-done | bytes 1048592 | tf_op jit(solution)/shard_map/reduce_scatter | solution.py:298
  1036.1 149.4 %reduce-scatter.22.cloned.1.call-done = bf16[256,5632]{1,0:T(8,128)(2,1)} async-done(((bf16[2048,5632]{1,0:T(8,128)(2,1)}), bf16[256,5632]{1,0:T(8,128)(2,1)}) %reduce-scatter.22.cloned.1.call-update) | async-done | bytes 2883600 | tf_op jit(solution)/shard_map/reduce_scatter | solution.py:229
  1185.5 149.6 %reduce-scatter.24.cloned.1.call-done = bf16[256,5632]{1,0:T(8,128)(2,1)} async-done(((bf16[2048,5632]{1,0:T(8,128)(2,1)}), bf16[256,5632]{1,0:T(8,128)(2,1)}) %reduce-scatter.24.cloned.1.call-update) | async-done | bytes 2883600 | tf_op jit(solution)/shard_map/reduce_scatter | solution.py:235
  1335.1 149.4 %reduce-scatter.26.cloned.1.call-done = bf16[704,2048]{1,0:T(8,128)(2,1)} async-done(((bf16[5632,2048]{1,0:T(8,128)(2,1)}), bf16[704,2048]{1,0:T(8,128)(2,1)}) %reduce-scatter.26.cloned.1.call-update) | async-done | bytes 2883600 | tf_op jit(solution)/shard_map/reduce_scatter | solution.py:241
  1486.4 14.1 fusion.92
  1500.5 4.4 all-to-all-start.6
  1505.0 4.7 copy.129
  1517.8 7.8 fusion.111
  1529.1 15.4 all-reduce.2
  1544.7 14.3 all-reduce.3
  1569.1 294.1 %all-reduce.7.cloned.1.call-done = (bf16[256,2048]{1,0:T(8,128)(2,1)}, bf16[256,128]{1,0:T(8,128)(2,1)}, bf16[256,128]{1,0:T(8,128)(2,1)}, bf16[256,2048]{1,0:T(...) async-done(((bf16[256,2048]{1,0:T(8,128)(2,1)}, bf16[256,128]{1,0:T(8,128)(2,1)}, bf16[256,128]{1,0:T(8,128)(2,1)}, ...) | async-done | bytes 10878992 | tf_op jit(solution)/shard_map/psum | solution.py:329
  1863.2 5.2 convert_element_type.319
  (395 shorter events, 217.1 us)
Async XLA Ops:
  7.2 62.2 %all-gather.8.cloned.1.call-start = ((), (), s32[]{:S(2)}) async-start(), calls=%async_computation.16 | async-start | bytes 9437184 | tf_op jit(solution)/shard_map/all_gather | solution.py:146
  7.9 231.5 %all-gather.10.cloned.1.call-start = ((), (), s32[]{:S(2)}) async-start(), calls=%async_computation.17 | async-start | bytes 9437184 | tf_op jit(solution)/shard_map/all_gather | solution.py:149
  8.7 266.6 %all-gather.12.cloned.1.call-start = ((), (), s32[]{:S(2)}) async-start(), calls=%async_computation.18 | async-start | bytes 25952256 | tf_op jit(solution)/shard_map/all_gather | solution.py:151
  9.4 384.1 %all-gather.14.cloned.1.call-start = ((), (), s32[]{:S(2)}) async-start(), calls=%async_computation.19 | async-start | bytes 25952256 | tf_op jit(solution)/shard_map/all_gather | solution.py:152
  10.0 11.0 copy-start.47
  10.0 28.6 %copy-start.6 = (bf16[2,128,2048]{2,1,0:T(8,128)(2,1)S(1)}, bf16[2,128,2048]{2,1,0:T(8,128)(2,1)}, u32[]{:S(2)}) copy-start(bf16[2,128,2048]{2,1,0:T(8,128)(2,1)} %param.22) | copy-start | bytes 3145732
  10.0 501.7 %all-gather.16.cloned.1.call-start = ((), (), s32[]{:S(2)}) async-start(), calls=%async_computation.20 | async-start | bytes 25952256 | tf_op jit(solution)/shard_map/all_gather | solution.py:153
  21.0 18.8 copy-start.41
  38.6 53.4 %copy-start.28 = (f32[128,128]{0,1:T(8,128)}, f32[128,128]{0,1:T(8,128)S(1)}, u32[]{:S(2)}) copy-start(f32[128,128]{0,1:T(8,128)S(1)} %get-tuple-element.441) | copy-start | bytes 196612
  38.6 53.4 %copy-start.30 = (f32[128,128]{0,1:T(8,128)}, f32[128,128]{0,1:T(8,128)S(1)}, u32[]{:S(2)}) copy-start(f32[128,128]{0,1:T(8,128)S(1)} %get-tuple-element.440) | copy-start | bytes 196612
  38.9 42.8 %copy-start.49 = (f32[2,128]{1,0:T(2,128)}, f32[2,128]{1,0:T(2,128)S(1)}, u32[]{:S(2)}) copy-start(f32[2,128]{1,0:T(2,128)S(1)} %fusion.101) | copy-start | bytes 3076
  39.8 101.4 %copy-start.1 = (bf16[2,128,2048]{2,1,0:T(8,128)(2,1)}, bf16[2,128,2048]{2,1,0:T(8,128)(2,1)S(1)}, u32[]{:S(2)}) copy-start(bf16[2,128,2048]{2,1,0:T(8,128)(2,1)S(1)} %fusion.103) | copy-start | bytes 3145732
  88.3 32.3 %copy-start.58 = (bf16[256]{0:T(256)(128)(2,1)S(1)}, bf16[256]{0:T(256)(128)(2,1)}, u32[]{:S(2)}) copy-start(bf16[256]{0:T(256)(128)(2,1)} %param.32) | copy-start | bytes 1540
  88.3 66.2 %all-to-all-start = ((bf16[2,128,16,128]{1,3,0,2:T(8,128)(2,1)}), bf16[2,128,16,128]{1,3,0,2:T(8,128)(2,1)S(1)}, u32[]{:S(2)}, u32[]{:S(2)}) async-start(bf16[2,128,16,128]{1,3,0,2:T(8,128)(2,1)} %copy.110), calls=%async_computation | async-start | bytes 2097152 | tf_op jit(solution)/shard_map/all_to_all | solution.py:191
  92.0 39.4 %copy-start.44 = (bf16[256,128]{1,0:T(8,128)(2,1)S(1)}, bf16[256,128]{1,0:T(8,128)(2,1)}, u32[]{:S(2)}) copy-start(bf16[256,128]{1,0:T(8,128)(2,1)} %param.30) | copy-start | bytes 196612
  129.1 24.8 %copy-start.54 = (s32[2]{0:T(128)S(1)}, s32[2]{0:T(128)}, u32[]{:S(2)}) copy-start(s32[2]{0:T(128)} %param.23) | copy-start | bytes 28
  198.0 4.6 copy-start.23
  198.0 4.6 copy-start.53
  198.0 31.5 %all-to-all-start.1 = ((bf16[2,1024,2,128]{3,2,0,1:T(2,128)(2,1)}), bf16[2,1024,2,128]{3,2,0,1:T(2,128)(2,1)}, u32[]{:S(2)}, u32[]{:S(2)}) async-start(bf16[2,1024,2,128]{3,2,0,1:T(2,128)(2,1)} %get-tuple-element.184), calls=%async_computation.1 | async-start | bytes 2097152 | tf_op jit(solution)/shard_map/all_to_all | solution.py:200
  229.5 328.1 %all-to-all-start.4 = ((bf16[2,128,16,128]{1,3,0,2:T(8,128)(2,1)}), bf16[2,128,16,128]{1,3,0,2:T(8,128)(2,1)}, u32[]{:S(2)}, u32[]{:S(2)}) async-start(bf16[2,128,16,128]{1,3,0,2:T(8,128)(2,1)} %copy.123), calls=%async_computation.4 | async-start | bytes 2097152 | tf_op jit(solution)/shard_map/all_to_all | solution.py:193
  233.8 5.6 copy-start.7
  239.4 7.6 copy-start.43
  247.3 146.2 %copy-start.12 = (bf16[256,2048]{1,0:T(8,128)(2,1)}, bf16[256,2048]{1,0:T(8,128)(2,1)S(1)}, u32[]{:S(2)}) copy-start(bf16[256,2048]{1,0:T(8,128)(2,1)S(1)} %multiply_convert_fusion.3) | copy-start | bytes 3145732
  557.6 18.9 %all-to-all-start.2 = ((bf16[2,128,16,128]{1,3,0,2:T(8,128)(2,1)}), bf16[2,128,16,128]{1,3,0,2:T(8,128)(2,1)S(1)}, u32[]{:S(2)}, u32[]{:S(2)}) async-start(bf16[2,128,16,128]{1,3,0,2:T(8,128)(2,1)} %copy.117), calls=%async_computation.2 | async-start | bytes 2097152 | tf_op jit(solution)/shard_map/all_to_all | solution.py:192
  564.4 6.5 copy-start.3
  576.5 19.7 %all-to-all-start.3 = ((bf16[2,128,16,128]{3,1,0,2:T(8,128)(2,1)}), bf16[2,128,16,128]{3,1,0,2:T(8,128)(2,1)}, u32[]{:S(2)}, u32[]{:S(2)}) async-start(bf16[2,128,16,128]{3,1,0,2:T(8,128)(2,1)} %copy.120), calls=%async_computation.3 | async-start | bytes 2097152 | tf_op jit(solution)/shard_map/all_to_all | solution.py:254
  580.8 188.0 %reduce-scatter.28.cloned.1.call-start = ((), (), s32[]{:S(2)}) async-start(), calls=%async_computation.29 | async-start | bytes 589824
  587.3 10.2 copy-start.24
  599.0 3.5 copy-start.55
  612.5 4.6 slice-start
  612.5 5.9 slice-start.1
  623.0 3.6 copy-start.9
  642.0 4.6 slice-start
  642.0 5.9 slice-start.1
  652.5 3.6 copy-start.9
  662.2 3.8 copy-start.56
  666.0 3.5 copy-start.55
  679.6 4.6 slice-start
  679.6 5.9 slice-start.1
  690.1 3.6 copy-start.9
  709.1 4.6 slice-start
  709.1 5.9 slice-start.1
  719.6 3.6 copy-start.9
  729.2 3.8 copy-start.56
  733.1 36.7 %copy-start.31 = (f32[128,128]{0,1:T(8,128)S(1)}, f32[128,128]{0,1:T(8,128)}, u32[]{:S(2)}) copy-start(f32[128,128]{0,1:T(8,128)} %copy-done.30) | copy-start | bytes 196612
  733.1 36.8 %copy-start.29 = (f32[128,128]{0,1:T(8,128)S(1)}, f32[128,128]{0,1:T(8,128)}, u32[]{:S(2)}) copy-start(f32[128,128]{0,1:T(8,128)} %copy-done.28) | copy-start | bytes 196612
  733.1 36.8 %copy-start.2 = (bf16[2,128,2048]{2,1,0:T(8,128)(2,1)S(1)}, bf16[2,128,2048]{2,1,0:T(8,128)(2,1)}, u32[]{:S(2)}) copy-start(bf16[2,128,2048]{2,1,0:T(8,128)(2,1)} %copy-done.1) | copy-start | bytes 3145732
  735.4 71.0 %reduce-scatter.12.cloned.1.call-start = ((), (), s32[]{:S(2)}) async-start(), calls=%async_computation.21 | async-start | bytes 589824 | tf_op jit(solution)/shard_map/reduce_scatter | solution.py:271
  736.2 158.8 %reduce-scatter.16.cloned.1.call-start = ((), (), s32[]{:S(2)}) async-start(), calls=%async_computation.23 | async-start | bytes 589824 | tf_op jit(solution)/shard_map/reduce_scatter | solution.py:304
  769.9 38.7 %copy-start.4 = (f32[256,2048]{1,0:T(8,128)S(1)}, f32[256,2048]{1,0:T(8,128)}, u32[]{:S(2)}) copy-start(f32[256,2048]{1,0:T(8,128)} %copy-done.3) | copy-start | bytes 6291460
  771.2 123.7 %reduce-scatter.18.cloned.1.call-start = ((), (), s32[]{:S(2)}) async-start(), calls=%async_computation.24 | async-start | bytes 589824 | tf_op jit(solution)/shard_map/reduce_scatter | solution.py:310
  808.5 152.4 %reduce-scatter.20.cloned.1.call-start = ((), (), s32[]{:S(2)}) async-start(), calls=%async_computation.25 | async-start | bytes 9437184 | tf_op jit(solution)/shard_map/reduce_scatter | solution.py:316
  820.5 4.5 copy-start.40
  820.5 4.6 copy-start.39
  820.5 21.2 %all-to-all-start.5 = ((bf16[2,1024,2,128]{3,2,0,1:T(2,128)(2,1)}), bf16[2,1024,2,128]{3,2,0,1:T(2,128)(2,1)}, u32[]{:S(2)}, u32[]{:S(2)}) async-start(bf16[2,1024,2,128]{3,2,0,1:T(2,128)(2,1)} %get-tuple-element.429), calls=%async_computation.5 | async-start | bytes 2097152 | tf_op jit(solution)/shard_map/all_to_all | solution.py:264
  824.9 211.2 %reduce-scatter.14.cloned.1.call-start = ((), (), s32[]{:S(2)}) async-start(), calls=%async_computation.22 | async-start | bytes 9437184 | tf_op jit(solution)/shard_map/reduce_scatter | solution.py:298
  854.0 331.5 %reduce-scatter.22.cloned.1.call-start = ((), (), s32[]{:S(2)}) async-start(), calls=%async_computation.26 | async-start | bytes 25952256 | tf_op jit(solution)/shard_map/reduce_scatter | solution.py:229
  868.0 467.1 %reduce-scatter.24.cloned.1.call-start = ((), (), s32[]{:S(2)}) async-start(), calls=%async_computation.27 | async-start | bytes 25952256 | tf_op jit(solution)/shard_map/reduce_scatter | solution.py:235
  880.8 603.7 %reduce-scatter.26.cloned.1.call-start = ((), (), s32[]{:S(2)}) async-start(), calls=%async_computation.28 | async-start | bytes 25952256 | tf_op jit(solution)/shard_map/reduce_scatter | solution.py:241
  894.8 968.3 %all-reduce.7.cloned.1.call-start = ((), (), s32[]{:S(2)}) async-start(), calls=%async_computation.30 | async-start | bytes 21757952 | tf_op jit(solution)/shard_map/psum | solution.py:329
  1500.5 59.6 %all-to-all-start.6 = ((bf16[2,1024,2,128]{3,2,0,1:T(2,128)(2,1)}), bf16[2,1024,2,128]{3,2,0,1:T(2,128)(2,1)}, u32[]{:S(2)}, u32[]{:S(2)}) async-start(bf16[2,1024,2,128]{3,2,0,1:T(2,128)(2,1)} %get-tuple-element.428), calls=%async_computation.7 | async-start | bytes 2097152 | tf_op jit(solution)/shard_map/all_to_all | solution.py:265
  1505.0 4.7 copy-start.15
  1517.8 7.9 copy-start.21
  1863.2 5.2 copy-start.27
  (45 other events, 75.5 us)
Sparse Core Ops, SparseCore 0:
  9.9 59.3 all-gather.7
  71.2 61.7 all-gather.9
  134.9 140.3 all-gather.11
  277.0 116.4 all-gather.13
  395.2 116.4 all-gather.15
  735.5 33.2 reduce-scatter.27
  772.2 34.1 reduce-scatter.11
  810.0 38.0 reduce-scatter.15
  852.1 34.1 reduce-scatter.17
  889.6 71.2 reduce-scatter.19
  964.8 71.2 reduce-scatter.13
  1039.6 145.8 reduce-scatter.21
  1189.1 145.8 reduce-scatter.23
  1338.5 145.8 reduce-scatter.25
  1487.8 375.3 all-reduce.6
where the time goes:
time: 1900 us; the launch traced here: 1890 us
  waiting for transfers between devices  1270 us (67%)
  matrix products  283 us (15%)
  local copies, waits for them, and re-layouts  114 us (6%)
  blocking collectives  114 us (6%)
  other arithmetic  56.1 us (3%)
  starting transfers between devices  30.3 us (2%)
    psum x1, waiting for transfers between devices, body(): lax.psum(attn_shares[1].astype(jnp.bfloat16), 'dp').astype(jnp.float32)  294 us
    reduce_scatter x1, waiting for transfers between devices, body(): lax.psum_scatter(outer_sum(normed_two, grad_up_pre).astype(jnp.bfloat16),...  150 us
    reduce_scatter x1, waiting for transfers between devices, body(): lax.psum_scatter(outer_sum(hidden, grad_branch).astype(jnp.bfloat16), 'se...  149 us
    reduce_scatter x1, waiting for transfers between devices, body(): lax.psum_scatter(outer_sum(normed_two, grad_gate_pre).astype(jnp.bfloat16...  149 us
    all_gather x1, waiting for transfers between devices, body(): lax.all_gather(w_up, 'seq', axis=0, tiled=True)  105 us
    all_gather x1, waiting for transfers between devices, body(): lax.all_gather(w_down, 'seq', axis=0, tiled=True)  105 us
    reduce_scatter x1, waiting for transfers between devices, body(): lax.psum_scatter(outer_sum(normed_one, grad_q_linear).astype(jnp.bfloat16...  75.2 us
    reduce_scatter x1, waiting for transfers between devices, body(): lax.psum_scatter(outer_sum(attn_seq, grad_proj).astype(jnp.bfloat16), 'se...  66 us
  transfers between devices with their start and end apart: 22, of which 16 were waited for; matrix products, arithmetic and copies ran while one was open for 15% of the time, Pallas kernels for 0%

commit v1 on v0

v1 whole, which is shorter than its diff:
```python
import functools
import math

import jax
import jax.numpy as jnp
from jax import lax
from jax.experimental import pallas as pl
from jax.experimental.pallas import tpu as pltpu
from jax.sharding import PartitionSpec as P

EPSILON = 1e-05
BF = jnp.bfloat16
F32 = jnp.float32
QUERY_ROWS = 256
VMEM_BYTES = 32 * 1024 * 1024


def dot_nn(left, right):
    return jnp.dot(left, right, preferred_element_type=F32)


def dot_nt(left, right):
    return lax.dot_general(left, right, (((1,), (1,)), ((), ())), preferred_element_type=F32)


def dot_tn(left, right):
    return lax.dot_general(left, right, (((0,), (0,)), ((), ())), preferred_element_type=F32)


def is_cube(count):
    return count == 8


def order_key(count):
    rank = lax.axis_index("seq")
    return rank if is_cube(count) else jnp.zeros_like(rank)


def swap(array, bit):
    return lax.ppermute(array, "seq", [(i, i ^ bit) for i in range(8)])


def add_rounded(*terms):
    total = terms[0].astype(F32)
    for term in terms[1:]:
        total = total + term.astype(F32)
    return total.astype(BF)


def gather_pieces(piece, count):
    if not is_cube(count):
        return lax.all_gather(piece, "seq", axis=0, tiled=False)
    half = piece.shape[0] // 2
    from_x = swap(piece, 2)
    from_y = swap(piece, 4)
    from_core = swap(piece, 1)
    far_low = swap(from_x[:half], 4)
    far_high = swap(from_y[half:], 2)
    core_x = swap(from_x, 1)
    core_y = swap(from_y, 1)
    far = jnp.concatenate([far_low, far_high], 0)
    core_far = swap(far, 1)
    return jnp.stack([piece, from_core, from_x, core_x, from_y, core_y, far, core_far], 0)


def scatter_pieces(parts, count):
    if not is_cube(count):
        return lax.psum_scatter(parts, "seq", scatter_dimension=0, tiled=False)
    half = parts.shape[1] // 2
    far = add_rounded(parts[6], swap(parts[7], 1))
    far_x = swap(far[:half], 2)
    far_y = swap(far[half:], 4)
    near_x = add_rounded(parts[2], swap(parts[3], 1))
    near_y = add_rounded(parts[4], swap(parts[5], 1))
    near_y = jnp.concatenate([add_rounded(near_y[:half], far_x), near_y[half:]], 0)
    near_x = jnp.concatenate([near_x[:half], add_rounded(near_x[half:], far_y)], 0)
    got_x = swap(near_x, 2)
    got_y = swap(near_y, 4)
    own = add_rounded(parts[0], swap(parts[1], 1))
    return add_rounded(own, got_x, got_y)


def rows_to_columns(weight):
    return lax.all_to_all(weight, "seq", split_axis=1, concat_axis=0, tiled=True)


def columns_to_rows(weight):
    return lax.all_to_all(weight, "seq", split_axis=0, concat_axis=1, tiled=True)


def load_keys(key_ref, kv_ref, rows_ref, count, head, column):
    chunk = kv_ref.shape[2]
    for place in range(count):
        rows_ref[place * chunk : (place + 1) * chunk, :] = kv_ref[
            place ^ key_ref, 0, :, column * head : (column + 1) * head
        ]


def transpose_rows(rows_ref, turned_ref):
    step = 128
    for start in range(0, rows_ref.shape[0], step):
        turned_ref[:, start : start + step] = (
            rows_ref[start : start + step, :].astype(F32).T.astype(BF)
        )


def masked_scores(keys, queries, limit):
    scores = dot_nt(keys, queries)
    key_pos = lax.broadcasted_iota(jnp.int32, scores.shape, 0)
    return jnp.where(key_pos <= limit, scores, -jnp.inf)


def forward_kernel(
    lengths_ref, key_ref, q_ref, kv_ref, attn_ref, lse_ref, keys, values, values_t
):
    count, _, chunk, _ = q_ref.shape
    head = keys.shape[1]
    total = keys.shape[0]
    block = min(QUERY_ROWS, total)
    per_block = block // chunk
    key = key_ref[0]
    length = lengths_ref[pl.program_id(0)]
    load_keys(key, kv_ref, keys, count, head, 0)
    load_keys(key, kv_ref, values, count, head, 1)
    transpose_rows(values, values_t)
    for start in range(0, total, block):
        limit_row = start + lax.broadcasted_iota(jnp.int32, (1, block), 1)
        limit = jnp.minimum(limit_row, length - 1)
        seen = start + block
        places = [(start // chunk + i) ^ key for i in range(per_block)]
        for h in range(q_ref.shape[3] // head):
            columns = slice(h * head, (h + 1) * head)
            queries = jnp.concatenate([q_ref[p, 0, :, columns] for p in places], 0)
            scores = masked_scores(keys[:seen, :], queries, limit)
            top = jnp.max(scores, 0, keepdims=True)
            weights = jnp.exp(scores - top)
            norm = jnp.sum(weights, 0, keepdims=True)
            mixed = dot_nn(values_t[:, :seen], weights.astype(BF)) / norm
            rows = mixed.T.astype(BF)
            for i, p in enumerate(places):
                attn_ref[p, 0, :, columns] = rows[i * chunk : (i + 1) * chunk]
            lse_ref[0, h : h + 1, start : start + block] = top + jnp.log(norm)


def attend_forward(queries, key_values, lengths, key, head):
    count, seqs, chunk, width = queries.shape
    total = count * chunk
    heads = width // head
    whole = lambda s, *_: (0, s, 0, 0)
    return pl.pallas_call(
        forward_kernel,
        grid_spec=pltpu.PrefetchScalarGridSpec(
            num_scalar_prefetch=2,
            grid=(seqs,),
            in_specs=[
                pl.BlockSpec((count, 1, chunk, width), whole),
                pl.BlockSpec((count, 1, chunk, 2 * head), whole),
            ],
            out_specs=[
                pl.BlockSpec((count, 1, chunk, width), whole),
                pl.BlockSpec((1, heads, total), lambda s, *_: (s, 0, 0)),
            ],
            scratch_shapes=[
                pltpu.VMEM((total, head), BF),
                pltpu.VMEM((total, head), BF),
                pltpu.VMEM((head, total), BF),
            ],
        ),
        out_shape=[
            jax.ShapeDtypeStruct(queries.shape, BF),
            jax.ShapeDtypeStruct((seqs, heads, total), F32),
        ],
        compiler_params=pltpu.CompilerParams(vmem_limit_bytes=VMEM_BYTES),
        cost_estimate=pl.CostEstimate(
            flops=2 * seqs * heads * total * total * head,
            bytes_accessed=4 * queries.size + 2 * key_values.size,
            transcendentals=seqs * heads * total * total // 2,
        ),
    )(lengths, key, queries, key_values)


def second_kernel(
    lengths_ref, key_ref, q_ref, up_ref, kv_ref, dq_ref, dkv_ref, keys, values, keys_t, dk, dv
):
    _, chunk, width = q_ref.shape
    count = kv_ref.shape[0]
    head = keys.shape[1]
    total = keys.shape[0]
    block = min(QUERY_ROWS, total)
    per_block = block // chunk
    key = key_ref[0]
    rank = key_ref[1]
    length = lengths_ref[pl.program_id(0)]
    load_keys(key, kv_ref, keys, count, head, 0)
    load_keys(key, kv_ref, values, count, head, 1)
    transpose_rows(keys, keys_t)
    dk[...] = jnp.zeros_like(dk)
    dv[...] = jnp.zeros_like(dv)
    own = rank * chunk + lax.broadcasted_iota(jnp.int32, (1, block), 1) % chunk
    limit = jnp.minimum(own, length - 1)
    live = rank * chunk + lax.broadcasted_iota(jnp.int32, (chunk, head), 0) < length
    for first in range(0, width // head, per_block):
        spans = [slice((first + i) * head, (first + i + 1) * head) for i in range(per_block)]
        queries = jnp.concatenate([q_ref[0, :, s] for s in spans], 0)
        upstream = jnp.concatenate(
            [jnp.where(live, up_ref[0, :, s].astype(F32), 0.0).astype(BF) for s in spans], 0
        )
        scores = masked_scores(keys[...], queries, limit)
        weights = jnp.exp(scores - jnp.max(scores, 0, keepdims=True))
        probs = weights * (1.0 / jnp.sum(weights, 0, keepdims=True))
        product = probs * dot_nt(values[...], upstream)
        d_scores = (product - probs * jnp.sum(product, 0, keepdims=True)).astype(BF)
        d_queries = dot_nn(keys_t[...], d_scores).T.astype(BF)
        for i, s in enumerate(spans):
            dq_ref[0, :, s] = d_queries[i * chunk : (i + 1) * chunk]
        dk[...] += dot_nn(d_scores, queries)
        dv[...] += dot_nn(probs.astype(BF), upstream)
    for place in range(count):
        rows = slice(place * chunk, (place + 1) * chunk)
        dkv_ref[place ^ key, 0, :, :head] = dk[rows, :]
        dkv_ref[place ^ key, 0, :, head:] = dv[rows, :]


def attend_second(queries, upstream, key_values, lengths, key, head):
    seqs, chunk, width = queries.shape
    count = key_values.shape[0]
    total = count * chunk
    whole = lambda s, *_: (0, s, 0, 0)
    local = pl.BlockSpec((1, chunk, width), lambda s, *_: (s, 0, 0))
    return pl.pallas_call(
        second_kernel,
        grid_spec=pltpu.PrefetchScalarGridSpec(
            num_scalar_prefetch=2,
            grid=(seqs,),
            in_specs=[local, local, pl.BlockSpec((count, 1, chunk, 2 * head), whole)],
            out_specs=[local, pl.BlockSpec((count, 1, chunk, 2 * head), whole)],
            scratch_shapes=[
                pltpu.VMEM((total, head), BF),
                pltpu.VMEM((total, head), BF),
                pltpu.VMEM((head, total), BF),
                pltpu.VMEM((total, head), F32),
                pltpu.VMEM((total, head), F32),
            ],
        ),
        out_shape=[
            jax.ShapeDtypeStruct(queries.shape, BF),
            jax.ShapeDtypeStruct(key_values.shape, F32),
        ],
        compiler_params=pltpu.CompilerParams(vmem_limit_bytes=VMEM_BYTES),
        cost_estimate=pl.CostEstimate(
            flops=20 * seqs * chunk * width * total // 2,
            bytes_accessed=6 * queries.size + 6 * key_values.size,
            transcendentals=seqs * chunk * width * total // head,
        ),
    )(lengths, key, queries, upstream, key_values)


def backward_kernel(
    lengths_ref,
    key_ref,
    q_ref,
    up_ref,
    attn_ref,
    kv_ref,
    lse_ref,
    more_ref,
    dq_ref,
    dkv_ref,
    keys,
    values,
    keys_t,
    dk,
    dv,
):
    count, _, chunk, width = q_ref.shape
    head = keys.shape[1]
    total = keys.shape[0]
    block = min(QUERY_ROWS, total)
    per_block = block // chunk
    key = key_ref[0]
    length = lengths_ref[pl.program_id(0)]
    load_keys(key, kv_ref, keys, count, head, 0)
    load_keys(key, kv_ref, values, count, head, 1)
    transpose_rows(keys, keys_t)
    for place in range(count):
        rows = slice(place * chunk, (place + 1) * chunk)
        dk[rows, :] = more_ref[place ^ key, 0, :, :head]
        dv[rows, :] = more_ref[place ^ key, 0, :, head:]
    for start in range(0, total, block):
        limit_row = start + lax.broadcasted_iota(jnp.int32, (1, block), 1)
        limit = jnp.minimum(limit_row, length - 1)
        seen = start + block
        places = [(start // chunk + i) ^ key for i in range(per_block)]
        for h in range(width // head):
            columns = slice(h * head, (h + 1) * head)
            queries = jnp.concatenate([q_ref[p, 0, :, columns] for p in places], 0)
            upstream = jnp.concatenate([up_ref[p, 0, :, columns] for p in places], 0)
            attn = jnp.concatenate([attn_ref[p, 0, :, columns] for p in places], 0)
            centre = jnp.sum((upstream.astype(F32) * attn.astype(F32)).T, 0, keepdims=True)
            scores = masked_scores(keys[:seen, :], queries, limit)
            probs = jnp.exp(scores - lse_ref[0, h : h + 1, start : start + block])
            d_probs = dot_nt(values[:seen, :], upstream)
            d_scores = (probs * (d_probs - centre)).astype(BF)
            d_queries = dot_nn(keys_t[:, :seen], d_scores).T.astype(BF)
            for i, p in enumerate(places):
                dq_ref[p, 0, :, columns] = d_queries[i * chunk : (i + 1) * chunk]
            dk[:seen, :] += dot_nn(d_scores, queries)
            dv[:seen, :] += dot_nn(probs.astype(BF), upstream)
    for place in range(count):
        rows = slice(place * chunk, (place + 1) * chunk)
        dkv_ref[place ^ key, 0, :, :head] = dk[rows, :].astype(BF)
        dkv_ref[place ^ key, 0, :, head:] = dv[rows, :].astype(BF)


def attend_backward(queries, upstream, attn, key_values, lse, more, lengths, key, head):
    count, seqs, chunk, width = queries.shape
    total = count * chunk
    heads = width // head
    whole = lambda s, *_: (0, s, 0, 0)
    by_head = pl.BlockSpec((count, 1, chunk, width), whole)
    shared = pl.BlockSpec((count, 1, chunk, 2 * head), whole)
    return pl.pallas_call(
        backward_kernel,
        grid_spec=pltpu.PrefetchScalarGridSpec(
            num_scalar_prefetch=2,
            grid=(seqs,),
            in_specs=[
                by_head,
                by_head,
                by_head,
                shared,
                pl.BlockSpec((1, heads, total), lambda s, *_: (s, 0, 0)),
                shared,
            ],
            out_specs=[by_head, shared],
            scratch_shapes=[
                pltpu.VMEM((total, head), BF),
                pltpu.VMEM((total, head), BF),
                pltpu.VMEM((head, total), BF),
                pltpu.VMEM((total, head), F32),
                pltpu.VMEM((total, head), F32),
            ],
        ),
        out_shape=[
            jax.ShapeDtypeStruct(queries.shape, BF),
            jax.ShapeDtypeStruct(key_values.shape, BF),
        ],
        compiler_params=pltpu.CompilerParams(vmem_limit_bytes=VMEM_BYTES),
        cost_estimate=pl.CostEstimate(
            flops=5 * seqs * heads * total * total * head,
            bytes_accessed=8 * queries.size + 8 * key_values.size,
            transcendentals=seqs * heads * total * total // 2,
        ),
    )(lengths, key, queries, upstream, attn, key_values, lse, more)


def rope_tables(positions, head_width):
    half_width = head_width // 2
    spacing = jnp.exp(
        jnp.arange(half_width).astype(F32) * (-2.0 * math.log(10000.0) / head_width)
    )
    angles = positions.astype(F32)[..., None] * spacing
    angles = jnp.concatenate([angles, angles], -1)
    return (jnp.cos(angles), jnp.sin(angles))


def rotate(vector, cosine, sine_table):
    half_width = vector.shape[-1] // 2
    turned = jnp.concatenate([-vector[..., half_width:], vector[..., :half_width]], -1)
    return vector * cosine + turned * sine_table


def rotate_back(gradient, cosine, sine_table):
    half_width = gradient.shape[-1] // 2
    scaled = gradient * sine_table
    turned = jnp.concatenate([scaled[..., half_width:], -scaled[..., :half_width]], -1)
    return gradient * cosine + turned


def rms_scale(values_in):
    return lax.rsqrt(jnp.mean(values_in * values_in, -1, keepdims=True) + EPSILON)


def norm_back(grad_normed, inputs, scale_rows, gain):
    weighted = grad_normed * gain
    cubed = scale_rows * scale_rows * scale_rows
    return scale_rows * weighted - inputs * cubed * jnp.mean(weighted * inputs, -1, keepdims=True)


def body(
    tokens,
    lengths,
    second_queries,
    cotangent,
    second_cotangent,
    gain_attn,
    w_query,
    w_key,
    w_value,
    w_out,
    gain_mlp,
    w_gate,
    w_up,
    w_down,
):
    count = lax.axis_size("seq")
    rank = lax.axis_index("seq")
    key = order_key(count)
    keys_of = jnp.stack([key, rank]).astype(jnp.int32)
    seqs, chunk, width = tokens.shape
    head = w_key.shape[1]
    rows = seqs * chunk
    all_rows = count * rows
    local_heads = w_query.shape[1] // head // count
    scale = 1.0 / math.sqrt(head)
    bf_sum = lambda share: lax.psum(share.astype(BF), "dp").astype(F32)

    gains = lax.all_gather(jnp.stack([gain_attn, gain_mlp]), "seq", axis=1, tiled=True).astype(F32)
    gain_one, gain_two = gains[0], gains[1]
    kv_mat = lax.all_gather(jnp.concatenate([w_key, w_value], 1), "seq", axis=0, tiled=True)
    query_cols = rows_to_columns(w_query)
    gate_cols = rows_to_columns(w_gate)
    up_cols = rows_to_columns(w_up)

    local_pos = rank * chunk + jnp.arange(chunk, dtype=jnp.int32)
    valid = (local_pos[None, :] < lengths[:, None]).astype(F32).reshape(rows, 1)
    owners = jnp.arange(count, dtype=jnp.int32) ^ key
    all_pos = owners[:, None] * chunk + jnp.arange(chunk, dtype=jnp.int32)[None, :]
    cosine, sine_table = rope_tables(all_pos, head)
    cos_kv, sin_kv = cosine[:, None], sine_table[:, None]
    cos_q, sin_q = cosine[:, None, :, None], sine_table[:, None, :, None]
    cos_own, sin_own = rope_tables(local_pos, head)

    inputs = tokens.reshape(rows, width)
    inputs_f = inputs.astype(F32)
    scale_one = rms_scale(inputs_f)
    all_inputs = gather_pieces(inputs, count).reshape(all_rows, width).astype(F32)
    normed_one = (all_inputs * rms_scale(all_inputs) * gain_one).astype(BF)
    q_linear = dot_nn(normed_one, query_cols).reshape(count, seqs, chunk, local_heads, head)
    queries = (rotate(q_linear, cos_q, sin_q) * scale).astype(BF)
    queries = queries.reshape(count, seqs, chunk, local_heads * head)
    kv_linear = dot_nn(normed_one, kv_mat).reshape(count, seqs, chunk, 2 * head)
    key_values = jnp.concatenate(
        [
            rotate(kv_linear[..., :head], cos_kv, sin_kv).astype(BF),
            kv_linear[..., head:].astype(BF),
        ],
        -1,
    )
    attn, lse = attend_forward(queries, key_values, lengths, keys_of, head)
    attn_rows = attn.reshape(all_rows, local_heads * head)
    proj_parts = dot_nn(attn_rows, w_out).astype(BF).reshape(count, rows, width)
    middle = inputs_f + scatter_pieces(proj_parts, count).astype(F32)

    grad_second, dkv_second = attend_second(
        second_queries, second_cotangent, key_values, lengths, keys_of, head
    )

    grad_out = cotangent.reshape(rows, width).astype(F32) * valid
    grad_branch = gather_pieces(grad_out.astype(BF), count).reshape(all_rows, width)
    scale_two = rms_scale(middle)
    normed_two_own = (middle * scale_two * gain_two).astype(BF)
    normed_two = gather_pieces(normed_two_own, count).reshape(all_rows, width)
    gate_pre = dot_nn(normed_two, gate_cols)
    up_pre = dot_nn(normed_two, up_cols)
    sigma = jax.nn.sigmoid(gate_pre)
    silu_gate = gate_pre * sigma
    hidden = (silu_gate * up_pre).astype(BF)
    grad_hidden = dot_nt(grad_branch, w_down)
    grad_gate_pre = (grad_hidden * up_pre * (sigma * (1.0 + gate_pre * (1.0 - sigma)))).astype(BF)
    grad_up_pre = (grad_hidden * silu_gate).astype(BF)
    normed_parts = (dot_nt(grad_gate_pre, gate_cols) + dot_nt(grad_up_pre, up_cols)).astype(BF)
    grad_normed_two = scatter_pieces(normed_parts.reshape(count, rows, width), count).astype(F32)
    grad_middle = grad_out + norm_back(grad_normed_two, middle, scale_two, gain_two)
    down_parts = dot_nn(hidden, w_down).astype(BF).reshape(count, rows, width)
    out = (middle + scatter_pieces(down_parts, count).astype(F32)).astype(BF)

    grad_w_down = bf_sum(dot_tn(hidden, grad_branch))
    grad_w_gate = bf_sum(columns_to_rows(dot_tn(normed_two, grad_gate_pre).astype(BF)))
    grad_w_up = bf_sum(columns_to_rows(dot_tn(normed_two, grad_up_pre).astype(BF)))

    grad_proj = gather_pieces(grad_middle.astype(BF), count).reshape(all_rows, width)
    grad_w_out = bf_sum(dot_tn(attn_rows, grad_proj))
    grad_attn = dot_nt(grad_proj, w_out).astype(BF).reshape(queries.shape)
    grad_q, dkv_parts = attend_backward(
        queries, grad_attn, attn, key_values, lse, dkv_second, lengths, keys_of, head
    )
    grad_q = grad_q.reshape(count, seqs, chunk, local_heads, head).astype(F32) * scale
    grad_q_linear = rotate_back(grad_q, cos_q, sin_q).astype(BF).reshape(all_rows, -1)
    grad_w_query = bf_sum(columns_to_rows(dot_tn(normed_one, grad_q_linear).astype(BF)))
    one_parts = dot_nt(grad_q_linear, query_cols).astype(BF).reshape(count, rows, width)
    dkv_own = scatter_pieces(dkv_parts.reshape(count, rows, 2 * head), count)
    dkv_own = dkv_own.reshape(seqs, chunk, 2 * head)
    grad_k_linear = rotate_back(dkv_own[..., :head].astype(F32), cos_own, sin_own).astype(BF)
    grad_kv_own = jnp.concatenate([grad_k_linear, dkv_own[..., head:]], -1).reshape(rows, 2 * head)
    grad_kv = gather_pieces(grad_kv_own, count).reshape(all_rows, 2 * head)
    own_columns = w_query.shape[0]
    normed_slice = lax.dynamic_slice_in_dim(normed_one, rank * own_columns, own_columns, 1)
    grad_w_kv = bf_sum(dot_tn(normed_slice, grad_kv))
    grad_normed_one = scatter_pieces(one_parts, count).astype(F32) + dot_nt(grad_kv_own, kv_mat)
    grad_tokens = grad_middle + norm_back(grad_normed_one, inputs_f, scale_one, gain_one)

    gain_shares = jnp.stack(
        [
            jnp.sum(grad_normed_one * (inputs_f * scale_one), 0),
            jnp.sum(grad_normed_two * (middle * scale_two), 0),
        ]
    )
    gain_sums = lax.psum(gain_shares, ("seq", "dp"))
    own_gain = gain_attn.shape[0]
    grad_gains = lax.dynamic_slice_in_dim(gain_sums, rank * own_gain, own_gain, 1)

    return (
        out.reshape(tokens.shape),
        grad_tokens.reshape(tokens.shape),
        grad_second,
        grad_gains[0],
        grad_w_query,
        grad_w_kv[:, :head],
        grad_w_kv[:, head:],
        grad_w_out,
        grad_gains[1],
        grad_w_gate,
        grad_w_up,
        grad_w_down,
    )


def solution(mesh):
    return jax.shard_map(
        body,
        mesh=mesh,
        in_specs=(
            P("dp", "seq", None),
            P("dp"),
            P("dp", "seq", None),
            P("dp", "seq", None),
            P("dp", "seq", None),
            P("seq"),
            P("seq", None),
            P("seq", None),
            P("seq", None),
            P("seq", None),
            P("seq"),
            P("seq", None),
            P("seq", None),
            P("seq", None),
        ),
        out_specs=(
            P("dp", "seq", None),
            P("dp", "seq", None),
            P("dp", "seq", None),
            P("seq"),
            P("seq", None),
            P("seq", None),
            P("seq", None),
            P("seq", None),
            P("seq"),
            P("seq", None),
            P("seq", None),
            P("seq", None),
        ),
        check_vma=False,
    )
```

time: 1900 us -> 1090 us (0.57)
  waiting for transfers between devices: 1270 us -> 452 us
  matrix products: 283 us -> 127 us
  starting transfers between devices: 30.3 us -> 93.1 us
  other arithmetic: 56.1 us -> 107 us
  Pallas kernels: 0 us -> 39.6 us
  local copies, waits for them, and re-layouts: 114 us -> 143 us
    reduce_scatter x8 -> x0, waiting for transfers between devices: 625 us -> none  [the longest x1 150 us: body(): lax.psum_scatter(outer_sum(normed_two, grad_up_pre).astype(jnp.bfloat16),...]
    all_gather x5 -> x1, waiting for transfers between devices: 266 us -> 0.01 us  [body(): lax.all_gather(jnp.concatenate([w_key, w_value], 1), 'seq', axis=0, tiled...]
    ppermute x0 -> x80, waiting for transfers between devices: none -> 219 us  [swap(): return lax.ppermute(array, 'seq', [(i, i ^ bit) for i in range(8)])]
    dot_general x41 -> x18, matrix products: 241 us -> 127 us  [the longest x6 44.9 us: dot_tn(): lax.dot_general(left, right, (((0,), (0,)), ((), ())), preferred_element_...]
    psum x1, waiting for transfers between devices: 294 us -> 222 us  [body(): bf_sum = lambda share: lax.psum(share.astype(BF), 'dp').astype(F32)]
    unnamed x112 -> x216, local copies, waits for them, and re-layouts: 16.7 us -> 82.6 us
    ppermute x0 -> x80, starting transfers between devices: none -> 65.7 us  [swap(): return lax.ppermute(array, 'seq', [(i, i ^ bit) for i in range(8)])]
    psum x1, blocking collectives: 14.3 us -> 58.8 us  [body(): gain_sums = lax.psum(gain_shares, ('seq', 'dp'))]
  transfers between devices with their start and end apart: 22 -> 88, of which waited for: 16 -> 26; matrix products, arithmetic and copies ran while one was open for 15% -> 25% of each run, Pallas kernels for 0% -> 4%
where the time goes in v1:
time: 1090 us; the launch traced here: 1080 us
  waiting for transfers between devices  452 us (41%)
  local copies, waits for them, and re-layouts  143 us (13%)
  matrix products  127 us (12%)
  other arithmetic  107 us (10%)
  blocking collectives  105 us (10%)
  starting transfers between devices  93.1 us (9%)
  Pallas kernels  39.6 us (4%)
  between operations  16 us (1%)
    psum x1, waiting for transfers between devices, body(): bf_sum = lambda share: lax.psum(share.astype(BF), 'dp').astype(F32)  222 us
    ppermute x80, waiting for transfers between devices, swap(): return lax.ppermute(array, 'seq', [(i, i ^ bit) for i in range(8)])  219 us
    unnamed x216, local copies, waits for them, and re-layouts  82.6 us
    ppermute x80, starting transfers between devices, swap(): return lax.ppermute(array, 'seq', [(i, i ^ bit) for i in range(8)])  65.7 us
    psum x1, blocking collectives, body(): gain_sums = lax.psum(gain_shares, ('seq', 'dp'))  58.8 us
    all_gather x1, blocking collectives, body(): lax.all_gather(jnp.stack([gain_attn, gain_mlp]), 'seq', axis=1, tiled=True)  46.6 us
    dot_general x6, matrix products, dot_tn(): lax.dot_general(left, right, (((0,), (0,)), ((), ())), preferred_element_...  44.9 us
    dot_general x6, matrix products, dot_nt(): lax.dot_general(left, right, (((1,), (1,)), ((), ())), preferred_element_...  43.9 us
  transfers between devices with their start and end apart: 88, of which 26 were waited for; matrix products, arithmetic and copies ran while one was open for 25% of the time, Pallas kernels for 4%

profile of v1, /device:TPU:0, one launch (start us, length us, event | category | flops | bytes accessed | tf_op | source)
XLA Modules:
  0.0 1083.3 jit_solution(16138326364866171745)
XLA Ops:
  7.2 3.0 collective-permute-start.1
  21.8 4.4 all-to-all-start
  30.2 46.6 %all_gather.6 = bf16[2,2048]{1,0:T(2,128)(2,1)S(1)} all-gather(bf16[2,256]{1,0:T(2,128)(2,1)S(1)} %pad_maximum_fusion.16), channel_id=1, replica_groups=mesh['dp'=4,'seq'=8] {'seq'}, dimensions={1}, use_global_device_ids=true | all-gather | bytes 9216 | tf_op jit(solution)/shard_map/all_gather | solution.py:418
  77.1 3.0 broadcast_multiply_fusion.2
  86.4 4.5 copy.69
  90.9 4.5 copy.71
  99.5 4.6 all-to-all-start.1
  126.7 23.3 %collective-permute-done.5 = bf16[128,2048]{1,0:T(8,128)(2,1)S(1)} collective-permute-done((bf16[128,2048]{1,0:T(8,128)(2,1)S(1)}, bf16[128,2048]{1,0:T(8,128)(2,1)S(1)}, u32[]{:S(2)}, u32[]{:S(2)}) %collective-permute-start.5) | collective-permute-done | bytes 524320 | tf_op jit(solution)/shard_map/ppermute | solution.py:40
  163.4 5.3 fusion.2
  181.7 9.7 shard_map.229
  195.8 3.1 bitcast_dynamic-update-slice_fusion.14
  211.0 4.9 all-to-all-start.2
  225.7 8.7 collective-permute-start.12
  234.5 27.2 %collective-permute-done.14 = bf16[128,2048]{1,0:T(8,128)(2,1)S(1)} collective-permute-done((bf16[128,2048]{1,0:T(8,128)(2,1)S(1)}, bf16[128,2048]{1,0:T(8,128)(2,1)S(1)}, u32[]{:S(2)}, u32[]{:S(2)}) %collective-permute-start.14) | collective-permute-done | bytes 524320 | tf_op jit(solution)/shard_map/ppermute | solution.py:40
  269.0 3.8 copy.84
  277.4 6.4 collective-permute-done.12
  283.8 3.7 collective-permute-done.15
  287.5 3.1 multiply_reduce_fusion.2
  294.7 11.3 %bitcast_convert_fusion = f32[2048,2048]{1,0:T(8,128)} fusion(bf16[8,256,2048]{2,1,0:T(8,128)(2,1)} %copy-done.20), kind=kLoop, calls=%fused_computation.238 | loop fusion | flops 4194304 | bytes 25165824 | tf_op jit(solution)/shard_map/convert_element_type | solution.py:437
  306.0 10.3 collective-permute-done.17
  337.8 11.1 %fusion.66 = f32[2048,704]{0,1:T(8,128)} fusion(bf16[2048,2048]{1,0:T(8,128)(2,1)} %bitcast.308, bf16[2048,704]{0,1:T(8,128)(2,1)S(1)} %bitcast.279), kind=kOutput, calls=%fused_computation.239 | convolution fusion | flops 5905580032 | bytes 17039360 | tf_op jit(solution)/shard_map/dot_general | solution.py:19
  348.9 8.0 fusion.67
  356.9 15.1 %multiply_convert_fusion.4 = (bf16[2048,704]{0,1:T(8,128)(2,1)}, bf16[2048,704]{0,1:T(8,128)(2,1)S(1)}, bf16[2048,704]{0,1:T(8,128)(2,1)}) fusion(f32[2048,704]{0,1:T(8,128)} %fusion.66, f32[2048,704]{0,1:T(8,128)} %fusion.67, bf16[2048,2048]{1,0:T(8,128)(2,1)} %bitcast.58, bf16[704,2048]{1,0:T(8,128)(2,1)S(1)} %copy-done), kind=kOutput, calls=%fused_computation.10 | convolution fusion | flops 5927206912 | bytes 31457280 | tf_op jit(solution)/shard_map/dot_general | solution.py:23
  372.0 10.3 fusion.68
  382.3 11.2 %add_convert_fusion = bf16[2048,2048]{1,0:T(8,128)(2,1)S(1)} fusion(f32[2048,2048]{1,0:T(8,128)} %fusion.68, bf16[2048,704]{0,1:T(8,128)(2,1)} %get-tuple-element.74, bf16[2048,704]{0,1:T(8,128)(2,1)S(1)} %bitcast.282), kind=kOutput, calls=%fused_computation.1 | convolution fusion | flops 5913968640 | bytes 30932992 | tf_op jit(solution)/shard_map/dot_general | solution.py:23
  395.7 3.0 copy-done.30
  399.8 19.7 %shard_map.230 = (bf16[2,128,2048]{2,1,0:T(8,128)(2,1)}, f32[8,2,128,256]{3,2,1,0:T(8,128)S(1)}) custom-call(s32[2]{0:T(128)S(1)} %copy-done.11, s32[2]{0:T(128)S(1)} %pad_add_fusion.key_ref, bf16[2,128,2048]{2,1,0:T(8,128)(2,1)S(1)} %copy-done.12, bf16[2,128,2048]{2,1,0:T(8,128)(2,1)S(1)} %copy-done.13, bf16[8,2,128,256]{3,2,1,0:T(8,128)(2,1)S(1)} %copy-done.7), custom_call_target="tpu_custom_call" | custom-call | flops 5368709120 | bytes 6291456 | tf_op jit(solution)/shard_map/pallas_call | solution.py:230
  421.3 8.8 multiply_convert_fusion
  430.1 5.3 add_convert_fusion.9
  437.1 8.6 convolution_convert_fusion.3
  447.5 4.6 all-to-all-start.5
  457.8 40.0 %collective-permute-done.46 = bf16[128,2048]{1,0:T(8,128)(2,1)S(1)} collective-permute-done((bf16[128,2048]{1,0:T(8,128)(2,1)}, bf16[128,2048]{1,0:T(8,128)(2,1)S(1)}, u32[]{:S(2)}, u32[]{:S(2)}) %collective-permute-start.46) | collective-permute-done | bytes 524320 | tf_op jit(solution)/shard_map/ppermute | solution.py:40
  499.6 8.5 convolution_convert_fusion.4
  509.9 9.9 collective-permute-done.44
  522.4 3.5 fusion.9
  529.0 10.8 convolution_convert_fusion.5
  539.8 10.5 collective-permute-done.49
  553.3 9.1 collective-permute-done.53
  571.4 10.3 shard_map.231
  583.7 3.1 reshape.674
  589.3 3.3 fusion.55
  594.2 3.2 fusion.21
  605.4 7.0 convolution_convert_fusion.7
  612.4 4.4 all-to-all-start.3
  621.5 11.2 %all-to-all-done.3 = bf16[8,256,256]{2,1,0:T(8,128)(2,1)} async-done(((bf16[8,256,256]{2,1,0:T(8,128)(2,1)}), bf16[8,256,256]{2,1,0:T(8,128)(2,1)}, u32[]{:S(2)}, u32[]{:S(2)}) %all-to-all-start.3) | async-done | bytes 1048608 | tf_op jit(solution)/shard_map/all_to_all | solution.py:88
  632.7 4.4 all-to-all-start.4
  637.2 7.0 convolution_convert_fusion.6
  648.3 24.2 %collective-permute-done.77 = bf16[128,256]{1,0:T(8,128)(2,1)S(1)} collective-permute-done((bf16[128,256]{1,0:T(8,128)(2,1)S(1)}, bf16[128,256]{1,0:T(8,128)(2,1)S(1)}, u32[]{:S(2)}, u32[]{:S(2)}) %collective-permute-start.77) | collective-permute-done | bytes 65568 | tf_op jit(solution)/shard_map/ppermute | solution.py:40
  674.0 3.1 convolution_convert_fusion.9
  679.5 9.0 convolution_convert_fusion.1
  690.8 4.4 convolution_convert_fusion
  697.7 4.6 add_convert_fusion.15
  713.7 4.7 collective-permute-done.27
  721.3 7.6 collective-permute-done.59
  731.8 5.6 collective-permute-done.62
  744.1 15.7 %collective-permute-done.60 = bf16[256,2048]{1,0:T(8,128)(2,1)S(1)} collective-permute-done((bf16[256,2048]{1,0:T(8,128)(2,1)S(1)}, bf16[256,2048]{1,0:T(8,128)(2,1)S(1)}, u32[]{:S(2)}, u32[]{:S(2)}) %collective-permute-start.60) | collective-permute-done | bytes 1048608 | tf_op jit(solution)/shard_map/ppermute | solution.py:40
  759.8 3.9 collective-permute-done.63
  763.7 3.6 fusion.15
  767.4 58.8 %psum.49 = f32[2,2048]{1,0:T(2,128)S(1)} all-reduce(f32[2,2048]{1,0:T(2,128)S(1)} %pad_maximum_fusion.15), channel_id=1, replica_groups=mesh['dp'=4,'seq'=8] {'seq','dp'}, use_global_device_ids=true, to_apply=%region_7.0 | all-reduce | flops 4096 | bytes 32768 | tf_op jit(solution)/shard_map/psum | solution.py:509
  826.9 6.4 fusion.12
  833.3 222.4 %all-reduce.3.cloned.1.call-done = (bf16[256,256]{1,0:T(8,128)(2,1)}, bf16[256,5632]{0,1:T(8,128)(2,1)}, bf16[256,5632]{0,1:T(8,128)(2,1)}, bf16[256,2048]{1,0:T...) async-done(((bf16[256,256]{1,0:T(8,128)(2,1)}, bf16[256,5632]{0,1:T(8,128)(2,1)}, bf16[256,5632]{0,1:T(8,128)(2,1)}, bf16[256,2048]{1,0:T(8,128)(2,1)}, ...) | async-done | bytes 10878992 | tf_op jit(solution)/shard_map/psum | solution.py:416
  1055.7 5.1 convert_element_type.764
  1060.8 5.1 copy.76
  1065.9 5.1 copy.77
  (490 shorter events, 234.7 us)
Async XLA Ops:
  7.2 156.2 %all-gather.2.cloned.1.call-start = ((), (), s32[]{:S(2)}) async-start(), calls=%async_computation.6 | async-start | bytes 1179648 | tf_op jit(solution)/shard_map/all_gather | solution.py:420
  7.2 99.2 %collective-permute-start.1 = (bf16[256,2048]{1,0:T(8,128)(2,1)}, bf16[256,2048]{1,0:T(8,128)(2,1)}, u32[]{:S(2)}, u32[]{:S(2)}) collective-permute-start(bf16[256,2048]{1,0:T(8,128)(2,1)} %bitcast.258), channel_id=1, source_target_pairs={{0,2},{1,3},{2,0},{3,1},{4,6},{5,7},{6,4},{7,5},{8,10},{9,11},{10,... | collective-permute-start | bytes 3145736 | tf_op jit(solution)/shard_map/ppermute | solution.py:40
  10.2 102.0 %collective-permute-start = (bf16[256,2048]{1,0:T(8,128)(2,1)}, bf16[256,2048]{1,0:T(8,128)(2,1)}, u32[]{:S(2)}, u32[]{:S(2)}) collective-permute-start(bf16[256,2048]{1,0:T(8,128)(2,1)} %bitcast.259), channel_id=1, source_target_pairs={{0,1},{1,0},{2,3},{3,2},{4,5},{5,4},{6,7},{7,6},{8,9},{9,8},{10,11... | collective-permute-start | bytes 3145736 | tf_op jit(solution)/shard_map/ppermute | solution.py:40
  10.2 99.3 %collective-permute-start.3 = (bf16[256,2048]{1,0:T(8,128)(2,1)}, bf16[256,2048]{1,0:T(8,128)(2,1)}, u32[]{:S(2)}, u32[]{:S(2)}) collective-permute-start(bf16[256,2048]{1,0:T(8,128)(2,1)} %bitcast.260), channel_id=1, source_target_pairs={{0,4},{1,5},{2,6},{3,7},{4,0},{5,1},{6,2},{7,3},{8,12},{9,13},{10,... | collective-permute-start | bytes 3145736 | tf_op jit(solution)/shard_map/ppermute | solution.py:40
  14.9 104.3 %collective-permute-start.33 = (bf16[256,2048]{1,0:T(8,128)(2,1)}, bf16[256,2048]{1,0:T(8,128)(2,1)}, u32[]{:S(2)}, u32[]{:S(2)}) collective-permute-start(bf16[256,2048]{1,0:T(8,128)(2,1)} %fusion.23), channel_id=1, source_target_pairs={{0,2},{1,3},{2,0},{3,1},{4,6},{5,7},{6,4},{7,5},{8,10},{9,11},{10,... | collective-permute-start | bytes 3145736 | tf_op jit(solution)/shard_map/ppermute | solution.py:40
  15.5 106.3 %collective-permute-start.35 = (bf16[256,2048]{1,0:T(8,128)(2,1)}, bf16[256,2048]{1,0:T(8,128)(2,1)}, u32[]{:S(2)}, u32[]{:S(2)}) collective-permute-start(bf16[256,2048]{1,0:T(8,128)(2,1)} %fusion.23), channel_id=1, source_target_pairs={{0,4},{1,5},{2,6},{3,7},{4,0},{5,1},{6,2},{7,3},{8,12},{9,13},{10,... | collective-permute-start | bytes 3145736 | tf_op jit(solution)/shard_map/ppermute | solution.py:40
  21.8 77.8 %all-to-all-start = ((bf16[256,8,256]{2,0,1:T(8,128)(2,1)}), bf16[256,8,256]{2,0,1:T(8,128)(2,1)}, u32[]{:S(2)}, u32[]{:S(2)}) async-start(bf16[256,8,256]{2,0,1:T(8,128)(2,1)} %copy.64), calls=%async_computation | async-start | bytes 2097152 | tf_op jit(solution)/shard_map/all_to_all | solution.py:84
  99.5 111.5 %all-to-all-start.1 = ((bf16[256,8,704]{0,2,1:T(8,128)(2,1)}), bf16[256,8,704]{0,2,1:T(8,128)(2,1)}, u32[]{:S(2)}, u32[]{:S(2)}) async-start(bf16[256,8,704]{0,2,1:T(8,128)(2,1)} %bitcast.267), calls=%async_computation.1 | async-start | bytes 5767168 | tf_op jit(solution)/shard_map/all_to_all | solution.py:84
  107.5 42.4 %collective-permute-start.5 = (bf16[128,2048]{1,0:T(8,128)(2,1)S(1)}, bf16[128,2048]{1,0:T(8,128)(2,1)S(1)}, u32[]{:S(2)}, u32[]{:S(2)}) collective-permute-start(bf16[128,2048]{1,0:T(8,128)(2,1)S(1)} %slice.435), channel_id=1, source_target_pairs={{0,4},{1,5},{2,6},{3,7},{4,0},{5,1},{6,2},{7,3},{8,12},{9,13},{10,... | collective-permute-start | bytes 1572872 | tf_op jit(solution)/shard_map/ppermute | solution.py:40
  110.7 40.3 %collective-permute-start.6 = (bf16[128,2048]{1,0:T(8,128)(2,1)S(1)}, bf16[128,2048]{1,0:T(8,128)(2,1)S(1)}, u32[]{:S(2)}, u32[]{:S(2)}) collective-permute-start(bf16[128,2048]{1,0:T(8,128)(2,1)S(1)} %slice.436), channel_id=1, source_target_pairs={{0,2},{1,3},{2,0},{3,1},{4,6},{5,7},{6,4},{7,5},{8,10},{9,11},{10,... | collective-permute-start | bytes 1572872 | tf_op jit(solution)/shard_map/ppermute | solution.py:40
  112.2 38.9 %collective-permute-start.2 = (bf16[256,2048]{1,0:T(8,128)(2,1)}, bf16[256,2048]{1,0:T(8,128)(2,1)S(1)}, u32[]{:S(2)}, u32[]{:S(2)}) collective-permute-start(bf16[256,2048]{1,0:T(8,128)(2,1)} %collective-permute-done.1), channel_id=1, source_target_pairs={{0,1},{1,0},{2,3},{3,2},{4,5},{5,4},{6,7},{7,6},{8,9},{9,8},{10,11... | collective-permute-start | bytes 3145736 | tf_op jit(solution)/shard_map/ppermute | solution.py:40
  119.3 76.5 %collective-permute-start.32 = (bf16[256,2048]{1,0:T(8,128)(2,1)}, bf16[256,2048]{1,0:T(8,128)(2,1)}, u32[]{:S(2)}, u32[]{:S(2)}) collective-permute-start(bf16[256,2048]{1,0:T(8,128)(2,1)} %fusion.23), channel_id=1, source_target_pairs={{0,1},{1,0},{2,3},{3,2},{4,5},{5,4},{6,7},{7,6},{8,9},{9,8},{10,11... | collective-permute-start | bytes 3145736 | tf_op jit(solution)/shard_map/ppermute | solution.py:40
  121.8 79.4 %collective-permute-start.37 = (bf16[128,2048]{1,0:T(8,128)(2,1)}, bf16[128,2048]{1,0:T(8,128)(2,1)}, u32[]{:S(2)}, u32[]{:S(2)}) collective-permute-start(bf16[128,2048]{1,0:T(8,128)(2,1)} %slice.475), channel_id=1, source_target_pairs={{0,4},{1,5},{2,6},{3,7},{4,0},{5,1},{6,2},{7,3},{8,12},{9,13},{10,... | collective-permute-start | bytes 1572872 | tf_op jit(solution)/shard_map/ppermute | solution.py:40
  149.9 53.5 %collective-permute-start.38 = (bf16[128,2048]{1,0:T(8,128)(2,1)}, bf16[128,2048]{1,0:T(8,128)(2,1)}, u32[]{:S(2)}, u32[]{:S(2)}) collective-permute-start(bf16[128,2048]{1,0:T(8,128)(2,1)} %slice.476), channel_id=1, source_target_pairs={{0,2},{1,3},{2,0},{3,1},{4,6},{5,7},{6,4},{7,5},{8,10},{9,11},{10,... | collective-permute-start | bytes 1572872 | tf_op jit(solution)/shard_map/ppermute | solution.py:40
  203.4 61.0 %collective-permute-start.36 = (bf16[256,2048]{1,0:T(8,128)(2,1)}, bf16[256,2048]{1,0:T(8,128)(2,1)}, u32[]{:S(2)}, u32[]{:S(2)}) collective-permute-start(bf16[256,2048]{1,0:T(8,128)(2,1)} %collective-permute-done.35), channel_id=1, source_target_pairs={{0,1},{1,0},{2,3},{3,2},{4,5},{5,4},{6,7},{7,6},{8,9},{9,8},{10,11... | collective-permute-start | bytes 3145736 | tf_op jit(solution)/shard_map/ppermute | solution.py:40
  205.5 69.6 %collective-permute-start.39 = (bf16[256,2048]{1,0:T(8,128)(2,1)}, bf16[256,2048]{1,0:T(8,128)(2,1)}, u32[]{:S(2)}, u32[]{:S(2)}) collective-permute-start(bf16[256,2048]{1,0:T(8,128)(2,1)} %constant_dynamic-update-slice_fusion.11), channel_id=1, source_target_pairs={{0,1},{1,0},{2,3},{3,2},{4,5},{5,4},{6,7},{7,6},{8,9},{9,8},{10,11... | collective-permute-start | bytes 3145736 | tf_op jit(solution)/shard_map/ppermute | solution.py:40
  209.5 15.0 %collective-permute-start.11 = (bf16[128,2048]{1,0:T(8,128)(2,1)}, bf16[128,2048]{1,0:T(8,128)(2,1)S(1)}, u32[]{:S(2)}, u32[]{:S(2)}) collective-permute-start(bf16[128,2048]{1,0:T(8,128)(2,1)} %get-tuple-element.127), channel_id=1, source_target_pairs={{0,4},{1,5},{2,6},{3,7},{4,0},{5,1},{6,2},{7,3},{8,12},{9,13},{10,... | collective-permute-start | bytes 1572872 | tf_op jit(solution)/shard_map/ppermute | solution.py:40
  211.0 61.8 %all-to-all-start.2 = ((bf16[256,8,704]{0,2,1:T(8,128)(2,1)}), bf16[256,8,704]{0,2,1:T(8,128)(2,1)}, u32[]{:S(2)}, u32[]{:S(2)}) async-start(bf16[256,8,704]{0,2,1:T(8,128)(2,1)} %bitcast.265), calls=%async_computation.2 | async-start | bytes 5767168 | tf_op jit(solution)/shard_map/all_to_all | solution.py:84
  218.4 59.0 %collective-permute-start.8 = (bf16[256,2048]{1,0:T(8,128)(2,1)}, bf16[256,2048]{1,0:T(8,128)(2,1)}, u32[]{:S(2)}, u32[]{:S(2)}) collective-permute-start(bf16[256,2048]{1,0:T(8,128)(2,1)} %get-tuple-element.98), channel_id=1, source_target_pairs={{0,1},{1,0},{2,3},{3,2},{4,5},{5,4},{6,7},{7,6},{8,9},{9,8},{10,11... | collective-permute-start | bytes 3145736 | tf_op jit(solution)/shard_map/ppermute | solution.py:40
  219.9 41.7 %collective-permute-start.14 = (bf16[128,2048]{1,0:T(8,128)(2,1)S(1)}, bf16[128,2048]{1,0:T(8,128)(2,1)S(1)}, u32[]{:S(2)}, u32[]{:S(2)}) collective-permute-start(bf16[128,2048]{1,0:T(8,128)(2,1)S(1)} %copy-done.56), channel_id=1, source_target_pairs={{0,2},{1,3},{2,0},{3,1},{4,6},{5,7},{6,4},{7,5},{8,10},{9,11},{10,... | collective-permute-start | bytes 1572872 | tf_op jit(solution)/shard_map/ppermute | solution.py:40
  225.7 58.1 %collective-permute-start.12 = (bf16[256,2048]{1,0:T(8,128)(2,1)}, bf16[256,2048]{1,0:T(8,128)(2,1)}, u32[]{:S(2)}, u32[]{:S(2)}) collective-permute-start(bf16[256,2048]{1,0:T(8,128)(2,1)} %pad_maximum_fusion.1), channel_id=1, source_target_pairs={{0,2},{1,3},{2,0},{3,1},{4,6},{5,7},{6,4},{7,5},{8,10},{9,11},{10,... | collective-permute-start | bytes 3145736 | tf_op jit(solution)/shard_map/ppermute | solution.py:40
  262.9 24.6 %collective-permute-start.15 = (bf16[256,2048]{1,0:T(8,128)(2,1)}, bf16[256,2048]{1,0:T(8,128)(2,1)}, u32[]{:S(2)}, u32[]{:S(2)}) collective-permute-start(bf16[256,2048]{1,0:T(8,128)(2,1)} %pad_maximum_fusion.2), channel_id=1, source_target_pairs={{0,4},{1,5},{2,6},{3,7},{4,0},{5,1},{6,2},{7,3},{8,12},{9,13},{10,... | collective-permute-start | bytes 3145736 | tf_op jit(solution)/shard_map/ppermute | solution.py:40
  292.7 23.7 %collective-permute-start.17 = (bf16[256,2048]{1,0:T(8,128)(2,1)}, bf16[256,2048]{1,0:T(8,128)(2,1)}, u32[]{:S(2)}, u32[]{:S(2)}) collective-permute-start(bf16[256,2048]{1,0:T(8,128)(2,1)} %get-tuple-element.151), channel_id=1, source_target_pairs={{0,2},{1,3},{2,0},{3,1},{4,6},{5,7},{6,4},{7,5},{8,10},{9,11},{10,... | collective-permute-start | bytes 3145736 | tf_op jit(solution)/shard_map/ppermute | solution.py:40
  293.2 25.7 %collective-permute-start.19 = (bf16[256,2048]{1,0:T(8,128)(2,1)}, bf16[256,2048]{1,0:T(8,128)(2,1)}, u32[]{:S(2)}, u32[]{:S(2)}) collective-permute-start(bf16[256,2048]{1,0:T(8,128)(2,1)} %get-tuple-element.151), channel_id=1, source_target_pairs={{0,4},{1,5},{2,6},{3,7},{4,0},{5,1},{6,2},{7,3},{8,12},{9,13},{10,... | collective-permute-start | bytes 3145736 | tf_op jit(solution)/shard_map/ppermute | solution.py:40
  294.7 26.5 %collective-permute-start.16 = (bf16[256,2048]{1,0:T(8,128)(2,1)}, bf16[256,2048]{1,0:T(8,128)(2,1)}, u32[]{:S(2)}, u32[]{:S(2)}) collective-permute-start(bf16[256,2048]{1,0:T(8,128)(2,1)} %get-tuple-element.151), channel_id=1, source_target_pairs={{0,1},{1,0},{2,3},{3,2},{4,5},{5,4},{6,7},{7,6},{8,9},{9,8},{10,11... | collective-permute-start | bytes 3145736 | tf_op jit(solution)/shard_map/ppermute | solution.py:40
  317.4 11.3 %collective-permute-start.21 = (bf16[128,2048]{1,0:T(8,128)(2,1)S(1)}, bf16[128,2048]{1,0:T(8,128)(2,1)S(1)}, u32[]{:S(2)}, u32[]{:S(2)}) collective-permute-start(bf16[128,2048]{1,0:T(8,128)(2,1)S(1)} %slice.459), channel_id=1, source_target_pairs={{0,4},{1,5},{2,6},{3,7},{4,0},{5,1},{6,2},{7,3},{8,12},{9,13},{10,... | collective-permute-start | bytes 1572872 | tf_op jit(solution)/shard_map/ppermute | solution.py:40
  320.1 11.0 %collective-permute-start.22 = (bf16[128,2048]{1,0:T(8,128)(2,1)S(1)}, bf16[128,2048]{1,0:T(8,128)(2,1)S(1)}, u32[]{:S(2)}, u32[]{:S(2)}) collective-permute-start(bf16[128,2048]{1,0:T(8,128)(2,1)S(1)} %slice.460), channel_id=1, source_target_pairs={{0,2},{1,3},{2,0},{3,1},{4,6},{5,7},{6,4},{7,5},{8,10},{9,11},{10,... | collective-permute-start | bytes 1572872 | tf_op jit(solution)/shard_map/ppermute | solution.py:40
  320.7 13.9 %collective-permute-start.20 = (bf16[256,2048]{1,0:T(8,128)(2,1)}, bf16[256,2048]{1,0:T(8,128)(2,1)S(1)}, u32[]{:S(2)}, u32[]{:S(2)}) collective-permute-start(bf16[256,2048]{1,0:T(8,128)(2,1)} %collective-permute-done.19), channel_id=1, source_target_pairs={{0,1},{1,0},{2,3},{3,2},{4,5},{5,4},{6,7},{7,6},{8,9},{9,8},{10,11... | collective-permute-start | bytes 3145736 | tf_op jit(solution)/shard_map/ppermute | solution.py:40
  398.8 31.4 %collective-permute-start.41 = (bf16[256,2048]{1,0:T(8,128)(2,1)}, bf16[256,2048]{1,0:T(8,128)(2,1)S(1)}, u32[]{:S(2)}, u32[]{:S(2)}) collective-permute-start(bf16[256,2048]{1,0:T(8,128)(2,1)} %get-tuple-element.87), channel_id=1, source_target_pairs={{0,1},{1,0},{2,3},{3,2},{4,5},{5,4},{6,7},{7,6},{8,9},{9,8},{10,11... | collective-permute-start | bytes 3145736 | tf_op jit(solution)/shard_map/ppermute | solution.py:40
  399.3 30.9 %collective-permute-start.42 = (bf16[256,2048]{1,0:T(8,128)(2,1)}, bf16[256,2048]{1,0:T(8,128)(2,1)}, u32[]{:S(2)}, u32[]{:S(2)}) collective-permute-start(bf16[256,2048]{1,0:T(8,128)(2,1)} %get-tuple-element.86), channel_id=1, source_target_pairs={{0,1},{1,0},{2,3},{3,2},{4,5},{5,4},{6,7},{7,6},{8,9},{9,8},{10,11... | collective-permute-start | bytes 3145736 | tf_op jit(solution)/shard_map/ppermute | solution.py:40
  399.3 30.9 %collective-permute-start.45 = (bf16[256,2048]{1,0:T(8,128)(2,1)}, bf16[256,2048]{1,0:T(8,128)(2,1)}, u32[]{:S(2)}, u32[]{:S(2)}) collective-permute-start(bf16[256,2048]{1,0:T(8,128)(2,1)} %get-tuple-element.85), channel_id=1, source_target_pairs={{0,1},{1,0},{2,3},{3,2},{4,5},{5,4},{6,7},{7,6},{8,9},{9,8},{10,11... | collective-permute-start | bytes 3145736 | tf_op jit(solution)/shard_map/ppermute | solution.py:40
  436.5 19.9 %collective-permute-start.43 = (bf16[128,2048]{1,0:T(8,128)(2,1)}, bf16[128,2048]{1,0:T(8,128)(2,1)S(1)}, u32[]{:S(2)}, u32[]{:S(2)}) collective-permute-start(bf16[128,2048]{1,0:T(8,128)(2,1)} %get-tuple-element.123), channel_id=1, source_target_pairs={{0,4},{1,5},{2,6},{3,7},{4,0},{5,1},{6,2},{7,3},{8,12},{9,13},{10,... | collective-permute-start | bytes 1572872 | tf_op jit(solution)/shard_map/ppermute | solution.py:40
  445.6 64.3 %collective-permute-start.40 = (bf16[256,2048]{1,0:T(8,128)(2,1)}, bf16[256,2048]{1,0:T(8,128)(2,1)}, u32[]{:S(2)}, u32[]{:S(2)}) collective-permute-start(bf16[256,2048]{1,0:T(8,128)(2,1)} %get-tuple-element.84), channel_id=1, source_target_pairs={{0,1},{1,0},{2,3},{3,2},{4,5},{5,4},{6,7},{7,6},{8,9},{9,8},{10,11... | collective-permute-start | bytes 3145736 | tf_op jit(solution)/shard_map/ppermute | solution.py:40
  447.5 164.9 %all-to-all-start.5 = ((bf16[8,256,704]{1,2,0:T(8,128)(2,1)}), bf16[8,256,704]{1,2,0:T(8,128)(2,1)}, u32[]{:S(2)}, u32[]{:S(2)}) async-start(bf16[8,256,704]{1,2,0:T(8,128)(2,1)} %bitcast.266), calls=%async_computation.5 | async-start | bytes 5767168 | tf_op jit(solution)/shard_map/all_to_all | solution.py:88
  453.3 44.5 %collective-permute-start.46 = (bf16[128,2048]{1,0:T(8,128)(2,1)}, bf16[128,2048]{1,0:T(8,128)(2,1)S(1)}, u32[]{:S(2)}, u32[]{:S(2)}) collective-permute-start(bf16[128,2048]{1,0:T(8,128)(2,1)} %get-tuple-element.124), channel_id=1, source_target_pairs={{0,2},{1,3},{2,0},{3,1},{4,6},{5,7},{6,4},{7,5},{8,10},{9,11},{10,... | collective-permute-start | bytes 1572872 | tf_op jit(solution)/shard_map/ppermute | solution.py:40
  457.7 62.2 %collective-permute-start.44 = (bf16[256,2048]{1,0:T(8,128)(2,1)S(1)}, bf16[256,2048]{1,0:T(8,128)(2,1)S(1)}, u32[]{:S(2)}, u32[]{:S(2)}) collective-permute-start(bf16[256,2048]{1,0:T(8,128)(2,1)S(1)} %pad_maximum_fusion.5), channel_id=1, source_target_pairs={{0,2},{1,3},{2,0},{3,1},{4,6},{5,7},{6,4},{7,5},{8,10},{9,11},{10,... | collective-permute-start | bytes 3145736 | tf_op jit(solution)/shard_map/ppermute | solution.py:40
  498.1 24.4 %collective-permute-start.47 = (bf16[256,2048]{1,0:T(8,128)(2,1)S(1)}, bf16[256,2048]{1,0:T(8,128)(2,1)S(1)}, u32[]{:S(2)}, u32[]{:S(2)}) collective-permute-start(bf16[256,2048]{1,0:T(8,128)(2,1)S(1)} %pad_maximum_fusion.6), channel_id=1, source_target_pairs={{0,4},{1,5},{2,6},{3,7},{4,0},{5,1},{6,2},{7,3},{8,12},{9,13},{10,... | collective-permute-start | bytes 3145736 | tf_op jit(solution)/shard_map/ppermute | solution.py:40
  526.9 23.4 %collective-permute-start.49 = (bf16[256,2048]{1,0:T(8,128)(2,1)S(1)}, bf16[256,2048]{1,0:T(8,128)(2,1)S(1)}, u32[]{:S(2)}, u32[]{:S(2)}) collective-permute-start(bf16[256,2048]{1,0:T(8,128)(2,1)S(1)} %get-tuple-element.153), channel_id=1, source_target_pairs={{0,2},{1,3},{2,0},{3,1},{4,6},{5,7},{6,4},{7,5},{8,10},{9,11},{10,... | collective-permute-start | bytes 3145736 | tf_op jit(solution)/shard_map/ppermute | solution.py:40
  527.6 24.3 %collective-permute-start.51 = (bf16[256,2048]{1,0:T(8,128)(2,1)S(1)}, bf16[256,2048]{1,0:T(8,128)(2,1)S(1)}, u32[]{:S(2)}, u32[]{:S(2)}) collective-permute-start(bf16[256,2048]{1,0:T(8,128)(2,1)S(1)} %get-tuple-element.153), channel_id=1, source_target_pairs={{0,4},{1,5},{2,6},{3,7},{4,0},{5,1},{6,2},{7,3},{8,12},{9,13},{10,... | collective-permute-start | bytes 3145736 | tf_op jit(solution)/shard_map/ppermute | solution.py:40
  529.0 24.1 %collective-permute-start.48 = (bf16[256,2048]{1,0:T(8,128)(2,1)S(1)}, bf16[256,2048]{1,0:T(8,128)(2,1)S(1)}, u32[]{:S(2)}, u32[]{:S(2)}) collective-permute-start(bf16[256,2048]{1,0:T(8,128)(2,1)S(1)} %get-tuple-element.153), channel_id=1, source_target_pairs={{0,1},{1,0},{2,3},{3,2},{4,5},{5,4},{6,7},{7,6},{8,9},{9,8},{10,11... | collective-permute-start | bytes 3145736 | tf_op jit(solution)/shard_map/ppermute | solution.py:40
  550.3 12.1 %collective-permute-start.53 = (bf16[128,2048]{1,0:T(8,128)(2,1)S(1)}, bf16[128,2048]{1,0:T(8,128)(2,1)S(1)}, u32[]{:S(2)}, u32[]{:S(2)}) collective-permute-start(bf16[128,2048]{1,0:T(8,128)(2,1)S(1)} %slice.491), channel_id=1, source_target_pairs={{0,4},{1,5},{2,6},{3,7},{4,0},{5,1},{6,2},{7,3},{8,12},{9,13},{10,... | collective-permute-start | bytes 1572872 | tf_op jit(solution)/shard_map/ppermute | solution.py:40
  593.4 23.3 %collective-permute-start.64 = (bf16[256,256]{1,0:T(8,128)(2,1)S(1)}, bf16[256,256]{1,0:T(8,128)(2,1)S(1)}, u32[]{:S(2)}, u32[]{:S(2)}) collective-permute-start(bf16[256,256]{1,0:T(8,128)(2,1)S(1)} %bitcast.312), channel_id=1, source_target_pairs={{0,1},{1,0},{2,3},{3,2},{4,5},{5,4},{6,7},{7,6},{8,9},{9,8},{10,11... | collective-permute-start | bytes 393224 | tf_op jit(solution)/shard_map/ppermute | solution.py:40
  602.5 14.3 %collective-permute-start.68 = (bf16[256,256]{1,0:T(8,128)(2,1)}, bf16[256,256]{1,0:T(8,128)(2,1)S(1)}, u32[]{:S(2)}, u32[]{:S(2)}) collective-permute-start(bf16[256,256]{1,0:T(8,128)(2,1)} %pad_maximum_fusion.11), channel_id=1, source_target_pairs={{0,2},{1,3},{2,0},{3,1},{4,6},{5,7},{6,4},{7,5},{8,10},{9,11},{10,... | collective-permute-start | bytes 393224 | tf_op jit(solution)/shard_map/ppermute | solution.py:40
  603.8 13.0 %collective-permute-start.71 = (bf16[256,256]{1,0:T(8,128)(2,1)}, bf16[256,256]{1,0:T(8,128)(2,1)}, u32[]{:S(2)}, u32[]{:S(2)}) collective-permute-start(bf16[256,256]{1,0:T(8,128)(2,1)} %pad_maximum_fusion.12), channel_id=1, source_target_pairs={{0,4},{1,5},{2,6},{3,7},{4,0},{5,1},{6,2},{7,3},{8,12},{9,13},{10,... | collective-permute-start | bytes 393224 | tf_op jit(solution)/shard_map/ppermute | solution.py:40
  612.4 20.3 %all-to-all-start.3 = ((bf16[8,256,256]{2,1,0:T(8,128)(2,1)}), bf16[8,256,256]{2,1,0:T(8,128)(2,1)}, u32[]{:S(2)}, u32[]{:S(2)}) async-start(bf16[8,256,256]{2,1,0:T(8,128)(2,1)} %bitcast.293), calls=%async_computation.3 | async-start | bytes 2097152 | tf_op jit(solution)/shard_map/all_to_all | solution.py:88
  618.0 26.2 %collective-permute-start.73 = (bf16[256,256]{1,0:T(8,128)(2,1)S(1)}, bf16[256,256]{1,0:T(8,128)(2,1)S(1)}, u32[]{:S(2)}, u32[]{:S(2)}) collective-permute-start(bf16[256,256]{1,0:T(8,128)(2,1)S(1)} %bitcast.287), channel_id=1, source_target_pairs={{0,2},{1,3},{2,0},{3,1},{4,6},{5,7},{6,4},{7,5},{8,10},{9,11},{10,... | collective-permute-start | bytes 393224 | tf_op jit(solution)/shard_map/ppermute | solution.py:40
  620.0 26.2 %collective-permute-start.75 = (bf16[256,256]{1,0:T(8,128)(2,1)S(1)}, bf16[256,256]{1,0:T(8,128)(2,1)S(1)}, u32[]{:S(2)}, u32[]{:S(2)}) collective-permute-start(bf16[256,256]{1,0:T(8,128)(2,1)S(1)} %bitcast.288), channel_id=1, source_target_pairs={{0,4},{1,5},{2,6},{3,7},{4,0},{5,1},{6,2},{7,3},{8,12},{9,13},{10,... | collective-permute-start | bytes 393224 | tf_op jit(solution)/shard_map/ppermute | solution.py:40
  621.5 26.8 %collective-permute-start.72 = (bf16[256,256]{1,0:T(8,128)(2,1)S(1)}, bf16[256,256]{1,0:T(8,128)(2,1)S(1)}, u32[]{:S(2)}, u32[]{:S(2)}) collective-permute-start(bf16[256,256]{1,0:T(8,128)(2,1)S(1)} %bitcast.289), channel_id=1, source_target_pairs={{0,1},{1,0},{2,3},{3,2},{4,5},{5,4},{6,7},{7,6},{8,9},{9,8},{10,11... | collective-permute-start | bytes 393224 | tf_op jit(solution)/shard_map/ppermute | solution.py:40
  632.7 46.8 %all-to-all-start.4 = ((bf16[8,256,704]{1,2,0:T(8,128)(2,1)}), bf16[8,256,704]{1,2,0:T(8,128)(2,1)}, u32[]{:S(2)}, u32[]{:S(2)}) async-start(bf16[8,256,704]{1,2,0:T(8,128)(2,1)} %bitcast.264), calls=%async_computation.4 | async-start | bytes 5767168 | tf_op jit(solution)/shard_map/all_to_all | solution.py:88
  637.1 418.6 %all-reduce.3.cloned.1.call-start = ((), (), s32[]{:S(2)}) async-start(), calls=%async_computation.7 | async-start | bytes 21757952 | tf_op jit(solution)/shard_map/psum | solution.py:416
  644.2 28.2 %collective-permute-start.77 = (bf16[128,256]{1,0:T(8,128)(2,1)S(1)}, bf16[128,256]{1,0:T(8,128)(2,1)S(1)}, u32[]{:S(2)}, u32[]{:S(2)}) collective-permute-start(bf16[128,256]{1,0:T(8,128)(2,1)S(1)} %slice.519), channel_id=1, source_target_pairs={{0,4},{1,5},{2,6},{3,7},{4,0},{5,1},{6,2},{7,3},{8,12},{9,13},{10,... | collective-permute-start | bytes 196616 | tf_op jit(solution)/shard_map/ppermute | solution.py:40
  646.2 26.4 %collective-permute-start.78 = (bf16[128,256]{1,0:T(8,128)(2,1)S(1)}, bf16[128,256]{1,0:T(8,128)(2,1)S(1)}, u32[]{:S(2)}, u32[]{:S(2)}) collective-permute-start(bf16[128,256]{1,0:T(8,128)(2,1)S(1)} %slice.520), channel_id=1, source_target_pairs={{0,2},{1,3},{2,0},{3,1},{4,6},{5,7},{6,4},{7,5},{8,10},{9,11},{10,... | collective-permute-start | bytes 196616 | tf_op jit(solution)/shard_map/ppermute | solution.py:40
  647.7 24.9 %collective-permute-start.74 = (bf16[256,256]{1,0:T(8,128)(2,1)S(1)}, bf16[256,256]{1,0:T(8,128)(2,1)S(1)}, u32[]{:S(2)}, u32[]{:S(2)}) collective-permute-start(bf16[256,256]{1,0:T(8,128)(2,1)S(1)} %collective-permute-done.73), channel_id=1, source_target_pairs={{0,1},{1,0},{2,3},{3,2},{4,5},{5,4},{6,7},{7,6},{8,9},{9,8},{10,11... | collective-permute-start | bytes 393224 | tf_op jit(solution)/shard_map/ppermute | solution.py:40
  647.7 24.9 %collective-permute-start.76 = (bf16[256,256]{1,0:T(8,128)(2,1)S(1)}, bf16[256,256]{1,0:T(8,128)(2,1)S(1)}, u32[]{:S(2)}, u32[]{:S(2)}) collective-permute-start(bf16[256,256]{1,0:T(8,128)(2,1)S(1)} %collective-permute-done.75), channel_id=1, source_target_pairs={{0,1},{1,0},{2,3},{3,2},{4,5},{5,4},{6,7},{7,6},{8,9},{9,8},{10,11... | collective-permute-start | bytes 393224 | tf_op jit(solution)/shard_map/ppermute | solution.py:40
  703.4 15.0 %collective-permute-start.27 = (bf16[128,2048]{1,0:T(8,128)(2,1)}, bf16[128,2048]{1,0:T(8,128)(2,1)S(1)}, u32[]{:S(2)}, u32[]{:S(2)}) collective-permute-start(bf16[128,2048]{1,0:T(8,128)(2,1)} %get-tuple-element.125), channel_id=1, source_target_pairs={{0,4},{1,5},{2,6},{3,7},{4,0},{5,1},{6,2},{7,3},{8,12},{9,13},{10,... | collective-permute-start | bytes 1572872 | tf_op jit(solution)/shard_map/ppermute | solution.py:40
  708.7 20.3 %collective-permute-start.59 = (bf16[128,2048]{1,0:T(8,128)(2,1)}, bf16[128,2048]{1,0:T(8,128)(2,1)}, u32[]{:S(2)}, u32[]{:S(2)}) collective-permute-start(bf16[128,2048]{1,0:T(8,128)(2,1)} %get-tuple-element.113), channel_id=1, source_target_pairs={{0,4},{1,5},{2,6},{3,7},{4,0},{5,1},{6,2},{7,3},{8,12},{9,13},{10,... | collective-permute-start | bytes 1572872 | tf_op jit(solution)/shard_map/ppermute | solution.py:40
  709.8 117.0 %collective-permute-start.24 = (bf16[256,2048]{1,0:T(8,128)(2,1)}, bf16[256,2048]{1,0:T(8,128)(2,1)}, u32[]{:S(2)}, u32[]{:S(2)}) collective-permute-start(bf16[256,2048]{1,0:T(8,128)(2,1)} %get-tuple-element.91), channel_id=1, source_target_pairs={{0,1},{1,0},{2,3},{3,2},{4,5},{5,4},{6,7},{7,6},{8,9},{9,8},{10,11... | collective-permute-start | bytes 3145736 | tf_op jit(solution)/shard_map/ppermute | solution.py:40
  711.1 29.1 %collective-permute-start.30 = (bf16[128,2048]{1,0:T(8,128)(2,1)}, bf16[128,2048]{1,0:T(8,128)(2,1)S(1)}, u32[]{:S(2)}, u32[]{:S(2)}) collective-permute-start(bf16[128,2048]{1,0:T(8,128)(2,1)} %get-tuple-element.126), channel_id=1, source_target_pairs={{0,2},{1,3},{2,0},{3,1},{4,6},{5,7},{6,4},{7,5},{8,10},{9,11},{10,... | collective-permute-start | bytes 1572872 | tf_op jit(solution)/shard_map/ppermute | solution.py:40
  719.6 22.8 %collective-permute-start.56 = (bf16[256,2048]{1,0:T(8,128)(2,1)S(1)}, bf16[256,2048]{1,0:T(8,128)(2,1)S(1)}, u32[]{:S(2)}, u32[]{:S(2)}) collective-permute-start(bf16[256,2048]{1,0:T(8,128)(2,1)S(1)} %copy-done.53), channel_id=1, source_target_pairs={{0,1},{1,0},{2,3},{3,2},{4,5},{5,4},{6,7},{7,6},{8,9},{9,8},{10,11... | collective-permute-start | bytes 3145736 | tf_op jit(solution)/shard_map/ppermute | solution.py:40
  719.7 17.6 %collective-permute-start.62 = (bf16[128,2048]{1,0:T(8,128)(2,1)S(1)}, bf16[128,2048]{1,0:T(8,128)(2,1)S(1)}, u32[]{:S(2)}, u32[]{:S(2)}) collective-permute-start(bf16[128,2048]{1,0:T(8,128)(2,1)S(1)} %copy-done.55), channel_id=1, source_target_pairs={{0,2},{1,3},{2,0},{3,1},{4,6},{5,7},{6,4},{7,5},{8,10},{9,11},{10,... | collective-permute-start | bytes 1572872 | tf_op jit(solution)/shard_map/ppermute | solution.py:40
  730.2 29.6 %collective-permute-start.60 = (bf16[256,2048]{1,0:T(8,128)(2,1)S(1)}, bf16[256,2048]{1,0:T(8,128)(2,1)S(1)}, u32[]{:S(2)}, u32[]{:S(2)}) collective-permute-start(bf16[256,2048]{1,0:T(8,128)(2,1)S(1)} %pad_maximum_fusion.7), channel_id=1, source_target_pairs={{0,2},{1,3},{2,0},{3,1},{4,6},{5,7},{6,4},{7,5},{8,10},{9,11},{10,... | collective-permute-start | bytes 3145736 | tf_op jit(solution)/shard_map/ppermute | solution.py:40
  737.6 26.2 %collective-permute-start.63 = (bf16[256,2048]{1,0:T(8,128)(2,1)S(1)}, bf16[256,2048]{1,0:T(8,128)(2,1)S(1)}, u32[]{:S(2)}, u32[]{:S(2)}) collective-permute-start(bf16[256,2048]{1,0:T(8,128)(2,1)S(1)} %pad_maximum_fusion.8), channel_id=1, source_target_pairs={{0,4},{1,5},{2,6},{3,7},{4,0},{5,1},{6,2},{7,3},{8,12},{9,13},{10,... | collective-permute-start | bytes 3145736 | tf_op jit(solution)/shard_map/ppermute | solution.py:40
  740.2 86.6 %collective-permute-start.28 = (bf16[256,2048]{1,0:T(8,128)(2,1)}, bf16[256,2048]{1,0:T(8,128)(2,1)}, u32[]{:S(2)}, u32[]{:S(2)}) collective-permute-start(bf16[256,2048]{1,0:T(8,128)(2,1)} %pad_maximum_fusion.3), channel_id=1, source_target_pairs={{0,2},{1,3},{2,0},{3,1},{4,6},{5,7},{6,4},{7,5},{8,10},{9,11},{10,... | collective-permute-start | bytes 3145736 | tf_op jit(solution)/shard_map/ppermute | solution.py:40
  742.4 84.4 %collective-permute-start.31 = (bf16[256,2048]{1,0:T(8,128)(2,1)}, bf16[256,2048]{1,0:T(8,128)(2,1)}, u32[]{:S(2)}, u32[]{:S(2)}) collective-permute-start(bf16[256,2048]{1,0:T(8,128)(2,1)} %pad_maximum_fusion.4), channel_id=1, source_target_pairs={{0,4},{1,5},{2,6},{3,7},{4,0},{5,1},{6,2},{7,3},{8,12},{9,13},{10,... | collective-permute-start | bytes 3145736 | tf_op jit(solution)/shard_map/ppermute | solution.py:40
  (107 other events, 2263.5 us)
Sparse Core Ops, SparseCore 0:
  17.4 29.4 all-gather.1
  679.6 376.0 all-reduce.2

commit v2 on v1

--- a/solution.py
+++ b/solution.py
@@ -13,6 +13,8 @@
 F32 = jnp.float32
 QUERY_ROWS = 256
 VMEM_BYTES = 32 * 1024 * 1024
+LIGHT = pl.CostEstimate(flops=1000, bytes_accessed=1000, transcendentals=0)
+MLP_VMEM_BYTES = 48 * 1024 * 1024
 
 
 def dot_nn(left, right):
@@ -47,26 +49,44 @@
     return total.astype(BF)
 
 
-def gather_pieces(piece, count):
+def after(value, *others):
+    return lax.optimization_barrier((value, others))[0]
+
+
+def gather_near(piece, count, *between):
     if not is_cube(count):
-        return lax.all_gather(piece, "seq", axis=0, tiled=False)
-    half = piece.shape[0] // 2
+        gathered = lax.all_gather(piece, "seq", axis=0, tiled=False)
+        return [gathered[j] for j in range(count)]
     from_x = swap(piece, 2)
     from_y = swap(piece, 4)
     from_core = swap(piece, 1)
-    far_low = swap(from_x[:half], 4)
-    far_high = swap(from_y[half:], 2)
-    core_x = swap(from_x, 1)
-    core_y = swap(from_y, 1)
-    far = jnp.concatenate([far_low, far_high], 0)
-    core_far = swap(far, 1)
-    return jnp.stack([piece, from_core, from_x, core_x, from_y, core_y, far, core_far], 0)
-
-
-def scatter_pieces(parts, count):
+    if between:
+        from_x, from_y = after([from_x, from_y], *between)
+    return [piece, from_core, from_x, swap(from_x, 1), from_y, swap(from_y, 1)]
+
+
+def gather_far(near, count):
     if not is_cube(count):
-        return lax.psum_scatter(parts, "seq", scatter_dimension=0, tiled=False)
-    half = parts.shape[1] // 2
+        return near[-2]
+    half = near[0].shape[0] // 2
+    return jnp.concatenate([swap(near[2][:half], 4), swap(near[4][half:], 2)], 0)
+
+
+def gather_last(near, far, count):
+    return swap(far, 1) if is_cube(count) else near[-1]
+
+
+def gather_pieces(piece, count):
+    near = gather_near(piece, count)
+    far = gather_far(near, count)
+    last = gather_last(near, far, count)
+    return (near if is_cube(count) else near[:-2]) + [far, last]
+
+
+def scatter_far(parts, count):
+    if not is_cube(count):
+        return parts
+    half = parts[0].shape[0] // 2
     far = add_rounded(parts[6], swap(parts[7], 1))
     far_x = swap(far[:half], 2)
     far_y = swap(far[half:], 4)
@@ -74,10 +94,34 @@
     near_y = add_rounded(parts[4], swap(parts[5], 1))
     near_y = jnp.concatenate([add_rounded(near_y[:half], far_x), near_y[half:]], 0)
     near_x = jnp.concatenate([near_x[:half], add_rounded(near_x[half:], far_y)], 0)
+    own = add_rounded(parts[0], swap(parts[1], 1))
+    return [own, near_x, near_y]
+
+
+def scatter_near(sums, count, *window):
+    if not is_cube(count):
+        return lax.psum_scatter(jnp.stack(sums), "seq", scatter_dimension=0, tiled=False)
+    own, near_x, near_y = sums
     got_x = swap(near_x, 2)
     got_y = swap(near_y, 4)
-    own = add_rounded(parts[0], swap(parts[1], 1))
-    return add_rounded(own, got_x, got_y)
+    return add_rounded(after(own, *window), got_x, got_y)
+
+
+def scatter_pieces(parts, count, *window):
+    return scatter_near(scatter_far(parts, count), count, *window)
+
+
+def gather_ordered(piece, count):
+    if not is_cube(count):
+        return lax.all_gather(piece, "seq", axis=0, tiled=False)
+    rank = lax.axis_index("seq")
+    held = piece
+    for bit in (4, 2, 1):
+        other = swap(held, bit)
+        upper = (rank & bit) != 0
+        held = jnp.stack([jnp.where(upper, other, held), jnp.where(upper, held, other)])
+    held = held.transpose(2, 1, 0, *range(3, held.ndim))
+    return held.reshape(count, *piece.shape)
 
 
 def rows_to_columns(weight):
@@ -86,6 +130,62 @@
 
 def columns_to_rows(weight):
     return lax.all_to_all(weight, "seq", split_axis=0, concat_axis=1, tiled=True)
+
+
+def send_dp(array, pairs):
+    return lax.ppermute(array, "dp", pairs)
+
+
+def line_share(array):
+    return lax.psum_scatter(array, "dp", scatter_dimension=0, tiled=True)
+
+
+def line_gather(share, *windows):
+    if lax.axis_size("dp") != 4:
+        gathered = lax.all_gather(share, "dp", axis=0, tiled=False)
+        return [[gathered[m]] for m in range(gathered.shape[0])]
+    ups, downs = [share], [share]
+    for step in range(3):
+        up, down = ups[-1], downs[-1]
+        if step and len(windows) >= step:
+            up, down = after([up, down], windows[step - 1])
+        ups.append(send_dp(up, [(i, i + 1) for i in range(step, 3)]))
+        downs.append(send_dp(down, [(i + 1, i) for i in range(3 - step)]))
+    return [[ups[k - m] if k > m else downs[m - k] for k in range(4)] for m in range(4)]
+
+
+def choose(options, place):
+    chosen = options[-1]
+    for k in range(len(options) - 2, -1, -1):
+        chosen = jnp.where(place == k, options[k], chosen)
+    return chosen
+
+
+def line_rows(gathered):
+    place = lax.axis_index("dp")
+    return jnp.concatenate([choose(options, place) for options in gathered], 0).astype(F32)
+
+
+def stage(always, work, *operands):
+    shapes = jax.eval_shape(work, *operands)
+    empty = lambda *_: jax.tree.map(lambda leaf: jnp.zeros(leaf.shape, leaf.dtype), shapes)
+    return lax.cond(always, work, empty, *operands)
+
+
+def small_sum(share, count):
+    if not is_cube(count) or lax.axis_size("dp") != 4:
+        own = lax.psum_scatter(share, "seq", scatter_dimension=0, tiled=False)
+        return lax.psum(own, "dp")
+    rank = lax.axis_index("seq")
+    kept = share
+    for bit in (4, 2, 1):
+        upper = (rank & bit) != 0
+        low, high = kept[:bit], kept[bit:]
+        kept = add_rounded(jnp.where(upper, high, low), swap(jnp.where(upper, low, high), bit))
+    kept = kept[0]
+    for bit in (1, 2):
+        kept = add_rounded(kept, send_dp(kept, [(i, i ^ bit) for i in range(4)]))
+    return kept
 
 
 def load_keys(key_ref, kv_ref, rows_ref, count, head, column):
@@ -171,11 +271,7 @@
             jax.ShapeDtypeStruct((seqs, heads, total), F32),
         ],
         compiler_params=pltpu.CompilerParams(vmem_limit_bytes=VMEM_BYTES),
-        cost_estimate=pl.CostEstimate(
-            flops=2 * seqs * heads * total * total * head,
-            bytes_accessed=4 * queries.size + 2 * key_values.size,
-            transcendentals=seqs * heads * total * total // 2,
-        ),
+        cost_estimate=LIGHT,
     )(lengths, key, queries, key_values)
 
 
@@ -247,11 +343,7 @@
             jax.ShapeDtypeStruct(key_values.shape, F32),
         ],
         compiler_params=pltpu.CompilerParams(vmem_limit_bytes=VMEM_BYTES),
-        cost_estimate=pl.CostEstimate(
-            flops=20 * seqs * chunk * width * total // 2,
-            bytes_accessed=6 * queries.size + 6 * key_values.size,
-            transcendentals=seqs * chunk * width * total // head,
-        ),
+        cost_estimate=LIGHT,
     )(lengths, key, queries, upstream, key_values)
 
 
@@ -264,8 +356,9 @@
     kv_ref,
     lse_ref,
     more_ref,
-    dq_ref,
-    dkv_ref,
+    cos_ref,
+    sin_ref,
+    grads_ref,
     keys,
     values,
     keys_t,
@@ -279,6 +372,7 @@
     per_block = block // chunk
     key = key_ref[0]
     length = lengths_ref[pl.program_id(0)]
+    scale = 1.0 / math.sqrt(head)
     load_keys(key, kv_ref, keys, count, head, 0)
     load_keys(key, kv_ref, values, count, head, 1)
     transpose_rows(keys, keys_t)
@@ -301,18 +395,24 @@
             probs = jnp.exp(scores - lse_ref[0, h : h + 1, start : start + block])
             d_probs = dot_nt(values[:seen, :], upstream)
             d_scores = (probs * (d_probs - centre)).astype(BF)
-            d_queries = dot_nn(keys_t[:, :seen], d_scores).T.astype(BF)
+            d_queries = dot_nn(keys_t[:, :seen], d_scores).T.astype(BF).astype(F32) * scale
+            span = slice(start, start + block)
+            d_queries = (
+                d_queries * cos_ref[span, :]
+                - pltpu.roll(d_queries, head // 2, 1) * sin_ref[span, :]
+            ).astype(BF)
             for i, p in enumerate(places):
-                dq_ref[p, 0, :, columns] = d_queries[i * chunk : (i + 1) * chunk]
+                grads_ref[p, 0, :, columns] = d_queries[i * chunk : (i + 1) * chunk]
             dk[:seen, :] += dot_nn(d_scores, queries)
             dv[:seen, :] += dot_nn(probs.astype(BF), upstream)
     for place in range(count):
         rows = slice(place * chunk, (place + 1) * chunk)
-        dkv_ref[place ^ key, 0, :, :head] = dk[rows, :].astype(BF)
-        dkv_ref[place ^ key, 0, :, head:] = dv[rows, :].astype(BF)
-
-
-def attend_backward(queries, upstream, attn, key_values, lse, more, lengths, key, head):
+        turned = dk[rows, :] * cos_ref[rows, :] - pltpu.roll(dk[rows, :], head // 2, 1) * sin_ref[rows, :]
+        grads_ref[place ^ key, 0, :, width : width + head] = turned.astype(BF)
+        grads_ref[place ^ key, 0, :, width + head :] = dv[rows, :].astype(BF)
+
+
+def attend_backward(queries, upstream, attn, key_values, lse, more, tables, lengths, key, head):
     count, seqs, chunk, width = queries.shape
     total = count * chunk
     heads = width // head
@@ -331,8 +431,10 @@
                 shared,
                 pl.BlockSpec((1, heads, total), lambda s, *_: (s, 0, 0)),
                 shared,
+                pl.BlockSpec((total, head), lambda s, *_: (0, 0)),
+                pl.BlockSpec((total, head), lambda s, *_: (0, 0)),
             ],
-            out_specs=[by_head, shared],
+            out_specs=pl.BlockSpec((count, 1, chunk, width + 2 * head), whole),
             scratch_shapes=[
                 pltpu.VMEM((total, head), BF),
                 pltpu.VMEM((total, head), BF),
@@ -341,17 +443,357 @@
                 pltpu.VMEM((total, head), F32),
             ],
         ),
-        out_shape=[
-            jax.ShapeDtypeStruct(queries.shape, BF),
-            jax.ShapeDtypeStruct(key_values.shape, BF),
+        out_shape=jax.ShapeDtypeStruct((count, seqs, chunk, width + 2 * head), BF),
+        compiler_params=pltpu.CompilerParams(vmem_limit_bytes=VMEM_BYTES),
+        cost_estimate=LIGHT,
+    )(lengths, key, queries, upstream, attn, key_values, lse, more, *tables)
+
+
+def front_kernel(key_ref, a_ref, b_ref, gain_ref, wq_ref, wkv_ref, cos_ref, sin_ref, *rest, first):
+    na_ref, nb_ref, q_ref, kv_ref = rest[-4:]
+    _, seqs, chunk, width = q_ref.shape
+    head = kv_ref.shape[3] // 2
+    scale = 1.0 / math.sqrt(head)
+    for i, piece in enumerate((a_ref, b_ref)):
+        inputs = piece[...].astype(F32)
+        normed = (
+            inputs
+            * lax.rsqrt(jnp.mean(inputs * inputs, -1, keepdims=True) + EPSILON)
+            * gain_ref[...]
+        ).astype(BF)
+        (na_ref, nb_ref)[i][...] = normed
+        q_linear = dot_nn(normed, wq_ref[...])
+        kv_linear = dot_nn(normed, wkv_ref[...])
+        span = pl.ds(pl.multiple_of(((first + i) ^ key_ref[0]) * chunk, chunk), chunk)
+        cosine, sine = cos_ref[span, :], sin_ref[span, :]
+        turn = lambda v: v * cosine + pltpu.roll(v, head // 2, 1) * sine
+        for s in range(seqs):
+            rows = slice(s * chunk, (s + 1) * chunk)
+            for h in range(width // head):
+                columns = slice(h * head, (h + 1) * head)
+                q_ref[i, s, :, columns] = (turn(q_linear[rows, columns]) * scale).astype(BF)
+            kv_ref[i, s, :, :head] = turn(kv_linear[rows, :head]).astype(BF)
+            kv_ref[i, s, :, head:] = kv_linear[rows, head:].astype(BF)
+
+
+def whole_spec(array):
+    return pl.BlockSpec(array.shape, lambda *_: (0,) * array.ndim)
+
+
+def pair_spec(shape, pair):
+    return pl.BlockSpec((2, *shape[1:]), lambda *_: (pair,) + (0,) * (len(shape) - 1))
+
+
+def front_pair(key, pieces, pair, gain, wq, wkv, tables, seqs, count, before):
+    rows, width = pieces[0].shape
+    chunk = rows // seqs
+    shapes = [
+        (count, seqs, chunk, wq.shape[1]),
+        (count, seqs, chunk, wkv.shape[1]),
+    ]
+    given = [*pieces, gain, wq, wkv, *tables]
+    return pl.pallas_call(
+        functools.partial(front_kernel, first=2 * pair),
+        grid_spec=pltpu.PrefetchScalarGridSpec(
+            num_scalar_prefetch=1,
+            grid=(1,),
+            in_specs=[whole_spec(a) for a in given] + [pl.BlockSpec(memory_space=pl.ANY)] * len(before),
+            out_specs=[whole_spec(pieces[0])] * 2 + [pair_spec(shape, pair) for shape in shapes],
+        ),
+        out_shape=[jax.ShapeDtypeStruct((rows, width), BF)] * 2
+        + [jax.ShapeDtypeStruct(shape, BF) for shape in shapes],
+        input_output_aliases={1 + len(given) + i: 2 + i for i in range(len(before))},
+        compiler_params=pltpu.CompilerParams(vmem_limit_bytes=VMEM_BYTES),
+        cost_estimate=LIGHT,
+    )(key, *given, *before)
+
+
+def mlp_kernel(na_hbm, nb_hbm, ga_hbm, gb_hbm, shares_hbm, down_hbm, *rest, first):
+    hidden_hbm, dgate_hbm, dup_hbm, pa_hbm, pb_hbm, oa_hbm, ob_hbm = rest[-18:-11]
+    normed, branch, both, down, hidden, dgate, dup, parts, outs, in_sems, out_sems = rest[-11:]
+    rows = na_hbm.shape[0]
+    low, high = pl.ds(0, rows), pl.ds(rows, rows)
+    lines, inner = shares_hbm.shape[0], down_hbm.shape[0]
+    places = [(shares_hbm.at[i], both.at[:, i]) for i in range(lines)]
+    places += [(na_hbm, normed.at[low]), (nb_hbm, normed.at[high])]
+    places += [(ga_hbm, branch.at[low]), (gb_hbm, branch.at[high]), (down_hbm, down)]
+    loads = [pltpu.make_async_copy(a, b, in_sems.at[i]) for i, (a, b) in enumerate(places)]
+    places = []
+    for stack, target in ((hidden, hidden_hbm), (dgate, dgate_hbm), (dup, dup_hbm)):
+        places += [(stack.at[low], target.at[first]), (stack.at[high], target.at[first + 1])]
+    places += [(outs.at[low], oa_hbm), (outs.at[high], ob_hbm)]
+    places += [(parts.at[low], pa_hbm), (parts.at[high], pb_hbm)]
+    stores = [pltpu.make_async_copy(a, b, out_sems.at[i]) for i, (a, b) in enumerate(places)]
+    for load in loads:
+        load.start()
+    for load in loads[: lines + 2]:
+        load.wait()
+    both_cols = both[...].reshape(-1, 2 * inner)
+    gate_up = dot_nn(normed[...], both_cols)
+    gate_pre, up_pre = gate_up[:, :inner], gate_up[:, inner:]
+    sigma = jax.nn.sigmoid(gate_pre)
+    silu_gate = gate_pre * sigma
+    slope = sigma * (1.0 + gate_pre * (1.0 - sigma))
+    hidden[...] = (silu_gate * up_pre).astype(BF)
+    stores[0].start()
+    stores[1].start()
+    for load in loads[lines + 2 :]:
+        load.wait()
+    grad_hidden = dot_nt(branch[...], down[...])
+    dgate[...] = (grad_hidden * up_pre * slope).astype(BF)
+    dup[...] = (grad_hidden * silu_gate).astype(BF)
+    for store in stores[2:6]:
+        store.start()
+    outs[...] = dot_nn(hidden[...], down[...]).astype(BF)
+    for store in stores[6:8]:
+        store.start()
+    for start, store in ((0, stores[8]), (rows, stores[9])):
+        span = slice(start, start + rows)
+        grads = dot_nt(jnp.concatenate([dgate[span, :], dup[span, :]], 1), both_cols)
+        parts[span, :] = grads.astype(BF)
+        store.start()
+    for store in stores:
+        store.wait()
+
+
+def mlp_pair(normed, branch, pair, shares, down, count, before):
+    rows, width = normed[0].shape
+    inner = down.shape[0]
+    lines, _, share_rows, _ = shares.shape
+    given = [*normed, *branch, shares, down]
+    anywhere = pl.BlockSpec(memory_space=pl.ANY)
+    stacked = jax.ShapeDtypeStruct((count, rows, inner), BF)
+    apart = jax.ShapeDtypeStruct((rows, width), BF)
+    return pl.pallas_call(
+        functools.partial(mlp_kernel, first=2 * pair),
+        in_specs=[anywhere] * (6 + len(before)),
+        out_specs=[anywhere] * 7,
+        out_shape=[stacked] * 3 + [apart] * 4,
+        scratch_shapes=[pltpu.VMEM((2 * rows, width), BF)] * 2
+        + [pltpu.VMEM((count, lines, share_rows, 2 * inner), BF), pltpu.VMEM(down.shape, BF)]
+        + [pltpu.VMEM((2 * rows, inner), BF)] * 3
+        + [pltpu.VMEM((2 * rows, width), BF)] * 2
+        + [pltpu.SemaphoreType.DMA((lines + 5,)), pltpu.SemaphoreType.DMA((10,))],
+        input_output_aliases={6 + i: i for i in range(len(before))},
+        compiler_params=pltpu.CompilerParams(vmem_limit_bytes=MLP_VMEM_BYTES),
+        cost_estimate=LIGHT,
+    )(*given, *before)
+
+
+def proj_kernel(a_ref, b_ref, w_ref, attn_ref, *rest, last):
+    dattn_ref, total_ref = rest[-2:]
+    seqs, chunk = attn_ref.shape[1:3]
+    total = None if len(rest) == 2 else rest[1][...]
+    for i, piece in enumerate((a_ref, b_ref)):
+        grads = piece[...]
+        d_attn = dot_nt(grads, w_ref[...]).astype(BF)
+        for s in range(seqs):
+            rows = slice(s * chunk, (s + 1) * chunk)
+            dattn_ref[i, s] = d_attn[rows]
+            share = dot_tn(attn_ref[i, s], grads[rows])
+            total = share if total is None else total + share
+    total_ref[...] = total.astype(total_ref.dtype)
+
+
+def proj_pair(pieces, pair, w_out, attn, count, before):
+    last = 2 * pair + 2 == count
+    rows, width = pieces[0].shape
+    given = [*pieces, w_out]
+    extra_specs = []
+    aliases = {}
+    if before:
+        extra_specs = [pl.BlockSpec(memory_space=pl.ANY), whole_spec(before[1])]
+        aliases = {4: 0} if last else {4: 0, 5: 1}
+    total = jax.ShapeDtypeStruct(w_out.shape, BF if last else F32)
+    return pl.pallas_call(
+        functools.partial(proj_kernel, last=last),
+        grid=(1,),
+        in_specs=[whole_spec(a) for a in given] + [pair_spec(attn.shape, pair)] + extra_specs,
+        out_specs=[pair_spec(attn.shape, pair), whole_spec(total)],
+        out_shape=[jax.ShapeDtypeStruct(attn.shape, BF), total],
+        input_output_aliases=aliases,
+        compiler_params=pltpu.CompilerParams(vmem_limit_bytes=VMEM_BYTES),
+        cost_estimate=LIGHT,
+    )(*given, attn, *before)
+
+
+def parts_kernel(*refs, count, turned):
+    lefts, weights = refs[: len(turned)], refs[len(turned) : 2 * len(turned)]
+    outs, (buffer, sems) = refs[2 * len(turned) : -2], refs[-2:]
+    order = (6, 7, 2, 3, 4, 5, 0, 1) if count == 8 else range(count)
+    stores = []
+    for j in order:
+        total = None
+        for left, weight, turn in zip(lefts, weights, turned):
+            share = (dot_nt if turn else dot_nn)(left[j], weight[...])
+            total = share if total is None else total + share
+        buffer[j] = total.astype(BF)
+        stores.append(pltpu.make_async_copy(buffer.at[j], outs[j], sems.at[j]))
+        stores[-1].start()
+    for store in stores:
+        store.wait()
+
+
+def parts_of(lefts, weights, turned):
+    count, rows = lefts[0].shape[:2]
+    width = weights[0].shape[0 if turned[0] else 1]
+    return pl.pallas_call(
+        functools.partial(parts_kernel, count=count, turned=turned),
+        grid=(1,),
+        in_specs=[whole_spec(a) for a in (*lefts, *weights)],
+        out_specs=[pl.BlockSpec(memory_space=pl.ANY)] * count,
+        out_shape=[jax.ShapeDtypeStruct((rows, width), BF)] * count,
+        scratch_shapes=[
+            pltpu.VMEM((count, rows, width), BF),
+            pltpu.SemaphoreType.DMA((count,)),
         ],
         compiler_params=pltpu.CompilerParams(vmem_limit_bytes=VMEM_BYTES),
-        cost_estimate=pl.CostEstimate(
-            flops=5 * seqs * heads * total * total * head,
-            bytes_accessed=8 * queries.size + 8 * key_values.size,
-            transcendentals=seqs * heads * total * total // 2,
+        cost_estimate=LIGHT,
+    )(*lefts, *weights)
+
+
+def outer_kernel(*refs, count, rights):
+    left = jnp.concatenate([ref[...] for ref in refs[:count]], 0)
+    left_t = left.T
+    for right, out in zip(refs[count : count + rights], refs[count + rights :]):
+        out[...] = dot_nn(left_t, right[...]).astype(BF)
+
+
+def outer_of(pieces, rights):
+    count = len(pieces)
+    rows, width = pieces[0].shape
+    step = min(256, width)
+    return pl.pallas_call(
+        functools.partial(outer_kernel, count=count, rights=len(rights)),
+        grid=(width // step,),
+        in_specs=[pl.BlockSpec((rows, step), lambda i: (0, i))] * count
+        + [pl.BlockSpec(right.shape, lambda i: (0, 0)) for right in rights],
+        out_specs=[pl.BlockSpec((step, right.shape[1]), lambda i: (i, 0)) for right in rights],
+        out_shape=[jax.ShapeDtypeStruct((width, right.shape[1]), BF) for right in rights],
+        compiler_params=pltpu.CompilerParams(vmem_limit_bytes=VMEM_BYTES),
+        cost_estimate=LIGHT,
+    )(*pieces, *rights)
+
+
+def inner_kernel(*refs, count, lefts):
+    pieces = refs[lefts : lefts + count]
+    outs, lefts_t = refs[lefts + count : 2 * lefts + count], refs[2 * lefts + count :]
+    rows = pieces[0].shape[0]
+
+    @pl.when(pl.program_id(0) == 0)
+    def _():
+        for left, left_t in zip(refs[:lefts], lefts_t):
+            for j in range(count):
+                span = slice(j * rows, (j + 1) * rows)
+                left_t[:, span] = left[span, :].T
+
+    right = jnp.concatenate([piece[...] for piece in pieces], 0)
+    for out, left_t in zip(outs, lefts_t):
+        out[...] = dot_nn(left_t[...], right).astype(BF)
+
+
+def inner_of(lefts, pieces):
+    count = len(pieces)
+    rows, width = pieces[0].shape
+    step = min(256, width)
+    columns = lefts[0].shape[1]
+    return pl.pallas_call(
+        functools.partial(inner_kernel, count=count, lefts=len(lefts)),
+        grid=(width // step,),
+        in_specs=[pl.BlockSpec(left.shape, lambda i: (0, 0)) for left in lefts]
+        + [pl.BlockSpec((rows, step), lambda i: (0, i))] * count,
+        out_specs=[pl.BlockSpec((columns, step), lambda i: (0, i))] * len(lefts),
+        out_shape=[jax.ShapeDtypeStruct((columns, width), BF)] * len(lefts),
+        scratch_shapes=[pltpu.VMEM((columns, count * rows), BF)] * len(lefts),
+        compiler_params=pltpu.CompilerParams(vmem_limit_bytes=VMEM_BYTES),
+        cost_estimate=LIGHT,
+    )(*lefts, *pieces)
+
+
+def turn_kernel(place_ref, *refs, lines):
+    options = len(refs) // lines
+    out_ref = refs[-1]
+    place = place_ref[0]
+    blocks = []
+    for m in range(lines):
+        blocks.append(choose([ref[...] for ref in refs[m * options : (m + 1) * options]], place))
+    turned = []
+    for j in range(blocks[0].shape[0]):
+        turned.append(jnp.concatenate([block[j].astype(F32) for block in blocks], 0).T)
+    out_ref[...] = jnp.concatenate(turned, 1)
+
+
+def turn_blocks(gathered):
+    lines = len(gathered)
+    count, columns, rows = gathered[0][0].shape
+    step = min(128, rows)
+    given = [option for options in gathered for option in options]
+    place = lax.axis_index("dp").astype(jnp.int32).reshape(1)
+    return pl.pallas_call(
+        functools.partial(turn_kernel, lines=lines),
+        grid_spec=pltpu.PrefetchScalarGridSpec(
+            num_scalar_prefetch=1,
+            grid=(rows // step,),
+            in_specs=[pl.BlockSpec((count, columns, step), lambda i, *_: (0, 0, i))] * len(given),
+            out_specs=pl.BlockSpec((step, count * lines * columns), lambda i, *_: (i, 0)),
         ),
-    )(lengths, key, queries, upstream, attn, key_values, lse, more)
+        out_shape=jax.ShapeDtypeStruct((rows, count * lines * columns), F32),
+        compiler_params=pltpu.CompilerParams(vmem_limit_bytes=VMEM_BYTES),
+        cost_estimate=LIGHT,
+    )(place, *given)
+
+
+def spread_rows(share_t, count):
+    columns, rows = share_t.shape
+    blocks = share_t.reshape(columns, count, rows // count).transpose(1, 0, 2)
+    return lax.all_to_all(blocks, "seq", split_axis=0, concat_axis=0, tiled=True)
+
+
+def pack_kernel(place_ref, gate_ref, up_ref, query_ref, out_ref):
+    count, rows, _ = out_ref.shape
+    inner = gate_ref.shape[1] // count
+    own = query_ref.shape[1] // count
+    gate, up = gate_ref[...], up_ref[...]
+    for j in range(count):
+        columns = slice(j * inner, (j + 1) * inner)
+        out_ref[j, :, : 2 * inner] = jnp.concatenate([gate[:, columns], up[:, columns]], 1)
+        for g in range(query_ref.shape[0] // rows):
+            start = 2 * inner + g * own
+            out_ref[j, :, start : start + own] = query_ref[
+                g * rows : (g + 1) * rows, j * own : (j + 1) * own
+            ]
+
+
+def pack_weights(w_gate, w_up, w_query, count):
+    lines = lax.axis_size("dp")
+    rows, columns = w_gate.shape[0] // lines, w_gate.shape[1]
+    place = lax.axis_index("dp").astype(jnp.int32).reshape(1)
+    share = pl.BlockSpec((rows, columns), lambda i, place: (place[0], 0))
+    shape = (count, rows, (2 * columns + lines * w_query.shape[1]) // count)
+    return pl.pallas_call(
+        pack_kernel,
+        grid_spec=pltpu.PrefetchScalarGridSpec(
+            num_scalar_prefetch=1,
+            grid=(1,),
+            in_specs=[share, share, whole_spec(w_query)],
+            out_specs=pl.BlockSpec(shape, lambda i, place: (0, 0, 0)),
+        ),
+        out_shape=jax.ShapeDtypeStruct(shape, BF),
+        compiler_params=pltpu.CompilerParams(vmem_limit_bytes=VMEM_BYTES),
+        cost_estimate=LIGHT,
+    )(place, w_gate, w_up, w_query)
+
+
+def share_weights(w_gate, w_up, w_query, count):
+    lines = lax.axis_size("dp")
+    inner = w_gate.shape[1] // count
+    own = w_query.shape[1] // count
+    packed = pack_weights(w_gate, w_up, w_query, count)
+    packed = lax.all_to_all(packed, "seq", split_axis=0, concat_axis=0, tiled=True)
+    rows = packed.shape[1]
+    query = packed[:, :, 2 * inner :].reshape(count, rows, lines, own).transpose(0, 2, 1, 3)
+    shares = lax.all_gather(packed[:, :, : 2 * inner], "dp", axis=0, tiled=False)
+    return query.reshape(count * lines * rows, own), shares
 
 
 def rope_tables(positions, head_width):
@@ -359,22 +801,10 @@
     spacing = jnp.exp(
         jnp.arange(half_width).astype(F32) * (-2.0 * math.log(10000.0) / head_width)
     )
-    angles = positions.astype(F32)[..., None] * spacing
-    angles = jnp.concatenate([angles, angles], -1)
-    return (jnp.cos(angles), jnp.sin(angles))
-
-
-def rotate(vector, cosine, sine_table):
-    half_width = vector.shape[-1] // 2
-    turned = jnp.concatenate([-vector[..., half_width:], vector[..., :half_width]], -1)
-    return vector * cosine + turned * sine_table
-
-
-def rotate_back(gradient, cosine, sine_table):
-    half_width = gradient.shape[-1] // 2
-    scaled = gradient * sine_table
-    turned = jnp.concatenate([scaled[..., half_width:], -scaled[..., :half_width]], -1)
-    return gradient * cosine + turned
+    angles = positions.astype(F32)[:, None] * spacing[None, :]
+    sines = jnp.sin(angles)
+    cosines = jnp.cos(angles)
+    return (jnp.concatenate([cosines, cosines], 1), jnp.concatenate([-sines, sines], 1))
 
 
 def rms_scale(values_in):
@@ -411,104 +841,165 @@
     head = w_key.shape[1]
     rows = seqs * chunk
     all_rows = count * rows
-    local_heads = w_query.shape[1] // head // count
-    scale = 1.0 / math.sqrt(head)
-    bf_sum = lambda share: lax.psum(share.astype(BF), "dp").astype(F32)
-
-    gains = lax.all_gather(jnp.stack([gain_attn, gain_mlp]), "seq", axis=1, tiled=True).astype(F32)
-    gain_one, gain_two = gains[0], gains[1]
-    kv_mat = lax.all_gather(jnp.concatenate([w_key, w_value], 1), "seq", axis=0, tiled=True)
-    query_cols = rows_to_columns(w_query)
-    gate_cols = rows_to_columns(w_gate)
-    up_cols = rows_to_columns(w_up)
+    own_columns = w_query.shape[0]
+
+    query_cols, shares = share_weights(w_gate, w_up, w_query, count)
+    gain_rows = jnp.zeros((16, 2 * head), BF)
+    gain_rows = gain_rows.at[:2, :own_columns].set(jnp.stack([gain_attn, gain_mlp]))
+    packed = jnp.concatenate([jnp.concatenate([w_key, w_value], 1), gain_rows], 0)
+    packed = gather_ordered(packed, count)
+    kv_mat = packed[:, :own_columns].reshape(width, 2 * head)
+    gain_one = packed[:, own_columns, :own_columns].reshape(1, width).astype(F32)
+    gain_two = packed[:, own_columns + 1, :own_columns].reshape(1, width).astype(F32)
 
     local_pos = rank * chunk + jnp.arange(chunk, dtype=jnp.int32)
     valid = (local_pos[None, :] < lengths[:, None]).astype(F32).reshape(rows, 1)
-    owners = jnp.arange(count, dtype=jnp.int32) ^ key
-    all_pos = owners[:, None] * chunk + jnp.arange(chunk, dtype=jnp.int32)[None, :]
-    cosine, sine_table = rope_tables(all_pos, head)
-    cos_kv, sin_kv = cosine[:, None], sine_table[:, None]
-    cos_q, sin_q = cosine[:, None, :, None], sine_table[:, None, :, None]
-    cos_own, sin_own = rope_tables(local_pos, head)
-
+    tables = rope_tables(jnp.arange(count * chunk, dtype=jnp.int32), head)
+
+    last_pair = count // 2 - 1
     inputs = tokens.reshape(rows, width)
+    front_of = lambda pair, two, before: front_pair(
+        keys_of, two, pair, gain_one, query_cols, kv_mat, tables, seqs, count, before
+    )
+    near = gather_near(inputs, count)
+    normed_one = []
+    stacks = []
+    far = gather_far(near, count)
+    for pair in range(last_pair):
+        *normed, queries, key_values = front_of(pair, near[2 * pair : 2 * pair + 2], stacks)
+        normed_one += normed
+        stacks = [queries, key_values]
+    last = gather_last(near, far, count)
+    grad_out = cotangent.reshape(rows, width).astype(F32) * valid
+    branch_near = gather_near(after(grad_out.astype(BF), far), count, stacks)
+    branch_far = gather_far(after(branch_near, stacks), count)
+    *normed, queries, key_values = front_of(last_pair, [far, last], stacks)
+    normed_one += normed
+    attn, lse = attend_forward(queries, key_values, lengths, keys_of, head)
+    attn, branch_far = lax.optimization_barrier((attn, branch_far))
+    proj_parts = parts_of([attn.reshape(count, rows, -1)], [w_out], (False,))
     inputs_f = inputs.astype(F32)
     scale_one = rms_scale(inputs_f)
-    all_inputs = gather_pieces(inputs, count).reshape(all_rows, width).astype(F32)
-    normed_one = (all_inputs * rms_scale(all_inputs) * gain_one).astype(BF)
-    q_linear = dot_nn(normed_one, query_cols).reshape(count, seqs, chunk, local_heads, head)
-    queries = (rotate(q_linear, cos_q, sin_q) * scale).astype(BF)
-    queries = queries.reshape(count, seqs, chunk, local_heads * head)
-    kv_linear = dot_nn(normed_one, kv_mat).reshape(count, seqs, chunk, 2 * head)
-    key_values = jnp.concatenate(
-        [
-            rotate(kv_linear[..., :head], cos_kv, sin_kv).astype(BF),
-            kv_linear[..., head:].astype(BF),
-        ],
-        -1,
+
+    branch_last = gather_last(branch_near, branch_far, count)
+    branch = (branch_near if is_cube(count) else branch_near[:-2]) + [branch_far, branch_last]
+    grad_second, dkv_second = attend_second(
+        after(second_queries, proj_parts), second_cotangent, key_values, lengths, keys_of, head
     )
-    attn, lse = attend_forward(queries, key_values, lengths, keys_of, head)
-    attn_rows = attn.reshape(all_rows, local_heads * head)
-    proj_parts = dot_nn(attn_rows, w_out).astype(BF).reshape(count, rows, width)
-    middle = inputs_f + scatter_pieces(proj_parts, count).astype(F32)
-
-    grad_second, dkv_second = attend_second(
-        second_queries, second_cotangent, key_values, lengths, keys_of, head
+    proj_sum = scatter_pieces(proj_parts, count, dkv_second)
+    proj_sum, shares = lax.optimization_barrier((proj_sum, shares))
+    middle = inputs_f + proj_sum.astype(F32)
+
+    scale_two = rms_scale(middle)
+    mlp_of = lambda pair, two, before: mlp_pair(
+        two, branch[2 * pair : 2 * pair + 2], pair, shares, w_down, count, before
     )
-
-    grad_out = cotangent.reshape(rows, width).astype(F32) * valid
-    grad_branch = gather_pieces(grad_out.astype(BF), count).reshape(all_rows, width)
-    scale_two = rms_scale(middle)
-    normed_two_own = (middle * scale_two * gain_two).astype(BF)
-    normed_two = gather_pieces(normed_two_own, count).reshape(all_rows, width)
-    gate_pre = dot_nn(normed_two, gate_cols)
-    up_pre = dot_nn(normed_two, up_cols)
-    sigma = jax.nn.sigmoid(gate_pre)
-    silu_gate = gate_pre * sigma
-    hidden = (silu_gate * up_pre).astype(BF)
-    grad_hidden = dot_nt(grad_branch, w_down)
-    grad_gate_pre = (grad_hidden * up_pre * (sigma * (1.0 + gate_pre * (1.0 - sigma)))).astype(BF)
-    grad_up_pre = (grad_hidden * silu_gate).astype(BF)
-    normed_parts = (dot_nt(grad_gate_pre, gate_cols) + dot_nt(grad_up_pre, up_cols)).astype(BF)
-    grad_normed_two = scatter_pieces(normed_parts.reshape(count, rows, width), count).astype(F32)
-    grad_middle = grad_out + norm_back(grad_normed_two, middle, scale_two, gain_two)
-    down_parts = dot_nn(hidden, w_down).astype(BF).reshape(count, rows, width)
-    out = (middle + scatter_pieces(down_parts, count).astype(F32)).astype(BF)
-
-    grad_w_down = bf_sum(dot_tn(hidden, grad_branch))
-    grad_w_gate = bf_sum(columns_to_rows(dot_tn(normed_two, grad_gate_pre).astype(BF)))
-    grad_w_up = bf_sum(columns_to_rows(dot_tn(normed_two, grad_up_pre).astype(BF)))
-
-    grad_proj = gather_pieces(grad_middle.astype(BF), count).reshape(all_rows, width)
-    grad_w_out = bf_sum(dot_tn(attn_rows, grad_proj))
-    grad_attn = dot_nt(grad_proj, w_out).astype(BF).reshape(queries.shape)
-    grad_q, dkv_parts = attend_backward(
-        queries, grad_attn, attn, key_values, lse, dkv_second, lengths, keys_of, head
+    near = gather_near((middle * scale_two * gain_two).astype(BF), count)
+    done = [mlp_of(0, near[:2], [])]
+    far = gather_far(after(near, done[-1][0]), count)
+    for pair in range(1, last_pair):
+        done.append(mlp_of(pair, near[2 * pair : 2 * pair + 2], done[-1][:3]))
+        if pair == 1:
+            far = after(far, done[-1][0])
+            last = gather_last(near, far, count)
+    done.append(mlp_of(last_pair, [far, last], done[-1][:3]))
+    hidden, grad_gate, grad_up = [stack.reshape(all_rows, -1) for stack in done[-1][:3]]
+    normed_parts = [part for step in done for part in step[3:5]]
+    out_parts = [part for step in done for part in step[5:]]
+    normed_two = (near if is_cube(count) else near[:-2]) + [far, last]
+    sync = lax.optimization_barrier
+    always = lengths[0] > 0
+    w_gate_share, w_up_share = inner_of([grad_gate, grad_up], normed_two)
+    split = queries.shape[-1]
+    gate_share = line_share(w_gate_share)
+
+    def sum_mlp_back(normed_parts, hidden, w_up_share):
+        two_sums = scatter_far(normed_parts, count)
+        (w_down_share,) = inner_of([hidden], branch)
+        grad_normed_two = scatter_near(two_sums, count, w_down_share).astype(F32)
+        grad_middle = grad_out + norm_back(grad_normed_two, middle, scale_two, gain_two)
+        gain_share = jnp.sum(grad_normed_two * (middle * scale_two), 0)
+        return grad_middle, gain_share, w_down_share, w_up_share
+
+    grad_middle, gain_share, w_down_share, w_up_share = stage(
+        always, sum_mlp_back, normed_parts, hidden, w_up_share
     )
-    grad_q = grad_q.reshape(count, seqs, chunk, local_heads, head).astype(F32) * scale
-    grad_q_linear = rotate_back(grad_q, cos_q, sin_q).astype(BF).reshape(all_rows, -1)
-    grad_w_query = bf_sum(columns_to_rows(dot_tn(normed_one, grad_q_linear).astype(BF)))
-    one_parts = dot_nt(grad_q_linear, query_cols).astype(BF).reshape(count, rows, width)
-    dkv_own = scatter_pieces(dkv_parts.reshape(count, rows, 2 * head), count)
-    dkv_own = dkv_own.reshape(seqs, chunk, 2 * head)
-    grad_k_linear = rotate_back(dkv_own[..., :head].astype(F32), cos_own, sin_own).astype(BF)
-    grad_kv_own = jnp.concatenate([grad_k_linear, dkv_own[..., head:]], -1).reshape(rows, 2 * head)
-    grad_kv = gather_pieces(grad_kv_own, count).reshape(all_rows, 2 * head)
-    own_columns = w_query.shape[0]
-    normed_slice = lax.dynamic_slice_in_dim(normed_one, rank * own_columns, own_columns, 1)
-    grad_w_kv = bf_sum(dot_tn(normed_slice, grad_kv))
-    grad_normed_one = scatter_pieces(one_parts, count).astype(F32) + dot_nt(grad_kv_own, kv_mat)
-    grad_tokens = grad_middle + norm_back(grad_normed_one, inputs_f, scale_one, gain_one)
-
-    gain_shares = jnp.stack(
-        [
-            jnp.sum(grad_normed_one * (inputs_f * scale_one), 0),
-            jnp.sum(grad_normed_two * (middle * scale_two), 0),
-        ]
+    w_up_share, gate_share = sync((w_up_share, gate_share))
+    up_share = line_share(w_up_share)
+
+    def project_back(grad_middle, gate_share, w_down_share):
+        near = gather_near(grad_middle.astype(BF), count)
+        gate_blocks = spread_rows(gate_share, count)
+        proj_of = lambda pair, two, before: proj_pair(two, pair, w_out, attn, count, before)
+        state = proj_of(0, near[:2], [])
+        far = gather_far(after(near, state[0]), count)
+        for pair in range(1, last_pair):
+            state = proj_of(pair, near[2 * pair : 2 * pair + 2], state)
+        last = gather_last(near, far, count)
+        grad_attn, w_out_share = proj_of(last_pair, [far, last], state)
+        return grad_attn, w_out_share, gate_blocks, w_down_share
+
+    grad_attn, w_out_share, gate_blocks, w_down_share = stage(
+        always, project_back, grad_middle, gate_share, w_down_share
     )
-    gain_sums = lax.psum(gain_shares, ("seq", "dp"))
+    w_down_share, up_share = sync((w_down_share, up_share))
+    down_share = line_share(w_down_share)
+
+    def attention_back(grad_attn, up_share, gate_blocks, out_parts, w_out_share):
+        out_sums = scatter_far(out_parts, count)
+        up_blocks = spread_rows(up_share, count)
+        grads = attend_backward(
+            queries, grad_attn, attn, key_values, lse, dkv_second, tables, lengths, keys_of, head
+        )
+        gate_blocks = line_gather(gate_blocks, grads)
+        grads = grads.reshape(count, rows, -1)
+        one_parts = parts_of(
+            [grads[..., :split], grads[..., split:]], [query_cols, kv_mat], (True, True)
+        )
+        (w_one_share,) = outer_of(normed_one, [grads.reshape(all_rows, -1)])
+        w_query_rows = columns_to_rows(after(w_one_share[:, :split], up_blocks))
+        lines = lax.axis_size("dp")
+        late = jnp.concatenate(
+            [w.reshape(lines, -1, w.shape[1]) for w in (w_out_share, w_query_rows)], 1
+        )
+        return one_parts, out_sums, w_one_share, late.reshape(-1, width), gate_blocks, up_blocks
+
+    one_parts, out_sums, w_one_share, late, gate_blocks, up_blocks = stage(
+        always, attention_back, grad_attn, up_share, gate_blocks, out_parts, w_out_share
+    )
+    late, down_share = sync((late, down_share))
+    late_share = line_share(late)
+
+    def sum_attention_back(one_parts, out_sums, up_blocks):
+        one_sums = scatter_far(one_parts, count)
+        out = (middle + scatter_near(out_sums, count).astype(F32)).astype(BF)
+        up_blocks = line_gather(up_blocks, one_sums)
+        grad_normed_one = scatter_near(one_sums, count).astype(F32)
+        grad_tokens = grad_middle + norm_back(grad_normed_one, inputs_f, scale_one, gain_one)
+        gain_share = jnp.sum(grad_normed_one * (inputs_f * scale_one), 0)
+        return out, grad_tokens, gain_share, up_blocks
+
+    out, grad_tokens, first_gain_share, up_blocks = stage(
+        always, sum_attention_back, one_parts, out_sums, up_blocks
+    )
+    late_share, down_share, up_blocks, first_gain_share = sync(
+        (late_share, down_share, up_blocks, first_gain_share)
+    )
+    down_blocks = line_gather(down_share)
+    late_blocks = line_gather(late_share)
     own_gain = gain_attn.shape[0]
-    grad_gains = lax.dynamic_slice_in_dim(gain_sums, rank * own_gain, own_gain, 1)
+    gain_shares = jnp.stack([first_gain_share, gain_share])
+    gain_shares = gain_shares.astype(BF).reshape(2, count, own_gain).transpose(1, 0, 2)
+    gain_shares = jnp.pad(gain_shares, ((0, 0), (0, 14), (0, 2 * head - own_gain)))
+    kv_shares = w_one_share[:, split:].reshape(count, own_columns, 2 * head)
+    small = small_sum(jnp.concatenate([kv_shares, gain_shares], 1), count).astype(F32)
+    grad_w_kv, grad_gains = small[:own_columns], small[own_columns : own_columns + 2, :own_gain]
+    grad_w_gate = turn_blocks(gate_blocks)
+    grad_w_up = turn_blocks(up_blocks)
+    grad_w_down = line_rows(down_blocks)
+    late_rows = line_rows(late_blocks).reshape(len(late_blocks), 2, -1, width)
+    w_out_sum = late_rows[:, 0].reshape(-1, width)
+    grad_w_query = late_rows[:, 1].reshape(-1, width)
 
     return (
         out.reshape(tokens.shape),
@@ -518,7 +1009,7 @@
         grad_w_query,
         grad_w_kv[:, :head],
         grad_w_kv[:, head:],
-        grad_w_out,
+        w_out_sum.astype(F32),
         grad_gains[1],
         grad_w_gate,
         grad_w_up,

time: 1090 us -> 759 us (0.70)
  waiting for transfers between devices: 452 us -> 273 us
  Pallas kernels: 39.6 us -> 191 us
  matrix products: 127 us -> 0 us
  blocking collectives: 105 us -> 0 us
  local copies, waits for them, and re-layouts: 143 us -> 90.5 us
  other arithmetic: 107 us -> 62.5 us
  starting transfers between devices: 93.1 us -> 119 us
    psum x1 -> x0, waiting for transfers between devices: 222 us -> none  [body(): bf_sum = lambda share: lax.psum(share.astype(BF), 'dp').astype(F32)]
    pallas_call x0 -> x20, Pallas kernels: none -> 149 us  [the longest x4 60 us: mlp_pair(): pl.pallas_call(functools.partial(mlp_kernel, first=2 * pair), in_specs=[a...]
    dot_general x18 -> x0, matrix products: 127 us -> none  [the longest x6 44.9 us: dot_tn(): lax.dot_general(left, right, (((0,), (0,)), ((), ())), preferred_element_...]
    ppermute x0 -> x26, waiting for transfers between devices: none -> 92.4 us  [send_dp(): return lax.ppermute(array, 'dp', pairs)]
    unnamed x216 -> x71, local copies, waits for them, and re-layouts: 82.6 us -> 16.9 us
    psum x1 -> x0, blocking collectives: 58.8 us -> none  [body(): gain_sums = lax.psum(gain_shares, ('seq', 'dp'))]
    ppermute x80 -> x70, waiting for transfers between devices: 219 us -> 162 us  [swap(): return lax.ppermute(array, 'seq', [(i, i ^ bit) for i in range(8)])]
    cond x0 -> x101, local copies, waits for them, and re-layouts: none -> 48 us
  transfers between devices with their start and end apart: 88 -> 105, of which waited for: 26 -> 46; matrix products, arithmetic and copies ran while one was open for 25% -> 17% of each run, Pallas kernels for 4% -> 21%
where the time goes in v2:
time: 759 us; the launch traced here: 751 us
  waiting for transfers between devices  273 us (36%)
  Pallas kernels  191 us (25%)
  starting transfers between devices  119 us (16%)
  local copies, waits for them, and re-layouts  90.5 us (12%)
  other arithmetic  62.5 us (8%)
  between operations  15 us (2%)
    ppermute x70, waiting for transfers between devices, swap(): return lax.ppermute(array, 'seq', [(i, i ^ bit) for i in range(8)])  162 us
    ppermute x26, waiting for transfers between devices, send_dp(): return lax.ppermute(array, 'dp', pairs)  92.4 us
    ppermute x70, starting transfers between devices, swap(): return lax.ppermute(array, 'seq', [(i, i ^ bit) for i in range(8)])  60.5 us
    pallas_call x4, Pallas kernels, mlp_pair(): pl.pallas_call(functools.partial(mlp_kernel, first=2 * pair), in_specs=[a...  60 us
    cond x101, local copies, waits for them, and re-layouts  48 us
    ppermute x26, starting transfers between devices, send_dp(): return lax.ppermute(array, 'dp', pairs)  40.9 us
    pallas_call x2, Pallas kernels, inner_of(): pl.pallas_call(functools.partial(inner_kernel, count=count, lefts=len(lef...  29.2 us
    convert_element_type x28, other arithmetic, add_rounded(): return total.astype(BF)  21.3 us
  transfers between devices with their start and end apart: 105, of which 46 were waited for; matrix products, arithmetic and copies ran while one was open for 17% of the time, Pallas kernels for 21%

profile of v2, /device:TPU:0, one launch (start us, length us, event | category | flops | bytes accessed | tf_op | source)
XLA Modules:
  0.0 751.5 jit_solution(16806319729260754599)
XLA Ops:
  21.2 4.6 all-to-all-start.3
  25.9 13.5 %collective-permute-done.49 = bf16[272,256]{1,0:T(8,128)(2,1)S(1)} collective-permute-done((bf16[272,256]{1,0:T(8,128)(2,1)S(1)}, bf16[272,256]{1,0:T(8,128)(2,1)S(1)}, u32[]{:S(2)}, u32[]{:S(2)}) %collective-permute-start.49) | collective-permute-done | bytes 139296 | tf_op jit(solution)/shard_map/ppermute | solution.py:42
  39.6 6.8 collective-permute-start.50
  46.4 3.2 convert_multiply_fusion.4
  52.5 14.7 %collective-permute-done.50 = bf16[2,272,256]{2,1,0:T(8,128)(2,1)S(1)} collective-permute-done((bf16[2,272,256]{2,1,0:T(8,128)(2,1)S(1)}, bf16[2,272,256]{2,1,0:T(8,128)(2,1)S(1)}, u32[]{:S(2)}, u32[]{:S(2)}) %collective-permute-start.50) | collective-permute-done | bytes 278560 | tf_op jit(solution)/shard_map/ppermute | solution.py:42
  68.0 8.8 %collective-permute-done.45 = bf16[128,2048]{1,0:T(8,128)(2,1)} collective-permute-done((bf16[128,2048]{1,0:T(8,128)(2,1)}, bf16[128,2048]{1,0:T(8,128)(2,1)}, u32[]{:S(2)}, u32[]{:S(2)}) %collective-permute-start.45) | collective-permute-done | bytes 524320 | tf_op jit(solution)/shard_map/ppermute | solution.py:42
  91.4 4.2 shard_map.230
  95.6 4.2 shard_map.231
  99.8 4.2 shard_map.232
  107.8 3.0 collective-permute-done.59.gb_hbm
  115.4 3.1 shard_map.233
  118.5 9.6 %shard_map.234 = (bf16[8,2,128,256]{3,2,1,0:T(8,128)(2,1)S(1)}, f32[2,2,1024]{2,1,0:T(2,128)S(1)}) custom-call(s32[2]{0:T(128)S(1)} %copy-done.72, s32[2]{0:T(128)S(1)} %pad_add_fusion.key_ref, bf16[8,2,128,256]{3,2,1,0:T(8,128)(2,1)S(1)} %get-tuple-element.463.q_ref, bf16[8,2,128,256]{3,2,1,0:T(8,128)(2,1)S(1)} %get-tuple-element.464.kv_ref), custom_call_target="tpu_custom_call" | custom-call | flops 1000 | bytes 1000 | tf_op jit(solution)/shard_map/pallas_call | solution.py:250
  128.5 4.2 shard_map.235
  140.4 9.6 %collective-permute-done.65 = bf16[128,2048]{1,0:T(8,128)(2,1)S(1)} collective-permute-done((bf16[128,2048]{1,0:T(8,128)(2,1)S(1)}, bf16[128,2048]{1,0:T(8,128)(2,1)S(1)}, u32[]{:S(2)}, u32[]{:S(2)}) %collective-permute-start.65) | collective-permute-done | bytes 524320 | tf_op jit(solution)/shard_map/ppermute | solution.py:42
  152.5 19.9 %shard_map.236 = (bf16[2,128,2048]{2,1,0:T(8,128)(2,1)}, f32[8,2,128,256]{3,2,1,0:T(8,128)}) custom-call(s32[2]{0:T(128)S(1)} %copy-done.72, s32[2]{0:T(128)S(1)} %pad_add_fusion.key_ref, bf16[2,128,2048]{2,1,0:T(8,128)(2,1)S(1)} %copy-done.18, bf16[2,128,2048]{2,1,0:T(8,128)(2,1)S(1)} %copy-done.19, bf16[8,2,128,256]{3,2,1,0:T(8,128)(2,1)S(1)} %get-tuple-element.464.kv_ref), custom_call_target="tpu_custom_call" | custom-call | flops 1000 | bytes 1000 | tf_op jit(solution)/shard_map/pallas_call | solution.py:326
  176.7 17.1 %all-gather.3.cloned.1.call-done = bf16[32,64,1408]{2,1,0:T(8,128)(2,1)} async-done(((bf16[8,64,1408]{2,1,0:T(8,128)(2,1)}), bf16[32,64,1408]{2,1,0:T(8,128)(2,1)}) %all-gather.3.cloned.1.call-update) | async-done | bytes 5767184 | tf_op jit(solution)/shard_map/all_gather | solution.py:795
  199.1 22.2 %collective-permute-done.71.na_hbm.refs_4_ = bf16[256,2048]{1,0:T(8,128)(2,1)S(1)} collective-permute-done((bf16[256,2048]{1,0:T(8,128)(2,1)S(1)}, bf16[256,2048]{1,0:T(8,128)(2,1)S(1)}, u32[]{:S(2)}, u32[]{:S(2)}) %collective-permute-start.71) | collective-permute-done | bytes 1048608 | tf_op jit(solution)/shard_map/ppermute | solution.py:42
  222.5 14.8 %shard_map.237 = (bf16[8,256,704]{2,1,0:T(8,128)(2,1)S(1)}, bf16[8,256,704]{2,1,0:T(8,128)(2,1)}, bf16[8,256,704]{2,1,0:T(8,128)(2,1)}, bf16[256,2048]{1,0:T(8,1...) custom-call(bf16[256,2048]{1,0:T(8,128)(2,1)S(1)} %multiply_convert_fusion.na_hbm.refs_2_,, ...), custom_call_target="tpu_custom_call" | custom-call | flops 1000 | bytes 1000 | tf_op jit(solution)/shard_map/pallas_call | solution.py:567
  239.8 15.0 %shard_map.238 = (bf16[8,256,704]{2,1,0:T(8,128)(2,1)S(1)}, bf16[8,256,704]{2,1,0:T(8,128)(2,1)}, bf16[8,256,704]{2,1,0:T(8,128)(2,1)}, bf16[256,2048]{1,0:T(8,1...) custom-call(bf16[256,2048]{1,0:T(8,128)(2,1)S(1)} %collective-permut, ...), custom_call_target="tpu_custom_call", output_to_operand_aliasing={{0}: (6, {}), {1}: (7, {}), {2}: (8, {})} | custom-call | flops 1000 | bytes 1000 | tf_op jit(solution)/shard_map/pallas_call | solution.py:567
  255.5 15.2 %shard_map.239 = (bf16[8,256,704]{2,1,0:T(8,128)(2,1)S(1)}, bf16[8,256,704]{2,1,0:T(8,128)(2,1)}, bf16[8,256,704]{2,1,0:T(8,128)(2,1)}, bf16[256,2048]{1,0:T(8,1...) custom-call(bf16[256,2048]{1,0:T(8,128)(2,1)S(1)} %collective-permut, ...), custom_call_target="tpu_custom_call", output_to_operand_aliasing={{0}: (6, {}), {1}: (7, {}), {2}: (8, {})} | custom-call | flops 1000 | bytes 1000 | tf_op jit(solution)/shard_map/pallas_call | solution.py:567
  270.7 15.0 %shard_map.240 = (bf16[8,256,704]{2,1,0:T(8,128)(2,1)S(1)}, bf16[8,256,704]{2,1,0:T(8,128)(2,1)}, bf16[8,256,704]{2,1,0:T(8,128)(2,1)}, bf16[256,2048]{1,0:T(8,1...) custom-call(bf16[256,2048]{1,0:T(8,128)(2,1)S(1)} %pad_maximum_fusio, ...), custom_call_target="tpu_custom_call", output_to_operand_aliasing={{0}: (6, {}), {1}: (7, {}), {2}: (8, {})} | custom-call | flops 1000 | bytes 1000 | tf_op jit(solution)/shard_map/pallas_call | solution.py:567
  285.7 3.0 copy-done
  290.6 17.5 %shard_map.241 = (bf16[704,2048]{1,0:T(8,128)(2,1)S(1)}, bf16[704,2048]{1,0:T(8,128)(2,1)}) custom-call(bf16[2048,704]{1,0:T(8,128)(2,1)S(1)} %bitcast.92, bf16[2048,704]{1,0:T(8,128)(2,1)S(1)} %bitcast.93, bf16[256,2048]{1,0:T(8,128)(2,1)S(1)} %multiply_convert_fusion.na_hbm.refs_2_, bf16[256,2048]{1,0:T(8,128)(2,1)S(1)} %collective-permute-done.70.nb_hbm.refs_3_, ...), custom_call_target="tpu_custom_call" | custom-call | flops 1000 | bytes 1000 | tf_op jit(solution)/shard_map/pallas_call | solution.py:700
  311.3 50.9 %conditional.4 = (f32[256,2048]{1,0:T(8,128)}, bf16[704,2048]{1,0:T(8,128)(2,1)}, bf16[704,2048]{1,0:T(8,128)(2,1)}, bf16[1,8,256]{2,0,1:T(2,128)(2,1)S(1)}) conditional(s32[]{:T(128)} %bitcast.20, () %tuple.73, (f32[256]{0:T(256)S(1)}, f32[256,1]{0,1:T(1,128)S(1)}, f32[256,1]{0,1:T(1,128)S(1)}, bf16[256,2048]{1,0:T(8,128)(2,1)}, ...), branch_computations={%region_1.2_spmd, %region_2.5_spmd} | conditional | flops 25167848 | bytes 116971016 | solution.py:172
  319.0 11.0 %collective-permute-done.23 = bf16[128,2048]{1,0:T(8,128)(2,1)S(1)} collective-permute-done((bf16[128,2048]{1,0:T(8,128)(2,1)S(1)}, bf16[128,2048]{1,0:T(8,128)(2,1)S(1)}, u32[]{:S(2)}, u32[]{:S(2)}) %collective-permute-start.23) | collective-permute-done | bytes 524320 | tf_op jit(solution)/shard_map/cond/branch_1_fun/ppermute | solution.py:42
  332.7 11.7 %branch_1_fun.8 = bf16[704,2048]{1,0:T(8,128)(2,1)} custom-call(bf16[2048,704]{1,0:T(8,128)(2,1)S(1)} %bitcast.104, bf16[256,2048]{1,0:T(8,128)(2,1)} %get-tuple-element.195.refs_1_, bf16[256,2048]{1,0:T(8,128)(2,1)S(1)} %copy-done.45, bf16[256,2048]{1,0:T(8,128)(2,1)} %get-tuple-element.197.refs_3_, bf16[256,2048]{1,0:T(8,128)(2,1)} %get-tuple-element.198.refs_4_, ...), custom_call_target="tpu_custom_call" | custom-call | flops 1000 | bytes 1000 | tf_op jit(solution)/shard_map/cond/branch_1_fun/pallas_call | solution.py:700
  346.8 8.0 %collective-permute-done.24 = bf16[256,2048]{1,0:T(8,128)(2,1)S(1)} collective-permute-done((bf16[256,2048]{1,0:T(8,128)(2,1)S(1)}, bf16[256,2048]{1,0:T(8,128)(2,1)S(1)}, u32[]{:S(2)}, u32[]{:S(2)}) %collective-permute-start.24) | collective-permute-done | bytes 1048608 | tf_op jit(solution)/shard_map/cond/branch_1_fun/ppermute | solution.py:42
  358.1 3.8 fusion.3
  363.2 65.9 %conditional.5 = (bf16[8,2,128,256]{3,2,1,0:T(8,128)(2,1)}, bf16[256,2048]{1,0:T(8,128)(2,1)}, bf16[8,176,256]{2,1,0:T(8,128)(2,1)}, bf16[704,2048]{1,0:T(8,128)(2,1)}) conditional(s32[]{:T(128)} %bitcast.20, () %tuple.72, (f32[256,2048]{1,0:T(8,128)}, bf16[256,2048]{1,0:T(8,128)(2,1)}, bf16[8,2,128,256]{3,2,1,0:T(8,128)(2,1)}, ...), branch_computations={%region_6.7_spmd, %region_7.8_spmd} | conditional | flops 528288 | bytes 100733592 | solution.py:172
  368.2 21.8 %collective-permute-done.1.a_ref = bf16[256,2048]{1,0:T(8,128)(2,1)S(1)} collective-permute-done((bf16[256,2048]{1,0:T(8,128)(2,1)S(1)}, bf16[256,2048]{1,0:T(8,128)(2,1)S(1)}, u32[]{:S(2)}, u32[]{:S(2)}) %collective-permute-start.1) | collective-permute-done | bytes 1048608 | tf_op jit(solution)/shard_map/cond/branch_1_fun/ppermute | solution.py:42
  397.3 10.9 %collective-permute-done.5 = bf16[128,2048]{1,0:T(8,128)(2,1)S(1)} collective-permute-done((bf16[128,2048]{1,0:T(8,128)(2,1)S(1)}, bf16[128,2048]{1,0:T(8,128)(2,1)S(1)}, u32[]{:S(2)}, u32[]{:S(2)}) %collective-permute-start.5) | collective-permute-done | bytes 524320 | tf_op jit(solution)/shard_map/cond/branch_1_fun/ppermute | solution.py:42
  411.5 4.2 all-to-all-start
  415.8 3.9 copy.128
  424.8 4.4 branch_1_fun.12
  430.7 106.4 %conditional.6 = (bf16[256,2048]{1,0:T(8,128)(2,1)}, bf16[256,2048]{1,0:T(8,128)(2,1)}, bf16[256,2048]{1,0:T(8,128)(2,1)}, bf16[256,2048]{1,0:T(8,128)(2,1)}, bf...) conditional(s32[]{:T(128)} %bitcast.20, () %tuple.71, ...), branch_computations={%region_9.10_spmd, %region_10.11_spmd} | conditional | flops 18877368 | bytes 164696208 | solution.py:172
  431.2 3.8 collective-permute-start.14
  438.8 4.2 all-to-all-start.1
  443.7 12.1 %branch_1_fun.13 = bf16[8,2,128,512]{3,2,1,0:T(8,128)(2,1)S(1)} custom-call(s32[2]{0:T(128)S(1)} %get-tuple-element.228.lengths_ref, s32[2]{0:T(128)S(1)} %get-tuple-element.229.key_ref, bf16[8,2,128,256]{3,2,1,0:T(8,128)(2,1)} %get-tuple-element.230.q_ref, bf16[8,2,128,256]{3,2,1,0:T(8,128)(2,1)} %get-tuple-element.231.up_ref, ...), custom_call_target="tpu_custom_call" | custom-call | flops 1000 | bytes 1000 | tf_op jit(solution)/shard_map/cond/branch_1_fun/pallas_call | solution.py:422
  455.9 7.2 branch_1_fun.15
  466.0 5.6 branch_1_fun.14
  479.8 4.3 all-to-all-start.2
  513.4 4.2 collective-permute-done.18
  520.9 2.8 copy.74
  526.0 3.2 pad_maximum_fusion.2
  533.8 3.1 collective-permute-done.19
  538.7 92.4 %conditional.7 = (bf16[2048]{0:T(1024)(128)(2,1)S(1)}, bf16[8,176,256]{2,1,0:T(8,128)(2,1)}, bf16[8,176,256]{2,1,0:T(8,128)(2,1)S(1)}, bf16[8,176,256]{2,1,0:T(8...) conditional(s32[]{:T(128)} %bitcast.20, () %tuple.70, ...), branch_computations={%region_11.12_spmd, %region_12.0_spmd} | conditional | flops 30931712 | bytes 121407320 | solution.py:172
  560.0 7.5 collective-permute-done.31
  577.8 14.3 %collective-permute-done.37 = bf16[8,176,256]{2,1,0:T(8,128)(2,1)} collective-permute-done((bf16[8,176,256]{2,1,0:T(8,128)(2,1)}, bf16[8,176,256]{2,1,0:T(8,128)(2,1)}, u32[]{:S(2)}, u32[]{:S(2)}) %collective-permute-start.37) | collective-permute-done | bytes 720928 | tf_op jit(solution)/shard_map/cond/branch_1_fun/ppermute | solution.py:136
  600.8 2.8 add_convert_fusion.13
  607.2 6.5 collective-permute-done.40
  618.7 3.6 fusion.9
  622.3 8.8 %collective-permute-done.41 = bf16[8,176,256]{2,1,0:T(8,128)(2,1)} collective-permute-done((bf16[8,176,256]{2,1,0:T(8,128)(2,1)}, bf16[8,176,256]{2,1,0:T(8,128)(2,1)}, u32[]{:S(2)}, u32[]{:S(2)}) %collective-permute-start.41) | collective-permute-done | bytes 720928 | tf_op jit(solution)/shard_map/cond/branch_1_fun/ppermute | solution.py:136
  633.2 10.2 %collective-permute-done.79 = bf16[4,272,256]{2,1,0:T(8,128)(2,1)S(1)} collective-permute-done((bf16[4,272,256]{2,1,0:T(8,128)(2,1)S(1)}, bf16[4,272,256]{2,1,0:T(8,128)(2,1)S(1)}, u32[]{:S(2)}, u32[]{:S(2)}) %collective-permute-start.79) | collective-permute-done | bytes 557088 | tf_op jit(solution)/shard_map/ppermute | solution.py:42
  643.7 2.7 collective-permute-start.80
  651.1 3.6 collective-permute-start.90
  657.5 2.8 collective-permute-done.87
  661.7 2.7 collective-permute-start.82
  664.4 25.1 %collective-permute-done.82 = bf16[272,256]{1,0:T(8,128)(2,1)S(1)} collective-permute-done((bf16[272,256]{1,0:T(8,128)(2,1)S(1)}, bf16[272,256]{1,0:T(8,128)(2,1)S(1)}, u32[]{:S(2)}, u32[]{:S(2)}) %collective-permute-start.82) | collective-permute-done | bytes 139296 | tf_op jit(solution)/shard_map/ppermute | solution.py:136
  692.5 6.8 shard_map.242
  699.3 6.6 shard_map.243
  710.0 3.4 collective-permute-done.94
  714.7 11.6 %collective-permute-done.89 = bf16[128,2048]{1,0:T(8,128)(2,1)S(1)} collective-permute-done((bf16[128,2048]{1,0:T(8,128)(2,1)}, bf16[128,2048]{1,0:T(8,128)(2,1)S(1)}, u32[]{:S(2)}, u32[]{:S(2)}) %collective-permute-start.89) | collective-permute-done | bytes 524320 | tf_op jit(solution)/shard_map/ppermute | solution.py:136
  730.8 9.3 %collective-permute-done.95 = bf16[176,2048]{1,0:T(8,128)(2,1)S(1)} collective-permute-done((bf16[176,2048]{1,0:T(8,128)(2,1)}, bf16[176,2048]{1,0:T(8,128)(2,1)S(1)}, u32[]{:S(2)}, u32[]{:S(2)}) %collective-permute-start.95) | collective-permute-done | bytes 720928 | tf_op jit(solution)/shard_map/ppermute | solution.py:136
  741.8 2.9 maximum_convert_fusion
  (475 shorter events, 240.2 us)
Async XLA Ops:
  7.2 83.9 %collective-permute-start.54 = (bf16[256,2048]{1,0:T(8,128)(2,1)}, bf16[256,2048]{1,0:T(8,128)(2,1)}, u32[]{:S(2)}, u32[]{:S(2)}) collective-permute-start(bf16[256,2048]{1,0:T(8,128)(2,1)} %bitcast.96), channel_id=1, source_target_pairs={{0,1},{1,0},{2,3},{3,2},{4,5},{5,4},{6,7},{7,6},{8,9},{9,8},{10,11... | collective-permute-start | bytes 3145736 | tf_op jit(solution)/shard_map/ppermute | solution.py:42
  7.7 41.8 %collective-permute-start.44 = (bf16[256,2048]{1,0:T(8,128)(2,1)}, bf16[256,2048]{1,0:T(8,128)(2,1)S(1)}, u32[]{:S(2)}, u32[]{:S(2)}) collective-permute-start(bf16[256,2048]{1,0:T(8,128)(2,1)} %bitcast.97), channel_id=1, source_target_pairs={{0,2},{1,3},{2,0},{3,1},{4,6},{5,7},{6,4},{7,5},{8,10},{9,11},{10,... | collective-permute-start | bytes 3145736 | tf_op jit(solution)/shard_map/ppermute | solution.py:42
  10.3 42.1 %collective-permute-start.46 = (bf16[256,2048]{1,0:T(8,128)(2,1)}, bf16[256,2048]{1,0:T(8,128)(2,1)S(1)}, u32[]{:S(2)}, u32[]{:S(2)}) collective-permute-start(bf16[256,2048]{1,0:T(8,128)(2,1)} %bitcast.98), channel_id=1, source_target_pairs={{0,4},{1,5},{2,6},{3,7},{4,0},{5,1},{6,2},{7,3},{8,12},{9,13},{10,... | collective-permute-start | bytes 3145736 | tf_op jit(solution)/shard_map/ppermute | solution.py:42
  14.0 25.5 %collective-permute-start.49 = (bf16[272,256]{1,0:T(8,128)(2,1)S(1)}, bf16[272,256]{1,0:T(8,128)(2,1)S(1)}, u32[]{:S(2)}, u32[]{:S(2)}) collective-permute-start(bf16[272,256]{1,0:T(8,128)(2,1)S(1)} %pad_maximum_fusion.17), channel_id=1, source_target_pairs={{0,4},{1,5},{2,6},{3,7},{4,0},{5,1},{6,2},{7,3},{8,12},{9,13},{10,... | collective-permute-start | bytes 417800 | tf_op jit(solution)/shard_map/ppermute | solution.py:42
  21.2 63.7 %all-to-all-start.3 = ((bf16[8,64,2432]{2,1,0:T(8,128)(2,1)}), bf16[8,64,2432]{2,1,0:T(8,128)(2,1)}, u32[]{:S(2)}, u32[]{:S(2)}) async-start(bf16[8,64,2432]{2,1,0:T(8,128)(2,1)} %shard_map.229), calls=%async_computation.3 | async-start | bytes 4980736 | tf_op jit(solution)/shard_map/all_to_all | solution.py:792
  25.8 168.0 %all-gather.3.cloned.1.call-start = ((), (), s32[]{:S(2)}) async-start(), calls=%async_computation.12 | async-start | bytes 7208960 | tf_op jit(solution)/shard_map/all_gather | solution.py:795
  39.6 27.7 %collective-permute-start.50 = (bf16[2,272,256]{2,1,0:T(8,128)(2,1)S(1)}, bf16[2,272,256]{2,1,0:T(8,128)(2,1)S(1)}, u32[]{:S(2)}, u32[]{:S(2)}) collective-permute-start(bf16[2,272,256]{2,1,0:T(8,128)(2,1)S(1)} %pad_maximum_fusion.16), channel_id=1, source_target_pairs={{0,2},{1,3},{2,0},{3,1},{4,6},{5,7},{6,4},{7,5},{8,10},{9,11},{10,... | collective-permute-start | bytes 835592 | tf_op jit(solution)/shard_map/ppermute | solution.py:42
  50.4 26.3 %collective-permute-start.45 = (bf16[128,2048]{1,0:T(8,128)(2,1)}, bf16[128,2048]{1,0:T(8,128)(2,1)}, u32[]{:S(2)}, u32[]{:S(2)}) collective-permute-start(bf16[128,2048]{1,0:T(8,128)(2,1)} %slice.238), channel_id=1, source_target_pairs={{0,4},{1,5},{2,6},{3,7},{4,0},{5,1},{6,2},{7,3},{8,12},{9,13},{10,... | collective-permute-start | bytes 1572872 | tf_op jit(solution)/shard_map/ppermute | solution.py:42
  52.4 25.8 %collective-permute-start.47 = (bf16[128,2048]{1,0:T(8,128)(2,1)S(1)}, bf16[128,2048]{1,0:T(8,128)(2,1)S(1)}, u32[]{:S(2)}, u32[]{:S(2)}) collective-permute-start(bf16[128,2048]{1,0:T(8,128)(2,1)S(1)} %slice.239), channel_id=1, source_target_pairs={{0,2},{1,3},{2,0},{3,1},{4,6},{5,7},{6,4},{7,5},{8,10},{9,11},{10,... | collective-permute-start | bytes 1572872 | tf_op jit(solution)/shard_map/ppermute | solution.py:42
  67.5 28.1 %collective-permute-start.53 = (bf16[256,2048]{1,0:T(8,128)(2,1)S(1)}, bf16[256,2048]{1,0:T(8,128)(2,1)}, u32[]{:S(2)}, u32[]{:S(2)}) collective-permute-start(bf16[256,2048]{1,0:T(8,128)(2,1)S(1)} %collective-permute-done.44.a_ref), channel_id=1, source_target_pairs={{0,1},{1,0},{2,3},{3,2},{4,5},{5,4},{6,7},{7,6},{8,9},{9,8},{10,11... | collective-permute-start | bytes 3145736 | tf_op jit(solution)/shard_map/ppermute | solution.py:42
  76.7 23.1 %collective-permute-start.52 = (bf16[256,2048]{1,0:T(8,128)(2,1)S(1)}, bf16[256,2048]{1,0:T(8,128)(2,1)}, u32[]{:S(2)}, u32[]{:S(2)}) collective-permute-start(bf16[256,2048]{1,0:T(8,128)(2,1)S(1)} %collective-permute-done.46.a_ref), channel_id=1, source_target_pairs={{0,1},{1,0},{2,3},{3,2},{4,5},{5,4},{6,7},{7,6},{8,9},{9,8},{10,11... | collective-permute-start | bytes 3145736 | tf_op jit(solution)/shard_map/ppermute | solution.py:42
  78.3 25.7 %collective-permute-start.56 = (bf16[256,2048]{1,0:T(8,128)(2,1)}, bf16[256,2048]{1,0:T(8,128)(2,1)}, u32[]{:S(2)}, u32[]{:S(2)}) collective-permute-start(bf16[256,2048]{1,0:T(8,128)(2,1)} %get-tuple-element.466.ga_hbm), channel_id=1, source_target_pairs={{0,2},{1,3},{2,0},{3,1},{4,6},{5,7},{6,4},{7,5},{8,10},{9,11},{10,... | collective-permute-start | bytes 3145736 | tf_op jit(solution)/shard_map/ppermute | solution.py:42
  80.1 24.7 %collective-permute-start.57 = (bf16[256,2048]{1,0:T(8,128)(2,1)}, bf16[256,2048]{1,0:T(8,128)(2,1)}, u32[]{:S(2)}, u32[]{:S(2)}) collective-permute-start(bf16[256,2048]{1,0:T(8,128)(2,1)} %get-tuple-element.466.ga_hbm), channel_id=1, source_target_pairs={{0,4},{1,5},{2,6},{3,7},{4,0},{5,1},{6,2},{7,3},{8,12},{9,13},{10,... | collective-permute-start | bytes 3145736 | tf_op jit(solution)/shard_map/ppermute | solution.py:42
  87.6 275.6 %reduce-scatter.5.cloned.1.call-start = ((), (), s32[]{:S(2)}) async-start(), calls=%async_computation.8 | async-start | bytes 3604480 | tf_op jit(solution)/shard_map/reduce_scatter | solution.py:140
  133.3 39.2 %collective-permute-start.62 = (bf16[256,2048]{1,0:T(8,128)(2,1)S(1)}, bf16[256,2048]{1,0:T(8,128)(2,1)S(1)}, u32[]{:S(2)}, u32[]{:S(2)}) collective-permute-start(bf16[256,2048]{1,0:T(8,128)(2,1)S(1)} %get-tuple-element.473), channel_id=1, source_target_pairs={{0,1},{1,0},{2,3},{3,2},{4,5},{5,4},{6,7},{7,6},{8,9},{9,8},{10,11... | collective-permute-start | bytes 3145736 | tf_op jit(solution)/shard_map/ppermute | solution.py:42
  150.2 24.5 %collective-permute-start.66 = (bf16[256,2048]{1,0:T(8,128)(2,1)S(1)}, bf16[256,2048]{1,0:T(8,128)(2,1)S(1)}, u32[]{:S(2)}, u32[]{:S(2)}) collective-permute-start(bf16[256,2048]{1,0:T(8,128)(2,1)S(1)} %pad_maximum_fusion.10), channel_id=1, source_target_pairs={{0,2},{1,3},{2,0},{3,1},{4,6},{5,7},{6,4},{7,5},{8,10},{9,11},{10,... | collective-permute-start | bytes 3145736 | tf_op jit(solution)/shard_map/ppermute | solution.py:42
  151.7 24.5 %collective-permute-start.69 = (bf16[256,2048]{1,0:T(8,128)(2,1)S(1)}, bf16[256,2048]{1,0:T(8,128)(2,1)S(1)}, u32[]{:S(2)}, u32[]{:S(2)}) collective-permute-start(bf16[256,2048]{1,0:T(8,128)(2,1)S(1)} %pad_maximum_fusion.11), channel_id=1, source_target_pairs={{0,4},{1,5},{2,6},{3,7},{4,0},{5,1},{6,2},{7,3},{8,12},{9,13},{10,... | collective-permute-start | bytes 3145736 | tf_op jit(solution)/shard_map/ppermute | solution.py:42
  196.1 25.2 %collective-permute-start.71 = (bf16[256,2048]{1,0:T(8,128)(2,1)S(1)}, bf16[256,2048]{1,0:T(8,128)(2,1)S(1)}, u32[]{:S(2)}, u32[]{:S(2)}) collective-permute-start(bf16[256,2048]{1,0:T(8,128)(2,1)S(1)} %multiply_convert_fusion.na_hbm.refs_2_), channel_id=1, source_target_pairs={{0,2},{1,3},{2,0},{3,1},{4,6},{5,7},{6,4},{7,5},{8,10},{9,11},{10,... | collective-permute-start | bytes 3145736 | tf_op jit(solution)/shard_map/ppermute | solution.py:42
  197.6 24.8 %collective-permute-start.73 = (bf16[256,2048]{1,0:T(8,128)(2,1)S(1)}, bf16[256,2048]{1,0:T(8,128)(2,1)S(1)}, u32[]{:S(2)}, u32[]{:S(2)}) collective-permute-start(bf16[256,2048]{1,0:T(8,128)(2,1)S(1)} %multiply_convert_fusion.na_hbm.refs_2_), channel_id=1, source_target_pairs={{0,4},{1,5},{2,6},{3,7},{4,0},{5,1},{6,2},{7,3},{8,12},{9,13},{10,... | collective-permute-start | bytes 3145736 | tf_op jit(solution)/shard_map/ppermute | solution.py:42
  199.1 23.4 %collective-permute-start.70 = (bf16[256,2048]{1,0:T(8,128)(2,1)S(1)}, bf16[256,2048]{1,0:T(8,128)(2,1)S(1)}, u32[]{:S(2)}, u32[]{:S(2)}) collective-permute-start(bf16[256,2048]{1,0:T(8,128)(2,1)S(1)} %multiply_convert_fusion.na_hbm.refs_2_), channel_id=1, source_target_pairs={{0,1},{1,0},{2,3},{3,2},{4,5},{5,4},{6,7},{7,6},{8,9},{9,8},{10,11... | collective-permute-start | bytes 3145736 | tf_op jit(solution)/shard_map/ppermute | solution.py:42
  239.8 30.9 %collective-permute-start.78 = (bf16[256,2048]{1,0:T(8,128)(2,1)S(1)}, bf16[256,2048]{1,0:T(8,128)(2,1)}, u32[]{:S(2)}, u32[]{:S(2)}) collective-permute-start(bf16[256,2048]{1,0:T(8,128)(2,1)S(1)} %pad_maximum_fusion.9.ga_hbm), channel_id=1, source_target_pairs={{0,1},{1,0},{2,3},{3,2},{4,5},{5,4},{6,7},{7,6},{8,9},{9,8},{10,11... | collective-permute-start | bytes 3145736 | tf_op jit(solution)/shard_map/ppermute | solution.py:42
  309.8 119.4 %reduce-scatter.7.cloned.1.call-start = ((), (), s32[]{:S(2)}) async-start(), calls=%async_computation.9 | async-start | bytes 3604480 | tf_op jit(solution)/shard_map/reduce_scatter | solution.py:140
  311.9 34.2 %collective-permute-start.20 = (bf16[256,2048]{1,0:T(8,128)(2,1)}, bf16[256,2048]{1,0:T(8,128)(2,1)S(1)}, u32[]{:S(2)}, u32[]{:S(2)}) collective-permute-start(bf16[256,2048]{1,0:T(8,128)(2,1)} %get-tuple-element.193), channel_id=1, source_target_pairs={{0,1},{1,0},{2,3},{3,2},{4,5},{5,4},{6,7},{7,6},{8,9},{9,8},{10,11... | collective-permute-start | bytes 3145736 | tf_op jit(solution)/shard_map/cond/branch_1_fun/ppermute | solution.py:42
  330.3 24.5 %collective-permute-start.24 = (bf16[256,2048]{1,0:T(8,128)(2,1)S(1)}, bf16[256,2048]{1,0:T(8,128)(2,1)S(1)}, u32[]{:S(2)}, u32[]{:S(2)}) collective-permute-start(bf16[256,2048]{1,0:T(8,128)(2,1)S(1)} %pad_maximum_fusion), channel_id=1, source_target_pairs={{0,2},{1,3},{2,0},{3,1},{4,6},{5,7},{6,4},{7,5},{8,10},{9,11},{10,... | collective-permute-start | bytes 3145736 | tf_op jit(solution)/shard_map/cond/branch_1_fun/ppermute | solution.py:42
  331.8 24.3 %collective-permute-start.27 = (bf16[256,2048]{1,0:T(8,128)(2,1)S(1)}, bf16[256,2048]{1,0:T(8,128)(2,1)S(1)}, u32[]{:S(2)}, u32[]{:S(2)}) collective-permute-start(bf16[256,2048]{1,0:T(8,128)(2,1)S(1)} %pad_maximum_fusion.1), channel_id=1, source_target_pairs={{0,4},{1,5},{2,6},{3,7},{4,0},{5,1},{6,2},{7,3},{8,12},{9,13},{10,... | collective-permute-start | bytes 3145736 | tf_op jit(solution)/shard_map/cond/branch_1_fun/ppermute | solution.py:42
  363.2 173.9 %reduce-scatter.9.cloned.1.call-start = ((), (), s32[]{:S(2)}) async-start(), calls=%async_computation.10 | async-start | bytes 3604480 | tf_op jit(solution)/shard_map/reduce_scatter | solution.py:140
  365.2 24.8 %collective-permute-start.1 = (bf16[256,2048]{1,0:T(8,128)(2,1)S(1)}, bf16[256,2048]{1,0:T(8,128)(2,1)S(1)}, u32[]{:S(2)}, u32[]{:S(2)}) collective-permute-start(bf16[256,2048]{1,0:T(8,128)(2,1)S(1)} %convert_element_type.320.a_ref), channel_id=1, source_target_pairs={{0,2},{1,3},{2,0},{3,1},{4,6},{5,7},{6,4},{7,5},{8,10},{9,11},{10,... | collective-permute-start | bytes 3145736 | tf_op jit(solution)/shard_map/cond/branch_1_fun/ppermute | solution.py:42
  366.7 24.4 %collective-permute-start.3 = (bf16[256,2048]{1,0:T(8,128)(2,1)S(1)}, bf16[256,2048]{1,0:T(8,128)(2,1)S(1)}, u32[]{:S(2)}, u32[]{:S(2)}) collective-permute-start(bf16[256,2048]{1,0:T(8,128)(2,1)S(1)} %convert_element_type.320.a_ref), channel_id=1, source_target_pairs={{0,4},{1,5},{2,6},{3,7},{4,0},{5,1},{6,2},{7,3},{8,12},{9,13},{10,... | collective-permute-start | bytes 3145736 | tf_op jit(solution)/shard_map/cond/branch_1_fun/ppermute | solution.py:42
  368.2 23.0 %collective-permute-start = (bf16[256,2048]{1,0:T(8,128)(2,1)S(1)}, bf16[256,2048]{1,0:T(8,128)(2,1)S(1)}, u32[]{:S(2)}, u32[]{:S(2)}) collective-permute-start(bf16[256,2048]{1,0:T(8,128)(2,1)S(1)} %convert_element_type.320.a_ref), channel_id=1, source_target_pairs={{0,1},{1,0},{2,3},{3,2},{4,5},{5,4},{6,7},{7,6},{8,9},{9,8},{10,11... | collective-permute-start | bytes 3145736 | tf_op jit(solution)/shard_map/cond/branch_1_fun/ppermute | solution.py:42
  429.2 201.9 %reduce-scatter.11.cloned.1.call-start = ((), (), s32[]{:S(2)}) async-start(), calls=%async_computation.11 | async-start | bytes 2621440 | tf_op jit(solution)/shard_map/reduce_scatter | solution.py:140
  430.7 65.3 %collective-permute-start.10 = (bf16[256,2048]{1,0:T(8,128)(2,1)}, bf16[256,2048]{1,0:T(8,128)(2,1)}, u32[]{:S(2)}, u32[]{:S(2)}) collective-permute-start(bf16[256,2048]{1,0:T(8,128)(2,1)} %get-tuple-element.253), channel_id=1, source_target_pairs={{0,1},{1,0},{2,3},{3,2},{4,5},{5,4},{6,7},{7,6},{8,9},{9,8},{10,11... | collective-permute-start | bytes 3145736 | tf_op jit(solution)/shard_map/cond/branch_1_fun/ppermute | solution.py:42
  431.2 52.8 %collective-permute-start.14 = (bf16[8,176,256]{2,1,0:T(8,128)(2,1)}, bf16[8,176,256]{2,1,0:T(8,128)(2,1)}, u32[]{:S(2)}, u32[]{:S(2)}) collective-permute-start(bf16[8,176,256]{2,1,0:T(8,128)(2,1)} %get-tuple-element.902), channel_id=1, source_target_pairs={{0,8},{8,16},{16,24},{1,9},{9,17},{17,25},{2,10},{10,18},{18,26},{... | collective-permute-start | bytes 2162696 | tf_op jit(solution)/shard_map/cond/branch_1_fun/ppermute | solution.py:136
  435.0 51.2 %collective-permute-start.15 = (bf16[8,176,256]{2,1,0:T(8,128)(2,1)}, bf16[8,176,256]{2,1,0:T(8,128)(2,1)}, u32[]{:S(2)}, u32[]{:S(2)}) collective-permute-start(bf16[8,176,256]{2,1,0:T(8,128)(2,1)} %get-tuple-element.902), channel_id=1, source_target_pairs={{8,0},{16,8},{24,16},{9,1},{17,9},{25,17},{10,2},{18,10},{26,18},{... | collective-permute-start | bytes 2162696 | tf_op jit(solution)/shard_map/cond/branch_1_fun/ppermute | solution.py:136
  438.8 40.9 %all-to-all-start.1 = ((bf16[8,176,256]{2,1,0:T(8,128)(2,1)}), bf16[8,176,256]{2,1,0:T(8,128)(2,1)}, u32[]{:S(2)}, u32[]{:S(2)}) async-start(bf16[8,176,256]{2,1,0:T(8,128)(2,1)} %copy.73), calls=%async_computation.1 | async-start | bytes 1441792 | tf_op jit(solution)/shard_map/cond/branch_1_fun/all_to_all | solution.py:749
  443.1 57.0 %collective-permute-start.9 = (bf16[256,2048]{1,0:T(8,128)(2,1)}, bf16[256,2048]{1,0:T(8,128)(2,1)}, u32[]{:S(2)}, u32[]{:S(2)}) collective-permute-start(bf16[256,2048]{1,0:T(8,128)(2,1)} %get-tuple-element.251), channel_id=1, source_target_pairs={{0,1},{1,0},{2,3},{3,2},{4,5},{5,4},{6,7},{7,6},{8,9},{9,8},{10,11... | collective-permute-start | bytes 3145736 | tf_op jit(solution)/shard_map/cond/branch_1_fun/ppermute | solution.py:42
  443.4 61.0 %collective-permute-start.12 = (bf16[256,2048]{1,0:T(8,128)(2,1)}, bf16[256,2048]{1,0:T(8,128)(2,1)}, u32[]{:S(2)}, u32[]{:S(2)}) collective-permute-start(bf16[256,2048]{1,0:T(8,128)(2,1)} %get-tuple-element.255), channel_id=1, source_target_pairs={{0,1},{1,0},{2,3},{3,2},{4,5},{5,4},{6,7},{7,6},{8,9},{9,8},{10,11... | collective-permute-start | bytes 3145736 | tf_op jit(solution)/shard_map/cond/branch_1_fun/ppermute | solution.py:42
  479.8 41.1 %all-to-all-start.2 = ((bf16[8,256,256]{2,1,0:T(8,128)(2,1)}), bf16[8,256,256]{2,1,0:T(8,128)(2,1)}, u32[]{:S(2)}, u32[]{:S(2)}) async-start(bf16[8,256,256]{2,1,0:T(8,128)(2,1)} %bitcast.10), calls=%async_computation.2 | async-start | bytes 2097152 | tf_op jit(solution)/shard_map/cond/branch_1_fun/all_to_all | solution.py:132
  484.1 23.5 %collective-permute-start.8 = (bf16[256,2048]{1,0:T(8,128)(2,1)}, bf16[256,2048]{1,0:T(8,128)(2,1)S(1)}, u32[]{:S(2)}, u32[]{:S(2)}) collective-permute-start(bf16[256,2048]{1,0:T(8,128)(2,1)} %get-tuple-element.249), channel_id=1, source_target_pairs={{0,1},{1,0},{2,3},{3,2},{4,5},{5,4},{6,7},{7,6},{8,9},{9,8},{10,11... | collective-permute-start | bytes 3145736 | tf_op jit(solution)/shard_map/cond/branch_1_fun/ppermute | solution.py:42
  486.2 23.6 %collective-permute-start.16 = (bf16[8,176,256]{2,1,0:T(8,128)(2,1)}, bf16[8,176,256]{2,1,0:T(8,128)(2,1)}, u32[]{:S(2)}, u32[]{:S(2)}) collective-permute-start(bf16[8,176,256]{2,1,0:T(8,128)(2,1)} %collective-permute-done.14), channel_id=1, source_target_pairs={{8,16},{16,24},{9,17},{17,25},{10,18},{18,26},{11,19},{19,27},{12,... | collective-permute-start | bytes 2162696 | tf_op jit(solution)/shard_map/cond/branch_1_fun/ppermute | solution.py:136
  496.0 21.6 %collective-permute-start.18 = (bf16[8,176,256]{2,1,0:T(8,128)(2,1)}, bf16[8,176,256]{2,1,0:T(8,128)(2,1)}, u32[]{:S(2)}, u32[]{:S(2)}) collective-permute-start(bf16[8,176,256]{2,1,0:T(8,128)(2,1)} %collective-permute-done.15), channel_id=1, source_target_pairs={{8,0},{16,8},{9,1},{17,9},{10,2},{18,10},{11,3},{19,11},{12,4},{20... | collective-permute-start | bytes 2162696 | tf_op jit(solution)/shard_map/cond/branch_1_fun/ppermute | solution.py:136
  500.1 29.1 %collective-permute-start.11 = (bf16[128,2048]{1,0:T(8,128)(2,1)}, bf16[128,2048]{1,0:T(8,128)(2,1)}, u32[]{:S(2)}, u32[]{:S(2)}) collective-permute-start(bf16[128,2048]{1,0:T(8,128)(2,1)} %get-tuple-element.788), channel_id=1, source_target_pairs={{0,4},{1,5},{2,6},{3,7},{4,0},{5,1},{6,2},{7,3},{8,12},{9,13},{10,... | collective-permute-start | bytes 1572872 | tf_op jit(solution)/shard_map/cond/branch_1_fun/ppermute | solution.py:42
  504.5 27.0 %collective-permute-start.13 = (bf16[128,2048]{1,0:T(8,128)(2,1)}, bf16[128,2048]{1,0:T(8,128)(2,1)}, u32[]{:S(2)}, u32[]{:S(2)}) collective-permute-start(bf16[128,2048]{1,0:T(8,128)(2,1)} %get-tuple-element.787), channel_id=1, source_target_pairs={{0,2},{1,3},{2,0},{3,1},{4,6},{5,7},{6,4},{7,5},{8,10},{9,11},{10,... | collective-permute-start | bytes 1572872 | tf_op jit(solution)/shard_map/cond/branch_1_fun/ppermute | solution.py:42
  509.8 23.9 %collective-permute-start.17 = (bf16[8,176,256]{2,1,0:T(8,128)(2,1)}, bf16[8,176,256]{2,1,0:T(8,128)(2,1)}, u32[]{:S(2)}, u32[]{:S(2)}) collective-permute-start(bf16[8,176,256]{2,1,0:T(8,128)(2,1)} %collective-permute-done.16), channel_id=1, source_target_pairs={{16,24},{17,25},{18,26},{19,27},{20,28},{21,29},{22,30},{23,31}} | collective-permute-start | bytes 2162696 | tf_op jit(solution)/shard_map/cond/branch_1_fun/ppermute | solution.py:136
  517.6 19.3 %collective-permute-start.19 = (bf16[8,176,256]{2,1,0:T(8,128)(2,1)}, bf16[8,176,256]{2,1,0:T(8,128)(2,1)}, u32[]{:S(2)}, u32[]{:S(2)}) collective-permute-start(bf16[8,176,256]{2,1,0:T(8,128)(2,1)} %collective-permute-done.18), channel_id=1, source_target_pairs={{8,0},{9,1},{10,2},{11,3},{12,4},{13,5},{14,6},{15,7}} | collective-permute-start | bytes 2162696 | tf_op jit(solution)/shard_map/cond/branch_1_fun/ppermute | solution.py:136
  538.7 34.1 %collective-permute-start.36 = (bf16[8,176,256]{2,1,0:T(8,128)(2,1)}, bf16[8,176,256]{2,1,0:T(8,128)(2,1)S(1)}, u32[]{:S(2)}, u32[]{:S(2)}) collective-permute-start(bf16[8,176,256]{2,1,0:T(8,128)(2,1)} %get-tuple-element.940), channel_id=1, source_target_pairs={{0,8},{8,16},{16,24},{1,9},{9,17},{17,25},{2,10},{10,18},{18,26},{... | collective-permute-start | bytes 2162696 | tf_op jit(solution)/shard_map/cond/branch_1_fun/ppermute | solution.py:136
  541.1 51.1 %collective-permute-start.37 = (bf16[8,176,256]{2,1,0:T(8,128)(2,1)}, bf16[8,176,256]{2,1,0:T(8,128)(2,1)}, u32[]{:S(2)}, u32[]{:S(2)}) collective-permute-start(bf16[8,176,256]{2,1,0:T(8,128)(2,1)} %get-tuple-element.940), channel_id=1, source_target_pairs={{8,0},{16,8},{24,16},{9,1},{17,9},{25,17},{10,2},{18,10},{26,18},{... | collective-permute-start | bytes 2162696 | tf_op jit(solution)/shard_map/cond/branch_1_fun/ppermute | solution.py:136
  551.2 23.4 %collective-permute-start.28 = (bf16[256,2048]{1,0:T(8,128)(2,1)}, bf16[256,2048]{1,0:T(8,128)(2,1)S(1)}, u32[]{:S(2)}, u32[]{:S(2)}) collective-permute-start(bf16[256,2048]{1,0:T(8,128)(2,1)} %get-tuple-element.271), channel_id=1, source_target_pairs={{0,1},{1,0},{2,3},{3,2},{4,5},{5,4},{6,7},{7,6},{8,9},{9,8},{10,11... | collective-permute-start | bytes 3145736 | tf_op jit(solution)/shard_map/cond/branch_1_fun/ppermute | solution.py:42
  567.5 26.3 %collective-permute-start.42 = (bf16[256,2048]{1,0:T(8,128)(2,1)}, bf16[256,2048]{1,0:T(8,128)(2,1)S(1)}, u32[]{:S(2)}, u32[]{:S(2)}) collective-permute-start(bf16[256,2048]{1,0:T(8,128)(2,1)} %get-tuple-element.287), channel_id=1, source_target_pairs={{0,2},{1,3},{2,0},{3,1},{4,6},{5,7},{6,4},{7,5},{8,10},{9,11},{10,... | collective-permute-start | bytes 3145736 | tf_op jit(solution)/shard_map/cond/branch_1_fun/ppermute | solution.py:42
  571.2 29.6 %collective-permute-start.43 = (bf16[256,2048]{1,0:T(8,128)(2,1)}, bf16[256,2048]{1,0:T(8,128)(2,1)S(1)}, u32[]{:S(2)}, u32[]{:S(2)}) collective-permute-start(bf16[256,2048]{1,0:T(8,128)(2,1)} %get-tuple-element.288), channel_id=1, source_target_pairs={{0,4},{1,5},{2,6},{3,7},{4,0},{5,1},{6,2},{7,3},{8,12},{9,13},{10,... | collective-permute-start | bytes 3145736 | tf_op jit(solution)/shard_map/cond/branch_1_fun/ppermute | solution.py:42
  572.8 44.3 %collective-permute-start.32 = (bf16[256,2048]{1,0:T(8,128)(2,1)S(1)}, bf16[256,2048]{1,0:T(8,128)(2,1)S(1)}, u32[]{:S(2)}, u32[]{:S(2)}) collective-permute-start(bf16[256,2048]{1,0:T(8,128)(2,1)S(1)} %pad_maximum_fusion.5), channel_id=1, source_target_pairs={{0,2},{1,3},{2,0},{3,1},{4,6},{5,7},{6,4},{7,5},{8,10},{9,11},{10,... | collective-permute-start | bytes 3145736 | tf_op jit(solution)/shard_map/cond/branch_1_fun/ppermute | solution.py:42
  574.7 43.0 %collective-permute-start.35 = (bf16[256,2048]{1,0:T(8,128)(2,1)S(1)}, bf16[256,2048]{1,0:T(8,128)(2,1)S(1)}, u32[]{:S(2)}, u32[]{:S(2)}) collective-permute-start(bf16[256,2048]{1,0:T(8,128)(2,1)S(1)} %pad_maximum_fusion.6), channel_id=1, source_target_pairs={{0,4},{1,5},{2,6},{3,7},{4,0},{5,1},{6,2},{7,3},{8,12},{9,13},{10,... | collective-permute-start | bytes 3145736 | tf_op jit(solution)/shard_map/cond/branch_1_fun/ppermute | solution.py:42
  593.7 20.0 %collective-permute-start.40 = (bf16[8,176,256]{2,1,0:T(8,128)(2,1)}, bf16[8,176,256]{2,1,0:T(8,128)(2,1)}, u32[]{:S(2)}, u32[]{:S(2)}) collective-permute-start(bf16[8,176,256]{2,1,0:T(8,128)(2,1)} %collective-permute-done.37), channel_id=1, source_target_pairs={{8,0},{16,8},{9,1},{17,9},{10,2},{18,10},{11,3},{19,11},{12,4},{20... | collective-permute-start | bytes 2162696 | tf_op jit(solution)/shard_map/cond/branch_1_fun/ppermute | solution.py:136
  603.6 18.7 %collective-permute-start.39 = (bf16[8,176,256]{2,1,0:T(8,128)(2,1)}, bf16[8,176,256]{2,1,0:T(8,128)(2,1)}, u32[]{:S(2)}, u32[]{:S(2)}) collective-permute-start(bf16[8,176,256]{2,1,0:T(8,128)(2,1)} %collective-permute-done.38), channel_id=1, source_target_pairs={{16,24},{17,25},{18,26},{19,27},{20,28},{21,29},{22,30},{23,31}} | collective-permute-start | bytes 2162696 | tf_op jit(solution)/shard_map/cond/branch_1_fun/ppermute | solution.py:136
  651.1 38.5 %collective-permute-start.90 = (bf16[176,2048]{1,0:T(8,128)(2,1)S(1)}, bf16[176,2048]{1,0:T(8,128)(2,1)S(1)}, u32[]{:S(2)}, u32[]{:S(2)}) collective-permute-start(bf16[176,2048]{1,0:T(8,128)(2,1)S(1)} %copy-done.67), channel_id=1, source_target_pairs={{0,8},{8,16},{16,24},{1,9},{9,17},{17,25},{2,10},{10,18},{18,26},{... | collective-permute-start | bytes 2162696 | tf_op jit(solution)/shard_map/ppermute | solution.py:136
  654.8 36.5 %collective-permute-start.93 = (bf16[176,2048]{1,0:T(8,128)(2,1)S(1)}, bf16[176,2048]{1,0:T(8,128)(2,1)S(1)}, u32[]{:S(2)}, u32[]{:S(2)}) collective-permute-start(bf16[176,2048]{1,0:T(8,128)(2,1)S(1)} %copy-done.67), channel_id=1, source_target_pairs={{8,0},{16,8},{24,16},{9,1},{17,9},{25,17},{10,2},{18,10},{26,18},{... | collective-permute-start | bytes 2162696 | tf_op jit(solution)/shard_map/ppermute | solution.py:136
  656.1 49.8 %collective-permute-start.85 = (bf16[128,2048]{1,0:T(8,128)(2,1)}, bf16[128,2048]{1,0:T(8,128)(2,1)}, u32[]{:S(2)}, u32[]{:S(2)}) collective-permute-start(bf16[128,2048]{1,0:T(8,128)(2,1)} %collective-permute-done.84), channel_id=1, source_target_pairs={{8,16},{16,24},{9,17},{17,25},{10,18},{18,26},{11,19},{19,27},{12,... | collective-permute-start | bytes 1572872 | tf_op jit(solution)/shard_map/ppermute | solution.py:136
  660.3 46.3 %collective-permute-start.88 = (bf16[128,2048]{1,0:T(8,128)(2,1)}, bf16[128,2048]{1,0:T(8,128)(2,1)}, u32[]{:S(2)}, u32[]{:S(2)}) collective-permute-start(bf16[128,2048]{1,0:T(8,128)(2,1)} %collective-permute-done.87), channel_id=1, source_target_pairs={{8,0},{16,8},{9,1},{17,9},{10,2},{18,10},{11,3},{19,11},{12,4},{20... | collective-permute-start | bytes 1572872 | tf_op jit(solution)/shard_map/ppermute | solution.py:136
  661.7 27.8 %collective-permute-start.82 = (bf16[272,256]{1,0:T(8,128)(2,1)S(1)}, bf16[272,256]{1,0:T(8,128)(2,1)S(1)}, u32[]{:S(2)}, u32[]{:S(2)}) collective-permute-start(bf16[272,256]{1,0:T(8,128)(2,1)S(1)} %fusion.15), channel_id=1, source_target_pairs={{0,8},{8,0},{16,24},{24,16},{1,9},{9,1},{17,25},{25,17},{2,10},{10... | collective-permute-start | bytes 417800 | tf_op jit(solution)/shard_map/ppermute | solution.py:136
  689.6 18.4 %collective-permute-start.83 = (bf16[272,256]{1,0:T(8,128)(2,1)S(1)}, bf16[272,256]{1,0:T(8,128)(2,1)S(1)}, u32[]{:S(2)}, u32[]{:S(2)}) collective-permute-start(bf16[272,256]{1,0:T(8,128)(2,1)S(1)} %add_convert_fusion.32), channel_id=1, source_target_pairs={{0,16},{8,24},{16,0},{24,8},{1,17},{9,25},{17,1},{25,9},{2,18},{10... | collective-permute-start | bytes 417800 | tf_op jit(solution)/shard_map/ppermute | solution.py:136
  689.7 19.6 %collective-permute-start.91 = (bf16[176,2048]{1,0:T(8,128)(2,1)S(1)}, bf16[176,2048]{1,0:T(8,128)(2,1)}, u32[]{:S(2)}, u32[]{:S(2)}) collective-permute-start(bf16[176,2048]{1,0:T(8,128)(2,1)S(1)} %collective-permute-done.90), channel_id=1, source_target_pairs={{8,16},{16,24},{9,17},{17,25},{10,18},{18,26},{11,19},{19,27},{12,... | collective-permute-start | bytes 2162696 | tf_op jit(solution)/shard_map/ppermute | solution.py:136
  691.2 22.2 %collective-permute-start.94 = (bf16[176,2048]{1,0:T(8,128)(2,1)S(1)}, bf16[176,2048]{1,0:T(8,128)(2,1)}, u32[]{:S(2)}, u32[]{:S(2)}) collective-permute-start(bf16[176,2048]{1,0:T(8,128)(2,1)S(1)} %collective-permute-done.93), channel_id=1, source_target_pairs={{8,0},{16,8},{9,1},{17,9},{10,2},{18,10},{11,3},{19,11},{12,4},{20... | collective-permute-start | bytes 2162696 | tf_op jit(solution)/shard_map/ppermute | solution.py:136
  706.6 19.7 %collective-permute-start.89 = (bf16[128,2048]{1,0:T(8,128)(2,1)}, bf16[128,2048]{1,0:T(8,128)(2,1)S(1)}, u32[]{:S(2)}, u32[]{:S(2)}) collective-permute-start(bf16[128,2048]{1,0:T(8,128)(2,1)} %collective-permute-done.88), channel_id=1, source_target_pairs={{8,0},{9,1},{10,2},{11,3},{12,4},{13,5},{14,6},{15,7}} | collective-permute-start | bytes 1572872 | tf_op jit(solution)/shard_map/ppermute | solution.py:136
  709.3 21.6 %collective-permute-start.92 = (bf16[176,2048]{1,0:T(8,128)(2,1)}, bf16[176,2048]{1,0:T(8,128)(2,1)S(1)}, u32[]{:S(2)}, u32[]{:S(2)}) collective-permute-start(bf16[176,2048]{1,0:T(8,128)(2,1)} %collective-permute-done.91), channel_id=1, source_target_pairs={{16,24},{17,25},{18,26},{19,27},{20,28},{21,29},{22,30},{23,31}} | collective-permute-start | bytes 2162696 | tf_op jit(solution)/shard_map/ppermute | solution.py:136
  713.4 26.8 %collective-permute-start.95 = (bf16[176,2048]{1,0:T(8,128)(2,1)}, bf16[176,2048]{1,0:T(8,128)(2,1)S(1)}, u32[]{:S(2)}, u32[]{:S(2)}) collective-permute-start(bf16[176,2048]{1,0:T(8,128)(2,1)} %collective-permute-done.94), channel_id=1, source_target_pairs={{8,0},{9,1},{10,2},{11,3},{12,4},{13,5},{14,6},{15,7}} | collective-permute-start | bytes 2162696 | tf_op jit(solution)/shard_map/ppermute | solution.py:136
  (114 other events, 1252.8 us)
Sparse Core Ops, SparseCore 0:
  87.7 106.0 all-gather.2
  309.9 53.2 reduce-scatter.4
  365.5 56.0 reduce-scatter.6
  429.3 71.7 reduce-scatter.8
  537.3 57.7 reduce-scatter.10

commit v3 on v2

--- a/solution.py
+++ b/solution.py
@@ -60,16 +60,19 @@
     from_x = swap(piece, 2)
     from_y = swap(piece, 4)
     from_core = swap(piece, 1)
-    if between:
-        from_x, from_y = after([from_x, from_y], *between)
+    from_x, from_y = after([from_x, from_y], *between)
     return [piece, from_core, from_x, swap(from_x, 1), from_y, swap(from_y, 1)]
 
 
-def gather_far(near, count):
+def far_halves(near):
+    half = near[0].shape[0] // 2
+    return [swap(near[2][:half], 4), swap(near[4][half:], 2)]
+
+
+def gather_far(near, count, *window):
     if not is_cube(count):
         return near[-2]
-    half = near[0].shape[0] // 2
-    return jnp.concatenate([swap(near[2][:half], 4), swap(near[4][half:], 2)], 0)
+    return jnp.concatenate(after(far_halves(near), *window), 0)
 
 
 def gather_last(near, far, count):
@@ -83,13 +86,14 @@
     return (near if is_cube(count) else near[:-2]) + [far, last]
 
 
-def scatter_far(parts, count):
+def scatter_far(parts, count, *window):
     if not is_cube(count):
         return parts
     half = parts[0].shape[0] // 2
     far = add_rounded(parts[6], swap(parts[7], 1))
     far_x = swap(far[:half], 2)
     far_y = swap(far[half:], 4)
+    far_x, far_y = after([far_x, far_y], *window)
     near_x = add_rounded(parts[2], swap(parts[3], 1))
     near_y = add_rounded(parts[4], swap(parts[5], 1))
     near_y = jnp.concatenate([add_rounded(near_y[:half], far_x), near_y[half:]], 0)
@@ -132,60 +136,22 @@
     return lax.all_to_all(weight, "seq", split_axis=0, concat_axis=1, tiled=True)
 
 
-def send_dp(array, pairs):
-    return lax.ppermute(array, "dp", pairs)
-
-
-def line_share(array):
-    return lax.psum_scatter(array, "dp", scatter_dimension=0, tiled=True)
-
-
-def line_gather(share, *windows):
-    if lax.axis_size("dp") != 4:
-        gathered = lax.all_gather(share, "dp", axis=0, tiled=False)
-        return [[gathered[m]] for m in range(gathered.shape[0])]
-    ups, downs = [share], [share]
-    for step in range(3):
-        up, down = ups[-1], downs[-1]
-        if step and len(windows) >= step:
-            up, down = after([up, down], windows[step - 1])
-        ups.append(send_dp(up, [(i, i + 1) for i in range(step, 3)]))
-        downs.append(send_dp(down, [(i + 1, i) for i in range(3 - step)]))
-    return [[ups[k - m] if k > m else downs[m - k] for k in range(4)] for m in range(4)]
-
-
-def choose(options, place):
-    chosen = options[-1]
-    for k in range(len(options) - 2, -1, -1):
-        chosen = jnp.where(place == k, options[k], chosen)
-    return chosen
-
-
-def line_rows(gathered):
-    place = lax.axis_index("dp")
-    return jnp.concatenate([choose(options, place) for options in gathered], 0).astype(F32)
-
-
 def stage(always, work, *operands):
     shapes = jax.eval_shape(work, *operands)
     empty = lambda *_: jax.tree.map(lambda leaf: jnp.zeros(leaf.shape, leaf.dtype), shapes)
     return lax.cond(always, work, empty, *operands)
 
 
-def small_sum(share, count):
-    if not is_cube(count) or lax.axis_size("dp") != 4:
-        own = lax.psum_scatter(share, "seq", scatter_dimension=0, tiled=False)
-        return lax.psum(own, "dp")
+def small_scatter(share, count):
+    if not is_cube(count):
+        return lax.psum_scatter(share, "seq", scatter_dimension=0, tiled=False)
     rank = lax.axis_index("seq")
-    kept = share
-    for bit in (4, 2, 1):
+    for bit in (1, 2, 4):
         upper = (rank & bit) != 0
-        low, high = kept[:bit], kept[bit:]
-        kept = add_rounded(jnp.where(upper, high, low), swap(jnp.where(upper, low, high), bit))
-    kept = kept[0]
-    for bit in (1, 2):
-        kept = add_rounded(kept, send_dp(kept, [(i, i ^ bit) for i in range(4)]))
-    return kept
+        pairs = share.reshape(-1, 2, *share.shape[1:])
+        low, high = pairs[:, 0], pairs[:, 1]
+        share = add_rounded(jnp.where(upper, high, low), swap(jnp.where(upper, low, high), bit))
+    return share[0]
 
 
 def load_keys(key_ref, kv_ref, rows_ref, count, head, column):
@@ -508,76 +474,126 @@
     )(key, *given, *before)
 
 
-def mlp_kernel(na_hbm, nb_hbm, ga_hbm, gb_hbm, shares_hbm, down_hbm, *rest, first):
-    hidden_hbm, dgate_hbm, dup_hbm, pa_hbm, pb_hbm, oa_hbm, ob_hbm = rest[-18:-11]
-    normed, branch, both, down, hidden, dgate, dup, parts, outs, in_sems, out_sems = rest[-11:]
+def hidden_kernel(na_hbm, nb_hbm, ga_hbm, gb_hbm, shares_hbm, down_hbm, *rest, first):
+    hidden_hbm, dgate_hbm, dup_hbm = rest[-11:-8]
+    normed, branch, both, down, hidden, dgate, dup, sems = rest[-8:]
     rows = na_hbm.shape[0]
+    lines, inner = shares_hbm.shape[0], down_hbm.shape[0]
     low, high = pl.ds(0, rows), pl.ds(rows, rows)
-    lines, inner = shares_hbm.shape[0], down_hbm.shape[0]
     places = [(shares_hbm.at[i], both.at[:, i]) for i in range(lines)]
     places += [(na_hbm, normed.at[low]), (nb_hbm, normed.at[high])]
     places += [(ga_hbm, branch.at[low]), (gb_hbm, branch.at[high]), (down_hbm, down)]
-    loads = [pltpu.make_async_copy(a, b, in_sems.at[i]) for i, (a, b) in enumerate(places)]
+    loads = [pltpu.make_async_copy(a, b, sems.at[i]) for i, (a, b) in enumerate(places)]
     places = []
     for stack, target in ((hidden, hidden_hbm), (dgate, dgate_hbm), (dup, dup_hbm)):
         places += [(stack.at[low], target.at[first]), (stack.at[high], target.at[first + 1])]
-    places += [(outs.at[low], oa_hbm), (outs.at[high], ob_hbm)]
-    places += [(parts.at[low], pa_hbm), (parts.at[high], pb_hbm)]
-    stores = [pltpu.make_async_copy(a, b, out_sems.at[i]) for i, (a, b) in enumerate(places)]
+    stores = [
+        pltpu.make_async_copy(a, b, sems.at[len(loads) + i]) for i, (a, b) in enumerate(places)
+    ]
     for load in loads:
         load.start()
     for load in loads[: lines + 2]:
         load.wait()
-    both_cols = both[...].reshape(-1, 2 * inner)
-    gate_up = dot_nn(normed[...], both_cols)
+    gate_up = dot_nn(normed[...], both[...].reshape(-1, 2 * inner))
     gate_pre, up_pre = gate_up[:, :inner], gate_up[:, inner:]
     sigma = jax.nn.sigmoid(gate_pre)
     silu_gate = gate_pre * sigma
     slope = sigma * (1.0 + gate_pre * (1.0 - sigma))
     hidden[...] = (silu_gate * up_pre).astype(BF)
-    stores[0].start()
-    stores[1].start()
+    for store in stores[:2]:
+        store.start()
     for load in loads[lines + 2 :]:
         load.wait()
     grad_hidden = dot_nt(branch[...], down[...])
     dgate[...] = (grad_hidden * up_pre * slope).astype(BF)
     dup[...] = (grad_hidden * silu_gate).astype(BF)
-    for store in stores[2:6]:
-        store.start()
-    outs[...] = dot_nn(hidden[...], down[...]).astype(BF)
-    for store in stores[6:8]:
-        store.start()
-    for start, store in ((0, stores[8]), (rows, stores[9])):
-        span = slice(start, start + rows)
-        grads = dot_nt(jnp.concatenate([dgate[span, :], dup[span, :]], 1), both_cols)
-        parts[span, :] = grads.astype(BF)
+    for store in stores[2:]:
         store.start()
     for store in stores:
         store.wait()
 
 
-def mlp_pair(normed, branch, pair, shares, down, count, before):
+def hidden_pair(normed, branch, pair, shares, down, count, before):
     rows, width = normed[0].shape
     inner = down.shape[0]
     lines, _, share_rows, _ = shares.shape
     given = [*normed, *branch, shares, down]
     anywhere = pl.BlockSpec(memory_space=pl.ANY)
     stacked = jax.ShapeDtypeStruct((count, rows, inner), BF)
-    apart = jax.ShapeDtypeStruct((rows, width), BF)
-    return pl.pallas_call(
-        functools.partial(mlp_kernel, first=2 * pair),
+    return pl.pallas_call(
+        functools.partial(hidden_kernel, first=2 * pair),
         in_specs=[anywhere] * (6 + len(before)),
-        out_specs=[anywhere] * 7,
-        out_shape=[stacked] * 3 + [apart] * 4,
+        out_specs=[anywhere] * 3,
+        out_shape=[stacked] * 3,
         scratch_shapes=[pltpu.VMEM((2 * rows, width), BF)] * 2
         + [pltpu.VMEM((count, lines, share_rows, 2 * inner), BF), pltpu.VMEM(down.shape, BF)]
         + [pltpu.VMEM((2 * rows, inner), BF)] * 3
-        + [pltpu.VMEM((2 * rows, width), BF)] * 2
-        + [pltpu.SemaphoreType.DMA((lines + 5,)), pltpu.SemaphoreType.DMA((10,))],
+        + [pltpu.SemaphoreType.DMA((lines + 11,))],
         input_output_aliases={6 + i: i for i in range(len(before))},
         compiler_params=pltpu.CompilerParams(vmem_limit_bytes=MLP_VMEM_BYTES),
-        cost_estimate=LIGHT,
+        cost_estimate=pl.CostEstimate(
+            flops=20 * rows * width * inner,
+            bytes_accessed=6 * width * inner + 12 * rows * width,
+            transcendentals=2 * rows * inner,
+        ),
     )(*given, *before)
+
+
+def mlp_parts_kernel(hidden_hbm, dgate_hbm, dup_hbm, shares_hbm, down_hbm, *rest, first):
+    pa_hbm, pb_hbm, oa_hbm, ob_hbm = rest[:4]
+    hidden, dgate, dup, both, down, parts, outs, sems = rest[4:]
+    rows = pa_hbm.shape[0]
+    lines, inner = shares_hbm.shape[0], down_hbm.shape[0]
+    low, high = pl.ds(0, rows), pl.ds(rows, rows)
+    both_stacks = ((dgate_hbm, dgate), (dup_hbm, dup), (hidden_hbm, hidden))
+    places = [(stack.at[pl.ds(first, 2)], target) for stack, target in both_stacks]
+    places += [(shares_hbm.at[i], both.at[:, i]) for i in range(lines)]
+    places += [(down_hbm, down)]
+    loads = [pltpu.make_async_copy(a, b, sems.at[i]) for i, (a, b) in enumerate(places)]
+    places = [(parts.at[low], pa_hbm), (parts.at[high], pb_hbm)]
+    places += [(outs.at[low], oa_hbm), (outs.at[high], ob_hbm)]
+    stores = [
+        pltpu.make_async_copy(a, b, sems.at[len(loads) + i]) for i, (a, b) in enumerate(places)
+    ]
+    for load in loads:
+        load.start()
+    for load in loads[: lines + 3]:
+        load.wait()
+    both_cols = both[...].reshape(-1, 2 * inner)
+    for i in range(2):
+        grads = dot_nt(jnp.concatenate([dgate[i], dup[i]], 1), both_cols)
+        parts[i * rows : (i + 1) * rows, :] = grads.astype(BF)
+        stores[i].start()
+    loads[-1].wait()
+    for i in range(2):
+        outs[i * rows : (i + 1) * rows, :] = dot_nn(hidden[i], down[...]).astype(BF)
+        stores[2 + i].start()
+    for store in stores:
+        store.wait()
+
+
+def mlp_parts(stacks, pair, shares, down):
+    count, rows, inner = stacks[0].shape
+    width = down.shape[1]
+    lines, _, share_rows, _ = shares.shape
+    anywhere = pl.BlockSpec(memory_space=pl.ANY)
+    apart = jax.ShapeDtypeStruct((rows, width), BF)
+    return pl.pallas_call(
+        functools.partial(mlp_parts_kernel, first=2 * pair),
+        in_specs=[anywhere] * 5,
+        out_specs=[anywhere] * 4,
+        out_shape=[apart] * 4,
+        scratch_shapes=[pltpu.VMEM((2, rows, inner), BF)] * 3
+        + [pltpu.VMEM((count, lines, share_rows, 2 * inner), BF), pltpu.VMEM(down.shape, BF)]
+        + [pltpu.VMEM((2 * rows, width), BF)] * 2
+        + [pltpu.SemaphoreType.DMA((lines + 8,))],
+        compiler_params=pltpu.CompilerParams(vmem_limit_bytes=MLP_VMEM_BYTES),
+        cost_estimate=pl.CostEstimate(
+            flops=20 * rows * width * inner,
+            bytes_accessed=6 * width * inner + 12 * rows * width,
+            transcendentals=0,
+        ),
+    )(*stacks, shares, down)
 
 
 def proj_kernel(a_ref, b_ref, w_ref, attn_ref, *rest, last):
@@ -710,37 +726,23 @@
     )(*lefts, *pieces)
 
 
-def turn_kernel(place_ref, *refs, lines):
-    options = len(refs) // lines
-    out_ref = refs[-1]
-    place = place_ref[0]
-    blocks = []
-    for m in range(lines):
-        blocks.append(choose([ref[...] for ref in refs[m * options : (m + 1) * options]], place))
-    turned = []
-    for j in range(blocks[0].shape[0]):
-        turned.append(jnp.concatenate([block[j].astype(F32) for block in blocks], 0).T)
+def turn_kernel(blocks_ref, out_ref):
+    turned = [blocks_ref[j].astype(F32).T for j in range(blocks_ref.shape[0])]
     out_ref[...] = jnp.concatenate(turned, 1)
 
 
-def turn_blocks(gathered):
-    lines = len(gathered)
-    count, columns, rows = gathered[0][0].shape
+def turn_blocks(blocks):
+    count, columns, rows = blocks.shape
     step = min(128, rows)
-    given = [option for options in gathered for option in options]
-    place = lax.axis_index("dp").astype(jnp.int32).reshape(1)
-    return pl.pallas_call(
-        functools.partial(turn_kernel, lines=lines),
-        grid_spec=pltpu.PrefetchScalarGridSpec(
-            num_scalar_prefetch=1,
-            grid=(rows // step,),
-            in_specs=[pl.BlockSpec((count, columns, step), lambda i, *_: (0, 0, i))] * len(given),
-            out_specs=pl.BlockSpec((step, count * lines * columns), lambda i, *_: (i, 0)),
-        ),
-        out_shape=jax.ShapeDtypeStruct((rows, count * lines * columns), F32),
+    return pl.pallas_call(
+        turn_kernel,
+        grid=(rows // step,),
+        in_specs=[pl.BlockSpec((count, columns, step), lambda i: (0, 0, i))],
+        out_specs=pl.BlockSpec((step, count * columns), lambda i: (i, 0)),
+        out_shape=jax.ShapeDtypeStruct((rows, count * columns), F32),
         compiler_params=pltpu.CompilerParams(vmem_limit_bytes=VMEM_BYTES),
         cost_estimate=LIGHT,
-    )(place, *given)
+    )(blocks)
 
 
 def spread_rows(share_t, count):
@@ -749,51 +751,40 @@
     return lax.all_to_all(blocks, "seq", split_axis=0, concat_axis=0, tiled=True)
 
 
-def pack_kernel(place_ref, gate_ref, up_ref, query_ref, out_ref):
-    count, rows, _ = out_ref.shape
+def pack_kernel(place_ref, gate_ref, up_ref, out_ref):
+    count = out_ref.shape[0]
     inner = gate_ref.shape[1] // count
-    own = query_ref.shape[1] // count
     gate, up = gate_ref[...], up_ref[...]
     for j in range(count):
         columns = slice(j * inner, (j + 1) * inner)
-        out_ref[j, :, : 2 * inner] = jnp.concatenate([gate[:, columns], up[:, columns]], 1)
-        for g in range(query_ref.shape[0] // rows):
-            start = 2 * inner + g * own
-            out_ref[j, :, start : start + own] = query_ref[
-                g * rows : (g + 1) * rows, j * own : (j + 1) * own
-            ]
-
-
-def pack_weights(w_gate, w_up, w_query, count):
+        out_ref[j] = jnp.concatenate([gate[:, columns], up[:, columns]], 1)
+
+
+def pack_weights(w_gate, w_up, count):
     lines = lax.axis_size("dp")
     rows, columns = w_gate.shape[0] // lines, w_gate.shape[1]
     place = lax.axis_index("dp").astype(jnp.int32).reshape(1)
     share = pl.BlockSpec((rows, columns), lambda i, place: (place[0], 0))
-    shape = (count, rows, (2 * columns + lines * w_query.shape[1]) // count)
+    shape = (count, rows, 2 * columns // count)
     return pl.pallas_call(
         pack_kernel,
         grid_spec=pltpu.PrefetchScalarGridSpec(
             num_scalar_prefetch=1,
             grid=(1,),
-            in_specs=[share, share, whole_spec(w_query)],
+            in_specs=[share, share],
             out_specs=pl.BlockSpec(shape, lambda i, place: (0, 0, 0)),
         ),
         out_shape=jax.ShapeDtypeStruct(shape, BF),
         compiler_params=pltpu.CompilerParams(vmem_limit_bytes=VMEM_BYTES),
         cost_estimate=LIGHT,
-    )(place, w_gate, w_up, w_query)
+    )(place, w_gate, w_up)
 
 
 def share_weights(w_gate, w_up, w_query, count):
-    lines = lax.axis_size("dp")
-    inner = w_gate.shape[1] // count
-    own = w_query.shape[1] // count
-    packed = pack_weights(w_gate, w_up, w_query, count)
+    packed = pack_weights(w_gate, w_up, count)
     packed = lax.all_to_all(packed, "seq", split_axis=0, concat_axis=0, tiled=True)
-    rows = packed.shape[1]
-    query = packed[:, :, 2 * inner :].reshape(count, rows, lines, own).transpose(0, 2, 1, 3)
-    shares = lax.all_gather(packed[:, :, : 2 * inner], "dp", axis=0, tiled=False)
-    return query.reshape(count * lines * rows, own), shares
+    query = rows_to_columns(w_query + packed[0, 0, 0] * 0)
+    return query, lax.all_gather(packed, "dp", axis=0, tiled=False)
 
 
 def rope_tables(positions, head_width):
@@ -872,17 +863,14 @@
     last = gather_last(near, far, count)
     grad_out = cotangent.reshape(rows, width).astype(F32) * valid
     branch_near = gather_near(after(grad_out.astype(BF), far), count, stacks)
-    branch_far = gather_far(after(branch_near, stacks), count)
     *normed, queries, key_values = front_of(last_pair, [far, last], stacks)
     normed_one += normed
     attn, lse = attend_forward(queries, key_values, lengths, keys_of, head)
-    attn, branch_far = lax.optimization_barrier((attn, branch_far))
+    attn, branch_near = lax.optimization_barrier((attn, branch_near))
     proj_parts = parts_of([attn.reshape(count, rows, -1)], [w_out], (False,))
     inputs_f = inputs.astype(F32)
     scale_one = rms_scale(inputs_f)
 
-    branch_last = gather_last(branch_near, branch_far, count)
-    branch = (branch_near if is_cube(count) else branch_near[:-2]) + [branch_far, branch_last]
     grad_second, dkv_second = attend_second(
         after(second_queries, proj_parts), second_cotangent, key_values, lengths, keys_of, head
     )
@@ -891,115 +879,135 @@
     middle = inputs_f + proj_sum.astype(F32)
 
     scale_two = rms_scale(middle)
-    mlp_of = lambda pair, two, before: mlp_pair(
-        two, branch[2 * pair : 2 * pair + 2], pair, shares, w_down, count, before
-    )
-    near = gather_near((middle * scale_two * gain_two).astype(BF), count)
-    done = [mlp_of(0, near[:2], [])]
-    far = gather_far(after(near, done[-1][0]), count)
-    for pair in range(1, last_pair):
-        done.append(mlp_of(pair, near[2 * pair : 2 * pair + 2], done[-1][:3]))
-        if pair == 1:
-            far = after(far, done[-1][0])
-            last = gather_last(near, far, count)
-    done.append(mlp_of(last_pair, [far, last], done[-1][:3]))
-    hidden, grad_gate, grad_up = [stack.reshape(all_rows, -1) for stack in done[-1][:3]]
-    normed_parts = [part for step in done for part in step[3:5]]
-    out_parts = [part for step in done for part in step[5:]]
-    normed_two = (near if is_cube(count) else near[:-2]) + [far, last]
     sync = lax.optimization_barrier
     always = lengths[0] > 0
-    w_gate_share, w_up_share = inner_of([grad_gate, grad_up], normed_two)
+    hidden_of = lambda pair, two, before: tuple(
+        hidden_pair(two, branch[2 * pair : 2 * pair + 2], pair, shares, w_down, count, before)
+    )
+    normed_own = (middle * scale_two * gain_two).astype(BF)
+    branch = list(branch_near)
+
+    def middle_pairs(near, stacks):
+        for pair in range(1, last_pair):
+            stacks = hidden_of(pair, near[2 * pair : 2 * pair + 2], stacks)
+        return tuple(stacks)
+
+    if is_cube(count):
+        from_x, from_y, from_core = swap(normed_own, 2), swap(normed_own, 4), swap(normed_own, 1)
+        stacks = stage(always, lambda *two: hidden_of(0, two, []), normed_own, from_core)
+        from_x, from_y, stacks = sync((from_x, from_y, stacks))
+        near = [normed_own, from_core, from_x, swap(from_x, 1), from_y, swap(from_y, 1)]
+        halves, branch_halves = far_halves(near), far_halves(after(branch_near, stacks))
+        stacks = stage(always, middle_pairs, near, stacks)
+        halves, branch_halves, stacks = sync((halves, branch_halves, stacks))
+        far, branch_far = jnp.concatenate(halves, 0), jnp.concatenate(branch_halves, 0)
+        last = swap(far, 1)
+        branch += [branch_far, swap(branch_far, 1)]
+    else:
+        near = gather_near(normed_own, count)
+        stacks = middle_pairs(near, hidden_of(0, near[:2], []))
+        far, last = near[-2:]
+    stacks = hidden_of(last_pair, [far, last], list(stacks))
+    hidden, grad_gate, grad_up = [stack.reshape(all_rows, -1) for stack in stacks]
+    normed_two = (near if is_cube(count) else near[:-2]) + [far, last]
     split = queries.shape[-1]
-    gate_share = line_share(w_gate_share)
-
-    def sum_mlp_back(normed_parts, hidden, w_up_share):
-        two_sums = scatter_far(normed_parts, count)
-        (w_down_share,) = inner_of([hidden], branch)
-        grad_normed_two = scatter_near(two_sums, count, w_down_share).astype(F32)
+    (w_gate_share,) = inner_of([grad_gate], normed_two)
+    gate_sum = lax.psum(w_gate_share, "dp")
+
+    def parts_mlp(stacks, grad_up):
+        (w_up_share,) = inner_of([grad_up], normed_two)
+        parts = [mlp_parts(stacks, pair, shares, w_down) for pair in range(last_pair + 1)]
+        normed_parts = [part for step in parts for part in step[:2]]
+        return w_up_share, normed_parts, [part for step in parts for part in step[2:]]
+
+    w_up_share, normed_parts, out_parts = stage(always, parts_mlp, stacks, grad_up)
+
+    def scatter_mlp(normed_parts, hidden):
+        return scatter_far(normed_parts, count), inner_of([hidden], branch)[0]
+
+    two_sums, w_down_share = stage(always, scatter_mlp, normed_parts, hidden)
+    def sum_mlp(two_sums):
+        grad_normed_two = scatter_near(two_sums, count).astype(F32)
         grad_middle = grad_out + norm_back(grad_normed_two, middle, scale_two, gain_two)
-        gain_share = jnp.sum(grad_normed_two * (middle * scale_two), 0)
-        return grad_middle, gain_share, w_down_share, w_up_share
-
-    grad_middle, gain_share, w_down_share, w_up_share = stage(
-        always, sum_mlp_back, normed_parts, hidden, w_up_share
+        return grad_middle, jnp.sum(grad_normed_two * (middle * scale_two), 0)
+
+    grad_middle, gain_share = stage(always, sum_mlp, two_sums)
+    grad_middle, w_up_share, w_down_share, gate_sum = sync(
+        (grad_middle, w_up_share, w_down_share, gate_sum)
     )
-    w_up_share, gate_share = sync((w_up_share, gate_share))
-    up_share = line_share(w_up_share)
-
-    def project_back(grad_middle, gate_share, w_down_share):
+    up_sum, down_sum = lax.psum((w_up_share, w_down_share), "dp")
+    proj_of = lambda pair, two, before: proj_pair(two, pair, w_out, attn, count, before)
+
+    def gather_middle(grad_middle):
         near = gather_near(grad_middle.astype(BF), count)
-        gate_blocks = spread_rows(gate_share, count)
-        proj_of = lambda pair, two, before: proj_pair(two, pair, w_out, attn, count, before)
-        state = proj_of(0, near[:2], [])
-        far = gather_far(after(near, state[0]), count)
+        return near, proj_of(0, near[:2], [])
+
+    near, state = stage(always, gather_middle, grad_middle)
+
+    def project_back(near, state):
+        far = gather_far(near, count)
         for pair in range(1, last_pair):
             state = proj_of(pair, near[2 * pair : 2 * pair + 2], state)
         last = gather_last(near, far, count)
-        grad_attn, w_out_share = proj_of(last_pair, [far, last], state)
-        return grad_attn, w_out_share, gate_blocks, w_down_share
-
-    grad_attn, w_out_share, gate_blocks, w_down_share = stage(
-        always, project_back, grad_middle, gate_share, w_down_share
-    )
-    w_down_share, up_share = sync((w_down_share, up_share))
-    down_share = line_share(w_down_share)
-
-    def attention_back(grad_attn, up_share, gate_blocks, out_parts, w_out_share):
+        return proj_of(last_pair, [far, last], state)
+
+    grad_attn, w_out_share = stage(always, project_back, near, state)
+    grad_attn, gate_sum = sync((grad_attn, gate_sum))
+    gate_blocks = spread_rows(gate_sum, count)
+
+    def attention_back(grad_attn, out_parts):
         out_sums = scatter_far(out_parts, count)
-        up_blocks = spread_rows(up_share, count)
         grads = attend_backward(
             queries, grad_attn, attn, key_values, lse, dkv_second, tables, lengths, keys_of, head
         )
-        gate_blocks = line_gather(gate_blocks, grads)
         grads = grads.reshape(count, rows, -1)
         one_parts = parts_of(
             [grads[..., :split], grads[..., split:]], [query_cols, kv_mat], (True, True)
         )
+        return out_sums, one_parts, grads
+
+    out_sums, one_parts, grads = stage(always, attention_back, grad_attn, out_parts)
+    one_parts, grads, gate_blocks = sync((one_parts, grads, gate_blocks))
+
+    def scatter_attention(one_parts, grads):
         (w_one_share,) = outer_of(normed_one, [grads.reshape(all_rows, -1)])
-        w_query_rows = columns_to_rows(after(w_one_share[:, :split], up_blocks))
-        lines = lax.axis_size("dp")
-        late = jnp.concatenate(
-            [w.reshape(lines, -1, w.shape[1]) for w in (w_out_share, w_query_rows)], 1
-        )
-        return one_parts, out_sums, w_one_share, late.reshape(-1, width), gate_blocks, up_blocks
-
-    one_parts, out_sums, w_one_share, late, gate_blocks, up_blocks = stage(
-        always, attention_back, grad_attn, up_share, gate_blocks, out_parts, w_out_share
-    )
-    late, down_share = sync((late, down_share))
-    late_share = line_share(late)
-
-    def sum_attention_back(one_parts, out_sums, up_blocks):
-        one_sums = scatter_far(one_parts, count)
-        out = (middle + scatter_near(out_sums, count).astype(F32)).astype(BF)
-        up_blocks = line_gather(up_blocks, one_sums)
+        return scatter_far(one_parts, count), w_one_share
+
+    one_sums, w_one_share = stage(always, scatter_attention, one_parts, grads)
+    w_query_share = w_one_share[:, :split].reshape(count, own_columns, split)
+    w_query_share = lax.all_to_all(w_query_share, "seq", split_axis=0, concat_axis=0, tiled=True)
+    own_gain = gain_attn.shape[0]
+
+    def sum_attention(one_sums, w_one_share):
+        kv_shares = w_one_share[:, split:].reshape(count, own_columns, 2 * head)
+        w_kv_share = small_scatter(kv_shares, count)
         grad_normed_one = scatter_near(one_sums, count).astype(F32)
         grad_tokens = grad_middle + norm_back(grad_normed_one, inputs_f, scale_one, gain_one)
-        gain_share = jnp.sum(grad_normed_one * (inputs_f * scale_one), 0)
-        return out, grad_tokens, gain_share, up_blocks
-
-    out, grad_tokens, first_gain_share, up_blocks = stage(
-        always, sum_attention_back, one_parts, out_sums, up_blocks
+        gain_shares = jnp.stack([jnp.sum(grad_normed_one * (inputs_f * scale_one), 0), gain_share])
+        gain_shares = gain_shares.astype(BF).reshape(2, count, own_gain).transpose(1, 0, 2)
+        gain_shares = jnp.pad(gain_shares, ((0, 0), (0, 14), (0, 2 * head - own_gain)))
+        small = jnp.concatenate([w_kv_share, small_scatter(gain_shares, count)], 0)
+        return grad_tokens, small
+
+    grad_tokens, small = stage(always, sum_attention, one_sums, w_one_share)
+    small, w_query_share, w_out_share, up_sum, down_sum = sync(
+        (small, w_query_share, w_out_share, up_sum, down_sum)
     )
-    late_share, down_share, up_blocks, first_gain_share = sync(
-        (late_share, down_share, up_blocks, first_gain_share)
-    )
-    down_blocks = line_gather(down_share)
-    late_blocks = line_gather(late_share)
-    own_gain = gain_attn.shape[0]
-    gain_shares = jnp.stack([first_gain_share, gain_share])
-    gain_shares = gain_shares.astype(BF).reshape(2, count, own_gain).transpose(1, 0, 2)
-    gain_shares = jnp.pad(gain_shares, ((0, 0), (0, 14), (0, 2 * head - own_gain)))
-    kv_shares = w_one_share[:, split:].reshape(count, own_columns, 2 * head)
-    small = small_sum(jnp.concatenate([kv_shares, gain_shares], 1), count).astype(F32)
+    late = lax.psum((w_out_share, w_query_share.reshape(-1, split), small), "dp")
+    up_blocks = spread_rows(up_sum, count)
+
+    def sum_rest(out_sums, gate_blocks, down_sum):
+        out = (middle + scatter_near(out_sums, count).astype(F32)).astype(BF)
+        return out, turn_blocks(gate_blocks), down_sum.astype(F32)
+
+    out, grad_w_gate, grad_w_down = stage(always, sum_rest, out_sums, gate_blocks, down_sum)
+    out, up_blocks = sync((out, up_blocks))
+    grad_w_up = turn_blocks(up_blocks)
+    late, grad_w_up = sync((late, grad_w_up))
+    w_out_sum, grad_w_query, small = [each.astype(F32) for each in late]
+    grad_w_query = grad_w_query.reshape(count, own_columns, split).transpose(1, 0, 2)
+    grad_w_query = grad_w_query.reshape(own_columns, -1)
     grad_w_kv, grad_gains = small[:own_columns], small[own_columns : own_columns + 2, :own_gain]
-    grad_w_gate = turn_blocks(gate_blocks)
-    grad_w_up = turn_blocks(up_blocks)
-    grad_w_down = line_rows(down_blocks)
-    late_rows = line_rows(late_blocks).reshape(len(late_blocks), 2, -1, width)
-    w_out_sum = late_rows[:, 0].reshape(-1, width)
-    grad_w_query = late_rows[:, 1].reshape(-1, width)
 
     return (
         out.reshape(tokens.shape),

time: 759 us -> 732 us (0.964)
  starting transfers between devices: 119 us -> 77.9 us
  local copies, waits for them, and re-layouts: 90.5 us -> 60 us
  Pallas kernels: 191 us -> 220 us
  other arithmetic: 62.5 us -> 77.8 us
    ppermute x26 -> x0, waiting for transfers between devices: 92.4 us -> none  [send_dp(): return lax.ppermute(array, 'dp', pairs)]
    ppermute x70 -> x73, waiting for transfers between devices: 162 us -> 228 us  [swap(): return lax.ppermute(array, 'seq', [(i, i ^ bit) for i in range(8)])]
    cond x101 -> x42, local copies, waits for them, and re-layouts: 48 us -> 1.02 us
    ppermute x26 -> x0, starting transfers between devices: 40.9 us -> none  [send_dp(): return lax.ppermute(array, 'dp', pairs)]
    psum x0 -> x3, waiting for transfers between devices: none -> 32.1 us  [the longest x1 32 us: body(): lax.psum((w_out_share, w_query_share.reshape(-1, split), small), 'dp')]
    pallas_call x6 -> x10, Pallas kernels: 73.4 us -> 88.5 us  [the longest x4 42.6 us: hidden_pair(): pl.pallas_call(functools.partial(hidden_kernel, first=2 * pair), in_specs...]
    all_gather x1, waiting for transfers between devices: 17.1 us -> 7.11 us  [share_weights(): return (query, lax.all_gather(packed, 'dp', axis=0, tiled=False))]
    pallas_call x2 -> x3, Pallas kernels: 29.2 us -> 36.4 us  [inner_of(): pl.pallas_call(functools.partial(inner_kernel, count=count, lefts=len(lef...]
  transfers between devices with their start and end apart: 105 -> 82, of which waited for: 46 -> 34; matrix products, arithmetic and copies ran while one was open for 17% -> 14% of each run, Pallas kernels for 21% -> 27%
where the time goes in v3:
time: 732 us; the launch traced here: 722 us
  waiting for transfers between devices  269 us (37%)
  Pallas kernels  220 us (30%)
  starting transfers between devices  77.9 us (11%)
  other arithmetic  77.8 us (11%)
  local copies, waits for them, and re-layouts  60 us (8%)
  between operations  15.4 us (2%)
    ppermute x73, waiting for transfers between devices, swap(): return lax.ppermute(array, 'seq', [(i, i ^ bit) for i in range(8)])  228 us
    ppermute x73, starting transfers between devices, swap(): return lax.ppermute(array, 'seq', [(i, i ^ bit) for i in range(8)])  56.6 us
    pallas_call x4, Pallas kernels, hidden_pair(): pl.pallas_call(functools.partial(hidden_kernel, first=2 * pair), in_specs...  42.6 us
    pallas_call x4, Pallas kernels, mlp_parts(): pl.pallas_call(functools.partial(mlp_parts_kernel, first=2 * pair), in_sp...  37.4 us
    pallas_call x3, Pallas kernels, inner_of(): pl.pallas_call(functools.partial(inner_kernel, count=count, lefts=len(lef...  36.4 us
    psum x1, waiting for transfers between devices, body(): lax.psum((w_out_share, w_query_share.reshape(-1, split), small), 'dp')  32 us
    convert_element_type x27, other arithmetic, add_rounded(): return total.astype(BF)  26.9 us
    unnamed x72, local copies, waits for them, and re-layouts  20.1 us
  transfers between devices with their start and end apart: 82, of which 34 were waited for; matrix products, arithmetic and copies ran while one was open for 14% of the time, Pallas kernels for 27%

profile of v3, /device:TPU:0, one launch (start us, length us, event | category | flops | bytes accessed | tf_op | source)
XLA Modules:
  0.0 721.9 jit_solution(17999390030229985896)
XLA Ops:
  19.5 4.4 all-to-all-start
  24.0 18.9 %collective-permute-done.43 = bf16[272,256]{1,0:T(8,128)(2,1)S(1)} collective-permute-done((bf16[272,256]{1,0:T(8,128)(2,1)S(1)}, bf16[272,256]{1,0:T(8,128)(2,1)S(1)}, u32[]{:S(2)}, u32[]{:S(2)}) %collective-permute-start.43) | collective-permute-done | bytes 139296 | tf_op jit(solution)/shard_map/ppermute | solution.py:42
  46.1 3.2 convert_multiply_fusion.4
  49.3 5.8 collective-permute-done.44
  65.6 4.3 all-to-all-start.1
  78.0 3.3 fusion.28
  81.4 3.1 pad_maximum_fusion.10
  87.4 5.1 shard_map.230
  92.7 4.5 shard_map.231
  97.2 4.5 shard_map.232
  101.7 5.1 collective-permute-done.50
  107.4 4.8 shard_map.233
  112.2 9.4 %shard_map.234 = (bf16[8,2,128,256]{3,2,1,0:T(8,128)(2,1)S(1)}, f32[2,2,1024]{2,1,0:T(2,128)S(1)}) custom-call(s32[2]{0:T(128)S(1)} %copy-done.51, s32[2]{0:T(128)S(1)} %pad_add_fusion.key_ref, bf16[8,2,128,256]{3,2,1,0:T(8,128)(2,1)S(1)} %get-tuple-element.613.q_ref, bf16[8,2,128,256]{3,2,1,0:T(8,128)(2,1)S(1)} %get-tuple-element.614.kv_ref), custom_call_target="tpu_custom_call" | custom-call | flops 1000 | bytes 1000 | tf_op jit(solution)/shard_map/pallas_call | solution.py:216
  123.3 4.6 shard_map.235
  135.2 11.5 %collective-permute-done.57 = bf16[128,2048]{1,0:T(8,128)(2,1)S(1)} collective-permute-done((bf16[128,2048]{1,0:T(8,128)(2,1)S(1)}, bf16[128,2048]{1,0:T(8,128)(2,1)S(1)}, u32[]{:S(2)}, u32[]{:S(2)}) %collective-permute-start.57) | collective-permute-done | bytes 524320 | tf_op jit(solution)/shard_map/ppermute | solution.py:42
  150.6 19.5 %shard_map.236 = (bf16[2,128,2048]{2,1,0:T(8,128)(2,1)}, f32[8,2,128,256]{3,2,1,0:T(8,128)}) custom-call(s32[2]{0:T(128)S(1)} %copy-done.51, s32[2]{0:T(128)S(1)} %pad_add_fusion.key_ref, bf16[2,128,2048]{2,1,0:T(8,128)(2,1)S(1)} %copy-done.4, bf16[2,128,2048]{2,1,0:T(8,128)(2,1)S(1)} %copy-done.5, bf16[8,2,128,256]{3,2,1,0:T(8,128)(2,1)S(1)} %get-tuple-element.614.kv_ref), custom_call_target="tpu_custom_call" | custom-call | flops 1000 | bytes 1000 | tf_op jit(solution)/shard_map/pallas_call | solution.py:292
  173.5 7.1 all-gather.3.cloned.1.call-done
  187.2 10.9 %conditional.11 = ((bf16[8,256,704]{2,1,0:T(8,128)(2,1)}, bf16[8,256,704]{2,1,0:T(8,128)(2,1)}, bf16[8,256,704]{2,1,0:T(8,128)(2,1)})) conditional(s32[]{:T(128)} %bitcast.49, () %tuple.134, (bf16[256,2048]{1,0:T(8,128)(2,1)S(1)}, bf16[256,2048]{1,0:T(8,128)(2,1)}, bf16[256,2048]{1,0:T(8,128)(2,1)}, bf16[256,2048]{1,0:T(8,128)(2,1)}, ...), branch_computations={%region_1.2_spmd, %region_2.3_spmd} | conditional | flops 7381975040 | bytes 14942216 | solution.py:142
  187.2 10.7 %branch_1_fun.17 = (bf16[8,256,704]{2,1,0:T(8,128)(2,1)}, bf16[8,256,704]{2,1,0:T(8,128)(2,1)}, bf16[8,256,704]{2,1,0:T(8,128)(2,1)}) custom-call(bf16[256,2048]{1,0:T(8,128)(2,1)S(1)} %get-tuple-element.275.na_hbm, bf16[256,2048]{1,0:T(8,128)(2,1)} %get-tuple-element.276.nb_hbm, bf16[256,2048]{1,0:T(8,128)(2,1)} %get-tuple-element.277.ga_hbm, ...), custom_call_target="tpu_custom_call" | custom-call | flops 7381975040 | bytes 14942208 | tf_op jit(solution)/shard_map/cond/branch_1_fun/pallas_call | solution.py:523
  198.1 11.7 %collective-permute-done.62.refs_3_ = bf16[256,2048]{1,0:T(8,128)(2,1)} collective-permute-done((bf16[256,2048]{1,0:T(8,128)(2,1)S(1)}, bf16[256,2048]{1,0:T(8,128)(2,1)}, u32[]{:S(2)}, u32[]{:S(2)}) %collective-permute-start.62) | collective-permute-done | bytes 1048608 | tf_op jit(solution)/shard_map/ppermute | solution.py:42
  223.1 21.1 %conditional.12 = ((bf16[8,256,704]{2,1,0:T(8,128)(2,1)}, bf16[8,256,704]{2,1,0:T(8,128)(2,1)}, bf16[8,256,704]{2,1,0:T(8,128)(2,1)})) conditional(s32[]{:T(128)} %bitcast.49, () %tuple.138, (bf16[256,2048]{1,0:T(8,128)(2,1)}, bf16[256,2048]{1,0:T(8,128)(2,1)}, bf16[256,2048]{1,0:T(8,128)(2,1)}, bf16[256,2048]{1,0:T(8,128)(2,1)}, ...), branch_computations={%region_3.4_spmd, %region_4.5_spmd} | conditional | flops 14763950080 | bytes 68681816 | solution.py:142
  223.1 11.1 %branch_1_fun.18 = (bf16[8,256,704]{2,1,0:T(8,128)(2,1)}, bf16[8,256,704]{2,1,0:T(8,128)(2,1)}, bf16[8,256,704]{2,1,0:T(8,128)(2,1)}) custom-call(bf16[256,2048]{1,0:T(8,128)(2,1)} %get-tuple-element.287.na_hbm, bf16[256,2048]{1,0:T(8,128)(2,1)} %get-tuple-element.288.nb_hbm, ...), custom_call_target="tpu_custom_call", output_to_operand_aliasing={{0}: (6, {}), {1}: (7, {}), {2}: (8, {})} | custom-call | flops 7381975040 | bytes 14942208 | tf_op jit(solution)/shard_map/cond/branch_1_fun/pallas_call | solution.py:523
  234.2 9.7 %branch_1_fun.19 = (bf16[8,256,704]{2,1,0:T(8,128)(2,1)}, bf16[8,256,704]{2,1,0:T(8,128)(2,1)}, bf16[8,256,704]{2,1,0:T(8,128)(2,1)}) custom-call(bf16[256,2048]{1,0:T(8,128)(2,1)} %get-tuple-element.281.na_hbm, bf16[256,2048]{1,0:T(8,128)(2,1)} %get-tuple-element.282.nb_hbm, ...), custom_call_target="tpu_custom_call", output_to_operand_aliasing={{0}: (6, {}), {1}: (7, {}), {2}: (8, {})} | custom-call | flops 7381975040 | bytes 14942208 | tf_op jit(solution)/shard_map/cond/branch_1_fun/pallas_call | solution.py:523
  251.8 11.1 %shard_map.237 = (bf16[8,256,704]{2,1,0:T(8,128)(2,1)S(1)}, bf16[8,256,704]{2,1,0:T(8,128)(2,1)}, bf16[8,256,704]{2,1,0:T(8,128)(2,1)}) custom-call(bf16[256,2048]{1,0:T(8,128)(2,1)S(1)} %constant_dynamic-update-slice_fusion.4.na_hbm.refs_7_, ...), custom_call_target="tpu_custom_call", output_to_operand_aliasing={{0}: (6, {}), {1}: (7, {}), {2}: (8, {})} | custom-call | flops 7381975040 | bytes 14942208 | tf_op jit(solution)/shard_map/pallas_call | solution.py:523
  264.7 11.6 %shard_map.238 = bf16[704,2048]{1,0:T(8,128)(2,1)S(1)} custom-call(bf16[2048,704]{1,0:T(8,128)(2,1)} %bitcast.200, bf16[256,2048]{1,0:T(8,128)(2,1)S(1)} %multiply_convert_fusion.refs_1_, bf16[256,2048]{1,0:T(8,128)(2,1)} %collective-permute-done.64.refs_2_, bf16[256,2048]{1,0:T(8,128)(2,1)} %collective-permute-done.62.refs_3_, ...), custom_call_target="tpu_custom_call" | custom-call | flops 1000 | bytes 1000 | tf_op jit(solution)/shard_map/pallas_call | solution.py:716
  278.0 50.4 %conditional.13 = (bf16[704,2048]{1,0:T(8,128)(2,1)S(1)}, bf16[256,2048]{1,0:T(8,128)(2,1)}, bf16[256,2048]{1,0:T(8,128)(2,1)}, bf16[256,2048]{1,0:T(8,128)(2,1)...) conditional(s32[]{:T(128)} %bitcast.49, () %tuple.124, ...), branch_computations={%region_5.6_spmd, %region_6.7_spmd} | conditional | flops 29527900160 | bytes 94373064 | solution.py:142
  278.3 12.5 %branch_1_fun.20 = bf16[704,2048]{1,0:T(8,128)(2,1)S(1)} custom-call(bf16[2048,704]{1,0:T(8,128)(2,1)} %bitcast.201, bf16[256,2048]{1,0:T(8,128)(2,1)S(1)} %get-tuple-element.298.refs_1_, bf16[256,2048]{1,0:T(8,128)(2,1)} %get-tuple-element.299.refs_2_, bf16[256,2048]{1,0:T(8,128)(2,1)} %get-tuple-element.300.refs_3_, ...), custom_call_target="tpu_custom_call" | custom-call | flops 1000 | bytes 1000 | tf_op jit(solution)/shard_map/cond/branch_1_fun/pallas_call | solution.py:716
  290.8 9.2 %branch_1_fun.21 = (bf16[256,2048]{1,0:T(8,128)(2,1)}, bf16[256,2048]{1,0:T(8,128)(2,1)}, bf16[256,2048]{1,0:T(8,128)(2,1)}, bf16[256,2048]{1,0:T(8,128)(2,1)}) custom-call(bf16[8,256,704]{2,1,0:T(8,128)(2,1)S(1)} %copy-done.21, bf16[8,256,704]{2,1,0:T(8,128)(2,1)S(1)} %copy-done.22, bf16[8,256,704]{2,1,0:T(8,128)(2,1)S(1)} %copy-done.23, ...), custom_call_target="tpu_custom_call" | custom-call | flops 7381975040 | bytes 14942208 | tf_op jit(solution)/shard_map/cond/branch_1_fun/pallas_call | solution.py:581
  300.0 9.3 %branch_1_fun.22 = (bf16[256,2048]{1,0:T(8,128)(2,1)}, bf16[256,2048]{1,0:T(8,128)(2,1)}, bf16[256,2048]{1,0:T(8,128)(2,1)}, bf16[256,2048]{1,0:T(8,128)(2,1)}) custom-call(bf16[8,256,704]{2,1,0:T(8,128)(2,1)S(1)} %copy-done.21, bf16[8,256,704]{2,1,0:T(8,128)(2,1)S(1)} %copy-done.22, bf16[8,256,704]{2,1,0:T(8,128)(2,1)S(1)} %copy-done.23, ...), custom_call_target="tpu_custom_call" | custom-call | flops 7381975040 | bytes 14942208 | tf_op jit(solution)/shard_map/cond/branch_1_fun/pallas_call | solution.py:581
  309.3 9.6 %branch_1_fun.23 = (bf16[256,2048]{1,0:T(8,128)(2,1)}, bf16[256,2048]{1,0:T(8,128)(2,1)}, bf16[256,2048]{1,0:T(8,128)(2,1)}, bf16[256,2048]{1,0:T(8,128)(2,1)}) custom-call(bf16[8,256,704]{2,1,0:T(8,128)(2,1)S(1)} %copy-done.21, bf16[8,256,704]{2,1,0:T(8,128)(2,1)S(1)} %copy-done.22, bf16[8,256,704]{2,1,0:T(8,128)(2,1)S(1)} %copy-done.23, ...), custom_call_target="tpu_custom_call" | custom-call | flops 7381975040 | bytes 14942208 | tf_op jit(solution)/shard_map/cond/branch_1_fun/pallas_call | solution.py:581
  318.9 9.3 %branch_1_fun.24 = (bf16[256,2048]{1,0:T(8,128)(2,1)}, bf16[256,2048]{1,0:T(8,128)(2,1)}, bf16[256,2048]{1,0:T(8,128)(2,1)}, bf16[256,2048]{1,0:T(8,128)(2,1)}) custom-call(bf16[8,256,704]{2,1,0:T(8,128)(2,1)S(1)} %copy-done.21, bf16[8,256,704]{2,1,0:T(8,128)(2,1)S(1)} %copy-done.22, bf16[8,256,704]{2,1,0:T(8,128)(2,1)S(1)} %copy-done.23, ...), custom_call_target="tpu_custom_call" | custom-call | flops 7381975040 | bytes 14942208 | tf_op jit(solution)/shard_map/cond/branch_1_fun/pallas_call | solution.py:581
  330.0 30.8 %conditional.14 = (bf16[256,2048]{1,0:T(8,128)(2,1)S(1)}, bf16[256,2048]{1,0:T(8,128)(2,1)S(1)}, bf16[256,2048]{1,0:T(8,128)(2,1)S(1)}, bf16[704,2048]{1,0:T(8,128)(2,1)S(1)}) conditional(s32[]{:T(128)} %bitcast.49, () %tuple.145, (bf16[256,2048]{1,0:T(8,128)(2,1)}, bf16[256,2048]{1,0:T(8,128)(2,1)}, bf16[256,2048]{1,0:T(8,128)(2,1)}, ...), branch_computations={%region_7.8_spmd, %region_8.9_spmd} | conditional | flops 14681064 | bytes 49808684 | solution.py:142
  331.0 12.3 %branch_1_fun.25 = bf16[704,2048]{1,0:T(8,128)(2,1)S(1)} custom-call(bf16[2048,704]{1,0:T(8,128)(2,1)} %bitcast.199, bf16[256,2048]{1,0:T(8,128)(2,1)} %get-tuple-element.337.refs_1_, bf16[256,2048]{1,0:T(8,128)(2,1)} %get-tuple-element.338.refs_2_, bf16[256,2048]{1,0:T(8,128)(2,1)} %get-tuple-element.339.refs_3_, ...), custom_call_target="tpu_custom_call" | custom-call | flops 1000 | bytes 1000 | tf_op jit(solution)/shard_map/cond/branch_1_fun/pallas_call | solution.py:716
  352.3 6.8 collective-permute-done.23
  362.4 30.3 %conditional.15 = (f32[256,2048]{1,0:T(8,128)}, bf16[2048]{0:T(1024)(128)(2,1)S(1)}) conditional(s32[]{:T(128)} %bitcast.49, () %tuple.144, (f32[256]{0:T(256)S(1)}, f32[256,1]{0,1:T(1,128)S(1)}, f32[256,1]{0,1:T(1,128)S(1)}, bf16[256,2048]{1,0:T(8,128)(2,1)S(1)}, bf16[256,2048]{1,0:T(8,128)(2,1)S(1)}, /*index=5*/bf16[256,2048]{1,0:T(8,128)(2,1)S(1)}, ...), branch_computations={%region_9.10_spmd, %region_10.13_spmd} | conditional | flops 10486784 | bytes 38842520 | solution.py:142
  365.4 21.3 %collective-permute-done.11 = bf16[256,2048]{1,0:T(8,128)(2,1)S(1)} collective-permute-done((bf16[256,2048]{1,0:T(8,128)(2,1)S(1)}, bf16[256,2048]{1,0:T(8,128)(2,1)S(1)}, u32[]{:S(2)}, u32[]{:S(2)}) %collective-permute-start.11) | collective-permute-done | bytes 1048608 | tf_op jit(solution)/shard_map/cond/branch_1_fun/ppermute | solution.py:42
  392.7 30.8 %conditional.16 = (bf16[256,2048]{1,0:T(8,128)(2,1)}, bf16[256,2048]{1,0:T(8,128)(2,1)}, bf16[256,2048]{1,0:T(8,128)(2,1)}, bf16[256,2048]{1,0:T(8,128)(2,1)}, b...) conditional(s32[]{:T(128)} %bitcast.49, () %tuple.143, (f32[256,2048]{1,0:T(8,128)}, ...), branch_computations={%region_14.15_spmd, %region_15.16_spmd} | conditional | flops 525288 | bytes 28312828 | solution.py:142
  396.5 21.4 %collective-permute-done = bf16[256,2048]{1,0:T(8,128)(2,1)} collective-permute-done((bf16[256,2048]{1,0:T(8,128)(2,1)S(1)}, bf16[256,2048]{1,0:T(8,128)(2,1)}, u32[]{:S(2)}, u32[]{:S(2)}) %collective-permute-start) | collective-permute-done | bytes 1048608 | tf_op jit(solution)/shard_map/cond/branch_1_fun/ppermute | solution.py:42
  423.5 26.8 %conditional.17 = ((bf16[8,2,128,256]{3,2,1,0:T(8,128)(2,1)S(1)}, bf16[256,2048]{1,0:T(8,128)(2,1)})) conditional(s32[]{:T(128)} %bitcast.49, () %tuple.142, (bf16[256,2048]{1,0:T(8,128)(2,1)}, bf16[256,2048]{1,0:T(8,128)(2,1)}, bf16[256,2048]{1,0:T(8,128)(2,1)}, bf16[256,2048]{1,0:T(8,128)(2,1)}, bf16[8,2,128,256]{3,2,1,0:T(8,128)(2,1)S(1)}, ...), branch_computations={%region_16.17_spmd, %region_17.18_spmd} | conditional | flops 3000 | bytes 16780372 | solution.py:142
  427.3 11.5 %collective-permute-done.5 = bf16[128,2048]{1,0:T(8,128)(2,1)S(1)} collective-permute-done((bf16[128,2048]{1,0:T(8,128)(2,1)S(1)}, bf16[128,2048]{1,0:T(8,128)(2,1)S(1)}, u32[]{:S(2)}, u32[]{:S(2)}) %collective-permute-start.5) | collective-permute-done | bytes 524320 | tf_op jit(solution)/shard_map/cond/branch_1_fun/ppermute | solution.py:42
  440.5 3.4 branch_1_fun.27
  444.0 3.4 branch_1_fun.28
  450.2 4.0 copy.125
  454.2 4.6 all-to-all-start.2
  458.8 48.7 %conditional.18 = (bf16[256,2048]{1,0:T(8,128)(2,1)}, bf16[256,2048]{1,0:T(8,128)(2,1)}, bf16[256,2048]{1,0:T(8,128)(2,1)}, bf16[256,2048]{1,0:T(8,128)(2,1)}, b...) conditional(s32[]{:T(128)} %bitcast.49, () %tuple.123, ...), branch_computations={%region_18.19_spmd, %region_19.20_spmd} | conditional | flops 14682064 | bytes 58198384 | solution.py:142
  460.4 12.6 %branch_1_fun.30 = bf16[8,2,128,512]{3,2,1,0:T(8,128)(2,1)} custom-call(s32[2]{0:T(128)S(1)} %get-tuple-element.385.lengths_ref, s32[2]{0:T(128)S(1)} %get-tuple-element.386.key_ref, bf16[8,2,128,256]{3,2,1,0:T(8,128)(2,1)} %get-tuple-element.387.q_ref, bf16[8,2,128,256]{3,2,1,0:T(8,128)(2,1)} %get-tuple-element.388.up_ref, ...), custom_call_target="tpu_custom_call" | custom-call | flops 1000 | bytes 1000 | tf_op jit(solution)/shard_map/cond/branch_1_fun/pallas_call | solution.py:388
  474.8 6.9 branch_1_fun.31
  493.1 11.1 %collective-permute-done.29 = bf16[128,2048]{1,0:T(8,128)(2,1)S(1)} collective-permute-done((bf16[128,2048]{1,0:T(8,128)(2,1)S(1)}, bf16[128,2048]{1,0:T(8,128)(2,1)S(1)}, u32[]{:S(2)}, u32[]{:S(2)}) %collective-permute-start.29) | collective-permute-done | bytes 524320 | tf_op jit(solution)/shard_map/cond/branch_1_fun/ppermute | solution.py:42
  507.6 29.6 %conditional.19 = (bf16[256,2048]{1,0:T(8,128)(2,1)}, bf16[256,2048]{1,0:T(8,128)(2,1)}, bf16[256,2048]{1,0:T(8,128)(2,1)}, bf16[2048,512]{1,0:T(8,128)(2,1)S(1)}) conditional(s32[]{:T(128)} %bitcast.49, () %tuple.155, (bf16[256,2048]{1,0:T(8,128)(2,1)}, bf16[256,2048]{1,0:T(8,128)(2,1)}, bf16[256,2048]{1,0:T(8,128)(2,1)}, ...), branch_computations={%region_20.21_spmd, %region_21.22_spmd} | conditional | flops 14681064 | bytes 49808684 | solution.py:142
  508.8 9.8 %branch_1_fun.32 = bf16[2048,512]{1,0:T(8,128)(2,1)S(1)} custom-call(bf16[256,2048]{1,0:T(8,128)(2,1)} %get-tuple-element.415.refs_0_, bf16[256,2048]{1,0:T(8,128)(2,1)} %get-tuple-element.416.refs_1_, bf16[256,2048]{1,0:T(8,128)(2,1)} %get-tuple-element.417.refs_2_, bf16[256,2048]{1,0:T(8,128)(2,1)} %get-tuple-element.418.refs_3_, ...), custom_call_target="tpu_custom_call" | custom-call | flops 1000 | bytes 1000 | tf_op jit(solution)/shard_map/cond/branch_1_fun/pallas_call | solution.py:682
  528.0 6.4 collective-permute-done.35
  538.9 4.3 all-to-all-start.3
  545.1 56.9 %conditional.20 = (bf16[272,256]{1,0:T(8,128)(2,1)S(1)}, f32[2,128,2048]{2,1,0:T(8,128)}) conditional(s32[]{:T(128)} %bitcast.49, () %tuple.154, (bf16[2048,512]{1,0:T(8,128)(2,1)}, bf16[256,2048]{1,0:T(8,128)(2,1)}, bf16[256,2048]{1,0:T(8,128)(2,1)}, bf16[256,2048]{1,0:T(8,128)(2,1)}, f32[2,128,2048]{2,1,0:T(8,128)}, ...), branch_computations={%region_22.23_spmd, %region_23.0_spmd} | conditional | flops 14740232 | bytes 49960472 | solution.py:142
  554.5 31.2 %collective-permute-done.13 = bf16[2,256,256]{2,1,0:T(8,128)(2,1)S(1)} collective-permute-done((bf16[2,256,256]{2,1,0:T(8,128)(2,1)S(1)}, bf16[2,256,256]{2,1,0:T(8,128)(2,1)S(1)}, u32[]{:S(2)}, u32[]{:S(2)}) %collective-permute-start.13) | collective-permute-done | bytes 262176 | tf_op jit(solution)/shard_map/cond/branch_1_fun/ppermute | solution.py:42
  587.9 3.4 fusion.10
  598.5 3.5 fusion.9
  602.0 3.6 copy.124
  605.6 3.6 all-to-all-start.4
  609.9 58.9 %conditional.21 = (bf16[256,2048]{1,0:T(8,128)(2,1)}, f32[256,5632]{1,0:T(8,128)}, f32[704,2048]{1,0:T(8,128)}) conditional(s32[]{:T(128)} %bitcast.49, () %tuple.122, (bf16[256,2048]{1,0:T(8,128)(2,1)}, bf16[256,2048]{1,0:T(8,128)(2,1)}, bf16[256,2048]{1,0:T(8,128)(2,1)}, f32[256,2048]{1,0:T(8,128)}, bf16[8,704,256]{2,1,0:T(8,128)(2,1)}, ...), branch_computations={%region_29.30_spmd, %region_30.31_spmd} | conditional | flops 6161384 | bytes 43254920 | solution.py:142
  613.4 4.7 branch_1_fun.33
  618.1 3.3 convert_element_type.431
  621.4 44.4 %collective-permute-done.9 = bf16[256,2048]{1,0:T(8,128)(2,1)S(1)} collective-permute-done((bf16[256,2048]{1,0:T(8,128)(2,1)}, bf16[256,2048]{1,0:T(8,128)(2,1)S(1)}, u32[]{:S(2)}, u32[]{:S(2)}) %collective-permute-start.9) | collective-permute-done | bytes 1048608 | tf_op jit(solution)/shard_map/cond/branch_1_fun/ppermute | solution.py:42
  668.7 3.7 shard_map.239
  672.5 32.0 %all-reduce.10.cloned.1.call-done = (bf16[256,2048]{1,0:T(8,128)(2,1)}, bf16[2048,256]{1,0:T(8,128)(2,1)}, bf16[272,256]{1,0:T(8,128)(2,1)}) async-done(((bf16[256,2048]{1,0:T(8,128)(2,1)}, bf16[2048,256]{1,0:T(8,128)(2,1)}, bf16[272,256]{1,0:T(8,128)(2,1)}), (bf16[256,2048]{1,0:T(8,128)(2,1)}, bf16[2048,256]{1,0:T(8,128)(2,1)}, bf16[272,256]{1,0:T(8,128)(2,1)})) %all-reduce.10.cloned.1.call-update) | async-done | bytes 2236432 | tf_op jit(solution)/shard_map/psum | solution.py:996
  (388 shorter events, 195.7 us)
Async XLA Ops:
  7.2 47.9 %collective-permute-start.38 = (bf16[256,2048]{1,0:T(8,128)(2,1)}, bf16[256,2048]{1,0:T(8,128)(2,1)S(1)}, u32[]{:S(2)}, u32[]{:S(2)}) collective-permute-start(bf16[256,2048]{1,0:T(8,128)(2,1)} %bitcast.189), channel_id=1, source_target_pairs={{0,2},{1,3},{2,0},{3,1},{4,6},{5,7},{6,4},{7,5},{8,10},{9,11},{10,... | collective-permute-start | bytes 3145736 | tf_op jit(solution)/shard_map/ppermute | solution.py:42
  10.2 44.9 %collective-permute-start.39 = (bf16[256,2048]{1,0:T(8,128)(2,1)}, bf16[256,2048]{1,0:T(8,128)(2,1)S(1)}, u32[]{:S(2)}, u32[]{:S(2)}) collective-permute-start(bf16[256,2048]{1,0:T(8,128)(2,1)} %bitcast.190), channel_id=1, source_target_pairs={{0,4},{1,5},{2,6},{3,7},{4,0},{5,1},{6,2},{7,3},{8,12},{9,13},{10,... | collective-permute-start | bytes 3145736 | tf_op jit(solution)/shard_map/ppermute | solution.py:42
  11.7 75.3 %collective-permute-start.48 = (bf16[256,2048]{1,0:T(8,128)(2,1)}, bf16[256,2048]{1,0:T(8,128)(2,1)}, u32[]{:S(2)}, u32[]{:S(2)}) collective-permute-start(bf16[256,2048]{1,0:T(8,128)(2,1)} %bitcast.191), channel_id=1, source_target_pairs={{0,1},{1,0},{2,3},{3,2},{4,5},{5,4},{6,7},{7,6},{8,9},{9,8},{10,11... | collective-permute-start | bytes 3145736 | tf_op jit(solution)/shard_map/ppermute | solution.py:42
  13.9 29.0 %collective-permute-start.43 = (bf16[272,256]{1,0:T(8,128)(2,1)S(1)}, bf16[272,256]{1,0:T(8,128)(2,1)S(1)}, u32[]{:S(2)}, u32[]{:S(2)}) collective-permute-start(bf16[272,256]{1,0:T(8,128)(2,1)S(1)} %pad_maximum_fusion.13), channel_id=1, source_target_pairs={{0,4},{1,5},{2,6},{3,7},{4,0},{5,1},{6,2},{7,3},{8,12},{9,13},{10,... | collective-permute-start | bytes 417800 | tf_op jit(solution)/shard_map/ppermute | solution.py:42
  19.5 41.9 %all-to-all-start = ((bf16[8,64,1408]{2,1,0:T(8,128)(2,1)}), bf16[8,64,1408]{2,1,0:T(8,128)(2,1)}, u32[]{:S(2)}, u32[]{:S(2)}) async-start(bf16[8,64,1408]{2,1,0:T(8,128)(2,1)} %shard_map.229), calls=%async_computation | async-start | bytes 2883584 | tf_op jit(solution)/shard_map/all_to_all | solution.py:785
  56.0 14.7 %collective-permute-start.40 = (bf16[128,2048]{1,0:T(8,128)(2,1)}, bf16[128,2048]{1,0:T(8,128)(2,1)}, u32[]{:S(2)}, u32[]{:S(2)}) collective-permute-start(bf16[128,2048]{1,0:T(8,128)(2,1)} %slice.194), channel_id=1, source_target_pairs={{0,4},{1,5},{2,6},{3,7},{4,0},{5,1},{6,2},{7,3},{8,12},{9,13},{10,... | collective-permute-start | bytes 1572872 | tf_op jit(solution)/shard_map/ppermute | solution.py:42
  58.6 12.8 %collective-permute-start.41 = (bf16[128,2048]{1,0:T(8,128)(2,1)}, bf16[128,2048]{1,0:T(8,128)(2,1)}, u32[]{:S(2)}, u32[]{:S(2)}) collective-permute-start(bf16[128,2048]{1,0:T(8,128)(2,1)} %slice.195), channel_id=1, source_target_pairs={{0,2},{1,3},{2,0},{3,1},{4,6},{5,7},{6,4},{7,5},{8,10},{9,11},{10,... | collective-permute-start | bytes 1572872 | tf_op jit(solution)/shard_map/ppermute | solution.py:42
  60.9 15.7 %collective-permute-start.45 = (bf16[2,2,272,256]{3,2,1,0:T(8,128)(2,1)}, bf16[2,2,272,256]{3,2,1,0:T(8,128)(2,1)}, u32[]{:S(2)}, u32[]{:S(2)}) collective-permute-start(bf16[2,2,272,256]{3,2,1,0:T(8,128)(2,1)} %pad_maximum_fusion.9), channel_id=1, source_target_pairs={{0,1},{1,0},{2,3},{3,2},{4,5},{5,4},{6,7},{7,6},{8,9},{9,8},{10,11... | collective-permute-start | bytes 1671176 | tf_op jit(solution)/shard_map/ppermute | solution.py:42
  60.9 36.3 %collective-permute-start.46 = (bf16[256,2048]{1,0:T(8,128)(2,1)S(1)}, bf16[256,2048]{1,0:T(8,128)(2,1)}, u32[]{:S(2)}, u32[]{:S(2)}) collective-permute-start(bf16[256,2048]{1,0:T(8,128)(2,1)S(1)} %collective-permute-done.39.a_ref), channel_id=1, source_target_pairs={{0,1},{1,0},{2,3},{3,2},{4,5},{5,4},{6,7},{7,6},{8,9},{9,8},{10,11... | collective-permute-start | bytes 3145736 | tf_op jit(solution)/shard_map/ppermute | solution.py:42
  65.6 21.5 %all-to-all-start.1 = ((bf16[256,8,256]{2,0,1:T(8,128)(2,1)}), bf16[256,8,256]{2,0,1:T(8,128)(2,1)}, u32[]{:S(2)}, u32[]{:S(2)}) async-start(bf16[256,8,256]{2,0,1:T(8,128)(2,1)} %bitcast.187), calls=%async_computation.1 | async-start | bytes 2097152 | tf_op jit(solution)/shard_map/all_to_all | solution.py:132
  69.9 110.8 %all-gather.3.cloned.1.call-start = ((), (), s32[]{:S(2)}) async-start(), calls=%async_computation.6 | async-start | bytes 7208960 | tf_op jit(solution)/shard_map/all_gather | solution.py:787
  70.6 322.0 %all-reduce.8.cloned.1.call-start = ((), (), s32[]{:S(2)}) async-start(), calls=%async_computation.5 | async-start | bytes 5767168 | tf_op jit(solution)/shard_map/psum | solution.py:915
  70.7 21.8 %collective-permute-start.47 = (bf16[256,2048]{1,0:T(8,128)(2,1)S(1)}, bf16[256,2048]{1,0:T(8,128)(2,1)}, u32[]{:S(2)}, u32[]{:S(2)}) collective-permute-start(bf16[256,2048]{1,0:T(8,128)(2,1)S(1)} %collective-permute-done.38.a_ref), channel_id=1, source_target_pairs={{0,1},{1,0},{2,3},{3,2},{4,5},{5,4},{6,7},{7,6},{8,9},{9,8},{10,11... | collective-permute-start | bytes 3145736 | tf_op jit(solution)/shard_map/ppermute | solution.py:42
  75.2 31.7 %collective-permute-start.50 = (bf16[256,2048]{1,0:T(8,128)(2,1)}, bf16[256,2048]{1,0:T(8,128)(2,1)}, u32[]{:S(2)}, u32[]{:S(2)}) collective-permute-start(bf16[256,2048]{1,0:T(8,128)(2,1)} %get-tuple-element.634), channel_id=1, source_target_pairs={{0,2},{1,3},{2,0},{3,1},{4,6},{5,7},{6,4},{7,5},{8,10},{9,11},{10,... | collective-permute-start | bytes 3145736 | tf_op jit(solution)/shard_map/ppermute | solution.py:42
  76.7 30.2 %collective-permute-start.51 = (bf16[256,2048]{1,0:T(8,128)(2,1)}, bf16[256,2048]{1,0:T(8,128)(2,1)}, u32[]{:S(2)}, u32[]{:S(2)}) collective-permute-start(bf16[256,2048]{1,0:T(8,128)(2,1)} %get-tuple-element.634), channel_id=1, source_target_pairs={{0,4},{1,5},{2,6},{3,7},{4,0},{5,1},{6,2},{7,3},{8,12},{9,13},{10,... | collective-permute-start | bytes 3145736 | tf_op jit(solution)/shard_map/ppermute | solution.py:42
  87.0 20.4 %collective-permute-start.42 = (bf16[256,2048]{1,0:T(8,128)(2,1)}, bf16[256,2048]{1,0:T(8,128)(2,1)}, u32[]{:S(2)}, u32[]{:S(2)}) collective-permute-start(bf16[256,2048]{1,0:T(8,128)(2,1)} %constant_dynamic-update-slice_fusion.2.a_ref), channel_id=1, source_target_pairs={{0,1},{1,0},{2,3},{3,2},{4,5},{5,4},{6,7},{7,6},{8,9},{9,8},{10,11... | collective-permute-start | bytes 3145736 | tf_op jit(solution)/shard_map/ppermute | solution.py:42
  92.5 29.1 %collective-permute-start.49 = (bf16[256,2048]{1,0:T(8,128)(2,1)}, bf16[256,2048]{1,0:T(8,128)(2,1)S(1)}, u32[]{:S(2)}, u32[]{:S(2)}) collective-permute-start(bf16[256,2048]{1,0:T(8,128)(2,1)} %get-tuple-element.634), channel_id=1, source_target_pairs={{0,1},{1,0},{2,3},{3,2},{4,5},{5,4},{6,7},{7,6},{8,9},{9,8},{10,11... | collective-permute-start | bytes 3145736 | tf_op jit(solution)/shard_map/ppermute | solution.py:42
  106.9 14.8 %collective-permute-start.52 = (bf16[256,2048]{1,0:T(8,128)(2,1)}, bf16[256,2048]{1,0:T(8,128)(2,1)S(1)}, u32[]{:S(2)}, u32[]{:S(2)}) collective-permute-start(bf16[256,2048]{1,0:T(8,128)(2,1)} %collective-permute-done.50), channel_id=1, source_target_pairs={{0,1},{1,0},{2,3},{3,2},{4,5},{5,4},{6,7},{7,6},{8,9},{9,8},{10,11... | collective-permute-start | bytes 3145736 | tf_op jit(solution)/shard_map/ppermute | solution.py:42
  106.9 14.8 %collective-permute-start.53 = (bf16[256,2048]{1,0:T(8,128)(2,1)}, bf16[256,2048]{1,0:T(8,128)(2,1)S(1)}, u32[]{:S(2)}, u32[]{:S(2)}) collective-permute-start(bf16[256,2048]{1,0:T(8,128)(2,1)} %collective-permute-done.51), channel_id=1, source_target_pairs={{0,1},{1,0},{2,3},{3,2},{4,5},{5,4},{6,7},{7,6},{8,9},{9,8},{10,11... | collective-permute-start | bytes 3145736 | tf_op jit(solution)/shard_map/ppermute | solution.py:42
  128.6 41.5 %collective-permute-start.54 = (bf16[256,2048]{1,0:T(8,128)(2,1)S(1)}, bf16[256,2048]{1,0:T(8,128)(2,1)S(1)}, u32[]{:S(2)}, u32[]{:S(2)}) collective-permute-start(bf16[256,2048]{1,0:T(8,128)(2,1)S(1)} %get-tuple-element.621), channel_id=1, source_target_pairs={{0,1},{1,0},{2,3},{3,2},{4,5},{5,4},{6,7},{7,6},{8,9},{9,8},{10,11... | collective-permute-start | bytes 3145736 | tf_op jit(solution)/shard_map/ppermute | solution.py:42
  132.7 14.0 %collective-permute-start.57 = (bf16[128,2048]{1,0:T(8,128)(2,1)S(1)}, bf16[128,2048]{1,0:T(8,128)(2,1)S(1)}, u32[]{:S(2)}, u32[]{:S(2)}) collective-permute-start(bf16[128,2048]{1,0:T(8,128)(2,1)S(1)} %get-tuple-element.812), channel_id=1, source_target_pairs={{0,2},{1,3},{2,0},{3,1},{4,6},{5,7},{6,4},{7,5},{8,10},{9,11},{10,... | collective-permute-start | bytes 1572872 | tf_op jit(solution)/shard_map/ppermute | solution.py:42
  134.1 13.7 %collective-permute-start.58 = (bf16[128,2048]{1,0:T(8,128)(2,1)S(1)}, bf16[128,2048]{1,0:T(8,128)(2,1)S(1)}, u32[]{:S(2)}, u32[]{:S(2)}) collective-permute-start(bf16[128,2048]{1,0:T(8,128)(2,1)S(1)} %get-tuple-element.811), channel_id=1, source_target_pairs={{0,4},{1,5},{2,6},{3,7},{4,0},{5,1},{6,2},{7,3},{8,12},{9,13},{10,... | collective-permute-start | bytes 1572872 | tf_op jit(solution)/shard_map/ppermute | solution.py:42
  148.0 24.2 %collective-permute-start.61 = (bf16[256,2048]{1,0:T(8,128)(2,1)S(1)}, bf16[256,2048]{1,0:T(8,128)(2,1)S(1)}, u32[]{:S(2)}, u32[]{:S(2)}) collective-permute-start(bf16[256,2048]{1,0:T(8,128)(2,1)S(1)} %pad_maximum_fusion.8), channel_id=1, source_target_pairs={{0,4},{1,5},{2,6},{3,7},{4,0},{5,1},{6,2},{7,3},{8,12},{9,13},{10,... | collective-permute-start | bytes 3145736 | tf_op jit(solution)/shard_map/ppermute | solution.py:42
  149.0 24.0 %collective-permute-start.59 = (bf16[256,2048]{1,0:T(8,128)(2,1)S(1)}, bf16[256,2048]{1,0:T(8,128)(2,1)S(1)}, u32[]{:S(2)}, u32[]{:S(2)}) collective-permute-start(bf16[256,2048]{1,0:T(8,128)(2,1)S(1)} %pad_maximum_fusion.7), channel_id=1, source_target_pairs={{0,2},{1,3},{2,0},{3,1},{4,6},{5,7},{6,4},{7,5},{8,10},{9,11},{10,... | collective-permute-start | bytes 3145736 | tf_op jit(solution)/shard_map/ppermute | solution.py:42
  184.2 25.6 %collective-permute-start.62 = (bf16[256,2048]{1,0:T(8,128)(2,1)S(1)}, bf16[256,2048]{1,0:T(8,128)(2,1)}, u32[]{:S(2)}, u32[]{:S(2)}) collective-permute-start(bf16[256,2048]{1,0:T(8,128)(2,1)S(1)} %multiply_convert_fusion.refs_1_), channel_id=1, source_target_pairs={{0,2},{1,3},{2,0},{3,1},{4,6},{5,7},{6,4},{7,5},{8,10},{9,11},{10,... | collective-permute-start | bytes 3145736 | tf_op jit(solution)/shard_map/ppermute | solution.py:42
  185.6 25.3 %collective-permute-start.63 = (bf16[256,2048]{1,0:T(8,128)(2,1)S(1)}, bf16[256,2048]{1,0:T(8,128)(2,1)}, u32[]{:S(2)}, u32[]{:S(2)}) collective-permute-start(bf16[256,2048]{1,0:T(8,128)(2,1)S(1)} %multiply_convert_fusion.refs_1_), channel_id=1, source_target_pairs={{0,4},{1,5},{2,6},{3,7},{4,0},{5,1},{6,2},{7,3},{8,12},{9,13},{10,... | collective-permute-start | bytes 3145736 | tf_op jit(solution)/shard_map/ppermute | solution.py:42
  215.3 28.9 %collective-permute-start.65 = (bf16[128,2048]{1,0:T(8,128)(2,1)}, bf16[128,2048]{1,0:T(8,128)(2,1)}, u32[]{:S(2)}, u32[]{:S(2)}) collective-permute-start(bf16[128,2048]{1,0:T(8,128)(2,1)} %slice.206), channel_id=1, source_target_pairs={{0,4},{1,5},{2,6},{3,7},{4,0},{5,1},{6,2},{7,3},{8,12},{9,13},{10,... | collective-permute-start | bytes 1572872 | tf_op jit(solution)/shard_map/ppermute | solution.py:42
  216.7 27.4 %collective-permute-start.66 = (bf16[128,2048]{1,0:T(8,128)(2,1)}, bf16[128,2048]{1,0:T(8,128)(2,1)}, u32[]{:S(2)}, u32[]{:S(2)}) collective-permute-start(bf16[128,2048]{1,0:T(8,128)(2,1)} %slice.207), channel_id=1, source_target_pairs={{0,2},{1,3},{2,0},{3,1},{4,6},{5,7},{6,4},{7,5},{8,10},{9,11},{10,... | collective-permute-start | bytes 1572872 | tf_op jit(solution)/shard_map/ppermute | solution.py:42
  219.2 25.0 %collective-permute-start.67 = (bf16[128,2048]{1,0:T(8,128)(2,1)}, bf16[128,2048]{1,0:T(8,128)(2,1)}, u32[]{:S(2)}, u32[]{:S(2)}) collective-permute-start(bf16[128,2048]{1,0:T(8,128)(2,1)} %slice.208), channel_id=1, source_target_pairs={{0,4},{1,5},{2,6},{3,7},{4,0},{5,1},{6,2},{7,3},{8,12},{9,13},{10,... | collective-permute-start | bytes 1572872 | tf_op jit(solution)/shard_map/ppermute | solution.py:42
  221.6 22.6 %collective-permute-start.68 = (bf16[128,2048]{1,0:T(8,128)(2,1)}, bf16[128,2048]{1,0:T(8,128)(2,1)}, u32[]{:S(2)}, u32[]{:S(2)}) collective-permute-start(bf16[128,2048]{1,0:T(8,128)(2,1)} %slice.209), channel_id=1, source_target_pairs={{0,2},{1,3},{2,0},{3,1},{4,6},{5,7},{6,4},{7,5},{8,10},{9,11},{10,... | collective-permute-start | bytes 1572872 | tf_op jit(solution)/shard_map/ppermute | solution.py:42
  277.9 324.1 %all-reduce.12.cloned.1.call-start = ((), (), s32[]{:S(2)}) async-start(), calls=%async_computation.8 | async-start | bytes 11534336 | tf_op jit(solution)/shard_map/psum | solution.py:938
  330.0 13.4 %collective-permute-start.22 = (bf16[256,2048]{1,0:T(8,128)(2,1)}, bf16[256,2048]{1,0:T(8,128)(2,1)S(1)}, u32[]{:S(2)}, u32[]{:S(2)}) collective-permute-start(bf16[256,2048]{1,0:T(8,128)(2,1)} %get-tuple-element.331), channel_id=1, source_target_pairs={{0,1},{1,0},{2,3},{3,2},{4,5},{5,4},{6,7},{7,6},{8,9},{9,8},{10,11... | collective-permute-start | bytes 3145736 | tf_op jit(solution)/shard_map/cond/branch_1_fun/ppermute | solution.py:42
  330.2 16.9 %collective-permute-start.21 = (bf16[256,2048]{1,0:T(8,128)(2,1)}, bf16[256,2048]{1,0:T(8,128)(2,1)S(1)}, u32[]{:S(2)}, u32[]{:S(2)}) collective-permute-start(bf16[256,2048]{1,0:T(8,128)(2,1)} %get-tuple-element.329), channel_id=1, source_target_pairs={{0,1},{1,0},{2,3},{3,2},{4,5},{5,4},{6,7},{7,6},{8,9},{9,8},{10,11... | collective-permute-start | bytes 3145736 | tf_op jit(solution)/shard_map/cond/branch_1_fun/ppermute | solution.py:42
  330.5 19.9 %collective-permute-start.20 = (bf16[256,2048]{1,0:T(8,128)(2,1)}, bf16[256,2048]{1,0:T(8,128)(2,1)S(1)}, u32[]{:S(2)}, u32[]{:S(2)}) collective-permute-start(bf16[256,2048]{1,0:T(8,128)(2,1)} %get-tuple-element.327), channel_id=1, source_target_pairs={{0,1},{1,0},{2,3},{3,2},{4,5},{5,4},{6,7},{7,6},{8,9},{9,8},{10,11... | collective-permute-start | bytes 3145736 | tf_op jit(solution)/shard_map/cond/branch_1_fun/ppermute | solution.py:42
  330.7 18.0 %collective-permute-start.25 = (bf16[256,2048]{1,0:T(8,128)(2,1)}, bf16[256,2048]{1,0:T(8,128)(2,1)S(1)}, u32[]{:S(2)}, u32[]{:S(2)}) collective-permute-start(bf16[256,2048]{1,0:T(8,128)(2,1)} %get-tuple-element.334), channel_id=1, source_target_pairs={{0,1},{1,0},{2,3},{3,2},{4,5},{5,4},{6,7},{7,6},{8,9},{9,8},{10,11... | collective-permute-start | bytes 3145736 | tf_op jit(solution)/shard_map/cond/branch_1_fun/ppermute | solution.py:42
  345.1 14.1 %collective-permute-start.23 = (bf16[128,2048]{1,0:T(8,128)(2,1)S(1)}, bf16[128,2048]{1,0:T(8,128)(2,1)S(1)}, u32[]{:S(2)}, u32[]{:S(2)}) collective-permute-start(bf16[128,2048]{1,0:T(8,128)(2,1)S(1)} %get-tuple-element.793), channel_id=1, source_target_pairs={{0,2},{1,3},{2,0},{3,1},{4,6},{5,7},{6,4},{7,5},{8,10},{9,11},{10,... | collective-permute-start | bytes 1572872 | tf_op jit(solution)/shard_map/cond/branch_1_fun/ppermute | solution.py:42
  345.5 13.8 %collective-permute-start.24 = (bf16[128,2048]{1,0:T(8,128)(2,1)S(1)}, bf16[128,2048]{1,0:T(8,128)(2,1)S(1)}, u32[]{:S(2)}, u32[]{:S(2)}) collective-permute-start(bf16[128,2048]{1,0:T(8,128)(2,1)S(1)} %get-tuple-element.792), channel_id=1, source_target_pairs={{0,4},{1,5},{2,6},{3,7},{4,0},{5,1},{6,2},{7,3},{8,12},{9,13},{10,... | collective-permute-start | bytes 1572872 | tf_op jit(solution)/shard_map/cond/branch_1_fun/ppermute | solution.py:42
  362.4 24.3 %collective-permute-start.11 = (bf16[256,2048]{1,0:T(8,128)(2,1)S(1)}, bf16[256,2048]{1,0:T(8,128)(2,1)S(1)}, u32[]{:S(2)}, u32[]{:S(2)}) collective-permute-start(bf16[256,2048]{1,0:T(8,128)(2,1)S(1)} %get-tuple-element.351), channel_id=1, source_target_pairs={{0,4},{1,5},{2,6},{3,7},{4,0},{5,1},{6,2},{7,3},{8,12},{9,13},{10,... | collective-permute-start | bytes 3145736 | tf_op jit(solution)/shard_map/cond/branch_1_fun/ppermute | solution.py:42
  363.8 24.0 %collective-permute-start.10 = (bf16[256,2048]{1,0:T(8,128)(2,1)S(1)}, bf16[256,2048]{1,0:T(8,128)(2,1)S(1)}, u32[]{:S(2)}, u32[]{:S(2)}) collective-permute-start(bf16[256,2048]{1,0:T(8,128)(2,1)S(1)} %get-tuple-element.350), channel_id=1, source_target_pairs={{0,2},{1,3},{2,0},{3,1},{4,6},{5,7},{6,4},{7,5},{8,10},{9,11},{10,... | collective-permute-start | bytes 3145736 | tf_op jit(solution)/shard_map/cond/branch_1_fun/ppermute | solution.py:42
  394.5 23.4 %collective-permute-start = (bf16[256,2048]{1,0:T(8,128)(2,1)S(1)}, bf16[256,2048]{1,0:T(8,128)(2,1)}, u32[]{:S(2)}, u32[]{:S(2)}) collective-permute-start(bf16[256,2048]{1,0:T(8,128)(2,1)S(1)} %convert_element_type.359.a_ref), channel_id=1, source_target_pairs={{0,2},{1,3},{2,0},{3,1},{4,6},{5,7},{6,4},{7,5},{8,10},{9,11},{10,... | collective-permute-start | bytes 3145736 | tf_op jit(solution)/shard_map/cond/branch_1_fun/ppermute | solution.py:42
  396.0 22.9 %collective-permute-start.1 = (bf16[256,2048]{1,0:T(8,128)(2,1)S(1)}, bf16[256,2048]{1,0:T(8,128)(2,1)}, u32[]{:S(2)}, u32[]{:S(2)}) collective-permute-start(bf16[256,2048]{1,0:T(8,128)(2,1)S(1)} %convert_element_type.359.a_ref), channel_id=1, source_target_pairs={{0,4},{1,5},{2,6},{3,7},{4,0},{5,1},{6,2},{7,3},{8,12},{9,13},{10,... | collective-permute-start | bytes 3145736 | tf_op jit(solution)/shard_map/cond/branch_1_fun/ppermute | solution.py:42
  396.5 22.9 %collective-permute-start.4 = (bf16[256,2048]{1,0:T(8,128)(2,1)S(1)}, bf16[256,2048]{1,0:T(8,128)(2,1)S(1)}, u32[]{:S(2)}, u32[]{:S(2)}) collective-permute-start(bf16[256,2048]{1,0:T(8,128)(2,1)S(1)} %convert_element_type.359.a_ref), channel_id=1, source_target_pairs={{0,1},{1,0},{2,3},{3,2},{4,5},{5,4},{6,7},{7,6},{8,9},{9,8},{10,11... | collective-permute-start | bytes 3145736 | tf_op jit(solution)/shard_map/cond/branch_1_fun/ppermute | solution.py:42
  424.9 14.0 %collective-permute-start.5 = (bf16[128,2048]{1,0:T(8,128)(2,1)S(1)}, bf16[128,2048]{1,0:T(8,128)(2,1)S(1)}, u32[]{:S(2)}, u32[]{:S(2)}) collective-permute-start(bf16[128,2048]{1,0:T(8,128)(2,1)S(1)} %slice.142), channel_id=1, source_target_pairs={{0,4},{1,5},{2,6},{3,7},{4,0},{5,1},{6,2},{7,3},{8,12},{9,13},{10,... | collective-permute-start | bytes 1572872 | tf_op jit(solution)/shard_map/cond/branch_1_fun/ppermute | solution.py:42
  426.6 13.8 %collective-permute-start.6 = (bf16[128,2048]{1,0:T(8,128)(2,1)S(1)}, bf16[128,2048]{1,0:T(8,128)(2,1)S(1)}, u32[]{:S(2)}, u32[]{:S(2)}) collective-permute-start(bf16[128,2048]{1,0:T(8,128)(2,1)S(1)} %slice.143), channel_id=1, source_target_pairs={{0,2},{1,3},{2,0},{3,1},{4,6},{5,7},{6,4},{7,5},{8,10},{9,11},{10,... | collective-permute-start | bytes 1572872 | tf_op jit(solution)/shard_map/cond/branch_1_fun/ppermute | solution.py:42
  454.2 53.3 %all-to-all-start.2 = ((bf16[8,704,256]{2,1,0:T(8,128)(2,1)}), bf16[8,704,256]{2,1,0:T(8,128)(2,1)}, u32[]{:S(2)}, u32[]{:S(2)}) async-start(bf16[8,704,256]{2,1,0:T(8,128)(2,1)} %bitcast.202), calls=%async_computation.2 | async-start | bytes 5767168 | tf_op jit(solution)/shard_map/all_to_all | solution.py:751
  459.3 22.4 %collective-permute-start.28 = (bf16[256,2048]{1,0:T(8,128)(2,1)}, bf16[256,2048]{1,0:T(8,128)(2,1)S(1)}, u32[]{:S(2)}, u32[]{:S(2)}) collective-permute-start(bf16[256,2048]{1,0:T(8,128)(2,1)} %get-tuple-element.380), channel_id=1, source_target_pairs={{0,1},{1,0},{2,3},{3,2},{4,5},{5,4},{6,7},{7,6},{8,9},{9,8},{10,11... | collective-permute-start | bytes 3145736 | tf_op jit(solution)/shard_map/cond/branch_1_fun/ppermute | solution.py:42
  459.7 30.4 %collective-permute-start.26 = (bf16[256,2048]{1,0:T(8,128)(2,1)}, bf16[256,2048]{1,0:T(8,128)(2,1)S(1)}, u32[]{:S(2)}, u32[]{:S(2)}) collective-permute-start(bf16[256,2048]{1,0:T(8,128)(2,1)} %get-tuple-element.376), channel_id=1, source_target_pairs={{0,1},{1,0},{2,3},{3,2},{4,5},{5,4},{6,7},{7,6},{8,9},{9,8},{10,11... | collective-permute-start | bytes 3145736 | tf_op jit(solution)/shard_map/cond/branch_1_fun/ppermute | solution.py:42
  459.8 27.0 %collective-permute-start.27 = (bf16[256,2048]{1,0:T(8,128)(2,1)}, bf16[256,2048]{1,0:T(8,128)(2,1)S(1)}, u32[]{:S(2)}, u32[]{:S(2)}) collective-permute-start(bf16[256,2048]{1,0:T(8,128)(2,1)} %get-tuple-element.378), channel_id=1, source_target_pairs={{0,1},{1,0},{2,3},{3,2},{4,5},{5,4},{6,7},{7,6},{8,9},{9,8},{10,11... | collective-permute-start | bytes 3145736 | tf_op jit(solution)/shard_map/cond/branch_1_fun/ppermute | solution.py:42
  460.2 28.2 %collective-permute-start.31 = (bf16[256,2048]{1,0:T(8,128)(2,1)}, bf16[256,2048]{1,0:T(8,128)(2,1)S(1)}, u32[]{:S(2)}, u32[]{:S(2)}) collective-permute-start(bf16[256,2048]{1,0:T(8,128)(2,1)} %get-tuple-element.383), channel_id=1, source_target_pairs={{0,1},{1,0},{2,3},{3,2},{4,5},{5,4},{6,7},{7,6},{8,9},{9,8},{10,11... | collective-permute-start | bytes 3145736 | tf_op jit(solution)/shard_map/cond/branch_1_fun/ppermute | solution.py:42
  483.4 20.8 %collective-permute-start.29 = (bf16[128,2048]{1,0:T(8,128)(2,1)S(1)}, bf16[128,2048]{1,0:T(8,128)(2,1)S(1)}, u32[]{:S(2)}, u32[]{:S(2)}) collective-permute-start(bf16[128,2048]{1,0:T(8,128)(2,1)S(1)} %get-tuple-element.797), channel_id=1, source_target_pairs={{0,2},{1,3},{2,0},{3,1},{4,6},{5,7},{6,4},{7,5},{8,10},{9,11},{10,... | collective-permute-start | bytes 1572872 | tf_op jit(solution)/shard_map/cond/branch_1_fun/ppermute | solution.py:42
  485.3 19.7 %collective-permute-start.30 = (bf16[128,2048]{1,0:T(8,128)(2,1)S(1)}, bf16[128,2048]{1,0:T(8,128)(2,1)S(1)}, u32[]{:S(2)}, u32[]{:S(2)}) collective-permute-start(bf16[128,2048]{1,0:T(8,128)(2,1)S(1)} %get-tuple-element.796), channel_id=1, source_target_pairs={{0,4},{1,5},{2,6},{3,7},{4,0},{5,1},{6,2},{7,3},{8,12},{9,13},{10,... | collective-permute-start | bytes 1572872 | tf_op jit(solution)/shard_map/cond/branch_1_fun/ppermute | solution.py:42
  507.9 13.8 %collective-permute-start.33 = (bf16[256,2048]{1,0:T(8,128)(2,1)}, bf16[256,2048]{1,0:T(8,128)(2,1)S(1)}, u32[]{:S(2)}, u32[]{:S(2)}) collective-permute-start(bf16[256,2048]{1,0:T(8,128)(2,1)} %get-tuple-element.408), channel_id=1, source_target_pairs={{0,1},{1,0},{2,3},{3,2},{4,5},{5,4},{6,7},{7,6},{8,9},{9,8},{10,11... | collective-permute-start | bytes 3145736 | tf_op jit(solution)/shard_map/cond/branch_1_fun/ppermute | solution.py:42
  508.3 16.7 %collective-permute-start.32 = (bf16[256,2048]{1,0:T(8,128)(2,1)}, bf16[256,2048]{1,0:T(8,128)(2,1)S(1)}, u32[]{:S(2)}, u32[]{:S(2)}) collective-permute-start(bf16[256,2048]{1,0:T(8,128)(2,1)} %get-tuple-element.406), channel_id=1, source_target_pairs={{0,1},{1,0},{2,3},{3,2},{4,5},{5,4},{6,7},{7,6},{8,9},{9,8},{10,11... | collective-permute-start | bytes 3145736 | tf_op jit(solution)/shard_map/cond/branch_1_fun/ppermute | solution.py:42
  508.4 14.9 %collective-permute-start.37 = (bf16[256,2048]{1,0:T(8,128)(2,1)}, bf16[256,2048]{1,0:T(8,128)(2,1)S(1)}, u32[]{:S(2)}, u32[]{:S(2)}) collective-permute-start(bf16[256,2048]{1,0:T(8,128)(2,1)} %get-tuple-element.413), channel_id=1, source_target_pairs={{0,1},{1,0},{2,3},{3,2},{4,5},{5,4},{6,7},{7,6},{8,9},{9,8},{10,11... | collective-permute-start | bytes 3145736 | tf_op jit(solution)/shard_map/cond/branch_1_fun/ppermute | solution.py:42
  520.4 14.0 %collective-permute-start.35 = (bf16[128,2048]{1,0:T(8,128)(2,1)S(1)}, bf16[128,2048]{1,0:T(8,128)(2,1)S(1)}, u32[]{:S(2)}, u32[]{:S(2)}) collective-permute-start(bf16[128,2048]{1,0:T(8,128)(2,1)S(1)} %get-tuple-element.799), channel_id=1, source_target_pairs={{0,2},{1,3},{2,0},{3,1},{4,6},{5,7},{6,4},{7,5},{8,10},{9,11},{10,... | collective-permute-start | bytes 1572872 | tf_op jit(solution)/shard_map/cond/branch_1_fun/ppermute | solution.py:42
  521.0 13.7 %collective-permute-start.36 = (bf16[128,2048]{1,0:T(8,128)(2,1)S(1)}, bf16[128,2048]{1,0:T(8,128)(2,1)S(1)}, u32[]{:S(2)}, u32[]{:S(2)}) collective-permute-start(bf16[128,2048]{1,0:T(8,128)(2,1)S(1)} %get-tuple-element.798), channel_id=1, source_target_pairs={{0,4},{1,5},{2,6},{3,7},{4,0},{5,1},{6,2},{7,3},{8,12},{9,13},{10,... | collective-permute-start | bytes 1572872 | tf_op jit(solution)/shard_map/cond/branch_1_fun/ppermute | solution.py:42
  538.9 63.1 %all-to-all-start.3 = ((bf16[8,256,256]{2,1,0:T(8,128)(2,1)}), bf16[8,256,256]{2,1,0:T(8,128)(2,1)}, u32[]{:S(2)}, u32[]{:S(2)}) async-start(bf16[8,256,256]{2,1,0:T(8,128)(2,1)} %bitcast.212), calls=%async_computation.3 | async-start | bytes 2097152 | tf_op jit(solution)/shard_map/all_to_all | solution.py:978
  547.6 40.3 %collective-permute-start.16 = (bf16[256,2048]{1,0:T(8,128)(2,1)}, bf16[256,2048]{1,0:T(8,128)(2,1)}, u32[]{:S(2)}, u32[]{:S(2)}) collective-permute-start(bf16[256,2048]{1,0:T(8,128)(2,1)} %get-tuple-element.427), channel_id=1, source_target_pairs={{0,4},{1,5},{2,6},{3,7},{4,0},{5,1},{6,2},{7,3},{8,12},{9,13},{10,... | collective-permute-start | bytes 3145736 | tf_op jit(solution)/shard_map/cond/branch_1_fun/ppermute | solution.py:42
  549.3 38.6 %collective-permute-start.15 = (bf16[256,2048]{1,0:T(8,128)(2,1)}, bf16[256,2048]{1,0:T(8,128)(2,1)}, u32[]{:S(2)}, u32[]{:S(2)}) collective-permute-start(bf16[256,2048]{1,0:T(8,128)(2,1)} %get-tuple-element.426), channel_id=1, source_target_pairs={{0,2},{1,3},{2,0},{3,1},{4,6},{5,7},{6,4},{7,5},{8,10},{9,11},{10,... | collective-permute-start | bytes 3145736 | tf_op jit(solution)/shard_map/cond/branch_1_fun/ppermute | solution.py:42
  553.0 32.7 %collective-permute-start.13 = (bf16[2,256,256]{2,1,0:T(8,128)(2,1)S(1)}, bf16[2,256,256]{2,1,0:T(8,128)(2,1)S(1)}, u32[]{:S(2)}, u32[]{:S(2)}) collective-permute-start(bf16[2,256,256]{2,1,0:T(8,128)(2,1)S(1)} %fusion.16), channel_id=1, source_target_pairs={{0,2},{1,3},{2,0},{3,1},{4,6},{5,7},{6,4},{7,5},{8,10},{9,11},{10,... | collective-permute-start | bytes 786440 | tf_op jit(solution)/shard_map/cond/branch_1_fun/ppermute | solution.py:42
  605.6 63.1 %all-to-all-start.4 = ((bf16[8,704,256]{2,1,0:T(8,128)(2,1)}), bf16[8,704,256]{2,1,0:T(8,128)(2,1)S(1)}, u32[]{:S(2)}, u32[]{:S(2)}) async-start(bf16[8,704,256]{2,1,0:T(8,128)(2,1)} %bitcast.203), calls=%async_computation.4 | async-start | bytes 5767168 | tf_op jit(solution)/shard_map/all_to_all | solution.py:751
  609.3 95.2 %all-reduce.10.cloned.1.call-start = ((), (), s32[]{:S(2)}) async-start(), calls=%async_computation.7 | async-start | bytes 4472832 | tf_op jit(solution)/shard_map/psum | solution.py:996
  609.9 55.9 %collective-permute-start.9 = (bf16[256,2048]{1,0:T(8,128)(2,1)}, bf16[256,2048]{1,0:T(8,128)(2,1)S(1)}, u32[]{:S(2)}, u32[]{:S(2)}) collective-permute-start(bf16[256,2048]{1,0:T(8,128)(2,1)} %get-tuple-element.438), channel_id=1, source_target_pairs={{0,4},{1,5},{2,6},{3,7},{4,0},{5,1},{6,2},{7,3},{8,12},{9,13},{10,... | collective-permute-start | bytes 3145736 | tf_op jit(solution)/shard_map/cond/branch_1_fun/ppermute | solution.py:42
  611.9 54.0 %collective-permute-start.8 = (bf16[256,2048]{1,0:T(8,128)(2,1)}, bf16[256,2048]{1,0:T(8,128)(2,1)S(1)}, u32[]{:S(2)}, u32[]{:S(2)}) collective-permute-start(bf16[256,2048]{1,0:T(8,128)(2,1)} %get-tuple-element.437), channel_id=1, source_target_pairs={{0,2},{1,3},{2,0},{3,1},{4,6},{5,7},{6,4},{7,5},{8,10},{9,11},{10,... | collective-permute-start | bytes 3145736 | tf_op jit(solution)/shard_map/cond/branch_1_fun/ppermute | solution.py:42
  (75 other events, 647.4 us)
Sparse Core Ops, SparseCore 0:
  72.3 108.3 all-gather.2
  278.0 109.9 all-reduce.7
  392.8 203.6 all-reduce.11
  613.0 91.4 all-reduce.9

commit v4 on v3

--- a/solution.py
+++ b/solution.py
@@ -726,6 +726,33 @@
     )(*lefts, *pieces)
 
 
+def widen_kernel(query_ref, out_ref, small_ref, query_f, out_f, key_f, value_f, gains_f):
+    width, head = query_ref.shape[2], key_f.shape[1]
+    for j in range(query_ref.shape[0]):
+        query_f[:, j * width : (j + 1) * width] = query_ref[j].astype(F32)
+    out_f[...] = out_ref[...].astype(F32)
+    rows = key_f.shape[0]
+    key_f[...] = small_ref[:rows, :head].astype(F32)
+    value_f[...] = small_ref[:rows, head:].astype(F32)
+    gains_f[...] = small_ref[rows:, :].astype(F32)
+
+
+def widen(query_blocks, out_sum, small, head):
+    count, rows, width = query_blocks.shape
+    shapes = [(rows, count * width), out_sum.shape, (rows, head), (rows, head)]
+    shapes = [jax.ShapeDtypeStruct(shape, F32) for shape in (*shapes, (small.shape[0] - rows, 2 * head))]
+    given = [query_blocks, out_sum, small]
+    return pl.pallas_call(
+        widen_kernel,
+        grid=(1,),
+        in_specs=[whole_spec(a) for a in given],
+        out_specs=[whole_spec(a) for a in shapes],
+        out_shape=shapes,
+        compiler_params=pltpu.CompilerParams(vmem_limit_bytes=VMEM_BYTES),
+        cost_estimate=LIGHT,
+    )(*given)
+
+
 def turn_kernel(blocks_ref, out_ref):
     turned = [blocks_ref[j].astype(F32).T for j in range(blocks_ref.shape[0])]
     out_ref[...] = jnp.concatenate(turned, 1)
@@ -863,14 +890,17 @@
     last = gather_last(near, far, count)
     grad_out = cotangent.reshape(rows, width).astype(F32) * valid
     branch_near = gather_near(after(grad_out.astype(BF), far), count, stacks)
+    branch_far = gather_far(after(branch_near, stacks), count)
     *normed, queries, key_values = front_of(last_pair, [far, last], stacks)
     normed_one += normed
     attn, lse = attend_forward(queries, key_values, lengths, keys_of, head)
-    attn, branch_near = lax.optimization_barrier((attn, branch_near))
+    attn, branch_far = lax.optimization_barrier((attn, branch_far))
     proj_parts = parts_of([attn.reshape(count, rows, -1)], [w_out], (False,))
     inputs_f = inputs.astype(F32)
     scale_one = rms_scale(inputs_f)
 
+    branch_last = gather_last(branch_near, branch_far, count)
+    branch = (branch_near if is_cube(count) else branch_near[:-2]) + [branch_far, branch_last]
     grad_second, dkv_second = attend_second(
         after(second_queries, proj_parts), second_cotangent, key_values, lengths, keys_of, head
     )
@@ -885,7 +915,6 @@
         hidden_pair(two, branch[2 * pair : 2 * pair + 2], pair, shares, w_down, count, before)
     )
     normed_own = (middle * scale_two * gain_two).astype(BF)
-    branch = list(branch_near)
 
     def middle_pairs(near, stacks):
         for pair in range(1, last_pair):
@@ -897,12 +926,11 @@
         stacks = stage(always, lambda *two: hidden_of(0, two, []), normed_own, from_core)
         from_x, from_y, stacks = sync((from_x, from_y, stacks))
         near = [normed_own, from_core, from_x, swap(from_x, 1), from_y, swap(from_y, 1)]
-        halves, branch_halves = far_halves(near), far_halves(after(branch_near, stacks))
+        halves = far_halves(near)
         stacks = stage(always, middle_pairs, near, stacks)
-        halves, branch_halves, stacks = sync((halves, branch_halves, stacks))
-        far, branch_far = jnp.concatenate(halves, 0), jnp.concatenate(branch_halves, 0)
+        halves, stacks = sync((halves, stacks))
+        far = jnp.concatenate(halves, 0)
         last = swap(far, 1)
-        branch += [branch_far, swap(branch_far, 1)]
     else:
         near = gather_near(normed_own, count)
         stacks = middle_pairs(near, hidden_of(0, near[:2], []))
@@ -914,24 +942,24 @@
     (w_gate_share,) = inner_of([grad_gate], normed_two)
     gate_sum = lax.psum(w_gate_share, "dp")
 
-    def parts_mlp(stacks, grad_up):
-        (w_up_share,) = inner_of([grad_up], normed_two)
+    def parts_mlp(stacks):
         parts = [mlp_parts(stacks, pair, shares, w_down) for pair in range(last_pair + 1)]
         normed_parts = [part for step in parts for part in step[:2]]
-        return w_up_share, normed_parts, [part for step in parts for part in step[2:]]
-
-    w_up_share, normed_parts, out_parts = stage(always, parts_mlp, stacks, grad_up)
+        return normed_parts, [part for step in parts for part in step[2:]]
+
+    normed_parts, out_parts = stage(always, parts_mlp, stacks)
 
     def scatter_mlp(normed_parts, hidden):
         return scatter_far(normed_parts, count), inner_of([hidden], branch)[0]
 
     two_sums, w_down_share = stage(always, scatter_mlp, normed_parts, hidden)
-    def sum_mlp(two_sums):
-        grad_normed_two = scatter_near(two_sums, count).astype(F32)
+    def sum_mlp(two_sums, grad_up):
+        (w_up_share,) = inner_of([grad_up], normed_two)
+        grad_normed_two = scatter_near(two_sums, count, w_up_share).astype(F32)
         grad_middle = grad_out + norm_back(grad_normed_two, middle, scale_two, gain_two)
-        return grad_middle, jnp.sum(grad_normed_two * (middle * scale_two), 0)
-
-    grad_middle, gain_share = stage(always, sum_mlp, two_sums)
+        return grad_middle, jnp.sum(grad_normed_two * (middle * scale_two), 0), w_up_share
+
+    grad_middle, gain_share, w_up_share = stage(always, sum_mlp, two_sums, grad_up)
     grad_middle, w_up_share, w_down_share, gate_sum = sync(
         (grad_middle, w_up_share, w_down_share, gate_sum)
     )
@@ -964,23 +992,22 @@
         one_parts = parts_of(
             [grads[..., :split], grads[..., split:]], [query_cols, kv_mat], (True, True)
         )
-        return out_sums, one_parts, grads
-
-    out_sums, one_parts, grads = stage(always, attention_back, grad_attn, out_parts)
-    one_parts, grads, gate_blocks = sync((one_parts, grads, gate_blocks))
-
-    def scatter_attention(one_parts, grads):
         (w_one_share,) = outer_of(normed_one, [grads.reshape(all_rows, -1)])
-        return scatter_far(one_parts, count), w_one_share
-
-    one_sums, w_one_share = stage(always, scatter_attention, one_parts, grads)
+        return out_sums, one_parts, w_one_share
+
+    out_sums, one_parts, w_one_share = stage(always, attention_back, grad_attn, out_parts)
+    one_parts, w_one_share, gate_blocks = sync((one_parts, w_one_share, gate_blocks))
     w_query_share = w_one_share[:, :split].reshape(count, own_columns, split)
     w_query_share = lax.all_to_all(w_query_share, "seq", split_axis=0, concat_axis=0, tiled=True)
     own_gain = gain_attn.shape[0]
 
-    def sum_attention(one_sums, w_one_share):
+    def scatter_attention(one_parts, w_one_share):
         kv_shares = w_one_share[:, split:].reshape(count, own_columns, 2 * head)
-        w_kv_share = small_scatter(kv_shares, count)
+        return scatter_far(one_parts, count), small_scatter(kv_shares, count)
+
+    one_sums, w_kv_share = stage(always, scatter_attention, one_parts, w_one_share)
+
+    def sum_attention(one_sums, w_kv_share):
         grad_normed_one = scatter_near(one_sums, count).astype(F32)
         grad_tokens = grad_middle + norm_back(grad_normed_one, inputs_f, scale_one, gain_one)
         gain_shares = jnp.stack([jnp.sum(grad_normed_one * (inputs_f * scale_one), 0), gain_share])
@@ -989,36 +1016,36 @@
         small = jnp.concatenate([w_kv_share, small_scatter(gain_shares, count)], 0)
         return grad_tokens, small
 
-    grad_tokens, small = stage(always, sum_attention, one_sums, w_one_share)
+    grad_tokens, small = stage(always, sum_attention, one_sums, w_kv_share)
     small, w_query_share, w_out_share, up_sum, down_sum = sync(
         (small, w_query_share, w_out_share, up_sum, down_sum)
     )
     late = lax.psum((w_out_share, w_query_share.reshape(-1, split), small), "dp")
-    up_blocks = spread_rows(up_sum, count)
-
-    def sum_rest(out_sums, gate_blocks, down_sum):
+
+    def sum_rest(out_sums, gate_blocks, down_sum, up_sum):
+        up_blocks = spread_rows(up_sum, count)
         out = (middle + scatter_near(out_sums, count).astype(F32)).astype(BF)
-        return out, turn_blocks(gate_blocks), down_sum.astype(F32)
-
-    out, grad_w_gate, grad_w_down = stage(always, sum_rest, out_sums, gate_blocks, down_sum)
-    out, up_blocks = sync((out, up_blocks))
-    grad_w_up = turn_blocks(up_blocks)
+        return out, turn_blocks(gate_blocks), turn_blocks(up_blocks), down_sum.astype(F32)
+
+    out, grad_w_gate, grad_w_up, grad_w_down = stage(
+        always, sum_rest, out_sums, gate_blocks, down_sum, up_sum
+    )
     late, grad_w_up = sync((late, grad_w_up))
-    w_out_sum, grad_w_query, small = [each.astype(F32) for each in late]
-    grad_w_query = grad_w_query.reshape(count, own_columns, split).transpose(1, 0, 2)
-    grad_w_query = grad_w_query.reshape(own_columns, -1)
-    grad_w_kv, grad_gains = small[:own_columns], small[own_columns : own_columns + 2, :own_gain]
+    w_out_sum, w_query_sum, small = late
+    grad_w_query, w_out_sum, grad_w_key, grad_w_value, grad_gains = widen(
+        w_query_sum.reshape(count, own_columns, split), w_out_sum, small, head
+    )
 
     return (
         out.reshape(tokens.shape),
         grad_tokens.reshape(tokens.shape),
         grad_second,
-        grad_gains[0],
+        grad_gains[0, :own_gain],
         grad_w_query,
-        grad_w_kv[:, :head],
-        grad_w_kv[:, head:],
+        grad_w_key,
+        grad_w_value,
         w_out_sum.astype(F32),
-        grad_gains[1],
+        grad_gains[1, :own_gain],
         grad_w_gate,
         grad_w_up,
         grad_w_down,

time: 732 us -> 714 us (0.975)
  local copies, waits for them, and re-layouts: 60 us -> 47.6 us
  other arithmetic: 77.8 us -> 69.6 us
    psum x1, waiting for transfers between devices: 0.01 us -> 9.27 us  [body(): gate_sum = lax.psum(w_gate_share, 'dp')]
    psum x1, waiting for transfers between devices: 32 us -> 24 us  [body(): lax.psum((w_out_share, w_query_share.reshape(-1, split), small), 'dp')]
    unnamed x72 -> x60, local copies, waits for them, and re-layouts: 20.1 us -> 13.5 us
  transfers between devices with their start and end apart: 82 -> 82, of which waited for: 34 -> 41; matrix products, arithmetic and copies ran while one was open for 14% -> 14% of each run, Pallas kernels for 27% -> 28%
where the time goes in v4:
time: 714 us; the launch traced here: 703 us
  waiting for transfers between devices  269 us (38%)
  Pallas kernels  220 us (31%)
  starting transfers between devices  78.9 us (11%)
  other arithmetic  69.6 us (10%)
  local copies, waits for them, and re-layouts  47.6 us (7%)
  between operations  15.3 us (2%)
    ppermute x73, waiting for transfers between devices, swap(): return lax.ppermute(array, 'seq', [(i, i ^ bit) for i in range(8)])  224 us
    ppermute x73, starting transfers between devices, swap(): return lax.ppermute(array, 'seq', [(i, i ^ bit) for i in range(8)])  57.4 us
    pallas_call x4, Pallas kernels, hidden_pair(): pl.pallas_call(functools.partial(hidden_kernel, first=2 * pair), in_specs...  42.2 us
    pallas_call x4, Pallas kernels, mlp_parts(): pl.pallas_call(functools.partial(mlp_parts_kernel, first=2 * pair), in_sp...  38.8 us
    pallas_call x3, Pallas kernels, inner_of(): pl.pallas_call(functools.partial(inner_kernel, count=count, lefts=len(lef...  36.6 us
    psum x1, waiting for transfers between devices, body(): lax.psum((w_out_share, w_query_share.reshape(-1, split), small), 'dp')  24 us
    convert_element_type x27, other arithmetic, add_rounded(): return total.astype(BF)  22.7 us
    pallas_call x1, Pallas kernels, attend_second(): pl.pallas_call(second_kernel, grid_spec=pltpu.PrefetchScalarGridSpec(num_...  19.9 us
  transfers between devices with their start and end apart: 82, of which 41 were waited for; matrix products, arithmetic and copies ran while one was open for 14% of the time, Pallas kernels for 28%

profile of v4, /device:TPU:0, one launch (start us, length us, event | category | flops | bytes accessed | tf_op | source)
XLA Modules:
  0.0 703.3 jit_solution(90751574592334041)
XLA Ops:
  19.5 4.4 all-to-all-start.1
  24.0 18.9 %collective-permute-done.43 = bf16[272,256]{1,0:T(8,128)(2,1)S(1)} collective-permute-done((bf16[272,256]{1,0:T(8,128)(2,1)S(1)}, bf16[272,256]{1,0:T(8,128)(2,1)S(1)}, u32[]{:S(2)}, u32[]{:S(2)}) %collective-permute-start.43) | collective-permute-done | bytes 139296 | tf_op jit(solution)/shard_map/ppermute | solution.py:42
  46.1 3.2 convert_multiply_fusion.4
  49.3 5.8 collective-permute-done.44
  65.6 4.2 all-to-all-start.2
  86.2 5.1 shard_map.230
  91.3 4.7 shard_map.231
  96.0 4.5 shard_map.232
  100.5 6.4 collective-permute-done.50
  116.0 4.5 shard_map.233
  120.5 9.6 %shard_map.234 = (bf16[8,2,128,256]{3,2,1,0:T(8,128)(2,1)S(1)}, f32[2,2,1024]{2,1,0:T(2,128)S(1)}) custom-call(s32[2]{0:T(128)S(1)} %copy-done.52, s32[2]{0:T(128)S(1)} %pad_add_fusion.key_ref, bf16[8,2,128,256]{3,2,1,0:T(8,128)(2,1)S(1)} %get-tuple-element.619.q_ref, bf16[8,2,128,256]{3,2,1,0:T(8,128)(2,1)S(1)} %get-tuple-element.620.kv_ref), custom_call_target="tpu_custom_call" | custom-call | flops 1000 | bytes 1000 | tf_op jit(solution)/shard_map/pallas_call | solution.py:216
  131.2 4.2 shard_map.235
  142.7 11.5 %collective-permute-done.59 = bf16[128,2048]{1,0:T(8,128)(2,1)S(1)} collective-permute-done((bf16[128,2048]{1,0:T(8,128)(2,1)S(1)}, bf16[128,2048]{1,0:T(8,128)(2,1)S(1)}, u32[]{:S(2)}, u32[]{:S(2)}) %collective-permute-start.59) | collective-permute-done | bytes 524320 | tf_op jit(solution)/shard_map/ppermute | solution.py:42
  157.9 19.9 %shard_map.236 = (bf16[2,128,2048]{2,1,0:T(8,128)(2,1)}, f32[8,2,128,256]{3,2,1,0:T(8,128)}) custom-call(s32[2]{0:T(128)S(1)} %copy-done.52, s32[2]{0:T(128)S(1)} %pad_add_fusion.key_ref, bf16[2,128,2048]{2,1,0:T(8,128)(2,1)S(1)} %copy-done.4, bf16[2,128,2048]{2,1,0:T(8,128)(2,1)S(1)} %copy-done.5, bf16[8,2,128,256]{3,2,1,0:T(8,128)(2,1)S(1)} %get-tuple-element.620.kv_ref), custom_call_target="tpu_custom_call" | custom-call | flops 1000 | bytes 1000 | tf_op jit(solution)/shard_map/pallas_call | solution.py:292
  181.0 9.4 %all-gather.3.cloned.1.call-done = bf16[32,64,1408]{2,1,0:T(8,128)(2,1)} async-done(((bf16[8,64,1408]{2,1,0:T(8,128)(2,1)}), bf16[32,64,1408]{2,1,0:T(8,128)(2,1)}) %all-gather.3.cloned.1.call-update) | async-done | bytes 5767184 | tf_op jit(solution)/shard_map/all_gather | solution.py:814
  196.9 10.9 %conditional.11 = ((bf16[8,256,704]{2,1,0:T(8,128)(2,1)}, bf16[8,256,704]{2,1,0:T(8,128)(2,1)}, bf16[8,256,704]{2,1,0:T(8,128)(2,1)})) conditional(s32[]{:T(128)} %bitcast.54, () %tuple.139, (bf16[256,2048]{1,0:T(8,128)(2,1)S(1)}, bf16[256,2048]{1,0:T(8,128)(2,1)}, bf16[256,2048]{1,0:T(8,128)(2,1)}, bf16[256,2048]{1,0:T(8,128)(2,1)}, ...), branch_computations={%region_1.2_spmd, %region_2.3_spmd} | conditional | flops 7381975040 | bytes 14942216 | solution.py:142
  196.9 10.7 %branch_1_fun.18 = (bf16[8,256,704]{2,1,0:T(8,128)(2,1)}, bf16[8,256,704]{2,1,0:T(8,128)(2,1)}, bf16[8,256,704]{2,1,0:T(8,128)(2,1)}) custom-call(bf16[256,2048]{1,0:T(8,128)(2,1)S(1)} %get-tuple-element.279.na_hbm, bf16[256,2048]{1,0:T(8,128)(2,1)} %get-tuple-element.280.nb_hbm, bf16[256,2048]{1,0:T(8,128)(2,1)} %get-tuple-element.281.ga_hbm, ...), custom_call_target="tpu_custom_call" | custom-call | flops 7381975040 | bytes 14942208 | tf_op jit(solution)/shard_map/cond/branch_1_fun/pallas_call | solution.py:523
  207.8 11.7 %collective-permute-done.64.refs_3_ = bf16[256,2048]{1,0:T(8,128)(2,1)} collective-permute-done((bf16[256,2048]{1,0:T(8,128)(2,1)S(1)}, bf16[256,2048]{1,0:T(8,128)(2,1)}, u32[]{:S(2)}, u32[]{:S(2)}) %collective-permute-start.64) | collective-permute-done | bytes 1048608 | tf_op jit(solution)/shard_map/ppermute | solution.py:42
  227.0 21.3 %conditional.12 = ((bf16[8,256,704]{2,1,0:T(8,128)(2,1)}, bf16[8,256,704]{2,1,0:T(8,128)(2,1)}, bf16[8,256,704]{2,1,0:T(8,128)(2,1)})) conditional(s32[]{:T(128)} %bitcast.54, () %tuple.142, (bf16[256,2048]{1,0:T(8,128)(2,1)}, bf16[256,2048]{1,0:T(8,128)(2,1)}, bf16[256,2048]{1,0:T(8,128)(2,1)}, bf16[256,2048]{1,0:T(8,128)(2,1)}, ...), branch_computations={%region_3.4_spmd, %region_4.5_spmd} | conditional | flops 14763950080 | bytes 68681816 | solution.py:142
  227.1 11.1 %branch_1_fun.19 = (bf16[8,256,704]{2,1,0:T(8,128)(2,1)}, bf16[8,256,704]{2,1,0:T(8,128)(2,1)}, bf16[8,256,704]{2,1,0:T(8,128)(2,1)}) custom-call(bf16[256,2048]{1,0:T(8,128)(2,1)} %get-tuple-element.291.na_hbm, bf16[256,2048]{1,0:T(8,128)(2,1)} %get-tuple-element.292.nb_hbm, ...), custom_call_target="tpu_custom_call", output_to_operand_aliasing={{0}: (6, {}), {1}: (7, {}), {2}: (8, {})} | custom-call | flops 7381975040 | bytes 14942208 | tf_op jit(solution)/shard_map/cond/branch_1_fun/pallas_call | solution.py:523
  238.2 9.7 %branch_1_fun.20 = (bf16[8,256,704]{2,1,0:T(8,128)(2,1)}, bf16[8,256,704]{2,1,0:T(8,128)(2,1)}, bf16[8,256,704]{2,1,0:T(8,128)(2,1)}) custom-call(bf16[256,2048]{1,0:T(8,128)(2,1)} %get-tuple-element.285.na_hbm, bf16[256,2048]{1,0:T(8,128)(2,1)} %get-tuple-element.286.nb_hbm, ...), custom_call_target="tpu_custom_call", output_to_operand_aliasing={{0}: (6, {}), {1}: (7, {}), {2}: (8, {})} | custom-call | flops 7381975040 | bytes 14942208 | tf_op jit(solution)/shard_map/cond/branch_1_fun/pallas_call | solution.py:523
  253.4 10.8 %shard_map.237 = (bf16[8,256,704]{2,1,0:T(8,128)(2,1)}, bf16[8,256,704]{2,1,0:T(8,128)(2,1)}, bf16[8,256,704]{2,1,0:T(8,128)(2,1)}) custom-call(bf16[256,2048]{1,0:T(8,128)(2,1)S(1)} %constant_dynamic-update-slice_fusion.4.na_hbm.refs_7_, ...), custom_call_target="tpu_custom_call", output_to_operand_aliasing={{0}: (6, {}), {1}: (7, {}), {2}: (8, {})} | custom-call | flops 7381975040 | bytes 14942208 | tf_op jit(solution)/shard_map/pallas_call | solution.py:523
  264.2 11.6 %shard_map.238 = bf16[704,2048]{1,0:T(8,128)(2,1)S(1)} custom-call(bf16[2048,704]{1,0:T(8,128)(2,1)} %bitcast.203, bf16[256,2048]{1,0:T(8,128)(2,1)S(1)} %multiply_convert_fusion.refs_1_, bf16[256,2048]{1,0:T(8,128)(2,1)} %collective-permute-done.66.refs_2_, bf16[256,2048]{1,0:T(8,128)(2,1)} %collective-permute-done.64.refs_3_, ...), custom_call_target="tpu_custom_call" | custom-call | flops 1000 | bytes 1000 | tf_op jit(solution)/shard_map/pallas_call | solution.py:716
  277.4 39.1 %conditional.13 = (bf16[256,2048]{1,0:T(8,128)(2,1)S(1)}, bf16[256,2048]{1,0:T(8,128)(2,1)}, bf16[256,2048]{1,0:T(8,128)(2,1)S(1)}, bf16[256,2048]{1,0:T(8,128)(...) conditional(s32[]{:T(128)} %bitcast.54, () %tuple.127, ...), branch_computations={%region_5.6_spmd, %region_6.7_spmd} | conditional | flops 29527900160 | bytes 94372048 | solution.py:142
  277.5 10.7 %branch_1_fun.21 = (bf16[256,2048]{1,0:T(8,128)(2,1)S(1)}, bf16[256,2048]{1,0:T(8,128)(2,1)}, bf16[256,2048]{1,0:T(8,128)(2,1)}, bf16[256,2048]{1,0:T(8,128)(2,1)}) custom-call(bf16[8,256,704]{2,1,0:T(8,128)(2,1)} %get-tuple-element.301.hidden_hbm, bf16[8,256,704]{2,1,0:T(8,128)(2,1)} %get-tuple-element.302.dgate_hbm, ...), custom_call_target="tpu_custom_call" | custom-call | flops 7381975040 | bytes 14942208 | tf_op jit(solution)/shard_map/cond/branch_1_fun/pallas_call | solution.py:581
  288.2 9.5 %branch_1_fun.22 = (bf16[256,2048]{1,0:T(8,128)(2,1)S(1)}, bf16[256,2048]{1,0:T(8,128)(2,1)}, bf16[256,2048]{1,0:T(8,128)(2,1)}, bf16[256,2048]{1,0:T(8,128)(2,1)}) custom-call(bf16[8,256,704]{2,1,0:T(8,128)(2,1)S(1)} %copy-done.22, bf16[8,256,704]{2,1,0:T(8,128)(2,1)S(1)} %copy-done.23, bf16[8,256,704]{2,1,0:T(8,128)(2,1)S(1)} %copy-done.24, ...), custom_call_target="tpu_custom_call" | custom-call | flops 7381975040 | bytes 14942208 | tf_op jit(solution)/shard_map/cond/branch_1_fun/pallas_call | solution.py:581
  297.7 9.4 %branch_1_fun.23 = (bf16[256,2048]{1,0:T(8,128)(2,1)S(1)}, bf16[256,2048]{1,0:T(8,128)(2,1)}, bf16[256,2048]{1,0:T(8,128)(2,1)}, bf16[256,2048]{1,0:T(8,128)(2,1)}) custom-call(bf16[8,256,704]{2,1,0:T(8,128)(2,1)S(1)} %copy-done.22, bf16[8,256,704]{2,1,0:T(8,128)(2,1)S(1)} %copy-done.23, bf16[8,256,704]{2,1,0:T(8,128)(2,1)S(1)} %copy-done.24, ...), custom_call_target="tpu_custom_call" | custom-call | flops 7381975040 | bytes 14942208 | tf_op jit(solution)/shard_map/cond/branch_1_fun/pallas_call | solution.py:581
  307.2 9.2 %branch_1_fun.24 = (bf16[256,2048]{1,0:T(8,128)(2,1)}, bf16[256,2048]{1,0:T(8,128)(2,1)}, bf16[256,2048]{1,0:T(8,128)(2,1)}, bf16[256,2048]{1,0:T(8,128)(2,1)}) custom-call(bf16[8,256,704]{2,1,0:T(8,128)(2,1)S(1)} %copy-done.22, bf16[8,256,704]{2,1,0:T(8,128)(2,1)S(1)} %copy-done.23, bf16[8,256,704]{2,1,0:T(8,128)(2,1)S(1)} %copy-done.24, ...), custom_call_target="tpu_custom_call" | custom-call | flops 7381975040 | bytes 14942208 | tf_op jit(solution)/shard_map/cond/branch_1_fun/pallas_call | solution.py:581
  316.6 31.9 %conditional.14 = (bf16[256,2048]{1,0:T(8,128)(2,1)S(1)}, bf16[256,2048]{1,0:T(8,128)(2,1)S(1)}, bf16[256,2048]{1,0:T(8,128)(2,1)S(1)}, bf16[704,2048]{1,0:T(8,128)(2,1)S(1)}) conditional(s32[]{:T(128)} %bitcast.54, () %tuple.149, (bf16[256,2048]{1,0:T(8,128)(2,1)S(1)}, bf16[256,2048]{1,0:T(8,128)(2,1)}, bf16[256,2048]{1,0:T(8,128)(2,1)S(1)}, ...), branch_computations={%region_7.8_spmd, %region_8.9_spmd} | conditional | flops 14681064 | bytes 49808684 | solution.py:142
  317.7 12.1 %branch_1_fun.25 = bf16[704,2048]{1,0:T(8,128)(2,1)S(1)} custom-call(bf16[2048,704]{1,0:T(8,128)(2,1)} %bitcast.202, bf16[256,2048]{1,0:T(8,128)(2,1)} %get-tuple-element.333.refs_1_, bf16[256,2048]{1,0:T(8,128)(2,1)} %get-tuple-element.334.refs_2_, bf16[256,2048]{1,0:T(8,128)(2,1)} %get-tuple-element.335.refs_3_, ...), custom_call_target="tpu_custom_call" | custom-call | flops 1000 | bytes 1000 | tf_op jit(solution)/shard_map/cond/branch_1_fun/pallas_call | solution.py:716
  334.3 11.6 %collective-permute-done.20 = bf16[128,2048]{1,0:T(8,128)(2,1)S(1)} collective-permute-done((bf16[128,2048]{1,0:T(8,128)(2,1)S(1)}, bf16[128,2048]{1,0:T(8,128)(2,1)S(1)}, u32[]{:S(2)}, u32[]{:S(2)}) %collective-permute-start.20) | collective-permute-done | bytes 524320 | tf_op jit(solution)/shard_map/cond/branch_1_fun/ppermute | solution.py:42
  350.0 28.3 %conditional.15 = (f32[256,2048]{1,0:T(8,128)}, bf16[2048]{0:T(1024)(128)(2,1)S(1)}, bf16[704,2048]{1,0:T(8,128)(2,1)}) conditional(s32[]{:T(128)} %bitcast.54, () %tuple.148, (f32[256]{0:T(256)S(1)}, f32[256,1]{0,1:T(1,128)S(1)}, f32[256,1]{0,1:T(1,128)S(1)}, bf16[8,256,704]{2,1,0:T(8,128)(2,1)}, bf16[256,2048]{1,0:T(8,128)(2,1)S(1)}, ...), branch_computations={%region_9.10_spmd, %region_10.13_spmd} | conditional | flops 10487784 | bytes 38843528 | solution.py:142
  351.0 12.9 %branch_1_fun.26 = bf16[704,2048]{1,0:T(8,128)(2,1)} custom-call(bf16[2048,704]{1,0:T(8,128)(2,1)} %bitcast.204, bf16[256,2048]{1,0:T(8,128)(2,1)S(1)} %get-tuple-element.347.refs_1_, bf16[256,2048]{1,0:T(8,128)(2,1)} %get-tuple-element.348.refs_2_, bf16[256,2048]{1,0:T(8,128)(2,1)} %get-tuple-element.349.refs_3_, ...), custom_call_target="tpu_custom_call" | custom-call | flops 1000 | bytes 1000 | tf_op jit(solution)/shard_map/cond/branch_1_fun/pallas_call | solution.py:716
  363.9 10.8 %collective-permute-done.11 = bf16[256,2048]{1,0:T(8,128)(2,1)S(1)} collective-permute-done((bf16[256,2048]{1,0:T(8,128)(2,1)S(1)}, bf16[256,2048]{1,0:T(8,128)(2,1)S(1)}, u32[]{:S(2)}, u32[]{:S(2)}) %collective-permute-start.11) | collective-permute-done | bytes 1048608 | tf_op jit(solution)/shard_map/cond/branch_1_fun/ppermute | solution.py:42
  378.3 9.3 %all-reduce.8.cloned.1.call-done = bf16[704,2048]{1,0:T(8,128)(2,1)} async-done(((bf16[704,2048]{1,0:T(8,128)(2,1)}), bf16[704,2048]{1,0:T(8,128)(2,1)}) %all-reduce.8.cloned.1.call-update) | async-done | bytes 2883600 | tf_op jit(solution)/shard_map/psum | solution.py:943
  387.6 32.6 %conditional.16 = (bf16[256,2048]{1,0:T(8,128)(2,1)}, bf16[256,2048]{1,0:T(8,128)(2,1)}, bf16[256,2048]{1,0:T(8,128)(2,1)}, bf16[256,2048]{1,0:T(8,128)(2,1)}, b...) conditional(s32[]{:T(128)} %bitcast.54, () %tuple.147, (f32[256,2048]{1,0:T(8,128)}, ...), branch_computations={%region_14.15_spmd, %region_15.16_spmd} | conditional | flops 525288 | bytes 28312828 | solution.py:142
  392.5 22.0 %collective-permute-done = bf16[256,2048]{1,0:T(8,128)(2,1)} collective-permute-done((bf16[256,2048]{1,0:T(8,128)(2,1)S(1)}, bf16[256,2048]{1,0:T(8,128)(2,1)}, u32[]{:S(2)}, u32[]{:S(2)}) %collective-permute-start) | collective-permute-done | bytes 1048608 | tf_op jit(solution)/shard_map/cond/branch_1_fun/ppermute | solution.py:42
  420.2 27.7 %conditional.17 = ((bf16[8,2,128,256]{3,2,1,0:T(8,128)(2,1)S(1)}, bf16[256,2048]{1,0:T(8,128)(2,1)})) conditional(s32[]{:T(128)} %bitcast.54, () %tuple.146, (bf16[256,2048]{1,0:T(8,128)(2,1)}, bf16[256,2048]{1,0:T(8,128)(2,1)}, bf16[256,2048]{1,0:T(8,128)(2,1)}, bf16[256,2048]{1,0:T(8,128)(2,1)}, bf16[8,2,128,256]{3,2,1,0:T(8,128)(2,1)S(1)}, ...), branch_computations={%region_16.17_spmd, %region_17.18_spmd} | conditional | flops 3000 | bytes 16780372 | solution.py:142
  424.8 10.8 %collective-permute-done.5 = bf16[128,2048]{1,0:T(8,128)(2,1)S(1)} collective-permute-done((bf16[128,2048]{1,0:T(8,128)(2,1)S(1)}, bf16[128,2048]{1,0:T(8,128)(2,1)S(1)}, u32[]{:S(2)}, u32[]{:S(2)}) %collective-permute-start.5) | collective-permute-done | bytes 524320 | tf_op jit(solution)/shard_map/cond/branch_1_fun/ppermute | solution.py:42
  438.1 3.4 branch_1_fun.28
  441.6 3.5 branch_1_fun.29
  447.9 4.0 copy.126
  451.9 4.6 all-to-all-start.3
  456.5 49.3 %conditional.18 = (bf16[256,2048]{1,0:T(8,128)(2,1)}, bf16[256,2048]{1,0:T(8,128)(2,1)}, bf16[256,2048]{1,0:T(8,128)(2,1)}, bf16[256,2048]{1,0:T(8,128)(2,1)}, b...) conditional(s32[]{:T(128)} %bitcast.54, () %tuple.126, ...), branch_computations={%region_18.19_spmd, %region_19.20_spmd} | conditional | flops 14683064 | bytes 91754064 | solution.py:142
  458.0 11.7 %branch_1_fun.31 = bf16[8,2,128,512]{3,2,1,0:T(8,128)(2,1)S(1)} custom-call(s32[2]{0:T(128)S(1)} %get-tuple-element.391.lengths_ref, s32[2]{0:T(128)S(1)} %get-tuple-element.392.key_ref, bf16[8,2,128,256]{3,2,1,0:T(8,128)(2,1)} %get-tuple-element.393.q_ref, bf16[8,2,128,256]{3,2,1,0:T(8,128)(2,1)} %get-tuple-element.394.up_ref, ...), custom_call_target="tpu_custom_call" | custom-call | flops 1000 | bytes 1000 | tf_op jit(solution)/shard_map/cond/branch_1_fun/pallas_call | solution.py:388
  471.0 7.0 branch_1_fun.32
  478.1 7.9 %branch_1_fun.33 = bf16[2048,512]{1,0:T(8,128)(2,1)} custom-call(bf16[256,2048]{1,0:T(8,128)(2,1)S(1)} %copy-done.35, bf16[256,2048]{1,0:T(8,128)(2,1)S(1)} %copy-done.36, bf16[256,2048]{1,0:T(8,128)(2,1)S(1)} %copy-done.37, bf16[256,2048]{1,0:T(8,128)(2,1)S(1)} %copy-done.38, bf16[256,2048]{1,0:T(8,128)(2,1)S(1)} %copy-done.39, ...), custom_call_target="tpu_custom_call" | custom-call | flops 1000 | bytes 1000 | tf_op jit(solution)/shard_map/cond/branch_1_fun/pallas_call | solution.py:682
  497.4 4.7 collective-permute-done.26
  508.1 4.4 all-to-all-start.4
  514.5 42.2 %conditional.19 = (bf16[256,2048]{1,0:T(8,128)(2,1)}, bf16[256,2048]{1,0:T(8,128)(2,1)}, bf16[256,2048]{1,0:T(8,128)(2,1)}, bf16[256,256]{1,0:T(8,128)(2,1)S(1)}) conditional(s32[]{:T(128)} %bitcast.54, () %tuple.159, (bf16[256,2048]{1,0:T(8,128)(2,1)}, bf16[256,2048]{1,0:T(8,128)(2,1)}, bf16[256,2048]{1,0:T(8,128)(2,1)}, ...), branch_computations={%region_20.21_spmd, %region_21.22_spmd} | conditional | flops 17432584 | bytes 64094760 | solution.py:142
  523.6 8.9 %collective-permute-done.36 = bf16[2,256,256]{2,1,0:T(8,128)(2,1)S(1)} collective-permute-done((bf16[2,256,256]{2,1,0:T(8,128)(2,1)}, bf16[2,256,256]{2,1,0:T(8,128)(2,1)S(1)}, u32[]{:S(2)}, u32[]{:S(2)}) %collective-permute-start.36) | collective-permute-done | bytes 262176 | tf_op jit(solution)/shard_map/cond/branch_1_fun/ppermute | solution.py:42
  535.7 3.2 collective-permute-done.37
  549.2 4.4 collective-permute-done.32
  556.7 37.0 %conditional.20 = (bf16[272,256]{1,0:T(8,128)(2,1)S(1)}, f32[2,128,2048]{2,1,0:T(8,128)}) conditional(s32[]{:T(128)} %bitcast.54, () %tuple.158, (bf16[256,2048]{1,0:T(8,128)(2,1)}, bf16[256,2048]{1,0:T(8,128)(2,1)}, bf16[256,2048]{1,0:T(8,128)(2,1)}, f32[2,128,2048]{2,1,0:T(8,128)}, f32[256,1]{0,1:T(1,128)S(1)}, ...), branch_computations={%region_22.23_spmd, %region_23.0_spmd} | conditional | flops 11987720 | bytes 29377868 | solution.py:142
  561.2 18.9 %collective-permute-done.13 = bf16[256,2048]{1,0:T(8,128)(2,1)S(1)} collective-permute-done((bf16[256,2048]{1,0:T(8,128)(2,1)}, bf16[256,2048]{1,0:T(8,128)(2,1)S(1)}, u32[]{:S(2)}, u32[]{:S(2)}) %collective-permute-start.13) | collective-permute-done | bytes 1048608 | tf_op jit(solution)/shard_map/cond/branch_1_fun/ppermute | solution.py:42
  590.2 3.5 fusion.18
  595.9 70.5 %conditional.21 = (f32[256,5632]{1,0:T(8,128)}, f32[256,5632]{1,0:T(8,128)}, f32[704,2048]{1,0:T(8,128)}, bf16[2,128,2048]{2,1,0:T(8,128)(2,1)}) conditional(s32[]{:T(128)} %bitcast.54, () %tuple.125, (bf16[8,704,256]{2,1,0:T(8,128)(2,1)}, bf16[704,2048]{1,0:T(8,128)(2,1)}, bf16[704,2048]{1,0:T(8,128)(2,1)}, bf16[256,2048]{1,0:T(8,128)(2,1)}, ...), branch_computations={%region_29.30_spmd, %region_30.31_spmd} | conditional | flops 6162384 | bytes 57673880 | solution.py:142
  595.9 3.6 copy.125
  599.5 3.7 all-to-all-start
  606.6 4.7 branch_1_fun.34
  611.4 3.3 convert_element_type.420
  614.7 45.1 %collective-permute-done.9 = bf16[256,2048]{1,0:T(8,128)(2,1)S(1)} collective-permute-done((bf16[256,2048]{1,0:T(8,128)(2,1)}, bf16[256,2048]{1,0:T(8,128)(2,1)S(1)}, u32[]{:S(2)}, u32[]{:S(2)}) %collective-permute-start.9) | collective-permute-done | bytes 1048608 | tf_op jit(solution)/shard_map/cond/branch_1_fun/ppermute | solution.py:42
  662.7 3.7 branch_1_fun.35
  666.4 24.0 %all-reduce.10.cloned.1.call-done = (bf16[256,2048]{1,0:T(8,128)(2,1)}, bf16[2048,256]{1,0:T(8,128)(2,1)}, bf16[272,256]{1,0:T(8,128)(2,1)}) async-done(((bf16[256,2048]{1,0:T(8,128)(2,1)}, bf16[2048,256]{1,0:T(8,128)(2,1)}, bf16[272,256]{1,0:T(8,128)(2,1)}), (bf16[256,2048]{1,0:T(8,128)(2,1)}, bf16[2048,256]{1,0:T(8,128)(2,1)}, bf16[272,256]{1,0:T(8,128)(2,1)})) %all-reduce.10.cloned.1.call-update) | async-done | bytes 2236432 | tf_op jit(solution)/shard_map/psum | solution.py:1023
  (385 shorter events, 197.2 us)
Async XLA Ops:
  7.2 47.9 %collective-permute-start.38 = (bf16[256,2048]{1,0:T(8,128)(2,1)}, bf16[256,2048]{1,0:T(8,128)(2,1)S(1)}, u32[]{:S(2)}, u32[]{:S(2)}) collective-permute-start(bf16[256,2048]{1,0:T(8,128)(2,1)} %bitcast.191), channel_id=1, source_target_pairs={{0,2},{1,3},{2,0},{3,1},{4,6},{5,7},{6,4},{7,5},{8,10},{9,11},{10,... | collective-permute-start | bytes 3145736 | tf_op jit(solution)/shard_map/ppermute | solution.py:42
  10.2 44.9 %collective-permute-start.39 = (bf16[256,2048]{1,0:T(8,128)(2,1)}, bf16[256,2048]{1,0:T(8,128)(2,1)S(1)}, u32[]{:S(2)}, u32[]{:S(2)}) collective-permute-start(bf16[256,2048]{1,0:T(8,128)(2,1)} %bitcast.192), channel_id=1, source_target_pairs={{0,4},{1,5},{2,6},{3,7},{4,0},{5,1},{6,2},{7,3},{8,12},{9,13},{10,... | collective-permute-start | bytes 3145736 | tf_op jit(solution)/shard_map/ppermute | solution.py:42
  11.7 74.1 %collective-permute-start.48 = (bf16[256,2048]{1,0:T(8,128)(2,1)}, bf16[256,2048]{1,0:T(8,128)(2,1)}, u32[]{:S(2)}, u32[]{:S(2)}) collective-permute-start(bf16[256,2048]{1,0:T(8,128)(2,1)} %bitcast.193), channel_id=1, source_target_pairs={{0,1},{1,0},{2,3},{3,2},{4,5},{5,4},{6,7},{7,6},{8,9},{9,8},{10,11... | collective-permute-start | bytes 3145736 | tf_op jit(solution)/shard_map/ppermute | solution.py:42
  13.9 29.0 %collective-permute-start.43 = (bf16[272,256]{1,0:T(8,128)(2,1)S(1)}, bf16[272,256]{1,0:T(8,128)(2,1)S(1)}, u32[]{:S(2)}, u32[]{:S(2)}) collective-permute-start(bf16[272,256]{1,0:T(8,128)(2,1)S(1)} %pad_maximum_fusion.14), channel_id=1, source_target_pairs={{0,4},{1,5},{2,6},{3,7},{4,0},{5,1},{6,2},{7,3},{8,12},{9,13},{10,... | collective-permute-start | bytes 417800 | tf_op jit(solution)/shard_map/ppermute | solution.py:42
  19.5 41.9 %all-to-all-start.1 = ((bf16[8,64,1408]{2,1,0:T(8,128)(2,1)}), bf16[8,64,1408]{2,1,0:T(8,128)(2,1)}, u32[]{:S(2)}, u32[]{:S(2)}) async-start(bf16[8,64,1408]{2,1,0:T(8,128)(2,1)} %shard_map.229), calls=%async_computation.1 | async-start | bytes 2883584 | tf_op jit(solution)/shard_map/all_to_all | solution.py:812
  43.1 12.0 %collective-permute-start.44 = (bf16[2,272,256]{2,1,0:T(8,128)(2,1)S(1)}, bf16[2,272,256]{2,1,0:T(8,128)(2,1)S(1)}, u32[]{:S(2)}, u32[]{:S(2)}) collective-permute-start(bf16[2,272,256]{2,1,0:T(8,128)(2,1)S(1)} %pad_maximum_fusion.13), channel_id=1, source_target_pairs={{0,2},{1,3},{2,0},{3,1},{4,6},{5,7},{6,4},{7,5},{8,10},{9,11},{10,... | collective-permute-start | bytes 835592 | tf_op jit(solution)/shard_map/ppermute | solution.py:42
  56.0 13.9 %collective-permute-start.40 = (bf16[128,2048]{1,0:T(8,128)(2,1)}, bf16[128,2048]{1,0:T(8,128)(2,1)}, u32[]{:S(2)}, u32[]{:S(2)}) collective-permute-start(bf16[128,2048]{1,0:T(8,128)(2,1)} %slice.182), channel_id=1, source_target_pairs={{0,4},{1,5},{2,6},{3,7},{4,0},{5,1},{6,2},{7,3},{8,12},{9,13},{10,... | collective-permute-start | bytes 1572872 | tf_op jit(solution)/shard_map/ppermute | solution.py:42
  58.6 12.8 %collective-permute-start.41 = (bf16[128,2048]{1,0:T(8,128)(2,1)}, bf16[128,2048]{1,0:T(8,128)(2,1)}, u32[]{:S(2)}, u32[]{:S(2)}) collective-permute-start(bf16[128,2048]{1,0:T(8,128)(2,1)} %slice.183), channel_id=1, source_target_pairs={{0,2},{1,3},{2,0},{3,1},{4,6},{5,7},{6,4},{7,5},{8,10},{9,11},{10,... | collective-permute-start | bytes 1572872 | tf_op jit(solution)/shard_map/ppermute | solution.py:42
  60.9 15.7 %collective-permute-start.45 = (bf16[2,2,272,256]{3,2,1,0:T(8,128)(2,1)}, bf16[2,2,272,256]{3,2,1,0:T(8,128)(2,1)}, u32[]{:S(2)}, u32[]{:S(2)}) collective-permute-start(bf16[2,2,272,256]{3,2,1,0:T(8,128)(2,1)} %pad_maximum_fusion.10), channel_id=1, source_target_pairs={{0,1},{1,0},{2,3},{3,2},{4,5},{5,4},{6,7},{7,6},{8,9},{9,8},{10,11... | collective-permute-start | bytes 1671176 | tf_op jit(solution)/shard_map/ppermute | solution.py:42
  60.9 35.1 %collective-permute-start.46 = (bf16[256,2048]{1,0:T(8,128)(2,1)S(1)}, bf16[256,2048]{1,0:T(8,128)(2,1)}, u32[]{:S(2)}, u32[]{:S(2)}) collective-permute-start(bf16[256,2048]{1,0:T(8,128)(2,1)S(1)} %collective-permute-done.39.a_ref), channel_id=1, source_target_pairs={{0,1},{1,0},{2,3},{3,2},{4,5},{5,4},{6,7},{7,6},{8,9},{9,8},{10,11... | collective-permute-start | bytes 3145736 | tf_op jit(solution)/shard_map/ppermute | solution.py:42
  65.6 20.3 %all-to-all-start.2 = ((bf16[256,8,256]{2,0,1:T(8,128)(2,1)}), bf16[256,8,256]{2,0,1:T(8,128)(2,1)}, u32[]{:S(2)}, u32[]{:S(2)}) async-start(bf16[256,8,256]{2,0,1:T(8,128)(2,1)} %bitcast.187), calls=%async_computation.2 | async-start | bytes 2097152 | tf_op jit(solution)/shard_map/all_to_all | solution.py:132
  69.9 120.5 %all-gather.3.cloned.1.call-start = ((), (), s32[]{:S(2)}) async-start(), calls=%async_computation.6 | async-start | bytes 7208960 | tf_op jit(solution)/shard_map/all_gather | solution.py:814
  69.9 21.3 %collective-permute-start.47 = (bf16[256,2048]{1,0:T(8,128)(2,1)S(1)}, bf16[256,2048]{1,0:T(8,128)(2,1)}, u32[]{:S(2)}, u32[]{:S(2)}) collective-permute-start(bf16[256,2048]{1,0:T(8,128)(2,1)S(1)} %collective-permute-done.38.a_ref), channel_id=1, source_target_pairs={{0,1},{1,0},{2,3},{3,2},{4,5},{5,4},{6,7},{7,6},{8,9},{9,8},{10,11... | collective-permute-start | bytes 3145736 | tf_op jit(solution)/shard_map/ppermute | solution.py:42
  75.2 31.7 %collective-permute-start.50 = (bf16[256,2048]{1,0:T(8,128)(2,1)}, bf16[256,2048]{1,0:T(8,128)(2,1)}, u32[]{:S(2)}, u32[]{:S(2)}) collective-permute-start(bf16[256,2048]{1,0:T(8,128)(2,1)} %get-tuple-element.622), channel_id=1, source_target_pairs={{0,2},{1,3},{2,0},{3,1},{4,6},{5,7},{6,4},{7,5},{8,10},{9,11},{10,... | collective-permute-start | bytes 3145736 | tf_op jit(solution)/shard_map/ppermute | solution.py:42
  76.7 30.2 %collective-permute-start.51 = (bf16[256,2048]{1,0:T(8,128)(2,1)}, bf16[256,2048]{1,0:T(8,128)(2,1)}, u32[]{:S(2)}, u32[]{:S(2)}) collective-permute-start(bf16[256,2048]{1,0:T(8,128)(2,1)} %get-tuple-element.622), channel_id=1, source_target_pairs={{0,4},{1,5},{2,6},{3,7},{4,0},{5,1},{6,2},{7,3},{8,12},{9,13},{10,... | collective-permute-start | bytes 3145736 | tf_op jit(solution)/shard_map/ppermute | solution.py:42
  83.3 304.3 %all-reduce.8.cloned.1.call-start = ((), (), s32[]{:S(2)}) async-start(), calls=%async_computation.5 | async-start | bytes 5767168 | tf_op jit(solution)/shard_map/psum | solution.py:943
  85.8 21.5 %collective-permute-start.49 = (bf16[256,2048]{1,0:T(8,128)(2,1)}, bf16[256,2048]{1,0:T(8,128)(2,1)}, u32[]{:S(2)}, u32[]{:S(2)}) collective-permute-start(bf16[256,2048]{1,0:T(8,128)(2,1)} %get-tuple-element.622), channel_id=1, source_target_pairs={{0,1},{1,0},{2,3},{3,2},{4,5},{5,4},{6,7},{7,6},{8,9},{9,8},{10,11... | collective-permute-start | bytes 3145736 | tf_op jit(solution)/shard_map/ppermute | solution.py:42
  107.4 8.6 %collective-permute-start.42 = (bf16[256,2048]{1,0:T(8,128)(2,1)}, bf16[256,2048]{1,0:T(8,128)(2,1)S(1)}, u32[]{:S(2)}, u32[]{:S(2)}) collective-permute-start(bf16[256,2048]{1,0:T(8,128)(2,1)} %constant_dynamic-update-slice_fusion.2.a_ref), channel_id=1, source_target_pairs={{0,1},{1,0},{2,3},{3,2},{4,5},{5,4},{6,7},{7,6},{8,9},{9,8},{10,11... | collective-permute-start | bytes 3145736 | tf_op jit(solution)/shard_map/ppermute | solution.py:42
  112.7 17.4 %collective-permute-start.54 = (bf16[128,2048]{1,0:T(8,128)(2,1)S(1)}, bf16[128,2048]{1,0:T(8,128)(2,1)S(1)}, u32[]{:S(2)}, u32[]{:S(2)}) collective-permute-start(bf16[128,2048]{1,0:T(8,128)(2,1)S(1)} %slice.187), channel_id=1, source_target_pairs={{0,4},{1,5},{2,6},{3,7},{4,0},{5,1},{6,2},{7,3},{8,12},{9,13},{10,... | collective-permute-start | bytes 1572872 | tf_op jit(solution)/shard_map/ppermute | solution.py:42
  115.3 14.8 %collective-permute-start.55 = (bf16[128,2048]{1,0:T(8,128)(2,1)S(1)}, bf16[128,2048]{1,0:T(8,128)(2,1)S(1)}, u32[]{:S(2)}, u32[]{:S(2)}) collective-permute-start(bf16[128,2048]{1,0:T(8,128)(2,1)S(1)} %slice.188), channel_id=1, source_target_pairs={{0,2},{1,3},{2,0},{3,1},{4,6},{5,7},{6,4},{7,5},{8,10},{9,11},{10,... | collective-permute-start | bytes 1572872 | tf_op jit(solution)/shard_map/ppermute | solution.py:42
  136.1 41.8 %collective-permute-start.56 = (bf16[256,2048]{1,0:T(8,128)(2,1)S(1)}, bf16[256,2048]{1,0:T(8,128)(2,1)S(1)}, u32[]{:S(2)}, u32[]{:S(2)}) collective-permute-start(bf16[256,2048]{1,0:T(8,128)(2,1)S(1)} %get-tuple-element.631), channel_id=1, source_target_pairs={{0,1},{1,0},{2,3},{3,2},{4,5},{5,4},{6,7},{7,6},{8,9},{9,8},{10,11... | collective-permute-start | bytes 3145736 | tf_op jit(solution)/shard_map/ppermute | solution.py:42
  140.1 14.0 %collective-permute-start.59 = (bf16[128,2048]{1,0:T(8,128)(2,1)S(1)}, bf16[128,2048]{1,0:T(8,128)(2,1)S(1)}, u32[]{:S(2)}, u32[]{:S(2)}) collective-permute-start(bf16[128,2048]{1,0:T(8,128)(2,1)S(1)} %get-tuple-element.793), channel_id=1, source_target_pairs={{0,2},{1,3},{2,0},{3,1},{4,6},{5,7},{6,4},{7,5},{8,10},{9,11},{10,... | collective-permute-start | bytes 1572872 | tf_op jit(solution)/shard_map/ppermute | solution.py:42
  141.7 13.7 %collective-permute-start.60 = (bf16[128,2048]{1,0:T(8,128)(2,1)S(1)}, bf16[128,2048]{1,0:T(8,128)(2,1)S(1)}, u32[]{:S(2)}, u32[]{:S(2)}) collective-permute-start(bf16[128,2048]{1,0:T(8,128)(2,1)S(1)} %get-tuple-element.792), channel_id=1, source_target_pairs={{0,4},{1,5},{2,6},{3,7},{4,0},{5,1},{6,2},{7,3},{8,12},{9,13},{10,... | collective-permute-start | bytes 1572872 | tf_op jit(solution)/shard_map/ppermute | solution.py:42
  155.6 24.2 %collective-permute-start.63 = (bf16[256,2048]{1,0:T(8,128)(2,1)S(1)}, bf16[256,2048]{1,0:T(8,128)(2,1)S(1)}, u32[]{:S(2)}, u32[]{:S(2)}) collective-permute-start(bf16[256,2048]{1,0:T(8,128)(2,1)S(1)} %pad_maximum_fusion.9), channel_id=1, source_target_pairs={{0,4},{1,5},{2,6},{3,7},{4,0},{5,1},{6,2},{7,3},{8,12},{9,13},{10,... | collective-permute-start | bytes 3145736 | tf_op jit(solution)/shard_map/ppermute | solution.py:42
  156.5 23.9 %collective-permute-start.61 = (bf16[256,2048]{1,0:T(8,128)(2,1)S(1)}, bf16[256,2048]{1,0:T(8,128)(2,1)S(1)}, u32[]{:S(2)}, u32[]{:S(2)}) collective-permute-start(bf16[256,2048]{1,0:T(8,128)(2,1)S(1)} %pad_maximum_fusion.8), channel_id=1, source_target_pairs={{0,2},{1,3},{2,0},{3,1},{4,6},{5,7},{6,4},{7,5},{8,10},{9,11},{10,... | collective-permute-start | bytes 3145736 | tf_op jit(solution)/shard_map/ppermute | solution.py:42
  193.9 25.6 %collective-permute-start.64 = (bf16[256,2048]{1,0:T(8,128)(2,1)S(1)}, bf16[256,2048]{1,0:T(8,128)(2,1)}, u32[]{:S(2)}, u32[]{:S(2)}) collective-permute-start(bf16[256,2048]{1,0:T(8,128)(2,1)S(1)} %multiply_convert_fusion.refs_1_), channel_id=1, source_target_pairs={{0,2},{1,3},{2,0},{3,1},{4,6},{5,7},{6,4},{7,5},{8,10},{9,11},{10,... | collective-permute-start | bytes 3145736 | tf_op jit(solution)/shard_map/ppermute | solution.py:42
  195.4 25.3 %collective-permute-start.65 = (bf16[256,2048]{1,0:T(8,128)(2,1)S(1)}, bf16[256,2048]{1,0:T(8,128)(2,1)}, u32[]{:S(2)}, u32[]{:S(2)}) collective-permute-start(bf16[256,2048]{1,0:T(8,128)(2,1)S(1)} %multiply_convert_fusion.refs_1_), channel_id=1, source_target_pairs={{0,4},{1,5},{2,6},{3,7},{4,0},{5,1},{6,2},{7,3},{8,12},{9,13},{10,... | collective-permute-start | bytes 3145736 | tf_op jit(solution)/shard_map/ppermute | solution.py:42
  225.0 23.4 %collective-permute-start.67 = (bf16[128,2048]{1,0:T(8,128)(2,1)}, bf16[128,2048]{1,0:T(8,128)(2,1)}, u32[]{:S(2)}, u32[]{:S(2)}) collective-permute-start(bf16[128,2048]{1,0:T(8,128)(2,1)} %slice.196), channel_id=1, source_target_pairs={{0,4},{1,5},{2,6},{3,7},{4,0},{5,1},{6,2},{7,3},{8,12},{9,13},{10,... | collective-permute-start | bytes 1572872 | tf_op jit(solution)/shard_map/ppermute | solution.py:42
  226.5 21.9 %collective-permute-start.68 = (bf16[128,2048]{1,0:T(8,128)(2,1)}, bf16[128,2048]{1,0:T(8,128)(2,1)}, u32[]{:S(2)}, u32[]{:S(2)}) collective-permute-start(bf16[128,2048]{1,0:T(8,128)(2,1)} %slice.197), channel_id=1, source_target_pairs={{0,2},{1,3},{2,0},{3,1},{4,6},{5,7},{6,4},{7,5},{8,10},{9,11},{10,... | collective-permute-start | bytes 1572872 | tf_op jit(solution)/shard_map/ppermute | solution.py:42
  227.0 24.1 %collective-permute-start.72 = (bf16[256,2048]{1,0:T(8,128)(2,1)}, bf16[256,2048]{1,0:T(8,128)(2,1)}, u32[]{:S(2)}, u32[]{:S(2)}) collective-permute-start(bf16[256,2048]{1,0:T(8,128)(2,1)} %pad_maximum_fusion.7.ga_hbm), channel_id=1, source_target_pairs={{0,1},{1,0},{2,3},{3,2},{4,5},{5,4},{6,7},{7,6},{8,9},{9,8},{10,11... | collective-permute-start | bytes 3145736 | tf_op jit(solution)/shard_map/ppermute | solution.py:42
  277.4 318.5 %all-reduce.12.cloned.1.call-start = ((), (), s32[]{:S(2)}) async-start(), calls=%async_computation.8 | async-start | bytes 11534336 | tf_op jit(solution)/shard_map/psum | solution.py:966
  316.6 13.2 %collective-permute-start.19 = (bf16[256,2048]{1,0:T(8,128)(2,1)}, bf16[256,2048]{1,0:T(8,128)(2,1)S(1)}, u32[]{:S(2)}, u32[]{:S(2)}) collective-permute-start(bf16[256,2048]{1,0:T(8,128)(2,1)} %get-tuple-element.327), channel_id=1, source_target_pairs={{0,1},{1,0},{2,3},{3,2},{4,5},{5,4},{6,7},{7,6},{8,9},{9,8},{10,11... | collective-permute-start | bytes 3145736 | tf_op jit(solution)/shard_map/cond/branch_1_fun/ppermute | solution.py:42
  317.0 16.1 %collective-permute-start.18 = (bf16[256,2048]{1,0:T(8,128)(2,1)}, bf16[256,2048]{1,0:T(8,128)(2,1)S(1)}, u32[]{:S(2)}, u32[]{:S(2)}) collective-permute-start(bf16[256,2048]{1,0:T(8,128)(2,1)} %get-tuple-element.325), channel_id=1, source_target_pairs={{0,1},{1,0},{2,3},{3,2},{4,5},{5,4},{6,7},{7,6},{8,9},{9,8},{10,11... | collective-permute-start | bytes 3145736 | tf_op jit(solution)/shard_map/cond/branch_1_fun/ppermute | solution.py:42
  317.2 16.8 %collective-permute-start.17 = (bf16[256,2048]{1,0:T(8,128)(2,1)}, bf16[256,2048]{1,0:T(8,128)(2,1)S(1)}, u32[]{:S(2)}, u32[]{:S(2)}) collective-permute-start(bf16[256,2048]{1,0:T(8,128)(2,1)} %get-tuple-element.323), channel_id=1, source_target_pairs={{0,1},{1,0},{2,3},{3,2},{4,5},{5,4},{6,7},{7,6},{8,9},{9,8},{10,11... | collective-permute-start | bytes 3145736 | tf_op jit(solution)/shard_map/cond/branch_1_fun/ppermute | solution.py:42
  317.5 16.0 %collective-permute-start.22 = (bf16[256,2048]{1,0:T(8,128)(2,1)}, bf16[256,2048]{1,0:T(8,128)(2,1)S(1)}, u32[]{:S(2)}, u32[]{:S(2)}) collective-permute-start(bf16[256,2048]{1,0:T(8,128)(2,1)} %get-tuple-element.330), channel_id=1, source_target_pairs={{0,1},{1,0},{2,3},{3,2},{4,5},{5,4},{6,7},{7,6},{8,9},{9,8},{10,11... | collective-permute-start | bytes 3145736 | tf_op jit(solution)/shard_map/cond/branch_1_fun/ppermute | solution.py:42
  331.5 14.4 %collective-permute-start.20 = (bf16[128,2048]{1,0:T(8,128)(2,1)S(1)}, bf16[128,2048]{1,0:T(8,128)(2,1)S(1)}, u32[]{:S(2)}, u32[]{:S(2)}) collective-permute-start(bf16[128,2048]{1,0:T(8,128)(2,1)S(1)} %get-tuple-element.774), channel_id=1, source_target_pairs={{0,2},{1,3},{2,0},{3,1},{4,6},{5,7},{6,4},{7,5},{8,10},{9,11},{10,... | collective-permute-start | bytes 1572872 | tf_op jit(solution)/shard_map/cond/branch_1_fun/ppermute | solution.py:42
  332.8 14.2 %collective-permute-start.21 = (bf16[128,2048]{1,0:T(8,128)(2,1)S(1)}, bf16[128,2048]{1,0:T(8,128)(2,1)S(1)}, u32[]{:S(2)}, u32[]{:S(2)}) collective-permute-start(bf16[128,2048]{1,0:T(8,128)(2,1)S(1)} %get-tuple-element.773), channel_id=1, source_target_pairs={{0,4},{1,5},{2,6},{3,7},{4,0},{5,1},{6,2},{7,3},{8,12},{9,13},{10,... | collective-permute-start | bytes 1572872 | tf_op jit(solution)/shard_map/cond/branch_1_fun/ppermute | solution.py:42
  350.0 24.7 %collective-permute-start.11 = (bf16[256,2048]{1,0:T(8,128)(2,1)S(1)}, bf16[256,2048]{1,0:T(8,128)(2,1)S(1)}, u32[]{:S(2)}, u32[]{:S(2)}) collective-permute-start(bf16[256,2048]{1,0:T(8,128)(2,1)S(1)} %get-tuple-element.357), channel_id=1, source_target_pairs={{0,4},{1,5},{2,6},{3,7},{4,0},{5,1},{6,2},{7,3},{8,12},{9,13},{10,... | collective-permute-start | bytes 3145736 | tf_op jit(solution)/shard_map/cond/branch_1_fun/ppermute | solution.py:42
  350.3 24.5 %collective-permute-start.10 = (bf16[256,2048]{1,0:T(8,128)(2,1)S(1)}, bf16[256,2048]{1,0:T(8,128)(2,1)S(1)}, u32[]{:S(2)}, u32[]{:S(2)}) collective-permute-start(bf16[256,2048]{1,0:T(8,128)(2,1)S(1)} %get-tuple-element.356), channel_id=1, source_target_pairs={{0,2},{1,3},{2,0},{3,1},{4,6},{5,7},{6,4},{7,5},{8,10},{9,11},{10,... | collective-permute-start | bytes 3145736 | tf_op jit(solution)/shard_map/cond/branch_1_fun/ppermute | solution.py:42
  389.5 25.0 %collective-permute-start = (bf16[256,2048]{1,0:T(8,128)(2,1)S(1)}, bf16[256,2048]{1,0:T(8,128)(2,1)}, u32[]{:S(2)}, u32[]{:S(2)}) collective-permute-start(bf16[256,2048]{1,0:T(8,128)(2,1)S(1)} %convert_element_type.354.a_ref), channel_id=1, source_target_pairs={{0,2},{1,3},{2,0},{3,1},{4,6},{5,7},{6,4},{7,5},{8,10},{9,11},{10,... | collective-permute-start | bytes 3145736 | tf_op jit(solution)/shard_map/cond/branch_1_fun/ppermute | solution.py:42
  391.0 24.7 %collective-permute-start.1 = (bf16[256,2048]{1,0:T(8,128)(2,1)S(1)}, bf16[256,2048]{1,0:T(8,128)(2,1)}, u32[]{:S(2)}, u32[]{:S(2)}) collective-permute-start(bf16[256,2048]{1,0:T(8,128)(2,1)S(1)} %convert_element_type.354.a_ref), channel_id=1, source_target_pairs={{0,4},{1,5},{2,6},{3,7},{4,0},{5,1},{6,2},{7,3},{8,12},{9,13},{10,... | collective-permute-start | bytes 3145736 | tf_op jit(solution)/shard_map/cond/branch_1_fun/ppermute | solution.py:42
  392.5 23.7 %collective-permute-start.4 = (bf16[256,2048]{1,0:T(8,128)(2,1)S(1)}, bf16[256,2048]{1,0:T(8,128)(2,1)S(1)}, u32[]{:S(2)}, u32[]{:S(2)}) collective-permute-start(bf16[256,2048]{1,0:T(8,128)(2,1)S(1)} %convert_element_type.354.a_ref), channel_id=1, source_target_pairs={{0,1},{1,0},{2,3},{3,2},{4,5},{5,4},{6,7},{7,6},{8,9},{9,8},{10,11... | collective-permute-start | bytes 3145736 | tf_op jit(solution)/shard_map/cond/branch_1_fun/ppermute | solution.py:42
  421.6 14.0 %collective-permute-start.5 = (bf16[128,2048]{1,0:T(8,128)(2,1)S(1)}, bf16[128,2048]{1,0:T(8,128)(2,1)S(1)}, u32[]{:S(2)}, u32[]{:S(2)}) collective-permute-start(bf16[128,2048]{1,0:T(8,128)(2,1)S(1)} %slice.132), channel_id=1, source_target_pairs={{0,4},{1,5},{2,6},{3,7},{4,0},{5,1},{6,2},{7,3},{8,12},{9,13},{10,... | collective-permute-start | bytes 1572872 | tf_op jit(solution)/shard_map/cond/branch_1_fun/ppermute | solution.py:42
  424.2 13.7 %collective-permute-start.6 = (bf16[128,2048]{1,0:T(8,128)(2,1)S(1)}, bf16[128,2048]{1,0:T(8,128)(2,1)S(1)}, u32[]{:S(2)}, u32[]{:S(2)}) collective-permute-start(bf16[128,2048]{1,0:T(8,128)(2,1)S(1)} %slice.133), channel_id=1, source_target_pairs={{0,2},{1,3},{2,0},{3,1},{4,6},{5,7},{6,4},{7,5},{8,10},{9,11},{10,... | collective-permute-start | bytes 1572872 | tf_op jit(solution)/shard_map/cond/branch_1_fun/ppermute | solution.py:42
  451.9 53.9 %all-to-all-start.3 = ((bf16[8,704,256]{2,1,0:T(8,128)(2,1)}), bf16[8,704,256]{2,1,0:T(8,128)(2,1)}, u32[]{:S(2)}, u32[]{:S(2)}) async-start(bf16[8,704,256]{2,1,0:T(8,128)(2,1)} %bitcast.205), calls=%async_computation.3 | async-start | bytes 5767168 | tf_op jit(solution)/shard_map/all_to_all | solution.py:778
  456.9 29.1 %collective-permute-start.25 = (bf16[256,2048]{1,0:T(8,128)(2,1)}, bf16[256,2048]{1,0:T(8,128)(2,1)S(1)}, u32[]{:S(2)}, u32[]{:S(2)}) collective-permute-start(bf16[256,2048]{1,0:T(8,128)(2,1)} %get-tuple-element.386), channel_id=1, source_target_pairs={{0,1},{1,0},{2,3},{3,2},{4,5},{5,4},{6,7},{7,6},{8,9},{9,8},{10,11... | collective-permute-start | bytes 3145736 | tf_op jit(solution)/shard_map/cond/branch_1_fun/ppermute | solution.py:42
  457.4 36.9 %collective-permute-start.23 = (bf16[256,2048]{1,0:T(8,128)(2,1)}, bf16[256,2048]{1,0:T(8,128)(2,1)S(1)}, u32[]{:S(2)}, u32[]{:S(2)}) collective-permute-start(bf16[256,2048]{1,0:T(8,128)(2,1)} %get-tuple-element.382), channel_id=1, source_target_pairs={{0,1},{1,0},{2,3},{3,2},{4,5},{5,4},{6,7},{7,6},{8,9},{9,8},{10,11... | collective-permute-start | bytes 3145736 | tf_op jit(solution)/shard_map/cond/branch_1_fun/ppermute | solution.py:42
  457.5 33.6 %collective-permute-start.24 = (bf16[256,2048]{1,0:T(8,128)(2,1)}, bf16[256,2048]{1,0:T(8,128)(2,1)S(1)}, u32[]{:S(2)}, u32[]{:S(2)}) collective-permute-start(bf16[256,2048]{1,0:T(8,128)(2,1)} %get-tuple-element.384), channel_id=1, source_target_pairs={{0,1},{1,0},{2,3},{3,2},{4,5},{5,4},{6,7},{7,6},{8,9},{9,8},{10,11... | collective-permute-start | bytes 3145736 | tf_op jit(solution)/shard_map/cond/branch_1_fun/ppermute | solution.py:42
  457.9 34.8 %collective-permute-start.28 = (bf16[256,2048]{1,0:T(8,128)(2,1)}, bf16[256,2048]{1,0:T(8,128)(2,1)S(1)}, u32[]{:S(2)}, u32[]{:S(2)}) collective-permute-start(bf16[256,2048]{1,0:T(8,128)(2,1)} %get-tuple-element.389), channel_id=1, source_target_pairs={{0,1},{1,0},{2,3},{3,2},{4,5},{5,4},{6,7},{7,6},{8,9},{9,8},{10,11... | collective-permute-start | bytes 3145736 | tf_op jit(solution)/shard_map/cond/branch_1_fun/ppermute | solution.py:42
  487.7 14.3 %collective-permute-start.26 = (bf16[128,2048]{1,0:T(8,128)(2,1)S(1)}, bf16[128,2048]{1,0:T(8,128)(2,1)S(1)}, u32[]{:S(2)}, u32[]{:S(2)}) collective-permute-start(bf16[128,2048]{1,0:T(8,128)(2,1)S(1)} %get-tuple-element.778), channel_id=1, source_target_pairs={{0,2},{1,3},{2,0},{3,1},{4,6},{5,7},{6,4},{7,5},{8,10},{9,11},{10,... | collective-permute-start | bytes 1572872 | tf_op jit(solution)/shard_map/cond/branch_1_fun/ppermute | solution.py:42
  489.6 13.7 %collective-permute-start.27 = (bf16[128,2048]{1,0:T(8,128)(2,1)S(1)}, bf16[128,2048]{1,0:T(8,128)(2,1)S(1)}, u32[]{:S(2)}, u32[]{:S(2)}) collective-permute-start(bf16[128,2048]{1,0:T(8,128)(2,1)S(1)} %get-tuple-element.777), channel_id=1, source_target_pairs={{0,4},{1,5},{2,6},{3,7},{4,0},{5,1},{6,2},{7,3},{8,12},{9,13},{10,... | collective-permute-start | bytes 1572872 | tf_op jit(solution)/shard_map/cond/branch_1_fun/ppermute | solution.py:42
  508.1 85.7 %all-to-all-start.4 = ((bf16[8,256,256]{2,1,0:T(8,128)(2,1)}), bf16[8,256,256]{2,1,0:T(8,128)(2,1)}, u32[]{:S(2)}, u32[]{:S(2)}) async-start(bf16[8,256,256]{2,1,0:T(8,128)(2,1)} %bitcast.80), calls=%async_computation.4 | async-start | bytes 2097152 | tf_op jit(solution)/shard_map/all_to_all | solution.py:1001
  512.5 177.9 %all-reduce.10.cloned.1.call-start = ((), (), s32[]{:S(2)}) async-start(), calls=%async_computation.7 | async-start | bytes 4472832 | tf_op jit(solution)/shard_map/psum | solution.py:1023
  521.7 10.8 %collective-permute-start.36 = (bf16[2,256,256]{2,1,0:T(8,128)(2,1)}, bf16[2,256,256]{2,1,0:T(8,128)(2,1)S(1)}, u32[]{:S(2)}, u32[]{:S(2)}) collective-permute-start(bf16[2,256,256]{2,1,0:T(8,128)(2,1)} %fusion.10), channel_id=1, source_target_pairs={{0,2},{1,3},{2,0},{3,1},{4,6},{5,7},{6,4},{7,5},{8,10},{9,11},{10,... | collective-permute-start | bytes 786440 | tf_op jit(solution)/shard_map/cond/branch_1_fun/ppermute | solution.py:42
  523.6 15.4 %collective-permute-start.31 = (bf16[256,2048]{1,0:T(8,128)(2,1)}, bf16[256,2048]{1,0:T(8,128)(2,1)S(1)}, u32[]{:S(2)}, u32[]{:S(2)}) collective-permute-start(bf16[256,2048]{1,0:T(8,128)(2,1)} %get-tuple-element.424), channel_id=1, source_target_pairs={{0,1},{1,0},{2,3},{3,2},{4,5},{5,4},{6,7},{7,6},{8,9},{9,8},{10,11... | collective-permute-start | bytes 3145736 | tf_op jit(solution)/shard_map/cond/branch_1_fun/ppermute | solution.py:42
  535.2 11.0 %collective-permute-start.29 = (bf16[256,2048]{1,0:T(8,128)(2,1)}, bf16[256,2048]{1,0:T(8,128)(2,1)S(1)}, u32[]{:S(2)}, u32[]{:S(2)}) collective-permute-start(bf16[256,2048]{1,0:T(8,128)(2,1)} %get-tuple-element.420), channel_id=1, source_target_pairs={{0,1},{1,0},{2,3},{3,2},{4,5},{5,4},{6,7},{7,6},{8,9},{9,8},{10,11... | collective-permute-start | bytes 3145736 | tf_op jit(solution)/shard_map/cond/branch_1_fun/ppermute | solution.py:42
  535.7 8.8 %collective-permute-start.34 = (bf16[256,2048]{1,0:T(8,128)(2,1)}, bf16[256,2048]{1,0:T(8,128)(2,1)S(1)}, u32[]{:S(2)}, u32[]{:S(2)}) collective-permute-start(bf16[256,2048]{1,0:T(8,128)(2,1)} %get-tuple-element.427), channel_id=1, source_target_pairs={{0,1},{1,0},{2,3},{3,2},{4,5},{5,4},{6,7},{7,6},{8,9},{9,8},{10,11... | collective-permute-start | bytes 3145736 | tf_op jit(solution)/shard_map/cond/branch_1_fun/ppermute | solution.py:42
  540.7 12.9 %collective-permute-start.32 = (bf16[128,2048]{1,0:T(8,128)(2,1)S(1)}, bf16[128,2048]{1,0:T(8,128)(2,1)S(1)}, u32[]{:S(2)}, u32[]{:S(2)}) collective-permute-start(bf16[128,2048]{1,0:T(8,128)(2,1)S(1)} %get-tuple-element.780), channel_id=1, source_target_pairs={{0,2},{1,3},{2,0},{3,1},{4,6},{5,7},{6,4},{7,5},{8,10},{9,11},{10,... | collective-permute-start | bytes 1572872 | tf_op jit(solution)/shard_map/cond/branch_1_fun/ppermute | solution.py:42
  541.4 12.8 %collective-permute-start.33 = (bf16[128,2048]{1,0:T(8,128)(2,1)S(1)}, bf16[128,2048]{1,0:T(8,128)(2,1)S(1)}, u32[]{:S(2)}, u32[]{:S(2)}) collective-permute-start(bf16[128,2048]{1,0:T(8,128)(2,1)S(1)} %get-tuple-element.779), channel_id=1, source_target_pairs={{0,4},{1,5},{2,6},{3,7},{4,0},{5,1},{6,2},{7,3},{8,12},{9,13},{10,... | collective-permute-start | bytes 1572872 | tf_op jit(solution)/shard_map/cond/branch_1_fun/ppermute | solution.py:42
  556.7 23.4 %collective-permute-start.13 = (bf16[256,2048]{1,0:T(8,128)(2,1)}, bf16[256,2048]{1,0:T(8,128)(2,1)S(1)}, u32[]{:S(2)}, u32[]{:S(2)}) collective-permute-start(bf16[256,2048]{1,0:T(8,128)(2,1)} %get-tuple-element.433), channel_id=1, source_target_pairs={{0,4},{1,5},{2,6},{3,7},{4,0},{5,1},{6,2},{7,3},{8,12},{9,13},{10,... | collective-permute-start | bytes 3145736 | tf_op jit(solution)/shard_map/cond/branch_1_fun/ppermute | solution.py:42
  557.9 23.0 %collective-permute-start.12 = (bf16[256,2048]{1,0:T(8,128)(2,1)}, bf16[256,2048]{1,0:T(8,128)(2,1)}, u32[]{:S(2)}, u32[]{:S(2)}) collective-permute-start(bf16[256,2048]{1,0:T(8,128)(2,1)} %get-tuple-element.432), channel_id=1, source_target_pairs={{0,2},{1,3},{2,0},{3,1},{4,6},{5,7},{6,4},{7,5},{8,10},{9,11},{10,... | collective-permute-start | bytes 3145736 | tf_op jit(solution)/shard_map/cond/branch_1_fun/ppermute | solution.py:42
  599.5 63.2 %all-to-all-start = ((bf16[8,704,256]{2,1,0:T(8,128)(2,1)}), bf16[8,704,256]{2,1,0:T(8,128)(2,1)S(1)}, u32[]{:S(2)}, u32[]{:S(2)}) async-start(bf16[8,704,256]{2,1,0:T(8,128)(2,1)} %bitcast.206), calls=%async_computation | async-start | bytes 5767168 | tf_op jit(solution)/shard_map/cond/branch_1_fun/all_to_all | solution.py:778
  603.1 56.6 %collective-permute-start.9 = (bf16[256,2048]{1,0:T(8,128)(2,1)}, bf16[256,2048]{1,0:T(8,128)(2,1)S(1)}, u32[]{:S(2)}, u32[]{:S(2)}) collective-permute-start(bf16[256,2048]{1,0:T(8,128)(2,1)} %get-tuple-element.447), channel_id=1, source_target_pairs={{0,4},{1,5},{2,6},{3,7},{4,0},{5,1},{6,2},{7,3},{8,12},{9,13},{10,... | collective-permute-start | bytes 3145736 | tf_op jit(solution)/shard_map/cond/branch_1_fun/ppermute | solution.py:42
  605.2 54.7 %collective-permute-start.8 = (bf16[256,2048]{1,0:T(8,128)(2,1)}, bf16[256,2048]{1,0:T(8,128)(2,1)S(1)}, u32[]{:S(2)}, u32[]{:S(2)}) collective-permute-start(bf16[256,2048]{1,0:T(8,128)(2,1)} %get-tuple-element.446), channel_id=1, source_target_pairs={{0,2},{1,3},{2,0},{3,1},{4,6},{5,7},{6,4},{7,5},{8,10},{9,11},{10,... | collective-permute-start | bytes 3145736 | tf_op jit(solution)/shard_map/cond/branch_1_fun/ppermute | solution.py:42
  (76 other events, 654.4 us)
Sparse Core Ops, SparseCore 0:
  83.4 106.9 all-gather.2
  277.5 110.0 all-reduce.7
  390.6 205.2 all-reduce.11
  598.9 91.4 all-reduce.9

commit v5 on v4

--- a/solution.py
+++ b/solution.py
@@ -474,67 +474,88 @@
     )(key, *given, *before)
 
 
-def hidden_kernel(na_hbm, nb_hbm, ga_hbm, gb_hbm, shares_hbm, down_hbm, *rest, first):
-    hidden_hbm, dgate_hbm, dup_hbm = rest[-11:-8]
-    normed, branch, both, down, hidden, dgate, dup, sems = rest[-8:]
-    rows = na_hbm.shape[0]
+def hidden_kernel(*refs, first, pairs):
+    pieces, (shares_hbm, down_hbm) = refs[: 4 * pairs], refs[4 * pairs : 4 * pairs + 2]
+    hidden_hbm, dgate_hbm, dup_hbm = refs[-11:-8]
+    normed, branch, both, down, hidden, dgate, dup, sems = refs[-8:]
+    rows = pieces[0].shape[0]
     lines, inner = shares_hbm.shape[0], down_hbm.shape[0]
+    used = 0
+
+    def copies(places):
+        nonlocal used
+        made = [pltpu.make_async_copy(a, b, sems.at[used + i]) for i, (a, b) in enumerate(places)]
+        used += len(made)
+        return made
+
+    loads = copies([(shares_hbm.at[i], both.at[:, i]) for i in range(lines)])
+    loads_normed, loads_branch, loads_down = [], [], []
     low, high = pl.ds(0, rows), pl.ds(rows, rows)
-    places = [(shares_hbm.at[i], both.at[:, i]) for i in range(lines)]
-    places += [(na_hbm, normed.at[low]), (nb_hbm, normed.at[high])]
-    places += [(ga_hbm, branch.at[low]), (gb_hbm, branch.at[high]), (down_hbm, down)]
-    loads = [pltpu.make_async_copy(a, b, sems.at[i]) for i, (a, b) in enumerate(places)]
-    places = []
-    for stack, target in ((hidden, hidden_hbm), (dgate, dgate_hbm), (dup, dup_hbm)):
-        places += [(stack.at[low], target.at[first]), (stack.at[high], target.at[first + 1])]
-    stores = [
-        pltpu.make_async_copy(a, b, sems.at[len(loads) + i]) for i, (a, b) in enumerate(places)
-    ]
+    for p in range(pairs):
+        na, nb, ga, gb = pieces[4 * p : 4 * p + 4]
+        loads_normed.append(copies([(na, normed.at[p, low]), (nb, normed.at[p, high])]))
+        loads_branch.append(copies([(ga, branch.at[p, low]), (gb, branch.at[p, high])]))
+        if p == 0:
+            loads_down = copies([(down_hbm, down)])
+    for load in [*loads, *loads_normed[0], *loads_branch[0], *loads_down]:
+        load.start()
+    for p in range(1, pairs):
+        for load in [*loads_normed[p], *loads_branch[p]]:
+            load.start()
     for load in loads:
-        load.start()
-    for load in loads[: lines + 2]:
         load.wait()
-    gate_up = dot_nn(normed[...], both[...].reshape(-1, 2 * inner))
-    gate_pre, up_pre = gate_up[:, :inner], gate_up[:, inner:]
-    sigma = jax.nn.sigmoid(gate_pre)
-    silu_gate = gate_pre * sigma
-    slope = sigma * (1.0 + gate_pre * (1.0 - sigma))
-    hidden[...] = (silu_gate * up_pre).astype(BF)
-    for store in stores[:2]:
-        store.start()
-    for load in loads[lines + 2 :]:
-        load.wait()
-    grad_hidden = dot_nt(branch[...], down[...])
-    dgate[...] = (grad_hidden * up_pre * slope).astype(BF)
-    dup[...] = (grad_hidden * silu_gate).astype(BF)
-    for store in stores[2:]:
-        store.start()
+    stores = []
+    for p in range(pairs):
+        for load in loads_normed[p]:
+            load.wait()
+        gate_up = dot_nn(normed[p], both[...].reshape(-1, 2 * inner))
+        gate_pre, up_pre = gate_up[:, :inner], gate_up[:, inner:]
+        sigma = jax.nn.sigmoid(gate_pre)
+        silu_gate = gate_pre * sigma
+        slope = sigma * (1.0 + gate_pre * (1.0 - sigma))
+        for load in [*loads_branch[p], *(loads_down if p == 0 else [])]:
+            load.wait()
+        grad_hidden = dot_nt(branch[p], down[...])
+        hidden[p] = (silu_gate * up_pre).astype(BF)
+        dgate[p] = (grad_hidden * up_pre * slope).astype(BF)
+        dup[p] = (grad_hidden * silu_gate).astype(BF)
+        places = []
+        for stack, target in ((hidden, hidden_hbm), (dgate, dgate_hbm), (dup, dup_hbm)):
+            places += [(stack.at[p, low], target.at[first + 2 * p])]
+            places += [(stack.at[p, high], target.at[first + 2 * p + 1])]
+        stores += copies(places)
+        for store in stores[-6:]:
+            store.start()
     for store in stores:
         store.wait()
 
 
-def hidden_pair(normed, branch, pair, shares, down, count, before):
+def hidden_pairs(normed, branch, first, shares, down, count, before):
     rows, width = normed[0].shape
     inner = down.shape[0]
     lines, _, share_rows, _ = shares.shape
-    given = [*normed, *branch, shares, down]
+    pairs = len(normed) // 2
+    given = []
+    for p in range(0, 2 * pairs, 2):
+        given += [*normed[p : p + 2], *branch[p : p + 2]]
+    given += [shares, down]
     anywhere = pl.BlockSpec(memory_space=pl.ANY)
     stacked = jax.ShapeDtypeStruct((count, rows, inner), BF)
     return pl.pallas_call(
-        functools.partial(hidden_kernel, first=2 * pair),
-        in_specs=[anywhere] * (6 + len(before)),
+        functools.partial(hidden_kernel, first=first, pairs=pairs),
+        in_specs=[anywhere] * (len(given) + len(before)),
         out_specs=[anywhere] * 3,
         out_shape=[stacked] * 3,
-        scratch_shapes=[pltpu.VMEM((2 * rows, width), BF)] * 2
+        scratch_shapes=[pltpu.VMEM((pairs, 2 * rows, width), BF)] * 2
         + [pltpu.VMEM((count, lines, share_rows, 2 * inner), BF), pltpu.VMEM(down.shape, BF)]
-        + [pltpu.VMEM((2 * rows, inner), BF)] * 3
-        + [pltpu.SemaphoreType.DMA((lines + 11,))],
-        input_output_aliases={6 + i: i for i in range(len(before))},
+        + [pltpu.VMEM((pairs, 2 * rows, inner), BF)] * 3
+        + [pltpu.SemaphoreType.DMA((lines + 1 + 10 * pairs,))],
+        input_output_aliases={len(given) + i: i for i in range(len(before))},
         compiler_params=pltpu.CompilerParams(vmem_limit_bytes=MLP_VMEM_BYTES),
         cost_estimate=pl.CostEstimate(
-            flops=20 * rows * width * inner,
-            bytes_accessed=6 * width * inner + 12 * rows * width,
-            transcendentals=2 * rows * inner,
+            flops=20 * pairs * rows * width * inner,
+            bytes_accessed=6 * width * inner + 12 * pairs * rows * width,
+            transcendentals=2 * pairs * rows * inner,
         ),
     )(*given, *before)
 
@@ -778,9 +799,18 @@
     return lax.all_to_all(blocks, "seq", split_axis=0, concat_axis=0, tiled=True)
 
 
-def pack_kernel(place_ref, gate_ref, up_ref, out_ref):
-    count = out_ref.shape[0]
+def pack_kernel(place_ref, gate_hbm, up_hbm, out_ref, gate_ref, up_ref, sems):
+    count, rows, _ = out_ref.shape
     inner = gate_ref.shape[1] // count
+    span = pl.ds(pl.multiple_of(place_ref[0] * rows, rows), rows)
+    loads = [
+        pltpu.make_async_copy(gate_hbm.at[span], gate_ref, sems.at[0]),
+        pltpu.make_async_copy(up_hbm.at[span], up_ref, sems.at[1]),
+    ]
+    for load in loads:
+        load.start()
+    for load in loads:
+        load.wait()
     gate, up = gate_ref[...], up_ref[...]
     for j in range(count):
         columns = slice(j * inner, (j + 1) * inner)
@@ -791,15 +821,20 @@
     lines = lax.axis_size("dp")
     rows, columns = w_gate.shape[0] // lines, w_gate.shape[1]
     place = lax.axis_index("dp").astype(jnp.int32).reshape(1)
-    share = pl.BlockSpec((rows, columns), lambda i, place: (place[0], 0))
+    anywhere = pl.BlockSpec(memory_space=pl.ANY)
     shape = (count, rows, 2 * columns // count)
     return pl.pallas_call(
         pack_kernel,
         grid_spec=pltpu.PrefetchScalarGridSpec(
             num_scalar_prefetch=1,
             grid=(1,),
-            in_specs=[share, share],
+            in_specs=[anywhere, anywhere],
             out_specs=pl.BlockSpec(shape, lambda i, place: (0, 0, 0)),
+            scratch_shapes=[
+                pltpu.VMEM((rows, columns), BF),
+                pltpu.VMEM((rows, columns), BF),
+                pltpu.SemaphoreType.DMA((2,)),
+            ],
         ),
         out_shape=jax.ShapeDtypeStruct(shape, BF),
         compiler_params=pltpu.CompilerParams(vmem_limit_bytes=VMEM_BYTES),
@@ -911,14 +946,14 @@
     scale_two = rms_scale(middle)
     sync = lax.optimization_barrier
     always = lengths[0] > 0
-    hidden_of = lambda pair, two, before: tuple(
-        hidden_pair(two, branch[2 * pair : 2 * pair + 2], pair, shares, w_down, count, before)
+    hidden_of = lambda first, pieces, before: tuple(
+        hidden_pairs(pieces, branch[first : first + len(pieces)], first, shares, w_down, count, before)
     )
     normed_own = (middle * scale_two * gain_two).astype(BF)
 
     def middle_pairs(near, stacks):
-        for pair in range(1, last_pair):
-            stacks = hidden_of(pair, near[2 * pair : 2 * pair + 2], stacks)
+        for first in range(2, 2 * last_pair, 4):
+            stacks = hidden_of(first, near[first : min(first + 4, 2 * last_pair)], stacks)
         return tuple(stacks)
 
     if is_cube(count):
@@ -935,7 +970,7 @@
         near = gather_near(normed_own, count)
         stacks = middle_pairs(near, hidden_of(0, near[:2], []))
         far, last = near[-2:]
-    stacks = hidden_of(last_pair, [far, last], list(stacks))
+    stacks = hidden_of(2 * last_pair, [far, last], list(stacks))
     hidden, grad_gate, grad_up = [stack.reshape(all_rows, -1) for stack in stacks]
     normed_two = (near if is_cube(count) else near[:-2]) + [far, last]
     split = queries.shape[-1]

time: 714 us -> 712 us (level)
  waiting for transfers between devices: 269 us -> 259 us
  Pallas kernels: 220 us -> 228 us
    pallas_call x1, Pallas kernels: 19.9 us -> 30.8 us  [attend_second(): pl.pallas_call(second_kernel, grid_spec=pltpu.PrefetchScalarGridSpec(num_...]
    all_gather x1, waiting for transfers between devices: 9.44 us -> 0.02 us  [share_weights(): return (query, lax.all_gather(packed, 'dp', axis=0, tiled=False))]
    pallas_call x4 -> x3, Pallas kernels: 42.2 us -> 38.2 us  [hidden_pairs(): pl.pallas_call(functools.partial(hidden_kernel, first=first, pairs=pairs)...]
  transfers between devices with their start and end apart: 82 -> 82, of which waited for: 41 -> 41; matrix products, arithmetic and copies ran while one was open for 14% -> 14% of each run, Pallas kernels for 28% -> 29%
where the time goes in v5:
time: 712 us; the launch traced here: 701 us
  waiting for transfers between devices  259 us (36%)
  Pallas kernels  228 us (32%)
  starting transfers between devices  81.1 us (11%)
  other arithmetic  69.4 us (10%)
  local copies, waits for them, and re-layouts  45.4 us (6%)
  between operations  15.6 us (2%)
    ppermute x73, waiting for transfers between devices, swap(): return lax.ppermute(array, 'seq', [(i, i ^ bit) for i in range(8)])  220 us
    ppermute x73, starting transfers between devices, swap(): return lax.ppermute(array, 'seq', [(i, i ^ bit) for i in range(8)])  58.7 us
    pallas_call x4, Pallas kernels, mlp_parts(): pl.pallas_call(functools.partial(mlp_parts_kernel, first=2 * pair), in_sp...  38.3 us
    pallas_call x3, Pallas kernels, hidden_pairs(): pl.pallas_call(functools.partial(hidden_kernel, first=first, pairs=pairs)...  38.2 us
    pallas_call x3, Pallas kernels, inner_of(): pl.pallas_call(functools.partial(inner_kernel, count=count, lefts=len(lef...  36.7 us
    pallas_call x1, Pallas kernels, attend_second(): pl.pallas_call(second_kernel, grid_spec=pltpu.PrefetchScalarGridSpec(num_...  30.8 us
    psum x1, waiting for transfers between devices, body(): lax.psum((w_out_share, w_query_share.reshape(-1, split), small), 'dp')  23.5 us
    convert_element_type x27, other arithmetic, add_rounded(): return total.astype(BF)  22.8 us
  transfers between devices with their start and end apart: 82, of which 41 were waited for; matrix products, arithmetic and copies ran while one was open for 14% of the time, Pallas kernels for 29%

profile of v5, /device:TPU:0, one launch (start us, length us, event | category | flops | bytes accessed | tf_op | source)
XLA Modules:
  0.0 701.2 jit_solution(4360123532865268179)
XLA Ops:
  20.1 4.4 all-to-all-start.1
  24.7 18.3 %collective-permute-done.43 = bf16[272,256]{1,0:T(8,128)(2,1)S(1)} collective-permute-done((bf16[272,256]{1,0:T(8,128)(2,1)S(1)}, bf16[272,256]{1,0:T(8,128)(2,1)S(1)}, u32[]{:S(2)}, u32[]{:S(2)}) %collective-permute-start.43) | collective-permute-done | bytes 139296 | tf_op jit(solution)/shard_map/ppermute | solution.py:42
  46.1 3.2 convert_multiply_fusion.4
  49.3 5.8 collective-permute-done.44
  65.7 4.2 all-to-all-start.2
  75.8 3.1 fusion.30
  85.9 5.1 shard_map.230
  91.0 4.7 shard_map.231
  95.7 4.5 shard_map.232
  100.2 6.7 collective-permute-done.50
  107.4 3.8 collective-permute-done.52
  116.9 4.1 shard_map.233
  121.1 9.7 %shard_map.234 = (bf16[8,2,128,256]{3,2,1,0:T(8,128)(2,1)S(1)}, f32[2,2,1024]{2,1,0:T(2,128)S(1)}) custom-call(s32[2]{0:T(128)S(1)} %copy-done.55, s32[2]{0:T(128)S(1)} %pad_add_fusion.key_ref, bf16[8,2,128,256]{3,2,1,0:T(8,128)(2,1)S(1)} %get-tuple-element.616.q_ref, bf16[8,2,128,256]{3,2,1,0:T(8,128)(2,1)S(1)} %get-tuple-element.617.kv_ref), custom_call_target="tpu_custom_call" | custom-call | flops 1000 | bytes 1000 | tf_op jit(solution)/shard_map/pallas_call | solution.py:216
  131.9 4.2 shard_map.235
  143.3 11.5 %collective-permute-done.59 = bf16[128,2048]{1,0:T(8,128)(2,1)S(1)} collective-permute-done((bf16[128,2048]{1,0:T(8,128)(2,1)S(1)}, bf16[128,2048]{1,0:T(8,128)(2,1)S(1)}, u32[]{:S(2)}, u32[]{:S(2)}) %collective-permute-start.59) | collective-permute-done | bytes 524320 | tf_op jit(solution)/shard_map/ppermute | solution.py:42
  158.7 30.8 %shard_map.236 = (bf16[2,128,2048]{2,1,0:T(8,128)(2,1)}, f32[8,2,128,256]{3,2,1,0:T(8,128)}) custom-call(s32[2]{0:T(128)S(1)} %copy-done.55, s32[2]{0:T(128)S(1)} %pad_add_fusion.key_ref, bf16[2,128,2048]{2,1,0:T(8,128)(2,1)S(1)} %copy-done.6, bf16[2,128,2048]{2,1,0:T(8,128)(2,1)S(1)} %copy-done.7, bf16[8,2,128,256]{3,2,1,0:T(8,128)(2,1)S(1)} %get-tuple-element.617.kv_ref), custom_call_target="tpu_custom_call" | custom-call | flops 1000 | bytes 1000 | tf_op jit(solution)/shard_map/pallas_call | solution.py:292
  196.7 11.2 %conditional.11 = ((bf16[8,256,704]{2,1,0:T(8,128)(2,1)}, bf16[8,256,704]{2,1,0:T(8,128)(2,1)}, bf16[8,256,704]{2,1,0:T(8,128)(2,1)})) conditional(s32[]{:T(128)} %bitcast.54, () %tuple.139, (bf16[256,2048]{1,0:T(8,128)(2,1)S(1)}, bf16[256,2048]{1,0:T(8,128)(2,1)}, bf16[256,2048]{1,0:T(8,128)(2,1)}, bf16[256,2048]{1,0:T(8,128)(2,1)}, ...), branch_computations={%region_1.2_spmd, %region_2.3_spmd} | conditional | flops 7381975040 | bytes 14942216 | solution.py:142
  196.7 10.7 %branch_1_fun.17 = (bf16[8,256,704]{2,1,0:T(8,128)(2,1)}, bf16[8,256,704]{2,1,0:T(8,128)(2,1)}, bf16[8,256,704]{2,1,0:T(8,128)(2,1)}) custom-call(bf16[256,2048]{1,0:T(8,128)(2,1)S(1)} %get-tuple-element.279.refs_0_, bf16[256,2048]{1,0:T(8,128)(2,1)} %get-tuple-element.280.refs_1_, bf16[256,2048]{1,0:T(8,128)(2,1)} %get-tuple-element.281.refs_2_, ...), custom_call_target="tpu_custom_call" | custom-call | flops 7381975040 | bytes 14942208 | tf_op jit(solution)/shard_map/cond/branch_1_fun/pallas_call | solution.py:544
  207.8 11.7 %collective-permute-done.64.refs_3_ = bf16[256,2048]{1,0:T(8,128)(2,1)} collective-permute-done((bf16[256,2048]{1,0:T(8,128)(2,1)S(1)}, bf16[256,2048]{1,0:T(8,128)(2,1)}, u32[]{:S(2)}, u32[]{:S(2)}) %collective-permute-start.64) | collective-permute-done | bytes 1048608 | tf_op jit(solution)/shard_map/ppermute | solution.py:42
  226.2 16.8 %conditional.12 = ((bf16[8,256,704]{2,1,0:T(8,128)(2,1)}, bf16[8,256,704]{2,1,0:T(8,128)(2,1)}, bf16[8,256,704]{2,1,0:T(8,128)(2,1)})) conditional(s32[]{:T(128)} %bitcast.54, () %tuple.142, (bf16[256,2048]{1,0:T(8,128)(2,1)}, bf16[256,2048]{1,0:T(8,128)(2,1)}, bf16[256,2048]{1,0:T(8,128)(2,1)}, bf16[256,2048]{1,0:T(8,128)(2,1)}, ...), branch_computations={%region_3.4_spmd, %region_4.5_spmd} | conditional | flops 14763950080 | bytes 21233672 | solution.py:142
  226.2 16.6 %branch_1_fun.18 = (bf16[8,256,704]{2,1,0:T(8,128)(2,1)}, bf16[8,256,704]{2,1,0:T(8,128)(2,1)}, bf16[8,256,704]{2,1,0:T(8,128)(2,1)}) custom-call(bf16[256,2048]{1,0:T(8,128)(2,1)} %get-tuple-element.285.refs_0_, bf16[256,2048]{1,0:T(8,128)(2,1)} %get-tuple-element.286.refs_1_, ...), custom_call_target="tpu_custom_call", output_to_operand_aliasing={{0}: (10, {}), {1}: (11, {}), {2}: (12, {})} | custom-call | flops 14763950080 | bytes 21233664 | tf_op jit(solution)/shard_map/cond/branch_1_fun/pallas_call | solution.py:544
  248.0 10.8 %shard_map.237 = (bf16[8,256,704]{2,1,0:T(8,128)(2,1)}, bf16[8,256,704]{2,1,0:T(8,128)(2,1)}, bf16[8,256,704]{2,1,0:T(8,128)(2,1)}) custom-call(bf16[256,2048]{1,0:T(8,128)(2,1)S(1)} %constant_dynamic-update-slice_fusion.4.refs_0_.refs_7_, ...), custom_call_target="tpu_custom_call", output_to_operand_aliasing={{0}: (6, {}), {1}: (7, {}), {2}: (8, {})} | custom-call | flops 7381975040 | bytes 14942208 | tf_op jit(solution)/shard_map/pallas_call | solution.py:544
  258.9 11.6 %shard_map.238 = bf16[704,2048]{1,0:T(8,128)(2,1)S(1)} custom-call(bf16[2048,704]{1,0:T(8,128)(2,1)} %bitcast.203, bf16[256,2048]{1,0:T(8,128)(2,1)S(1)} %multiply_convert_fusion.refs_1_, bf16[256,2048]{1,0:T(8,128)(2,1)} %collective-permute-done.66.refs_2_, bf16[256,2048]{1,0:T(8,128)(2,1)} %collective-permute-done.64.refs_3_, ...), custom_call_target="tpu_custom_call" | custom-call | flops 1000 | bytes 1000 | tf_op jit(solution)/shard_map/pallas_call | solution.py:737
  272.2 38.8 %conditional.13 = (bf16[256,2048]{1,0:T(8,128)(2,1)S(1)}, bf16[256,2048]{1,0:T(8,128)(2,1)}, bf16[256,2048]{1,0:T(8,128)(2,1)S(1)}, bf16[256,2048]{1,0:T(8,128)(...) conditional(s32[]{:T(128)} %bitcast.54, () %tuple.127, ...), branch_computations={%region_5.6_spmd, %region_6.7_spmd} | conditional | flops 29527900160 | bytes 94372048 | solution.py:142
  272.2 10.2 %branch_1_fun.19 = (bf16[256,2048]{1,0:T(8,128)(2,1)S(1)}, bf16[256,2048]{1,0:T(8,128)(2,1)}, bf16[256,2048]{1,0:T(8,128)(2,1)}, bf16[256,2048]{1,0:T(8,128)(2,1)}) custom-call(bf16[8,256,704]{2,1,0:T(8,128)(2,1)} %get-tuple-element.298.hidden_hbm, bf16[8,256,704]{2,1,0:T(8,128)(2,1)} %get-tuple-element.299.dgate_hbm, ...), custom_call_target="tpu_custom_call" | custom-call | flops 7381975040 | bytes 14942208 | tf_op jit(solution)/shard_map/cond/branch_1_fun/pallas_call | solution.py:602
  282.4 9.4 %branch_1_fun.20 = (bf16[256,2048]{1,0:T(8,128)(2,1)S(1)}, bf16[256,2048]{1,0:T(8,128)(2,1)}, bf16[256,2048]{1,0:T(8,128)(2,1)}, bf16[256,2048]{1,0:T(8,128)(2,1)}) custom-call(bf16[8,256,704]{2,1,0:T(8,128)(2,1)S(1)} %copy-done.25, bf16[8,256,704]{2,1,0:T(8,128)(2,1)S(1)} %copy-done.26, bf16[8,256,704]{2,1,0:T(8,128)(2,1)S(1)} %copy-done.27, ...), custom_call_target="tpu_custom_call" | custom-call | flops 7381975040 | bytes 14942208 | tf_op jit(solution)/shard_map/cond/branch_1_fun/pallas_call | solution.py:602
  291.9 9.5 %branch_1_fun.21 = (bf16[256,2048]{1,0:T(8,128)(2,1)S(1)}, bf16[256,2048]{1,0:T(8,128)(2,1)}, bf16[256,2048]{1,0:T(8,128)(2,1)}, bf16[256,2048]{1,0:T(8,128)(2,1)}) custom-call(bf16[8,256,704]{2,1,0:T(8,128)(2,1)S(1)} %copy-done.25, bf16[8,256,704]{2,1,0:T(8,128)(2,1)S(1)} %copy-done.26, bf16[8,256,704]{2,1,0:T(8,128)(2,1)S(1)} %copy-done.27, ...), custom_call_target="tpu_custom_call" | custom-call | flops 7381975040 | bytes 14942208 | tf_op jit(solution)/shard_map/cond/branch_1_fun/pallas_call | solution.py:602
  301.4 9.2 %branch_1_fun.22 = (bf16[256,2048]{1,0:T(8,128)(2,1)}, bf16[256,2048]{1,0:T(8,128)(2,1)}, bf16[256,2048]{1,0:T(8,128)(2,1)}, bf16[256,2048]{1,0:T(8,128)(2,1)}) custom-call(bf16[8,256,704]{2,1,0:T(8,128)(2,1)S(1)} %copy-done.25, bf16[8,256,704]{2,1,0:T(8,128)(2,1)S(1)} %copy-done.26, bf16[8,256,704]{2,1,0:T(8,128)(2,1)S(1)} %copy-done.27, ...), custom_call_target="tpu_custom_call" | custom-call | flops 7381975040 | bytes 14942208 | tf_op jit(solution)/shard_map/cond/branch_1_fun/pallas_call | solution.py:602
  311.0 31.9 %conditional.14 = (bf16[256,2048]{1,0:T(8,128)(2,1)S(1)}, bf16[256,2048]{1,0:T(8,128)(2,1)S(1)}, bf16[256,2048]{1,0:T(8,128)(2,1)S(1)}, bf16[704,2048]{1,0:T(8,128)(2,1)S(1)}) conditional(s32[]{:T(128)} %bitcast.54, () %tuple.149, (bf16[256,2048]{1,0:T(8,128)(2,1)S(1)}, bf16[256,2048]{1,0:T(8,128)(2,1)}, bf16[256,2048]{1,0:T(8,128)(2,1)S(1)}, ...), branch_computations={%region_7.8_spmd, %region_8.9_spmd} | conditional | flops 14681064 | bytes 49808684 | solution.py:142
  312.1 12.2 %branch_1_fun.23 = bf16[704,2048]{1,0:T(8,128)(2,1)S(1)} custom-call(bf16[2048,704]{1,0:T(8,128)(2,1)} %bitcast.202, bf16[256,2048]{1,0:T(8,128)(2,1)} %get-tuple-element.330.refs_1_, bf16[256,2048]{1,0:T(8,128)(2,1)} %get-tuple-element.331.refs_2_, bf16[256,2048]{1,0:T(8,128)(2,1)} %get-tuple-element.332.refs_3_, ...), custom_call_target="tpu_custom_call" | custom-call | flops 1000 | bytes 1000 | tf_op jit(solution)/shard_map/cond/branch_1_fun/pallas_call | solution.py:737
  329.2 11.0 %collective-permute-done.20 = bf16[128,2048]{1,0:T(8,128)(2,1)S(1)} collective-permute-done((bf16[128,2048]{1,0:T(8,128)(2,1)S(1)}, bf16[128,2048]{1,0:T(8,128)(2,1)S(1)}, u32[]{:S(2)}, u32[]{:S(2)}) %collective-permute-start.20) | collective-permute-done | bytes 524320 | tf_op jit(solution)/shard_map/cond/branch_1_fun/ppermute | solution.py:42
  344.5 28.4 %conditional.15 = (f32[256,2048]{1,0:T(8,128)}, bf16[2048]{0:T(1024)(128)(2,1)S(1)}, bf16[704,2048]{1,0:T(8,128)(2,1)}) conditional(s32[]{:T(128)} %bitcast.54, () %tuple.148, (f32[256]{0:T(256)S(1)}, f32[256,1]{0,1:T(1,128)S(1)}, f32[256,1]{0,1:T(1,128)S(1)}, bf16[8,256,704]{2,1,0:T(8,128)(2,1)}, bf16[256,2048]{1,0:T(8,128)(2,1)S(1)}, ...), branch_computations={%region_9.10_spmd, %region_10.13_spmd} | conditional | flops 10487784 | bytes 38843528 | solution.py:142
  346.5 13.0 %branch_1_fun.24 = bf16[704,2048]{1,0:T(8,128)(2,1)} custom-call(bf16[2048,704]{1,0:T(8,128)(2,1)} %bitcast.204, bf16[256,2048]{1,0:T(8,128)(2,1)S(1)} %get-tuple-element.344.refs_1_, bf16[256,2048]{1,0:T(8,128)(2,1)} %get-tuple-element.345.refs_2_, bf16[256,2048]{1,0:T(8,128)(2,1)} %get-tuple-element.346.refs_3_, ...), custom_call_target="tpu_custom_call" | custom-call | flops 1000 | bytes 1000 | tf_op jit(solution)/shard_map/cond/branch_1_fun/pallas_call | solution.py:737
  359.5 9.3 %collective-permute-done.11 = bf16[256,2048]{1,0:T(8,128)(2,1)S(1)} collective-permute-done((bf16[256,2048]{1,0:T(8,128)(2,1)S(1)}, bf16[256,2048]{1,0:T(8,128)(2,1)S(1)}, u32[]{:S(2)}, u32[]{:S(2)}) %collective-permute-start.11) | collective-permute-done | bytes 1048608 | tf_op jit(solution)/shard_map/cond/branch_1_fun/ppermute | solution.py:42
  372.9 12.3 %all-reduce.8.cloned.1.call-done = bf16[704,2048]{1,0:T(8,128)(2,1)} async-done(((bf16[704,2048]{1,0:T(8,128)(2,1)}), bf16[704,2048]{1,0:T(8,128)(2,1)}) %all-reduce.8.cloned.1.call-update) | async-done | bytes 2883600 | tf_op jit(solution)/shard_map/psum | solution.py:978
  385.2 32.6 %conditional.16 = (bf16[256,2048]{1,0:T(8,128)(2,1)}, bf16[256,2048]{1,0:T(8,128)(2,1)}, bf16[256,2048]{1,0:T(8,128)(2,1)}, bf16[256,2048]{1,0:T(8,128)(2,1)}, b...) conditional(s32[]{:T(128)} %bitcast.54, () %tuple.147, (f32[256,2048]{1,0:T(8,128)}, ...), branch_computations={%region_14.15_spmd, %region_15.16_spmd} | conditional | flops 525288 | bytes 28312828 | solution.py:142
  390.1 22.0 %collective-permute-done = bf16[256,2048]{1,0:T(8,128)(2,1)} collective-permute-done((bf16[256,2048]{1,0:T(8,128)(2,1)S(1)}, bf16[256,2048]{1,0:T(8,128)(2,1)}, u32[]{:S(2)}, u32[]{:S(2)}) %collective-permute-start) | collective-permute-done | bytes 1048608 | tf_op jit(solution)/shard_map/cond/branch_1_fun/ppermute | solution.py:42
  417.8 27.7 %conditional.17 = ((bf16[8,2,128,256]{3,2,1,0:T(8,128)(2,1)S(1)}, bf16[256,2048]{1,0:T(8,128)(2,1)})) conditional(s32[]{:T(128)} %bitcast.54, () %tuple.146, (bf16[256,2048]{1,0:T(8,128)(2,1)}, bf16[256,2048]{1,0:T(8,128)(2,1)}, bf16[256,2048]{1,0:T(8,128)(2,1)}, bf16[256,2048]{1,0:T(8,128)(2,1)}, bf16[8,2,128,256]{3,2,1,0:T(8,128)(2,1)S(1)}, ...), branch_computations={%region_16.17_spmd, %region_17.18_spmd} | conditional | flops 3000 | bytes 16780372 | solution.py:142
  422.4 10.8 %collective-permute-done.5 = bf16[128,2048]{1,0:T(8,128)(2,1)S(1)} collective-permute-done((bf16[128,2048]{1,0:T(8,128)(2,1)S(1)}, bf16[128,2048]{1,0:T(8,128)(2,1)S(1)}, u32[]{:S(2)}, u32[]{:S(2)}) %collective-permute-start.5) | collective-permute-done | bytes 524320 | tf_op jit(solution)/shard_map/cond/branch_1_fun/ppermute | solution.py:42
  435.7 3.4 branch_1_fun.26
  439.1 3.5 branch_1_fun.27
  445.5 4.0 copy.123
  449.4 4.6 all-to-all-start.3
  454.0 49.2 %conditional.18 = (bf16[256,2048]{1,0:T(8,128)(2,1)}, bf16[256,2048]{1,0:T(8,128)(2,1)}, bf16[256,2048]{1,0:T(8,128)(2,1)}, bf16[256,2048]{1,0:T(8,128)(2,1)}, b...) conditional(s32[]{:T(128)} %bitcast.54, () %tuple.126, ...), branch_computations={%region_18.19_spmd, %region_19.20_spmd} | conditional | flops 14683064 | bytes 91754064 | solution.py:142
  455.4 11.7 %branch_1_fun.29 = bf16[8,2,128,512]{3,2,1,0:T(8,128)(2,1)S(1)} custom-call(s32[2]{0:T(128)S(1)} %get-tuple-element.388.lengths_ref, s32[2]{0:T(128)S(1)} %get-tuple-element.389.key_ref, bf16[8,2,128,256]{3,2,1,0:T(8,128)(2,1)} %get-tuple-element.390.q_ref, bf16[8,2,128,256]{3,2,1,0:T(8,128)(2,1)} %get-tuple-element.391.up_ref, ...), custom_call_target="tpu_custom_call" | custom-call | flops 1000 | bytes 1000 | tf_op jit(solution)/shard_map/cond/branch_1_fun/pallas_call | solution.py:388
  468.4 7.0 branch_1_fun.30
  475.4 7.9 %branch_1_fun.31 = bf16[2048,512]{1,0:T(8,128)(2,1)} custom-call(bf16[256,2048]{1,0:T(8,128)(2,1)S(1)} %copy-done.39, bf16[256,2048]{1,0:T(8,128)(2,1)S(1)} %copy-done.40, bf16[256,2048]{1,0:T(8,128)(2,1)S(1)} %copy-done.41, bf16[256,2048]{1,0:T(8,128)(2,1)S(1)} %copy-done.42, bf16[256,2048]{1,0:T(8,128)(2,1)S(1)} %copy-done.43, ...), custom_call_target="tpu_custom_call" | custom-call | flops 1000 | bytes 1000 | tf_op jit(solution)/shard_map/cond/branch_1_fun/pallas_call | solution.py:703
  494.7 4.6 collective-permute-done.26
  505.5 4.5 all-to-all-start.4
  512.7 41.0 %conditional.19 = (bf16[256,2048]{1,0:T(8,128)(2,1)}, bf16[256,2048]{1,0:T(8,128)(2,1)}, bf16[256,2048]{1,0:T(8,128)(2,1)}, bf16[256,256]{1,0:T(8,128)(2,1)S(1)}) conditional(s32[]{:T(128)} %bitcast.54, () %tuple.159, (bf16[256,2048]{1,0:T(8,128)(2,1)}, bf16[256,2048]{1,0:T(8,128)(2,1)}, bf16[256,2048]{1,0:T(8,128)(2,1)}, ...), branch_computations={%region_20.21_spmd, %region_21.22_spmd} | conditional | flops 17432584 | bytes 64094760 | solution.py:142
  522.0 8.1 %collective-permute-done.36 = bf16[2,256,256]{2,1,0:T(8,128)(2,1)S(1)} collective-permute-done((bf16[2,256,256]{2,1,0:T(8,128)(2,1)}, bf16[2,256,256]{2,1,0:T(8,128)(2,1)S(1)}, u32[]{:S(2)}, u32[]{:S(2)}) %collective-permute-start.36) | collective-permute-done | bytes 262176 | tf_op jit(solution)/shard_map/cond/branch_1_fun/ppermute | solution.py:42
  533.2 3.2 collective-permute-done.37
  546.5 4.6 collective-permute-done.32
  553.7 37.5 %conditional.20 = (bf16[272,256]{1,0:T(8,128)(2,1)S(1)}, f32[2,128,2048]{2,1,0:T(8,128)}) conditional(s32[]{:T(128)} %bitcast.54, () %tuple.158, (bf16[256,2048]{1,0:T(8,128)(2,1)}, bf16[256,2048]{1,0:T(8,128)(2,1)}, bf16[256,2048]{1,0:T(8,128)(2,1)}, f32[2,128,2048]{2,1,0:T(8,128)}, f32[256,1]{0,1:T(1,128)S(1)}, ...), branch_computations={%region_22.23_spmd, %region_23.0_spmd} | conditional | flops 11987720 | bytes 29377868 | solution.py:142
  558.7 18.4 %collective-permute-done.13 = bf16[256,2048]{1,0:T(8,128)(2,1)S(1)} collective-permute-done((bf16[256,2048]{1,0:T(8,128)(2,1)}, bf16[256,2048]{1,0:T(8,128)(2,1)S(1)}, u32[]{:S(2)}, u32[]{:S(2)}) %collective-permute-start.13) | collective-permute-done | bytes 1048608 | tf_op jit(solution)/shard_map/cond/branch_1_fun/ppermute | solution.py:42
  587.7 3.5 fusion.18
  593.5 71.0 %conditional.21 = (f32[256,5632]{1,0:T(8,128)}, f32[256,5632]{1,0:T(8,128)}, f32[704,2048]{1,0:T(8,128)}, bf16[2,128,2048]{2,1,0:T(8,128)(2,1)S(1)}) conditional(s32[]{:T(128)} %bitcast.54, () %tuple.125, (bf16[8,704,256]{2,1,0:T(8,128)(2,1)}, bf16[704,2048]{1,0:T(8,128)(2,1)}, bf16[704,2048]{1,0:T(8,128)(2,1)}, bf16[256,2048]{1,0:T(8,128)(2,1)}, ...), branch_computations={%region_29.30_spmd, %region_30.31_spmd} | conditional | flops 6162384 | bytes 49285244 | solution.py:142
  593.5 3.6 copy.122
  597.1 4.4 all-to-all-start
  604.9 4.7 branch_1_fun.32
  609.7 3.3 convert_element_type.420
  613.0 45.0 %collective-permute-done.9 = bf16[256,2048]{1,0:T(8,128)(2,1)S(1)} collective-permute-done((bf16[256,2048]{1,0:T(8,128)(2,1)}, bf16[256,2048]{1,0:T(8,128)(2,1)S(1)}, u32[]{:S(2)}, u32[]{:S(2)}) %collective-permute-start.9) | collective-permute-done | bytes 1048608 | tf_op jit(solution)/shard_map/cond/branch_1_fun/ppermute | solution.py:42
  659.9 4.6 branch_1_fun.33
  664.5 23.5 %all-reduce.10.cloned.1.call-done = (bf16[256,2048]{1,0:T(8,128)(2,1)}, bf16[2048,256]{1,0:T(8,128)(2,1)}, bf16[272,256]{1,0:T(8,128)(2,1)}) async-done(((bf16[256,2048]{1,0:T(8,128)(2,1)}, bf16[2048,256]{1,0:T(8,128)(2,1)}, bf16[272,256]{1,0:T(8,128)(2,1)}), (bf16[256,2048]{1,0:T(8,128)(2,1)}, bf16[2048,256]{1,0:T(8,128)(2,1)}, bf16[272,256]{1,0:T(8,128)(2,1)})) %all-reduce.10.cloned.1.call-update) | async-done | bytes 2236432 | tf_op jit(solution)/shard_map/psum | solution.py:1058
  (386 shorter events, 190.6 us)
Async XLA Ops:
  7.2 48.0 %collective-permute-start.38 = (bf16[256,2048]{1,0:T(8,128)(2,1)}, bf16[256,2048]{1,0:T(8,128)(2,1)S(1)}, u32[]{:S(2)}, u32[]{:S(2)}) collective-permute-start(bf16[256,2048]{1,0:T(8,128)(2,1)} %bitcast.191), channel_id=1, source_target_pairs={{0,2},{1,3},{2,0},{3,1},{4,6},{5,7},{6,4},{7,5},{8,10},{9,11},{10,... | collective-permute-start | bytes 3145736 | tf_op jit(solution)/shard_map/ppermute | solution.py:42
  10.2 45.0 %collective-permute-start.39 = (bf16[256,2048]{1,0:T(8,128)(2,1)}, bf16[256,2048]{1,0:T(8,128)(2,1)S(1)}, u32[]{:S(2)}, u32[]{:S(2)}) collective-permute-start(bf16[256,2048]{1,0:T(8,128)(2,1)} %bitcast.192), channel_id=1, source_target_pairs={{0,4},{1,5},{2,6},{3,7},{4,0},{5,1},{6,2},{7,3},{8,12},{9,13},{10,... | collective-permute-start | bytes 3145736 | tf_op jit(solution)/shard_map/ppermute | solution.py:42
  11.7 72.8 %collective-permute-start.48 = (bf16[256,2048]{1,0:T(8,128)(2,1)}, bf16[256,2048]{1,0:T(8,128)(2,1)}, u32[]{:S(2)}, u32[]{:S(2)}) collective-permute-start(bf16[256,2048]{1,0:T(8,128)(2,1)} %bitcast.193), channel_id=1, source_target_pairs={{0,1},{1,0},{2,3},{3,2},{4,5},{5,4},{6,7},{7,6},{8,9},{9,8},{10,11... | collective-permute-start | bytes 3145736 | tf_op jit(solution)/shard_map/ppermute | solution.py:42
  13.9 29.0 %collective-permute-start.43 = (bf16[272,256]{1,0:T(8,128)(2,1)S(1)}, bf16[272,256]{1,0:T(8,128)(2,1)S(1)}, u32[]{:S(2)}, u32[]{:S(2)}) collective-permute-start(bf16[272,256]{1,0:T(8,128)(2,1)S(1)} %pad_maximum_fusion.14), channel_id=1, source_target_pairs={{0,4},{1,5},{2,6},{3,7},{4,0},{5,1},{6,2},{7,3},{8,12},{9,13},{10,... | collective-permute-start | bytes 417800 | tf_op jit(solution)/shard_map/ppermute | solution.py:42
  20.1 41.3 %all-to-all-start.1 = ((bf16[8,64,1408]{2,1,0:T(8,128)(2,1)}), bf16[8,64,1408]{2,1,0:T(8,128)(2,1)}, u32[]{:S(2)}, u32[]{:S(2)}) async-start(bf16[8,64,1408]{2,1,0:T(8,128)(2,1)} %shard_map.229), calls=%async_computation.1 | async-start | bytes 2883584 | tf_op jit(solution)/shard_map/all_to_all | solution.py:847
  43.1 12.0 %collective-permute-start.44 = (bf16[2,272,256]{2,1,0:T(8,128)(2,1)S(1)}, bf16[2,272,256]{2,1,0:T(8,128)(2,1)S(1)}, u32[]{:S(2)}, u32[]{:S(2)}) collective-permute-start(bf16[2,272,256]{2,1,0:T(8,128)(2,1)S(1)} %pad_maximum_fusion.13), channel_id=1, source_target_pairs={{0,2},{1,3},{2,0},{3,1},{4,6},{5,7},{6,4},{7,5},{8,10},{9,11},{10,... | collective-permute-start | bytes 835592 | tf_op jit(solution)/shard_map/ppermute | solution.py:42
  56.0 14.0 %collective-permute-start.40 = (bf16[128,2048]{1,0:T(8,128)(2,1)}, bf16[128,2048]{1,0:T(8,128)(2,1)}, u32[]{:S(2)}, u32[]{:S(2)}) collective-permute-start(bf16[128,2048]{1,0:T(8,128)(2,1)} %slice.182), channel_id=1, source_target_pairs={{0,4},{1,5},{2,6},{3,7},{4,0},{5,1},{6,2},{7,3},{8,12},{9,13},{10,... | collective-permute-start | bytes 1572872 | tf_op jit(solution)/shard_map/ppermute | solution.py:42
  58.6 12.8 %collective-permute-start.41 = (bf16[128,2048]{1,0:T(8,128)(2,1)}, bf16[128,2048]{1,0:T(8,128)(2,1)}, u32[]{:S(2)}, u32[]{:S(2)}) collective-permute-start(bf16[128,2048]{1,0:T(8,128)(2,1)} %slice.183), channel_id=1, source_target_pairs={{0,2},{1,3},{2,0},{3,1},{4,6},{5,7},{6,4},{7,5},{8,10},{9,11},{10,... | collective-permute-start | bytes 1572872 | tf_op jit(solution)/shard_map/ppermute | solution.py:42
  61.0 14.2 %collective-permute-start.45 = (bf16[2,2,272,256]{3,2,1,0:T(8,128)(2,1)}, bf16[2,2,272,256]{3,2,1,0:T(8,128)(2,1)}, u32[]{:S(2)}, u32[]{:S(2)}) collective-permute-start(bf16[2,2,272,256]{3,2,1,0:T(8,128)(2,1)} %pad_maximum_fusion.10), channel_id=1, source_target_pairs={{0,1},{1,0},{2,3},{3,2},{4,5},{5,4},{6,7},{7,6},{8,9},{9,8},{10,11... | collective-permute-start | bytes 1671176 | tf_op jit(solution)/shard_map/ppermute | solution.py:42
  61.0 34.7 %collective-permute-start.46 = (bf16[256,2048]{1,0:T(8,128)(2,1)S(1)}, bf16[256,2048]{1,0:T(8,128)(2,1)}, u32[]{:S(2)}, u32[]{:S(2)}) collective-permute-start(bf16[256,2048]{1,0:T(8,128)(2,1)S(1)} %collective-permute-done.39.a_ref), channel_id=1, source_target_pairs={{0,1},{1,0},{2,3},{3,2},{4,5},{5,4},{6,7},{7,6},{8,9},{9,8},{10,11... | collective-permute-start | bytes 3145736 | tf_op jit(solution)/shard_map/ppermute | solution.py:42
  65.7 20.2 %all-to-all-start.2 = ((bf16[256,8,256]{2,0,1:T(8,128)(2,1)}), bf16[256,8,256]{2,0,1:T(8,128)(2,1)}, u32[]{:S(2)}, u32[]{:S(2)}) async-start(bf16[256,8,256]{2,0,1:T(8,128)(2,1)} %bitcast.214), calls=%async_computation.2 | async-start | bytes 2097152 | tf_op jit(solution)/shard_map/all_to_all | solution.py:132
  69.9 120.5 %all-gather.3.cloned.1.call-start = ((), (), s32[]{:S(2)}) async-start(), calls=%async_computation.6 | async-start | bytes 7208960 | tf_op jit(solution)/shard_map/all_gather | solution.py:849
  70.0 21.0 %collective-permute-start.47 = (bf16[256,2048]{1,0:T(8,128)(2,1)S(1)}, bf16[256,2048]{1,0:T(8,128)(2,1)}, u32[]{:S(2)}, u32[]{:S(2)}) collective-permute-start(bf16[256,2048]{1,0:T(8,128)(2,1)S(1)} %collective-permute-done.38.a_ref), channel_id=1, source_target_pairs={{0,1},{1,0},{2,3},{3,2},{4,5},{5,4},{6,7},{7,6},{8,9},{9,8},{10,11... | collective-permute-start | bytes 3145736 | tf_op jit(solution)/shard_map/ppermute | solution.py:42
  73.6 33.3 %collective-permute-start.50 = (bf16[256,2048]{1,0:T(8,128)(2,1)}, bf16[256,2048]{1,0:T(8,128)(2,1)}, u32[]{:S(2)}, u32[]{:S(2)}) collective-permute-start(bf16[256,2048]{1,0:T(8,128)(2,1)} %get-tuple-element.619), channel_id=1, source_target_pairs={{0,2},{1,3},{2,0},{3,1},{4,6},{5,7},{6,4},{7,5},{8,10},{9,11},{10,... | collective-permute-start | bytes 3145736 | tf_op jit(solution)/shard_map/ppermute | solution.py:42
  75.2 31.7 %collective-permute-start.51 = (bf16[256,2048]{1,0:T(8,128)(2,1)}, bf16[256,2048]{1,0:T(8,128)(2,1)}, u32[]{:S(2)}, u32[]{:S(2)}) collective-permute-start(bf16[256,2048]{1,0:T(8,128)(2,1)} %get-tuple-element.619), channel_id=1, source_target_pairs={{0,4},{1,5},{2,6},{3,7},{4,0},{5,1},{6,2},{7,3},{8,12},{9,13},{10,... | collective-permute-start | bytes 3145736 | tf_op jit(solution)/shard_map/ppermute | solution.py:42
  81.9 303.3 %all-reduce.8.cloned.1.call-start = ((), (), s32[]{:S(2)}) async-start(), calls=%async_computation.5 | async-start | bytes 5767168 | tf_op jit(solution)/shard_map/psum | solution.py:978
  84.5 23.0 %collective-permute-start.49 = (bf16[256,2048]{1,0:T(8,128)(2,1)}, bf16[256,2048]{1,0:T(8,128)(2,1)}, u32[]{:S(2)}, u32[]{:S(2)}) collective-permute-start(bf16[256,2048]{1,0:T(8,128)(2,1)} %get-tuple-element.619), channel_id=1, source_target_pairs={{0,1},{1,0},{2,3},{3,2},{4,5},{5,4},{6,7},{7,6},{8,9},{9,8},{10,11... | collective-permute-start | bytes 3145736 | tf_op jit(solution)/shard_map/ppermute | solution.py:42
  107.4 9.5 %collective-permute-start.42 = (bf16[256,2048]{1,0:T(8,128)(2,1)S(1)}, bf16[256,2048]{1,0:T(8,128)(2,1)S(1)}, u32[]{:S(2)}, u32[]{:S(2)}) collective-permute-start(bf16[256,2048]{1,0:T(8,128)(2,1)S(1)} %copy-done.5), channel_id=1, source_target_pairs={{0,1},{1,0},{2,3},{3,2},{4,5},{5,4},{6,7},{7,6},{8,9},{9,8},{10,11... | collective-permute-start | bytes 3145736 | tf_op jit(solution)/shard_map/ppermute | solution.py:42
  113.7 17.1 %collective-permute-start.54 = (bf16[128,2048]{1,0:T(8,128)(2,1)S(1)}, bf16[128,2048]{1,0:T(8,128)(2,1)S(1)}, u32[]{:S(2)}, u32[]{:S(2)}) collective-permute-start(bf16[128,2048]{1,0:T(8,128)(2,1)S(1)} %slice.187), channel_id=1, source_target_pairs={{0,4},{1,5},{2,6},{3,7},{4,0},{5,1},{6,2},{7,3},{8,12},{9,13},{10,... | collective-permute-start | bytes 1572872 | tf_op jit(solution)/shard_map/ppermute | solution.py:42
  116.3 14.5 %collective-permute-start.55 = (bf16[128,2048]{1,0:T(8,128)(2,1)S(1)}, bf16[128,2048]{1,0:T(8,128)(2,1)S(1)}, u32[]{:S(2)}, u32[]{:S(2)}) collective-permute-start(bf16[128,2048]{1,0:T(8,128)(2,1)S(1)} %slice.188), channel_id=1, source_target_pairs={{0,2},{1,3},{2,0},{3,1},{4,6},{5,7},{6,4},{7,5},{8,10},{9,11},{10,... | collective-permute-start | bytes 1572872 | tf_op jit(solution)/shard_map/ppermute | solution.py:42
  136.8 52.7 %collective-permute-start.56 = (bf16[256,2048]{1,0:T(8,128)(2,1)S(1)}, bf16[256,2048]{1,0:T(8,128)(2,1)S(1)}, u32[]{:S(2)}, u32[]{:S(2)}) collective-permute-start(bf16[256,2048]{1,0:T(8,128)(2,1)S(1)} %get-tuple-element.628), channel_id=1, source_target_pairs={{0,1},{1,0},{2,3},{3,2},{4,5},{5,4},{6,7},{7,6},{8,9},{9,8},{10,11... | collective-permute-start | bytes 3145736 | tf_op jit(solution)/shard_map/ppermute | solution.py:42
  140.8 14.0 %collective-permute-start.59 = (bf16[128,2048]{1,0:T(8,128)(2,1)S(1)}, bf16[128,2048]{1,0:T(8,128)(2,1)S(1)}, u32[]{:S(2)}, u32[]{:S(2)}) collective-permute-start(bf16[128,2048]{1,0:T(8,128)(2,1)S(1)} %get-tuple-element.790), channel_id=1, source_target_pairs={{0,2},{1,3},{2,0},{3,1},{4,6},{5,7},{6,4},{7,5},{8,10},{9,11},{10,... | collective-permute-start | bytes 1572872 | tf_op jit(solution)/shard_map/ppermute | solution.py:42
  142.4 13.7 %collective-permute-start.60 = (bf16[128,2048]{1,0:T(8,128)(2,1)S(1)}, bf16[128,2048]{1,0:T(8,128)(2,1)S(1)}, u32[]{:S(2)}, u32[]{:S(2)}) collective-permute-start(bf16[128,2048]{1,0:T(8,128)(2,1)S(1)} %get-tuple-element.789), channel_id=1, source_target_pairs={{0,4},{1,5},{2,6},{3,7},{4,0},{5,1},{6,2},{7,3},{8,12},{9,13},{10,... | collective-permute-start | bytes 1572872 | tf_op jit(solution)/shard_map/ppermute | solution.py:42
  156.3 33.6 %collective-permute-start.63 = (bf16[256,2048]{1,0:T(8,128)(2,1)S(1)}, bf16[256,2048]{1,0:T(8,128)(2,1)S(1)}, u32[]{:S(2)}, u32[]{:S(2)}) collective-permute-start(bf16[256,2048]{1,0:T(8,128)(2,1)S(1)} %pad_maximum_fusion.9), channel_id=1, source_target_pairs={{0,4},{1,5},{2,6},{3,7},{4,0},{5,1},{6,2},{7,3},{8,12},{9,13},{10,... | collective-permute-start | bytes 3145736 | tf_op jit(solution)/shard_map/ppermute | solution.py:42
  157.1 32.7 %collective-permute-start.61 = (bf16[256,2048]{1,0:T(8,128)(2,1)S(1)}, bf16[256,2048]{1,0:T(8,128)(2,1)S(1)}, u32[]{:S(2)}, u32[]{:S(2)}) collective-permute-start(bf16[256,2048]{1,0:T(8,128)(2,1)S(1)} %pad_maximum_fusion.8), channel_id=1, source_target_pairs={{0,2},{1,3},{2,0},{3,1},{4,6},{5,7},{6,4},{7,5},{8,10},{9,11},{10,... | collective-permute-start | bytes 3145736 | tf_op jit(solution)/shard_map/ppermute | solution.py:42
  193.9 25.7 %collective-permute-start.64 = (bf16[256,2048]{1,0:T(8,128)(2,1)S(1)}, bf16[256,2048]{1,0:T(8,128)(2,1)}, u32[]{:S(2)}, u32[]{:S(2)}) collective-permute-start(bf16[256,2048]{1,0:T(8,128)(2,1)S(1)} %multiply_convert_fusion.refs_1_), channel_id=1, source_target_pairs={{0,2},{1,3},{2,0},{3,1},{4,6},{5,7},{6,4},{7,5},{8,10},{9,11},{10,... | collective-permute-start | bytes 3145736 | tf_op jit(solution)/shard_map/ppermute | solution.py:42
  194.5 25.3 %collective-permute-start.65 = (bf16[256,2048]{1,0:T(8,128)(2,1)S(1)}, bf16[256,2048]{1,0:T(8,128)(2,1)}, u32[]{:S(2)}, u32[]{:S(2)}) collective-permute-start(bf16[256,2048]{1,0:T(8,128)(2,1)S(1)} %multiply_convert_fusion.refs_1_), channel_id=1, source_target_pairs={{0,4},{1,5},{2,6},{3,7},{4,0},{5,1},{6,2},{7,3},{8,12},{9,13},{10,... | collective-permute-start | bytes 3145736 | tf_op jit(solution)/shard_map/ppermute | solution.py:42
  224.2 18.9 %collective-permute-start.67 = (bf16[128,2048]{1,0:T(8,128)(2,1)}, bf16[128,2048]{1,0:T(8,128)(2,1)}, u32[]{:S(2)}, u32[]{:S(2)}) collective-permute-start(bf16[128,2048]{1,0:T(8,128)(2,1)} %slice.196), channel_id=1, source_target_pairs={{0,4},{1,5},{2,6},{3,7},{4,0},{5,1},{6,2},{7,3},{8,12},{9,13},{10,... | collective-permute-start | bytes 1572872 | tf_op jit(solution)/shard_map/ppermute | solution.py:42
  225.6 17.4 %collective-permute-start.68 = (bf16[128,2048]{1,0:T(8,128)(2,1)}, bf16[128,2048]{1,0:T(8,128)(2,1)}, u32[]{:S(2)}, u32[]{:S(2)}) collective-permute-start(bf16[128,2048]{1,0:T(8,128)(2,1)} %slice.197), channel_id=1, source_target_pairs={{0,2},{1,3},{2,0},{3,1},{4,6},{5,7},{6,4},{7,5},{8,10},{9,11},{10,... | collective-permute-start | bytes 1572872 | tf_op jit(solution)/shard_map/ppermute | solution.py:42
  226.2 19.6 %collective-permute-start.72 = (bf16[256,2048]{1,0:T(8,128)(2,1)}, bf16[256,2048]{1,0:T(8,128)(2,1)}, u32[]{:S(2)}, u32[]{:S(2)}) collective-permute-start(bf16[256,2048]{1,0:T(8,128)(2,1)} %pad_maximum_fusion.7.refs_2_), channel_id=1, source_target_pairs={{0,1},{1,0},{2,3},{3,2},{4,5},{5,4},{6,7},{7,6},{8,9},{9,8},{10,11... | collective-permute-start | bytes 3145736 | tf_op jit(solution)/shard_map/ppermute | solution.py:42
  272.1 321.4 %all-reduce.12.cloned.1.call-start = ((), (), s32[]{:S(2)}) async-start(), calls=%async_computation.8 | async-start | bytes 11534336 | tf_op jit(solution)/shard_map/psum | solution.py:1001
  311.0 13.3 %collective-permute-start.19 = (bf16[256,2048]{1,0:T(8,128)(2,1)}, bf16[256,2048]{1,0:T(8,128)(2,1)S(1)}, u32[]{:S(2)}, u32[]{:S(2)}) collective-permute-start(bf16[256,2048]{1,0:T(8,128)(2,1)} %get-tuple-element.324), channel_id=1, source_target_pairs={{0,1},{1,0},{2,3},{3,2},{4,5},{5,4},{6,7},{7,6},{8,9},{9,8},{10,11... | collective-permute-start | bytes 3145736 | tf_op jit(solution)/shard_map/cond/branch_1_fun/ppermute | solution.py:42
  311.4 16.5 %collective-permute-start.18 = (bf16[256,2048]{1,0:T(8,128)(2,1)}, bf16[256,2048]{1,0:T(8,128)(2,1)S(1)}, u32[]{:S(2)}, u32[]{:S(2)}) collective-permute-start(bf16[256,2048]{1,0:T(8,128)(2,1)} %get-tuple-element.322), channel_id=1, source_target_pairs={{0,1},{1,0},{2,3},{3,2},{4,5},{5,4},{6,7},{7,6},{8,9},{9,8},{10,11... | collective-permute-start | bytes 3145736 | tf_op jit(solution)/shard_map/cond/branch_1_fun/ppermute | solution.py:42
  311.6 17.3 %collective-permute-start.17 = (bf16[256,2048]{1,0:T(8,128)(2,1)}, bf16[256,2048]{1,0:T(8,128)(2,1)S(1)}, u32[]{:S(2)}, u32[]{:S(2)}) collective-permute-start(bf16[256,2048]{1,0:T(8,128)(2,1)} %get-tuple-element.320), channel_id=1, source_target_pairs={{0,1},{1,0},{2,3},{3,2},{4,5},{5,4},{6,7},{7,6},{8,9},{9,8},{10,11... | collective-permute-start | bytes 3145736 | tf_op jit(solution)/shard_map/cond/branch_1_fun/ppermute | solution.py:42
  312.0 16.5 %collective-permute-start.22 = (bf16[256,2048]{1,0:T(8,128)(2,1)}, bf16[256,2048]{1,0:T(8,128)(2,1)S(1)}, u32[]{:S(2)}, u32[]{:S(2)}) collective-permute-start(bf16[256,2048]{1,0:T(8,128)(2,1)} %get-tuple-element.327), channel_id=1, source_target_pairs={{0,1},{1,0},{2,3},{3,2},{4,5},{5,4},{6,7},{7,6},{8,9},{9,8},{10,11... | collective-permute-start | bytes 3145736 | tf_op jit(solution)/shard_map/cond/branch_1_fun/ppermute | solution.py:42
  326.0 14.2 %collective-permute-start.20 = (bf16[128,2048]{1,0:T(8,128)(2,1)S(1)}, bf16[128,2048]{1,0:T(8,128)(2,1)S(1)}, u32[]{:S(2)}, u32[]{:S(2)}) collective-permute-start(bf16[128,2048]{1,0:T(8,128)(2,1)S(1)} %get-tuple-element.771), channel_id=1, source_target_pairs={{0,2},{1,3},{2,0},{3,1},{4,6},{5,7},{6,4},{7,5},{8,10},{9,11},{10,... | collective-permute-start | bytes 1572872 | tf_op jit(solution)/shard_map/cond/branch_1_fun/ppermute | solution.py:42
  327.6 13.8 %collective-permute-start.21 = (bf16[128,2048]{1,0:T(8,128)(2,1)S(1)}, bf16[128,2048]{1,0:T(8,128)(2,1)S(1)}, u32[]{:S(2)}, u32[]{:S(2)}) collective-permute-start(bf16[128,2048]{1,0:T(8,128)(2,1)S(1)} %get-tuple-element.770), channel_id=1, source_target_pairs={{0,4},{1,5},{2,6},{3,7},{4,0},{5,1},{6,2},{7,3},{8,12},{9,13},{10,... | collective-permute-start | bytes 1572872 | tf_op jit(solution)/shard_map/cond/branch_1_fun/ppermute | solution.py:42
  344.5 24.3 %collective-permute-start.11 = (bf16[256,2048]{1,0:T(8,128)(2,1)S(1)}, bf16[256,2048]{1,0:T(8,128)(2,1)S(1)}, u32[]{:S(2)}, u32[]{:S(2)}) collective-permute-start(bf16[256,2048]{1,0:T(8,128)(2,1)S(1)} %get-tuple-element.354), channel_id=1, source_target_pairs={{0,4},{1,5},{2,6},{3,7},{4,0},{5,1},{6,2},{7,3},{8,12},{9,13},{10,... | collective-permute-start | bytes 3145736 | tf_op jit(solution)/shard_map/cond/branch_1_fun/ppermute | solution.py:42
  345.1 24.3 %collective-permute-start.10 = (bf16[256,2048]{1,0:T(8,128)(2,1)S(1)}, bf16[256,2048]{1,0:T(8,128)(2,1)S(1)}, u32[]{:S(2)}, u32[]{:S(2)}) collective-permute-start(bf16[256,2048]{1,0:T(8,128)(2,1)S(1)} %get-tuple-element.353), channel_id=1, source_target_pairs={{0,2},{1,3},{2,0},{3,1},{4,6},{5,7},{6,4},{7,5},{8,10},{9,11},{10,... | collective-permute-start | bytes 3145736 | tf_op jit(solution)/shard_map/cond/branch_1_fun/ppermute | solution.py:42
  387.1 25.0 %collective-permute-start = (bf16[256,2048]{1,0:T(8,128)(2,1)S(1)}, bf16[256,2048]{1,0:T(8,128)(2,1)}, u32[]{:S(2)}, u32[]{:S(2)}) collective-permute-start(bf16[256,2048]{1,0:T(8,128)(2,1)S(1)} %convert_element_type.354.a_ref), channel_id=1, source_target_pairs={{0,2},{1,3},{2,0},{3,1},{4,6},{5,7},{6,4},{7,5},{8,10},{9,11},{10,... | collective-permute-start | bytes 3145736 | tf_op jit(solution)/shard_map/cond/branch_1_fun/ppermute | solution.py:42
  388.6 24.7 %collective-permute-start.1 = (bf16[256,2048]{1,0:T(8,128)(2,1)S(1)}, bf16[256,2048]{1,0:T(8,128)(2,1)}, u32[]{:S(2)}, u32[]{:S(2)}) collective-permute-start(bf16[256,2048]{1,0:T(8,128)(2,1)S(1)} %convert_element_type.354.a_ref), channel_id=1, source_target_pairs={{0,4},{1,5},{2,6},{3,7},{4,0},{5,1},{6,2},{7,3},{8,12},{9,13},{10,... | collective-permute-start | bytes 3145736 | tf_op jit(solution)/shard_map/cond/branch_1_fun/ppermute | solution.py:42
  390.1 23.7 %collective-permute-start.4 = (bf16[256,2048]{1,0:T(8,128)(2,1)S(1)}, bf16[256,2048]{1,0:T(8,128)(2,1)S(1)}, u32[]{:S(2)}, u32[]{:S(2)}) collective-permute-start(bf16[256,2048]{1,0:T(8,128)(2,1)S(1)} %convert_element_type.354.a_ref), channel_id=1, source_target_pairs={{0,1},{1,0},{2,3},{3,2},{4,5},{5,4},{6,7},{7,6},{8,9},{9,8},{10,11... | collective-permute-start | bytes 3145736 | tf_op jit(solution)/shard_map/cond/branch_1_fun/ppermute | solution.py:42
  419.1 14.0 %collective-permute-start.5 = (bf16[128,2048]{1,0:T(8,128)(2,1)S(1)}, bf16[128,2048]{1,0:T(8,128)(2,1)S(1)}, u32[]{:S(2)}, u32[]{:S(2)}) collective-permute-start(bf16[128,2048]{1,0:T(8,128)(2,1)S(1)} %slice.132), channel_id=1, source_target_pairs={{0,4},{1,5},{2,6},{3,7},{4,0},{5,1},{6,2},{7,3},{8,12},{9,13},{10,... | collective-permute-start | bytes 1572872 | tf_op jit(solution)/shard_map/cond/branch_1_fun/ppermute | solution.py:42
  421.8 13.7 %collective-permute-start.6 = (bf16[128,2048]{1,0:T(8,128)(2,1)S(1)}, bf16[128,2048]{1,0:T(8,128)(2,1)S(1)}, u32[]{:S(2)}, u32[]{:S(2)}) collective-permute-start(bf16[128,2048]{1,0:T(8,128)(2,1)S(1)} %slice.133), channel_id=1, source_target_pairs={{0,2},{1,3},{2,0},{3,1},{4,6},{5,7},{6,4},{7,5},{8,10},{9,11},{10,... | collective-permute-start | bytes 1572872 | tf_op jit(solution)/shard_map/cond/branch_1_fun/ppermute | solution.py:42
  449.4 53.7 %all-to-all-start.3 = ((bf16[8,704,256]{2,1,0:T(8,128)(2,1)}), bf16[8,704,256]{2,1,0:T(8,128)(2,1)}, u32[]{:S(2)}, u32[]{:S(2)}) async-start(bf16[8,704,256]{2,1,0:T(8,128)(2,1)} %bitcast.205), calls=%async_computation.3 | async-start | bytes 5767168 | tf_op jit(solution)/shard_map/all_to_all | solution.py:799
  454.3 29.1 %collective-permute-start.25 = (bf16[256,2048]{1,0:T(8,128)(2,1)}, bf16[256,2048]{1,0:T(8,128)(2,1)S(1)}, u32[]{:S(2)}, u32[]{:S(2)}) collective-permute-start(bf16[256,2048]{1,0:T(8,128)(2,1)} %get-tuple-element.383), channel_id=1, source_target_pairs={{0,1},{1,0},{2,3},{3,2},{4,5},{5,4},{6,7},{7,6},{8,9},{9,8},{10,11... | collective-permute-start | bytes 3145736 | tf_op jit(solution)/shard_map/cond/branch_1_fun/ppermute | solution.py:42
  454.8 36.9 %collective-permute-start.23 = (bf16[256,2048]{1,0:T(8,128)(2,1)}, bf16[256,2048]{1,0:T(8,128)(2,1)S(1)}, u32[]{:S(2)}, u32[]{:S(2)}) collective-permute-start(bf16[256,2048]{1,0:T(8,128)(2,1)} %get-tuple-element.379), channel_id=1, source_target_pairs={{0,1},{1,0},{2,3},{3,2},{4,5},{5,4},{6,7},{7,6},{8,9},{9,8},{10,11... | collective-permute-start | bytes 3145736 | tf_op jit(solution)/shard_map/cond/branch_1_fun/ppermute | solution.py:42
  454.9 33.5 %collective-permute-start.24 = (bf16[256,2048]{1,0:T(8,128)(2,1)}, bf16[256,2048]{1,0:T(8,128)(2,1)S(1)}, u32[]{:S(2)}, u32[]{:S(2)}) collective-permute-start(bf16[256,2048]{1,0:T(8,128)(2,1)} %get-tuple-element.381), channel_id=1, source_target_pairs={{0,1},{1,0},{2,3},{3,2},{4,5},{5,4},{6,7},{7,6},{8,9},{9,8},{10,11... | collective-permute-start | bytes 3145736 | tf_op jit(solution)/shard_map/cond/branch_1_fun/ppermute | solution.py:42
  455.3 34.8 %collective-permute-start.28 = (bf16[256,2048]{1,0:T(8,128)(2,1)}, bf16[256,2048]{1,0:T(8,128)(2,1)S(1)}, u32[]{:S(2)}, u32[]{:S(2)}) collective-permute-start(bf16[256,2048]{1,0:T(8,128)(2,1)} %get-tuple-element.386), channel_id=1, source_target_pairs={{0,1},{1,0},{2,3},{3,2},{4,5},{5,4},{6,7},{7,6},{8,9},{9,8},{10,11... | collective-permute-start | bytes 3145736 | tf_op jit(solution)/shard_map/cond/branch_1_fun/ppermute | solution.py:42
  485.0 14.3 %collective-permute-start.26 = (bf16[128,2048]{1,0:T(8,128)(2,1)S(1)}, bf16[128,2048]{1,0:T(8,128)(2,1)S(1)}, u32[]{:S(2)}, u32[]{:S(2)}) collective-permute-start(bf16[128,2048]{1,0:T(8,128)(2,1)S(1)} %get-tuple-element.775), channel_id=1, source_target_pairs={{0,2},{1,3},{2,0},{3,1},{4,6},{5,7},{6,4},{7,5},{8,10},{9,11},{10,... | collective-permute-start | bytes 1572872 | tf_op jit(solution)/shard_map/cond/branch_1_fun/ppermute | solution.py:42
  486.9 13.7 %collective-permute-start.27 = (bf16[128,2048]{1,0:T(8,128)(2,1)S(1)}, bf16[128,2048]{1,0:T(8,128)(2,1)S(1)}, u32[]{:S(2)}, u32[]{:S(2)}) collective-permute-start(bf16[128,2048]{1,0:T(8,128)(2,1)S(1)} %get-tuple-element.774), channel_id=1, source_target_pairs={{0,4},{1,5},{2,6},{3,7},{4,0},{5,1},{6,2},{7,3},{8,12},{9,13},{10,... | collective-permute-start | bytes 1572872 | tf_op jit(solution)/shard_map/cond/branch_1_fun/ppermute | solution.py:42
  505.5 85.8 %all-to-all-start.4 = ((bf16[8,256,256]{2,1,0:T(8,128)(2,1)}), bf16[8,256,256]{2,1,0:T(8,128)(2,1)}, u32[]{:S(2)}, u32[]{:S(2)}) async-start(bf16[8,256,256]{2,1,0:T(8,128)(2,1)} %bitcast.80), calls=%async_computation.4 | async-start | bytes 2097152 | tf_op jit(solution)/shard_map/all_to_all | solution.py:1036
  510.0 178.0 %all-reduce.10.cloned.1.call-start = ((), (), s32[]{:S(2)}) async-start(), calls=%async_computation.7 | async-start | bytes 4472832 | tf_op jit(solution)/shard_map/psum | solution.py:1058
  520.1 10.0 %collective-permute-start.36 = (bf16[2,256,256]{2,1,0:T(8,128)(2,1)}, bf16[2,256,256]{2,1,0:T(8,128)(2,1)S(1)}, u32[]{:S(2)}, u32[]{:S(2)}) collective-permute-start(bf16[2,256,256]{2,1,0:T(8,128)(2,1)} %fusion.10), channel_id=1, source_target_pairs={{0,2},{1,3},{2,0},{3,1},{4,6},{5,7},{6,4},{7,5},{8,10},{9,11},{10,... | collective-permute-start | bytes 786440 | tf_op jit(solution)/shard_map/cond/branch_1_fun/ppermute | solution.py:42
  522.0 14.5 %collective-permute-start.31 = (bf16[256,2048]{1,0:T(8,128)(2,1)}, bf16[256,2048]{1,0:T(8,128)(2,1)S(1)}, u32[]{:S(2)}, u32[]{:S(2)}) collective-permute-start(bf16[256,2048]{1,0:T(8,128)(2,1)} %get-tuple-element.421), channel_id=1, source_target_pairs={{0,1},{1,0},{2,3},{3,2},{4,5},{5,4},{6,7},{7,6},{8,9},{9,8},{10,11... | collective-permute-start | bytes 3145736 | tf_op jit(solution)/shard_map/cond/branch_1_fun/ppermute | solution.py:42
  532.7 10.8 %collective-permute-start.29 = (bf16[256,2048]{1,0:T(8,128)(2,1)}, bf16[256,2048]{1,0:T(8,128)(2,1)S(1)}, u32[]{:S(2)}, u32[]{:S(2)}) collective-permute-start(bf16[256,2048]{1,0:T(8,128)(2,1)} %get-tuple-element.417), channel_id=1, source_target_pairs={{0,1},{1,0},{2,3},{3,2},{4,5},{5,4},{6,7},{7,6},{8,9},{9,8},{10,11... | collective-permute-start | bytes 3145736 | tf_op jit(solution)/shard_map/cond/branch_1_fun/ppermute | solution.py:42
  533.2 8.6 %collective-permute-start.34 = (bf16[256,2048]{1,0:T(8,128)(2,1)}, bf16[256,2048]{1,0:T(8,128)(2,1)S(1)}, u32[]{:S(2)}, u32[]{:S(2)}) collective-permute-start(bf16[256,2048]{1,0:T(8,128)(2,1)} %get-tuple-element.424), channel_id=1, source_target_pairs={{0,1},{1,0},{2,3},{3,2},{4,5},{5,4},{6,7},{7,6},{8,9},{9,8},{10,11... | collective-permute-start | bytes 3145736 | tf_op jit(solution)/shard_map/cond/branch_1_fun/ppermute | solution.py:42
  538.2 12.9 %collective-permute-start.32 = (bf16[128,2048]{1,0:T(8,128)(2,1)S(1)}, bf16[128,2048]{1,0:T(8,128)(2,1)S(1)}, u32[]{:S(2)}, u32[]{:S(2)}) collective-permute-start(bf16[128,2048]{1,0:T(8,128)(2,1)S(1)} %get-tuple-element.777), channel_id=1, source_target_pairs={{0,2},{1,3},{2,0},{3,1},{4,6},{5,7},{6,4},{7,5},{8,10},{9,11},{10,... | collective-permute-start | bytes 1572872 | tf_op jit(solution)/shard_map/cond/branch_1_fun/ppermute | solution.py:42
  538.6 12.6 %collective-permute-start.33 = (bf16[128,2048]{1,0:T(8,128)(2,1)S(1)}, bf16[128,2048]{1,0:T(8,128)(2,1)S(1)}, u32[]{:S(2)}, u32[]{:S(2)}) collective-permute-start(bf16[128,2048]{1,0:T(8,128)(2,1)S(1)} %get-tuple-element.776), channel_id=1, source_target_pairs={{0,4},{1,5},{2,6},{3,7},{4,0},{5,1},{6,2},{7,3},{8,12},{9,13},{10,... | collective-permute-start | bytes 1572872 | tf_op jit(solution)/shard_map/cond/branch_1_fun/ppermute | solution.py:42
  553.7 23.4 %collective-permute-start.13 = (bf16[256,2048]{1,0:T(8,128)(2,1)}, bf16[256,2048]{1,0:T(8,128)(2,1)S(1)}, u32[]{:S(2)}, u32[]{:S(2)}) collective-permute-start(bf16[256,2048]{1,0:T(8,128)(2,1)} %get-tuple-element.430), channel_id=1, source_target_pairs={{0,4},{1,5},{2,6},{3,7},{4,0},{5,1},{6,2},{7,3},{8,12},{9,13},{10,... | collective-permute-start | bytes 3145736 | tf_op jit(solution)/shard_map/cond/branch_1_fun/ppermute | solution.py:42
  555.2 23.2 %collective-permute-start.12 = (bf16[256,2048]{1,0:T(8,128)(2,1)}, bf16[256,2048]{1,0:T(8,128)(2,1)}, u32[]{:S(2)}, u32[]{:S(2)}) collective-permute-start(bf16[256,2048]{1,0:T(8,128)(2,1)} %get-tuple-element.429), channel_id=1, source_target_pairs={{0,2},{1,3},{2,0},{3,1},{4,6},{5,7},{6,4},{7,5},{8,10},{9,11},{10,... | collective-permute-start | bytes 3145736 | tf_op jit(solution)/shard_map/cond/branch_1_fun/ppermute | solution.py:42
  597.1 62.8 %all-to-all-start = ((bf16[8,704,256]{2,1,0:T(8,128)(2,1)}), bf16[8,704,256]{2,1,0:T(8,128)(2,1)}, u32[]{:S(2)}, u32[]{:S(2)}) async-start(bf16[8,704,256]{2,1,0:T(8,128)(2,1)} %bitcast.206), calls=%async_computation | async-start | bytes 5767168 | tf_op jit(solution)/shard_map/cond/branch_1_fun/all_to_all | solution.py:799
  601.5 56.5 %collective-permute-start.9 = (bf16[256,2048]{1,0:T(8,128)(2,1)}, bf16[256,2048]{1,0:T(8,128)(2,1)S(1)}, u32[]{:S(2)}, u32[]{:S(2)}) collective-permute-start(bf16[256,2048]{1,0:T(8,128)(2,1)} %get-tuple-element.444), channel_id=1, source_target_pairs={{0,4},{1,5},{2,6},{3,7},{4,0},{5,1},{6,2},{7,3},{8,12},{9,13},{10,... | collective-permute-start | bytes 3145736 | tf_op jit(solution)/shard_map/cond/branch_1_fun/ppermute | solution.py:42
  603.4 54.7 %collective-permute-start.8 = (bf16[256,2048]{1,0:T(8,128)(2,1)}, bf16[256,2048]{1,0:T(8,128)(2,1)S(1)}, u32[]{:S(2)}, u32[]{:S(2)}) collective-permute-start(bf16[256,2048]{1,0:T(8,128)(2,1)} %get-tuple-element.443), channel_id=1, source_target_pairs={{0,2},{1,3},{2,0},{3,1},{4,6},{5,7},{6,4},{7,5},{8,10},{9,11},{10,... | collective-permute-start | bytes 3145736 | tf_op jit(solution)/shard_map/cond/branch_1_fun/ppermute | solution.py:42
  (77 other events, 659.9 us)
Sparse Core Ops, SparseCore 0:
  82.0 106.9 all-gather.2
  272.2 112.9 all-reduce.7
  388.2 205.2 all-reduce.11
  596.5 91.4 all-reduce.9

commit v6 on v5

--- a/solution.py
+++ b/solution.py
@@ -261,8 +261,9 @@
     own = rank * chunk + lax.broadcasted_iota(jnp.int32, (1, block), 1) % chunk
     limit = jnp.minimum(own, length - 1)
     live = rank * chunk + lax.broadcasted_iota(jnp.int32, (chunk, head), 0) < length
-    for first in range(0, width // head, per_block):
-        spans = [slice((first + i) * head, (first + i + 1) * head) for i in range(per_block)]
+    def heads(turn, carry):
+        starts = [(turn * per_block + i) * head for i in range(per_block)]
+        spans = [pl.ds(pl.multiple_of(start, head), head) for start in starts]
         queries = jnp.concatenate([q_ref[0, :, s] for s in spans], 0)
         upstream = jnp.concatenate(
             [jnp.where(live, up_ref[0, :, s].astype(F32), 0.0).astype(BF) for s in spans], 0
@@ -277,6 +278,9 @@
             dq_ref[0, :, s] = d_queries[i * chunk : (i + 1) * chunk]
         dk[...] += dot_nn(d_scores, queries)
         dv[...] += dot_nn(probs.astype(BF), upstream)
+        return carry
+
+    lax.fori_loop(0, width // head // per_block, heads, 0)
     for place in range(count):
         rows = slice(place * chunk, (place + 1) * chunk)
         dkv_ref[place ^ key, 0, :, :head] = dk[rows, :]

time: 712 us -> 713 us (level)
  transfers between devices with their start and end apart: 82 -> 82, of which waited for: 41 -> 41; matrix products, arithmetic and copies ran while one was open for 14% -> 14% of each run, Pallas kernels for 29% -> 30%
where the time goes in v6:
time: 713 us; the launch traced here: 706 us
  waiting for transfers between devices  260 us (36%)
  Pallas kernels  233 us (33%)
  starting transfers between devices  81.1 us (11%)
  other arithmetic  69.4 us (10%)
  local copies, waits for them, and re-layouts  45.4 us (6%)
  between operations  15.4 us (2%)
    ppermute x73, waiting for transfers between devices, swap(): return lax.ppermute(array, 'seq', [(i, i ^ bit) for i in range(8)])  220 us
    ppermute x73, starting transfers between devices, swap(): return lax.ppermute(array, 'seq', [(i, i ^ bit) for i in range(8)])  58.8 us
    pallas_call x4, Pallas kernels, mlp_parts(): pl.pallas_call(functools.partial(mlp_parts_kernel, first=2 * pair), in_sp...  38.4 us
    pallas_call x3, Pallas kernels, hidden_pairs(): pl.pallas_call(functools.partial(hidden_kernel, first=first, pairs=pairs)...  38.2 us
    pallas_call x3, Pallas kernels, inner_of(): pl.pallas_call(functools.partial(inner_kernel, count=count, lefts=len(lef...  36.7 us
    pallas_call x1, Pallas kernels, attend_second(): pl.pallas_call(second_kernel, grid_spec=pltpu.PrefetchScalarGridSpec(num_...  35.7 us
    psum x1, waiting for transfers between devices, body(): lax.psum((w_out_share, w_query_share.reshape(-1, split), small), 'dp')  23.5 us
    convert_element_type x27, other arithmetic, add_rounded(): return total.astype(BF)  22.8 us
  transfers between devices with their start and end apart: 82, of which 41 were waited for; matrix products, arithmetic and copies ran while one was open for 14% of the time, Pallas kernels for 30%

profile of v6, /device:TPU:0, one launch (start us, length us, event | category | flops | bytes accessed | tf_op | source)
XLA Modules:
  0.0 706.1 jit_solution(7473399746111210280)
XLA Ops:
  20.1 4.4 all-to-all-start.1
  24.7 18.3 %collective-permute-done.43 = bf16[272,256]{1,0:T(8,128)(2,1)S(1)} collective-permute-done((bf16[272,256]{1,0:T(8,128)(2,1)S(1)}, bf16[272,256]{1,0:T(8,128)(2,1)S(1)}, u32[]{:S(2)}, u32[]{:S(2)}) %collective-permute-start.43) | collective-permute-done | bytes 139296 | tf_op jit(solution)/shard_map/ppermute | solution.py:42
  46.1 3.2 convert_multiply_fusion.4
  49.3 5.8 collective-permute-done.44
  65.7 4.2 all-to-all-start.2
  75.8 3.1 fusion.30
  85.9 5.1 shard_map.230
  91.0 4.7 shard_map.231
  95.7 4.5 shard_map.232
  100.2 6.7 collective-permute-done.50
  107.4 3.8 collective-permute-done.52
  116.9 4.1 shard_map.233
  121.1 9.7 %shard_map.234 = (bf16[8,2,128,256]{3,2,1,0:T(8,128)(2,1)S(1)}, f32[2,2,1024]{2,1,0:T(2,128)S(1)}) custom-call(s32[2]{0:T(128)S(1)} %copy-done.55, s32[2]{0:T(128)S(1)} %pad_add_fusion.key_ref, bf16[8,2,128,256]{3,2,1,0:T(8,128)(2,1)S(1)} %get-tuple-element.616.q_ref, bf16[8,2,128,256]{3,2,1,0:T(8,128)(2,1)S(1)} %get-tuple-element.617.kv_ref), custom_call_target="tpu_custom_call" | custom-call | flops 1000 | bytes 1000 | tf_op jit(solution)/shard_map/pallas_call | solution.py:216
  131.9 4.2 shard_map.235
  143.3 11.5 %collective-permute-done.59 = bf16[128,2048]{1,0:T(8,128)(2,1)S(1)} collective-permute-done((bf16[128,2048]{1,0:T(8,128)(2,1)S(1)}, bf16[128,2048]{1,0:T(8,128)(2,1)S(1)}, u32[]{:S(2)}, u32[]{:S(2)}) %collective-permute-start.59) | collective-permute-done | bytes 524320 | tf_op jit(solution)/shard_map/ppermute | solution.py:42
  158.7 35.7 %shard_map.236 = (bf16[2,128,2048]{2,1,0:T(8,128)(2,1)}, f32[8,2,128,256]{3,2,1,0:T(8,128)}) custom-call(s32[2]{0:T(128)S(1)} %copy-done.55, s32[2]{0:T(128)S(1)} %pad_add_fusion.key_ref, bf16[2,128,2048]{2,1,0:T(8,128)(2,1)S(1)} %copy-done.6, bf16[2,128,2048]{2,1,0:T(8,128)(2,1)S(1)} %copy-done.7, bf16[8,2,128,256]{3,2,1,0:T(8,128)(2,1)S(1)} %get-tuple-element.617.kv_ref), custom_call_target="tpu_custom_call" | custom-call | flops 1000 | bytes 1000 | tf_op jit(solution)/shard_map/pallas_call | solution.py:296
  201.6 10.8 %conditional.11 = ((bf16[8,256,704]{2,1,0:T(8,128)(2,1)}, bf16[8,256,704]{2,1,0:T(8,128)(2,1)}, bf16[8,256,704]{2,1,0:T(8,128)(2,1)})) conditional(s32[]{:T(128)} %bitcast.54, () %tuple.139, (bf16[256,2048]{1,0:T(8,128)(2,1)S(1)}, bf16[256,2048]{1,0:T(8,128)(2,1)}, bf16[256,2048]{1,0:T(8,128)(2,1)}, bf16[256,2048]{1,0:T(8,128)(2,1)}, ...), branch_computations={%region_1.2_spmd, %region_2.3_spmd} | conditional | flops 7381975040 | bytes 14942216 | solution.py:142
  201.6 10.8 %branch_1_fun.17 = (bf16[8,256,704]{2,1,0:T(8,128)(2,1)}, bf16[8,256,704]{2,1,0:T(8,128)(2,1)}, bf16[8,256,704]{2,1,0:T(8,128)(2,1)}) custom-call(bf16[256,2048]{1,0:T(8,128)(2,1)S(1)} %get-tuple-element.279.refs_0_, bf16[256,2048]{1,0:T(8,128)(2,1)} %get-tuple-element.280.refs_1_, bf16[256,2048]{1,0:T(8,128)(2,1)} %get-tuple-element.281.refs_2_, ...), custom_call_target="tpu_custom_call" | custom-call | flops 7381975040 | bytes 14942208 | tf_op jit(solution)/shard_map/cond/branch_1_fun/pallas_call | solution.py:548
  212.4 12.1 %collective-permute-done.64.refs_3_ = bf16[256,2048]{1,0:T(8,128)(2,1)} collective-permute-done((bf16[256,2048]{1,0:T(8,128)(2,1)S(1)}, bf16[256,2048]{1,0:T(8,128)(2,1)}, u32[]{:S(2)}, u32[]{:S(2)}) %collective-permute-start.64) | collective-permute-done | bytes 1048608 | tf_op jit(solution)/shard_map/ppermute | solution.py:42
  231.2 17.0 %conditional.12 = ((bf16[8,256,704]{2,1,0:T(8,128)(2,1)}, bf16[8,256,704]{2,1,0:T(8,128)(2,1)}, bf16[8,256,704]{2,1,0:T(8,128)(2,1)})) conditional(s32[]{:T(128)} %bitcast.54, () %tuple.142, (bf16[256,2048]{1,0:T(8,128)(2,1)}, bf16[256,2048]{1,0:T(8,128)(2,1)}, bf16[256,2048]{1,0:T(8,128)(2,1)}, bf16[256,2048]{1,0:T(8,128)(2,1)}, ...), branch_computations={%region_3.4_spmd, %region_4.5_spmd} | conditional | flops 14763950080 | bytes 21233672 | solution.py:142
  231.2 16.6 %branch_1_fun.18 = (bf16[8,256,704]{2,1,0:T(8,128)(2,1)}, bf16[8,256,704]{2,1,0:T(8,128)(2,1)}, bf16[8,256,704]{2,1,0:T(8,128)(2,1)}) custom-call(bf16[256,2048]{1,0:T(8,128)(2,1)} %get-tuple-element.285.refs_0_, bf16[256,2048]{1,0:T(8,128)(2,1)} %get-tuple-element.286.refs_1_, ...), custom_call_target="tpu_custom_call", output_to_operand_aliasing={{0}: (10, {}), {1}: (11, {}), {2}: (12, {})} | custom-call | flops 14763950080 | bytes 21233664 | tf_op jit(solution)/shard_map/cond/branch_1_fun/pallas_call | solution.py:548
  253.2 10.8 %shard_map.237 = (bf16[8,256,704]{2,1,0:T(8,128)(2,1)}, bf16[8,256,704]{2,1,0:T(8,128)(2,1)}, bf16[8,256,704]{2,1,0:T(8,128)(2,1)}) custom-call(bf16[256,2048]{1,0:T(8,128)(2,1)S(1)} %constant_dynamic-update-slice_fusion.4.refs_0_.refs_7_, ...), custom_call_target="tpu_custom_call", output_to_operand_aliasing={{0}: (6, {}), {1}: (7, {}), {2}: (8, {})} | custom-call | flops 7381975040 | bytes 14942208 | tf_op jit(solution)/shard_map/pallas_call | solution.py:548
  264.1 11.6 %shard_map.238 = bf16[704,2048]{1,0:T(8,128)(2,1)S(1)} custom-call(bf16[2048,704]{1,0:T(8,128)(2,1)} %bitcast.203, bf16[256,2048]{1,0:T(8,128)(2,1)S(1)} %multiply_convert_fusion.refs_1_, bf16[256,2048]{1,0:T(8,128)(2,1)} %collective-permute-done.66.refs_2_, bf16[256,2048]{1,0:T(8,128)(2,1)} %collective-permute-done.64.refs_3_, ...), custom_call_target="tpu_custom_call" | custom-call | flops 1000 | bytes 1000 | tf_op jit(solution)/shard_map/pallas_call | solution.py:741
  277.3 38.8 %conditional.13 = (bf16[256,2048]{1,0:T(8,128)(2,1)S(1)}, bf16[256,2048]{1,0:T(8,128)(2,1)}, bf16[256,2048]{1,0:T(8,128)(2,1)S(1)}, bf16[256,2048]{1,0:T(8,128)(...) conditional(s32[]{:T(128)} %bitcast.54, () %tuple.127, ...), branch_computations={%region_5.6_spmd, %region_6.7_spmd} | conditional | flops 29527900160 | bytes 94372048 | solution.py:142
  277.4 10.3 %branch_1_fun.19 = (bf16[256,2048]{1,0:T(8,128)(2,1)S(1)}, bf16[256,2048]{1,0:T(8,128)(2,1)}, bf16[256,2048]{1,0:T(8,128)(2,1)}, bf16[256,2048]{1,0:T(8,128)(2,1)}) custom-call(bf16[8,256,704]{2,1,0:T(8,128)(2,1)} %get-tuple-element.298.hidden_hbm, bf16[8,256,704]{2,1,0:T(8,128)(2,1)} %get-tuple-element.299.dgate_hbm, ...), custom_call_target="tpu_custom_call" | custom-call | flops 7381975040 | bytes 14942208 | tf_op jit(solution)/shard_map/cond/branch_1_fun/pallas_call | solution.py:606
  287.8 9.4 %branch_1_fun.20 = (bf16[256,2048]{1,0:T(8,128)(2,1)S(1)}, bf16[256,2048]{1,0:T(8,128)(2,1)}, bf16[256,2048]{1,0:T(8,128)(2,1)}, bf16[256,2048]{1,0:T(8,128)(2,1)}) custom-call(bf16[8,256,704]{2,1,0:T(8,128)(2,1)S(1)} %copy-done.25, bf16[8,256,704]{2,1,0:T(8,128)(2,1)S(1)} %copy-done.26, bf16[8,256,704]{2,1,0:T(8,128)(2,1)S(1)} %copy-done.27, ...), custom_call_target="tpu_custom_call" | custom-call | flops 7381975040 | bytes 14942208 | tf_op jit(solution)/shard_map/cond/branch_1_fun/pallas_call | solution.py:606
  297.2 9.5 %branch_1_fun.21 = (bf16[256,2048]{1,0:T(8,128)(2,1)S(1)}, bf16[256,2048]{1,0:T(8,128)(2,1)}, bf16[256,2048]{1,0:T(8,128)(2,1)}, bf16[256,2048]{1,0:T(8,128)(2,1)}) custom-call(bf16[8,256,704]{2,1,0:T(8,128)(2,1)S(1)} %copy-done.25, bf16[8,256,704]{2,1,0:T(8,128)(2,1)S(1)} %copy-done.26, bf16[8,256,704]{2,1,0:T(8,128)(2,1)S(1)} %copy-done.27, ...), custom_call_target="tpu_custom_call" | custom-call | flops 7381975040 | bytes 14942208 | tf_op jit(solution)/shard_map/cond/branch_1_fun/pallas_call | solution.py:606
  306.7 9.2 %branch_1_fun.22 = (bf16[256,2048]{1,0:T(8,128)(2,1)}, bf16[256,2048]{1,0:T(8,128)(2,1)}, bf16[256,2048]{1,0:T(8,128)(2,1)}, bf16[256,2048]{1,0:T(8,128)(2,1)}) custom-call(bf16[8,256,704]{2,1,0:T(8,128)(2,1)S(1)} %copy-done.25, bf16[8,256,704]{2,1,0:T(8,128)(2,1)S(1)} %copy-done.26, bf16[8,256,704]{2,1,0:T(8,128)(2,1)S(1)} %copy-done.27, ...), custom_call_target="tpu_custom_call" | custom-call | flops 7381975040 | bytes 14942208 | tf_op jit(solution)/shard_map/cond/branch_1_fun/pallas_call | solution.py:606
  316.1 31.9 %conditional.14 = (bf16[256,2048]{1,0:T(8,128)(2,1)S(1)}, bf16[256,2048]{1,0:T(8,128)(2,1)S(1)}, bf16[256,2048]{1,0:T(8,128)(2,1)S(1)}, bf16[704,2048]{1,0:T(8,128)(2,1)S(1)}) conditional(s32[]{:T(128)} %bitcast.54, () %tuple.149, (bf16[256,2048]{1,0:T(8,128)(2,1)S(1)}, bf16[256,2048]{1,0:T(8,128)(2,1)}, bf16[256,2048]{1,0:T(8,128)(2,1)S(1)}, ...), branch_computations={%region_7.8_spmd, %region_8.9_spmd} | conditional | flops 14681064 | bytes 49808684 | solution.py:142
  317.2 12.2 %branch_1_fun.23 = bf16[704,2048]{1,0:T(8,128)(2,1)S(1)} custom-call(bf16[2048,704]{1,0:T(8,128)(2,1)} %bitcast.202, bf16[256,2048]{1,0:T(8,128)(2,1)} %get-tuple-element.330.refs_1_, bf16[256,2048]{1,0:T(8,128)(2,1)} %get-tuple-element.331.refs_2_, bf16[256,2048]{1,0:T(8,128)(2,1)} %get-tuple-element.332.refs_3_, ...), custom_call_target="tpu_custom_call" | custom-call | flops 1000 | bytes 1000 | tf_op jit(solution)/shard_map/cond/branch_1_fun/pallas_call | solution.py:741
  334.4 11.0 %collective-permute-done.20 = bf16[128,2048]{1,0:T(8,128)(2,1)S(1)} collective-permute-done((bf16[128,2048]{1,0:T(8,128)(2,1)S(1)}, bf16[128,2048]{1,0:T(8,128)(2,1)S(1)}, u32[]{:S(2)}, u32[]{:S(2)}) %collective-permute-start.20) | collective-permute-done | bytes 524320 | tf_op jit(solution)/shard_map/cond/branch_1_fun/ppermute | solution.py:42
  349.6 28.5 %conditional.15 = (f32[256,2048]{1,0:T(8,128)}, bf16[2048]{0:T(1024)(128)(2,1)S(1)}, bf16[704,2048]{1,0:T(8,128)(2,1)}) conditional(s32[]{:T(128)} %bitcast.54, () %tuple.148, (f32[256]{0:T(256)S(1)}, f32[256,1]{0,1:T(1,128)S(1)}, f32[256,1]{0,1:T(1,128)S(1)}, bf16[8,256,704]{2,1,0:T(8,128)(2,1)}, bf16[256,2048]{1,0:T(8,128)(2,1)S(1)}, ...), branch_computations={%region_9.10_spmd, %region_10.13_spmd} | conditional | flops 10487784 | bytes 38843528 | solution.py:142
  351.6 13.0 %branch_1_fun.24 = bf16[704,2048]{1,0:T(8,128)(2,1)} custom-call(bf16[2048,704]{1,0:T(8,128)(2,1)} %bitcast.204, bf16[256,2048]{1,0:T(8,128)(2,1)S(1)} %get-tuple-element.344.refs_1_, bf16[256,2048]{1,0:T(8,128)(2,1)} %get-tuple-element.345.refs_2_, bf16[256,2048]{1,0:T(8,128)(2,1)} %get-tuple-element.346.refs_3_, ...), custom_call_target="tpu_custom_call" | custom-call | flops 1000 | bytes 1000 | tf_op jit(solution)/shard_map/cond/branch_1_fun/pallas_call | solution.py:741
  364.6 9.4 %collective-permute-done.11 = bf16[256,2048]{1,0:T(8,128)(2,1)S(1)} collective-permute-done((bf16[256,2048]{1,0:T(8,128)(2,1)S(1)}, bf16[256,2048]{1,0:T(8,128)(2,1)S(1)}, u32[]{:S(2)}, u32[]{:S(2)}) %collective-permute-start.11) | collective-permute-done | bytes 1048608 | tf_op jit(solution)/shard_map/cond/branch_1_fun/ppermute | solution.py:42
  378.1 12.3 %all-reduce.8.cloned.1.call-done = bf16[704,2048]{1,0:T(8,128)(2,1)} async-done(((bf16[704,2048]{1,0:T(8,128)(2,1)}), bf16[704,2048]{1,0:T(8,128)(2,1)}) %all-reduce.8.cloned.1.call-update) | async-done | bytes 2883600 | tf_op jit(solution)/shard_map/psum | solution.py:982
  390.4 32.6 %conditional.16 = (bf16[256,2048]{1,0:T(8,128)(2,1)}, bf16[256,2048]{1,0:T(8,128)(2,1)}, bf16[256,2048]{1,0:T(8,128)(2,1)}, bf16[256,2048]{1,0:T(8,128)(2,1)}, b...) conditional(s32[]{:T(128)} %bitcast.54, () %tuple.147, (f32[256,2048]{1,0:T(8,128)}, ...), branch_computations={%region_14.15_spmd, %region_15.16_spmd} | conditional | flops 525288 | bytes 28312828 | solution.py:142
  395.3 22.0 %collective-permute-done = bf16[256,2048]{1,0:T(8,128)(2,1)} collective-permute-done((bf16[256,2048]{1,0:T(8,128)(2,1)S(1)}, bf16[256,2048]{1,0:T(8,128)(2,1)}, u32[]{:S(2)}, u32[]{:S(2)}) %collective-permute-start) | collective-permute-done | bytes 1048608 | tf_op jit(solution)/shard_map/cond/branch_1_fun/ppermute | solution.py:42
  423.0 27.9 %conditional.17 = ((bf16[8,2,128,256]{3,2,1,0:T(8,128)(2,1)S(1)}, bf16[256,2048]{1,0:T(8,128)(2,1)})) conditional(s32[]{:T(128)} %bitcast.54, () %tuple.146, (bf16[256,2048]{1,0:T(8,128)(2,1)}, bf16[256,2048]{1,0:T(8,128)(2,1)}, bf16[256,2048]{1,0:T(8,128)(2,1)}, bf16[256,2048]{1,0:T(8,128)(2,1)}, bf16[8,2,128,256]{3,2,1,0:T(8,128)(2,1)S(1)}, ...), branch_computations={%region_16.17_spmd, %region_17.18_spmd} | conditional | flops 3000 | bytes 16780372 | solution.py:142
  427.8 10.8 %collective-permute-done.5 = bf16[128,2048]{1,0:T(8,128)(2,1)S(1)} collective-permute-done((bf16[128,2048]{1,0:T(8,128)(2,1)S(1)}, bf16[128,2048]{1,0:T(8,128)(2,1)S(1)}, u32[]{:S(2)}, u32[]{:S(2)}) %collective-permute-start.5) | collective-permute-done | bytes 524320 | tf_op jit(solution)/shard_map/cond/branch_1_fun/ppermute | solution.py:42
  441.1 3.4 branch_1_fun.26
  444.6 3.5 branch_1_fun.27
  450.9 4.0 copy.123
  454.9 4.6 all-to-all-start.3
  459.5 49.1 %conditional.18 = (bf16[256,2048]{1,0:T(8,128)(2,1)}, bf16[256,2048]{1,0:T(8,128)(2,1)}, bf16[256,2048]{1,0:T(8,128)(2,1)}, bf16[256,2048]{1,0:T(8,128)(2,1)}, b...) conditional(s32[]{:T(128)} %bitcast.54, () %tuple.126, ...), branch_computations={%region_18.19_spmd, %region_19.20_spmd} | conditional | flops 14683064 | bytes 91754064 | solution.py:142
  460.8 11.7 %branch_1_fun.29 = bf16[8,2,128,512]{3,2,1,0:T(8,128)(2,1)S(1)} custom-call(s32[2]{0:T(128)S(1)} %get-tuple-element.388.lengths_ref, s32[2]{0:T(128)S(1)} %get-tuple-element.389.key_ref, bf16[8,2,128,256]{3,2,1,0:T(8,128)(2,1)} %get-tuple-element.390.q_ref, bf16[8,2,128,256]{3,2,1,0:T(8,128)(2,1)} %get-tuple-element.391.up_ref, ...), custom_call_target="tpu_custom_call" | custom-call | flops 1000 | bytes 1000 | tf_op jit(solution)/shard_map/cond/branch_1_fun/pallas_call | solution.py:392
  473.8 7.0 branch_1_fun.30
  480.8 7.9 %branch_1_fun.31 = bf16[2048,512]{1,0:T(8,128)(2,1)} custom-call(bf16[256,2048]{1,0:T(8,128)(2,1)S(1)} %copy-done.39, bf16[256,2048]{1,0:T(8,128)(2,1)S(1)} %copy-done.40, bf16[256,2048]{1,0:T(8,128)(2,1)S(1)} %copy-done.41, bf16[256,2048]{1,0:T(8,128)(2,1)S(1)} %copy-done.42, bf16[256,2048]{1,0:T(8,128)(2,1)S(1)} %copy-done.43, ...), custom_call_target="tpu_custom_call" | custom-call | flops 1000 | bytes 1000 | tf_op jit(solution)/shard_map/cond/branch_1_fun/pallas_call | solution.py:707
  500.1 4.6 collective-permute-done.26
  510.9 4.5 all-to-all-start.4
  518.0 41.0 %conditional.19 = (bf16[256,2048]{1,0:T(8,128)(2,1)}, bf16[256,2048]{1,0:T(8,128)(2,1)}, bf16[256,2048]{1,0:T(8,128)(2,1)}, bf16[256,256]{1,0:T(8,128)(2,1)S(1)}) conditional(s32[]{:T(128)} %bitcast.54, () %tuple.159, (bf16[256,2048]{1,0:T(8,128)(2,1)}, bf16[256,2048]{1,0:T(8,128)(2,1)}, bf16[256,2048]{1,0:T(8,128)(2,1)}, ...), branch_computations={%region_20.21_spmd, %region_21.22_spmd} | conditional | flops 17432584 | bytes 64094760 | solution.py:142
  527.3 8.1 %collective-permute-done.36 = bf16[2,256,256]{2,1,0:T(8,128)(2,1)S(1)} collective-permute-done((bf16[2,256,256]{2,1,0:T(8,128)(2,1)}, bf16[2,256,256]{2,1,0:T(8,128)(2,1)S(1)}, u32[]{:S(2)}, u32[]{:S(2)}) %collective-permute-start.36) | collective-permute-done | bytes 262176 | tf_op jit(solution)/shard_map/cond/branch_1_fun/ppermute | solution.py:42
  538.6 3.2 collective-permute-done.37
  551.8 4.6 collective-permute-done.32
  559.1 37.5 %conditional.20 = (bf16[272,256]{1,0:T(8,128)(2,1)S(1)}, f32[2,128,2048]{2,1,0:T(8,128)}) conditional(s32[]{:T(128)} %bitcast.54, () %tuple.158, (bf16[256,2048]{1,0:T(8,128)(2,1)}, bf16[256,2048]{1,0:T(8,128)(2,1)}, bf16[256,2048]{1,0:T(8,128)(2,1)}, f32[2,128,2048]{2,1,0:T(8,128)}, f32[256,1]{0,1:T(1,128)S(1)}, ...), branch_computations={%region_22.23_spmd, %region_23.0_spmd} | conditional | flops 11987720 | bytes 29377868 | solution.py:142
  564.1 18.4 %collective-permute-done.13 = bf16[256,2048]{1,0:T(8,128)(2,1)S(1)} collective-permute-done((bf16[256,2048]{1,0:T(8,128)(2,1)}, bf16[256,2048]{1,0:T(8,128)(2,1)S(1)}, u32[]{:S(2)}, u32[]{:S(2)}) %collective-permute-start.13) | collective-permute-done | bytes 1048608 | tf_op jit(solution)/shard_map/cond/branch_1_fun/ppermute | solution.py:42
  593.1 3.5 fusion.18
  598.7 71.0 %conditional.21 = (f32[256,5632]{1,0:T(8,128)}, f32[256,5632]{1,0:T(8,128)}, f32[704,2048]{1,0:T(8,128)}, bf16[2,128,2048]{2,1,0:T(8,128)(2,1)S(1)}) conditional(s32[]{:T(128)} %bitcast.54, () %tuple.125, (bf16[8,704,256]{2,1,0:T(8,128)(2,1)}, bf16[704,2048]{1,0:T(8,128)(2,1)}, bf16[704,2048]{1,0:T(8,128)(2,1)}, bf16[256,2048]{1,0:T(8,128)(2,1)}, ...), branch_computations={%region_29.30_spmd, %region_30.31_spmd} | conditional | flops 6162384 | bytes 49285244 | solution.py:142
  598.7 3.6 copy.122
  602.3 4.4 all-to-all-start
  610.1 4.7 branch_1_fun.32
  614.9 3.3 convert_element_type.420
  618.2 45.0 %collective-permute-done.9 = bf16[256,2048]{1,0:T(8,128)(2,1)S(1)} collective-permute-done((bf16[256,2048]{1,0:T(8,128)(2,1)}, bf16[256,2048]{1,0:T(8,128)(2,1)S(1)}, u32[]{:S(2)}, u32[]{:S(2)}) %collective-permute-start.9) | collective-permute-done | bytes 1048608 | tf_op jit(solution)/shard_map/cond/branch_1_fun/ppermute | solution.py:42
  665.1 4.6 branch_1_fun.33
  669.7 23.5 %all-reduce.10.cloned.1.call-done = (bf16[256,2048]{1,0:T(8,128)(2,1)}, bf16[2048,256]{1,0:T(8,128)(2,1)}, bf16[272,256]{1,0:T(8,128)(2,1)}) async-done(((bf16[256,2048]{1,0:T(8,128)(2,1)}, bf16[2048,256]{1,0:T(8,128)(2,1)}, bf16[272,256]{1,0:T(8,128)(2,1)}), (bf16[256,2048]{1,0:T(8,128)(2,1)}, bf16[2048,256]{1,0:T(8,128)(2,1)}, bf16[272,256]{1,0:T(8,128)(2,1)})) %all-reduce.10.cloned.1.call-update) | async-done | bytes 2236432 | tf_op jit(solution)/shard_map/psum | solution.py:1062
  (386 shorter events, 190.4 us)
Async XLA Ops:
  7.2 48.0 %collective-permute-start.38 = (bf16[256,2048]{1,0:T(8,128)(2,1)}, bf16[256,2048]{1,0:T(8,128)(2,1)S(1)}, u32[]{:S(2)}, u32[]{:S(2)}) collective-permute-start(bf16[256,2048]{1,0:T(8,128)(2,1)} %bitcast.191), channel_id=1, source_target_pairs={{0,2},{1,3},{2,0},{3,1},{4,6},{5,7},{6,4},{7,5},{8,10},{9,11},{10,... | collective-permute-start | bytes 3145736 | tf_op jit(solution)/shard_map/ppermute | solution.py:42
  10.2 45.0 %collective-permute-start.39 = (bf16[256,2048]{1,0:T(8,128)(2,1)}, bf16[256,2048]{1,0:T(8,128)(2,1)S(1)}, u32[]{:S(2)}, u32[]{:S(2)}) collective-permute-start(bf16[256,2048]{1,0:T(8,128)(2,1)} %bitcast.192), channel_id=1, source_target_pairs={{0,4},{1,5},{2,6},{3,7},{4,0},{5,1},{6,2},{7,3},{8,12},{9,13},{10,... | collective-permute-start | bytes 3145736 | tf_op jit(solution)/shard_map/ppermute | solution.py:42
  11.7 72.8 %collective-permute-start.48 = (bf16[256,2048]{1,0:T(8,128)(2,1)}, bf16[256,2048]{1,0:T(8,128)(2,1)}, u32[]{:S(2)}, u32[]{:S(2)}) collective-permute-start(bf16[256,2048]{1,0:T(8,128)(2,1)} %bitcast.193), channel_id=1, source_target_pairs={{0,1},{1,0},{2,3},{3,2},{4,5},{5,4},{6,7},{7,6},{8,9},{9,8},{10,11... | collective-permute-start | bytes 3145736 | tf_op jit(solution)/shard_map/ppermute | solution.py:42
  13.9 29.0 %collective-permute-start.43 = (bf16[272,256]{1,0:T(8,128)(2,1)S(1)}, bf16[272,256]{1,0:T(8,128)(2,1)S(1)}, u32[]{:S(2)}, u32[]{:S(2)}) collective-permute-start(bf16[272,256]{1,0:T(8,128)(2,1)S(1)} %pad_maximum_fusion.14), channel_id=1, source_target_pairs={{0,4},{1,5},{2,6},{3,7},{4,0},{5,1},{6,2},{7,3},{8,12},{9,13},{10,... | collective-permute-start | bytes 417800 | tf_op jit(solution)/shard_map/ppermute | solution.py:42
  20.1 41.3 %all-to-all-start.1 = ((bf16[8,64,1408]{2,1,0:T(8,128)(2,1)}), bf16[8,64,1408]{2,1,0:T(8,128)(2,1)}, u32[]{:S(2)}, u32[]{:S(2)}) async-start(bf16[8,64,1408]{2,1,0:T(8,128)(2,1)} %shard_map.229), calls=%async_computation.1 | async-start | bytes 2883584 | tf_op jit(solution)/shard_map/all_to_all | solution.py:851
  43.1 12.0 %collective-permute-start.44 = (bf16[2,272,256]{2,1,0:T(8,128)(2,1)S(1)}, bf16[2,272,256]{2,1,0:T(8,128)(2,1)S(1)}, u32[]{:S(2)}, u32[]{:S(2)}) collective-permute-start(bf16[2,272,256]{2,1,0:T(8,128)(2,1)S(1)} %pad_maximum_fusion.13), channel_id=1, source_target_pairs={{0,2},{1,3},{2,0},{3,1},{4,6},{5,7},{6,4},{7,5},{8,10},{9,11},{10,... | collective-permute-start | bytes 835592 | tf_op jit(solution)/shard_map/ppermute | solution.py:42
  56.0 14.0 %collective-permute-start.40 = (bf16[128,2048]{1,0:T(8,128)(2,1)}, bf16[128,2048]{1,0:T(8,128)(2,1)}, u32[]{:S(2)}, u32[]{:S(2)}) collective-permute-start(bf16[128,2048]{1,0:T(8,128)(2,1)} %slice.182), channel_id=1, source_target_pairs={{0,4},{1,5},{2,6},{3,7},{4,0},{5,1},{6,2},{7,3},{8,12},{9,13},{10,... | collective-permute-start | bytes 1572872 | tf_op jit(solution)/shard_map/ppermute | solution.py:42
  58.6 12.8 %collective-permute-start.41 = (bf16[128,2048]{1,0:T(8,128)(2,1)}, bf16[128,2048]{1,0:T(8,128)(2,1)}, u32[]{:S(2)}, u32[]{:S(2)}) collective-permute-start(bf16[128,2048]{1,0:T(8,128)(2,1)} %slice.183), channel_id=1, source_target_pairs={{0,2},{1,3},{2,0},{3,1},{4,6},{5,7},{6,4},{7,5},{8,10},{9,11},{10,... | collective-permute-start | bytes 1572872 | tf_op jit(solution)/shard_map/ppermute | solution.py:42
  61.0 14.2 %collective-permute-start.45 = (bf16[2,2,272,256]{3,2,1,0:T(8,128)(2,1)}, bf16[2,2,272,256]{3,2,1,0:T(8,128)(2,1)}, u32[]{:S(2)}, u32[]{:S(2)}) collective-permute-start(bf16[2,2,272,256]{3,2,1,0:T(8,128)(2,1)} %pad_maximum_fusion.10), channel_id=1, source_target_pairs={{0,1},{1,0},{2,3},{3,2},{4,5},{5,4},{6,7},{7,6},{8,9},{9,8},{10,11... | collective-permute-start | bytes 1671176 | tf_op jit(solution)/shard_map/ppermute | solution.py:42
  61.0 34.7 %collective-permute-start.46 = (bf16[256,2048]{1,0:T(8,128)(2,1)S(1)}, bf16[256,2048]{1,0:T(8,128)(2,1)}, u32[]{:S(2)}, u32[]{:S(2)}) collective-permute-start(bf16[256,2048]{1,0:T(8,128)(2,1)S(1)} %collective-permute-done.39.a_ref), channel_id=1, source_target_pairs={{0,1},{1,0},{2,3},{3,2},{4,5},{5,4},{6,7},{7,6},{8,9},{9,8},{10,11... | collective-permute-start | bytes 3145736 | tf_op jit(solution)/shard_map/ppermute | solution.py:42
  65.7 20.2 %all-to-all-start.2 = ((bf16[256,8,256]{2,0,1:T(8,128)(2,1)}), bf16[256,8,256]{2,0,1:T(8,128)(2,1)}, u32[]{:S(2)}, u32[]{:S(2)}) async-start(bf16[256,8,256]{2,0,1:T(8,128)(2,1)} %bitcast.214), calls=%async_computation.2 | async-start | bytes 2097152 | tf_op jit(solution)/shard_map/all_to_all | solution.py:132
  69.9 125.5 %all-gather.3.cloned.1.call-start = ((), (), s32[]{:S(2)}) async-start(), calls=%async_computation.6 | async-start | bytes 7208960 | tf_op jit(solution)/shard_map/all_gather | solution.py:853
  70.0 21.0 %collective-permute-start.47 = (bf16[256,2048]{1,0:T(8,128)(2,1)S(1)}, bf16[256,2048]{1,0:T(8,128)(2,1)}, u32[]{:S(2)}, u32[]{:S(2)}) collective-permute-start(bf16[256,2048]{1,0:T(8,128)(2,1)S(1)} %collective-permute-done.38.a_ref), channel_id=1, source_target_pairs={{0,1},{1,0},{2,3},{3,2},{4,5},{5,4},{6,7},{7,6},{8,9},{9,8},{10,11... | collective-permute-start | bytes 3145736 | tf_op jit(solution)/shard_map/ppermute | solution.py:42
  73.6 33.3 %collective-permute-start.50 = (bf16[256,2048]{1,0:T(8,128)(2,1)}, bf16[256,2048]{1,0:T(8,128)(2,1)}, u32[]{:S(2)}, u32[]{:S(2)}) collective-permute-start(bf16[256,2048]{1,0:T(8,128)(2,1)} %get-tuple-element.619), channel_id=1, source_target_pairs={{0,2},{1,3},{2,0},{3,1},{4,6},{5,7},{6,4},{7,5},{8,10},{9,11},{10,... | collective-permute-start | bytes 3145736 | tf_op jit(solution)/shard_map/ppermute | solution.py:42
  75.2 31.7 %collective-permute-start.51 = (bf16[256,2048]{1,0:T(8,128)(2,1)}, bf16[256,2048]{1,0:T(8,128)(2,1)}, u32[]{:S(2)}, u32[]{:S(2)}) collective-permute-start(bf16[256,2048]{1,0:T(8,128)(2,1)} %get-tuple-element.619), channel_id=1, source_target_pairs={{0,4},{1,5},{2,6},{3,7},{4,0},{5,1},{6,2},{7,3},{8,12},{9,13},{10,... | collective-permute-start | bytes 3145736 | tf_op jit(solution)/shard_map/ppermute | solution.py:42
  81.9 308.5 %all-reduce.8.cloned.1.call-start = ((), (), s32[]{:S(2)}) async-start(), calls=%async_computation.5 | async-start | bytes 5767168 | tf_op jit(solution)/shard_map/psum | solution.py:982
  84.5 23.0 %collective-permute-start.49 = (bf16[256,2048]{1,0:T(8,128)(2,1)}, bf16[256,2048]{1,0:T(8,128)(2,1)}, u32[]{:S(2)}, u32[]{:S(2)}) collective-permute-start(bf16[256,2048]{1,0:T(8,128)(2,1)} %get-tuple-element.619), channel_id=1, source_target_pairs={{0,1},{1,0},{2,3},{3,2},{4,5},{5,4},{6,7},{7,6},{8,9},{9,8},{10,11... | collective-permute-start | bytes 3145736 | tf_op jit(solution)/shard_map/ppermute | solution.py:42
  107.4 9.5 %collective-permute-start.42 = (bf16[256,2048]{1,0:T(8,128)(2,1)S(1)}, bf16[256,2048]{1,0:T(8,128)(2,1)S(1)}, u32[]{:S(2)}, u32[]{:S(2)}) collective-permute-start(bf16[256,2048]{1,0:T(8,128)(2,1)S(1)} %copy-done.5), channel_id=1, source_target_pairs={{0,1},{1,0},{2,3},{3,2},{4,5},{5,4},{6,7},{7,6},{8,9},{9,8},{10,11... | collective-permute-start | bytes 3145736 | tf_op jit(solution)/shard_map/ppermute | solution.py:42
  113.7 17.1 %collective-permute-start.54 = (bf16[128,2048]{1,0:T(8,128)(2,1)S(1)}, bf16[128,2048]{1,0:T(8,128)(2,1)S(1)}, u32[]{:S(2)}, u32[]{:S(2)}) collective-permute-start(bf16[128,2048]{1,0:T(8,128)(2,1)S(1)} %slice.187), channel_id=1, source_target_pairs={{0,4},{1,5},{2,6},{3,7},{4,0},{5,1},{6,2},{7,3},{8,12},{9,13},{10,... | collective-permute-start | bytes 1572872 | tf_op jit(solution)/shard_map/ppermute | solution.py:42
  116.3 14.5 %collective-permute-start.55 = (bf16[128,2048]{1,0:T(8,128)(2,1)S(1)}, bf16[128,2048]{1,0:T(8,128)(2,1)S(1)}, u32[]{:S(2)}, u32[]{:S(2)}) collective-permute-start(bf16[128,2048]{1,0:T(8,128)(2,1)S(1)} %slice.188), channel_id=1, source_target_pairs={{0,2},{1,3},{2,0},{3,1},{4,6},{5,7},{6,4},{7,5},{8,10},{9,11},{10,... | collective-permute-start | bytes 1572872 | tf_op jit(solution)/shard_map/ppermute | solution.py:42
  136.8 57.6 %collective-permute-start.56 = (bf16[256,2048]{1,0:T(8,128)(2,1)S(1)}, bf16[256,2048]{1,0:T(8,128)(2,1)S(1)}, u32[]{:S(2)}, u32[]{:S(2)}) collective-permute-start(bf16[256,2048]{1,0:T(8,128)(2,1)S(1)} %get-tuple-element.628), channel_id=1, source_target_pairs={{0,1},{1,0},{2,3},{3,2},{4,5},{5,4},{6,7},{7,6},{8,9},{9,8},{10,11... | collective-permute-start | bytes 3145736 | tf_op jit(solution)/shard_map/ppermute | solution.py:42
  140.8 14.0 %collective-permute-start.59 = (bf16[128,2048]{1,0:T(8,128)(2,1)S(1)}, bf16[128,2048]{1,0:T(8,128)(2,1)S(1)}, u32[]{:S(2)}, u32[]{:S(2)}) collective-permute-start(bf16[128,2048]{1,0:T(8,128)(2,1)S(1)} %get-tuple-element.790), channel_id=1, source_target_pairs={{0,2},{1,3},{2,0},{3,1},{4,6},{5,7},{6,4},{7,5},{8,10},{9,11},{10,... | collective-permute-start | bytes 1572872 | tf_op jit(solution)/shard_map/ppermute | solution.py:42
  142.4 13.7 %collective-permute-start.60 = (bf16[128,2048]{1,0:T(8,128)(2,1)S(1)}, bf16[128,2048]{1,0:T(8,128)(2,1)S(1)}, u32[]{:S(2)}, u32[]{:S(2)}) collective-permute-start(bf16[128,2048]{1,0:T(8,128)(2,1)S(1)} %get-tuple-element.789), channel_id=1, source_target_pairs={{0,4},{1,5},{2,6},{3,7},{4,0},{5,1},{6,2},{7,3},{8,12},{9,13},{10,... | collective-permute-start | bytes 1572872 | tf_op jit(solution)/shard_map/ppermute | solution.py:42
  156.3 38.5 %collective-permute-start.63 = (bf16[256,2048]{1,0:T(8,128)(2,1)S(1)}, bf16[256,2048]{1,0:T(8,128)(2,1)S(1)}, u32[]{:S(2)}, u32[]{:S(2)}) collective-permute-start(bf16[256,2048]{1,0:T(8,128)(2,1)S(1)} %pad_maximum_fusion.9), channel_id=1, source_target_pairs={{0,4},{1,5},{2,6},{3,7},{4,0},{5,1},{6,2},{7,3},{8,12},{9,13},{10,... | collective-permute-start | bytes 3145736 | tf_op jit(solution)/shard_map/ppermute | solution.py:42
  157.1 37.7 %collective-permute-start.61 = (bf16[256,2048]{1,0:T(8,128)(2,1)S(1)}, bf16[256,2048]{1,0:T(8,128)(2,1)S(1)}, u32[]{:S(2)}, u32[]{:S(2)}) collective-permute-start(bf16[256,2048]{1,0:T(8,128)(2,1)S(1)} %pad_maximum_fusion.8), channel_id=1, source_target_pairs={{0,2},{1,3},{2,0},{3,1},{4,6},{5,7},{6,4},{7,5},{8,10},{9,11},{10,... | collective-permute-start | bytes 3145736 | tf_op jit(solution)/shard_map/ppermute | solution.py:42
  198.9 25.7 %collective-permute-start.64 = (bf16[256,2048]{1,0:T(8,128)(2,1)S(1)}, bf16[256,2048]{1,0:T(8,128)(2,1)}, u32[]{:S(2)}, u32[]{:S(2)}) collective-permute-start(bf16[256,2048]{1,0:T(8,128)(2,1)S(1)} %multiply_convert_fusion.refs_1_), channel_id=1, source_target_pairs={{0,2},{1,3},{2,0},{3,1},{4,6},{5,7},{6,4},{7,5},{8,10},{9,11},{10,... | collective-permute-start | bytes 3145736 | tf_op jit(solution)/shard_map/ppermute | solution.py:42
  199.5 25.3 %collective-permute-start.65 = (bf16[256,2048]{1,0:T(8,128)(2,1)S(1)}, bf16[256,2048]{1,0:T(8,128)(2,1)}, u32[]{:S(2)}, u32[]{:S(2)}) collective-permute-start(bf16[256,2048]{1,0:T(8,128)(2,1)S(1)} %multiply_convert_fusion.refs_1_), channel_id=1, source_target_pairs={{0,4},{1,5},{2,6},{3,7},{4,0},{5,1},{6,2},{7,3},{8,12},{9,13},{10,... | collective-permute-start | bytes 3145736 | tf_op jit(solution)/shard_map/ppermute | solution.py:42
  229.1 19.1 %collective-permute-start.67 = (bf16[128,2048]{1,0:T(8,128)(2,1)}, bf16[128,2048]{1,0:T(8,128)(2,1)}, u32[]{:S(2)}, u32[]{:S(2)}) collective-permute-start(bf16[128,2048]{1,0:T(8,128)(2,1)} %slice.196), channel_id=1, source_target_pairs={{0,4},{1,5},{2,6},{3,7},{4,0},{5,1},{6,2},{7,3},{8,12},{9,13},{10,... | collective-permute-start | bytes 1572872 | tf_op jit(solution)/shard_map/ppermute | solution.py:42
  230.6 17.6 %collective-permute-start.68 = (bf16[128,2048]{1,0:T(8,128)(2,1)}, bf16[128,2048]{1,0:T(8,128)(2,1)}, u32[]{:S(2)}, u32[]{:S(2)}) collective-permute-start(bf16[128,2048]{1,0:T(8,128)(2,1)} %slice.197), channel_id=1, source_target_pairs={{0,2},{1,3},{2,0},{3,1},{4,6},{5,7},{6,4},{7,5},{8,10},{9,11},{10,... | collective-permute-start | bytes 1572872 | tf_op jit(solution)/shard_map/ppermute | solution.py:42
  231.2 19.8 %collective-permute-start.72 = (bf16[256,2048]{1,0:T(8,128)(2,1)}, bf16[256,2048]{1,0:T(8,128)(2,1)}, u32[]{:S(2)}, u32[]{:S(2)}) collective-permute-start(bf16[256,2048]{1,0:T(8,128)(2,1)} %pad_maximum_fusion.7.refs_2_), channel_id=1, source_target_pairs={{0,1},{1,0},{2,3},{3,2},{4,5},{5,4},{6,7},{7,6},{8,9},{9,8},{10,11... | collective-permute-start | bytes 3145736 | tf_op jit(solution)/shard_map/ppermute | solution.py:42
  277.3 321.4 %all-reduce.12.cloned.1.call-start = ((), (), s32[]{:S(2)}) async-start(), calls=%async_computation.8 | async-start | bytes 11534336 | tf_op jit(solution)/shard_map/psum | solution.py:1005
  316.1 13.3 %collective-permute-start.19 = (bf16[256,2048]{1,0:T(8,128)(2,1)}, bf16[256,2048]{1,0:T(8,128)(2,1)S(1)}, u32[]{:S(2)}, u32[]{:S(2)}) collective-permute-start(bf16[256,2048]{1,0:T(8,128)(2,1)} %get-tuple-element.324), channel_id=1, source_target_pairs={{0,1},{1,0},{2,3},{3,2},{4,5},{5,4},{6,7},{7,6},{8,9},{9,8},{10,11... | collective-permute-start | bytes 3145736 | tf_op jit(solution)/shard_map/cond/branch_1_fun/ppermute | solution.py:42
  316.6 16.5 %collective-permute-start.18 = (bf16[256,2048]{1,0:T(8,128)(2,1)}, bf16[256,2048]{1,0:T(8,128)(2,1)S(1)}, u32[]{:S(2)}, u32[]{:S(2)}) collective-permute-start(bf16[256,2048]{1,0:T(8,128)(2,1)} %get-tuple-element.322), channel_id=1, source_target_pairs={{0,1},{1,0},{2,3},{3,2},{4,5},{5,4},{6,7},{7,6},{8,9},{9,8},{10,11... | collective-permute-start | bytes 3145736 | tf_op jit(solution)/shard_map/cond/branch_1_fun/ppermute | solution.py:42
  316.7 17.3 %collective-permute-start.17 = (bf16[256,2048]{1,0:T(8,128)(2,1)}, bf16[256,2048]{1,0:T(8,128)(2,1)S(1)}, u32[]{:S(2)}, u32[]{:S(2)}) collective-permute-start(bf16[256,2048]{1,0:T(8,128)(2,1)} %get-tuple-element.320), channel_id=1, source_target_pairs={{0,1},{1,0},{2,3},{3,2},{4,5},{5,4},{6,7},{7,6},{8,9},{9,8},{10,11... | collective-permute-start | bytes 3145736 | tf_op jit(solution)/shard_map/cond/branch_1_fun/ppermute | solution.py:42
  317.1 16.5 %collective-permute-start.22 = (bf16[256,2048]{1,0:T(8,128)(2,1)}, bf16[256,2048]{1,0:T(8,128)(2,1)S(1)}, u32[]{:S(2)}, u32[]{:S(2)}) collective-permute-start(bf16[256,2048]{1,0:T(8,128)(2,1)} %get-tuple-element.327), channel_id=1, source_target_pairs={{0,1},{1,0},{2,3},{3,2},{4,5},{5,4},{6,7},{7,6},{8,9},{9,8},{10,11... | collective-permute-start | bytes 3145736 | tf_op jit(solution)/shard_map/cond/branch_1_fun/ppermute | solution.py:42
  331.1 14.2 %collective-permute-start.20 = (bf16[128,2048]{1,0:T(8,128)(2,1)S(1)}, bf16[128,2048]{1,0:T(8,128)(2,1)S(1)}, u32[]{:S(2)}, u32[]{:S(2)}) collective-permute-start(bf16[128,2048]{1,0:T(8,128)(2,1)S(1)} %get-tuple-element.771), channel_id=1, source_target_pairs={{0,2},{1,3},{2,0},{3,1},{4,6},{5,7},{6,4},{7,5},{8,10},{9,11},{10,... | collective-permute-start | bytes 1572872 | tf_op jit(solution)/shard_map/cond/branch_1_fun/ppermute | solution.py:42
  332.7 13.8 %collective-permute-start.21 = (bf16[128,2048]{1,0:T(8,128)(2,1)S(1)}, bf16[128,2048]{1,0:T(8,128)(2,1)S(1)}, u32[]{:S(2)}, u32[]{:S(2)}) collective-permute-start(bf16[128,2048]{1,0:T(8,128)(2,1)S(1)} %get-tuple-element.770), channel_id=1, source_target_pairs={{0,4},{1,5},{2,6},{3,7},{4,0},{5,1},{6,2},{7,3},{8,12},{9,13},{10,... | collective-permute-start | bytes 1572872 | tf_op jit(solution)/shard_map/cond/branch_1_fun/ppermute | solution.py:42
  349.6 24.3 %collective-permute-start.11 = (bf16[256,2048]{1,0:T(8,128)(2,1)S(1)}, bf16[256,2048]{1,0:T(8,128)(2,1)S(1)}, u32[]{:S(2)}, u32[]{:S(2)}) collective-permute-start(bf16[256,2048]{1,0:T(8,128)(2,1)S(1)} %get-tuple-element.354), channel_id=1, source_target_pairs={{0,4},{1,5},{2,6},{3,7},{4,0},{5,1},{6,2},{7,3},{8,12},{9,13},{10,... | collective-permute-start | bytes 3145736 | tf_op jit(solution)/shard_map/cond/branch_1_fun/ppermute | solution.py:42
  350.3 24.3 %collective-permute-start.10 = (bf16[256,2048]{1,0:T(8,128)(2,1)S(1)}, bf16[256,2048]{1,0:T(8,128)(2,1)S(1)}, u32[]{:S(2)}, u32[]{:S(2)}) collective-permute-start(bf16[256,2048]{1,0:T(8,128)(2,1)S(1)} %get-tuple-element.353), channel_id=1, source_target_pairs={{0,2},{1,3},{2,0},{3,1},{4,6},{5,7},{6,4},{7,5},{8,10},{9,11},{10,... | collective-permute-start | bytes 3145736 | tf_op jit(solution)/shard_map/cond/branch_1_fun/ppermute | solution.py:42
  392.3 25.0 %collective-permute-start = (bf16[256,2048]{1,0:T(8,128)(2,1)S(1)}, bf16[256,2048]{1,0:T(8,128)(2,1)}, u32[]{:S(2)}, u32[]{:S(2)}) collective-permute-start(bf16[256,2048]{1,0:T(8,128)(2,1)S(1)} %convert_element_type.354.a_ref), channel_id=1, source_target_pairs={{0,2},{1,3},{2,0},{3,1},{4,6},{5,7},{6,4},{7,5},{8,10},{9,11},{10,... | collective-permute-start | bytes 3145736 | tf_op jit(solution)/shard_map/cond/branch_1_fun/ppermute | solution.py:42
  393.8 24.7 %collective-permute-start.1 = (bf16[256,2048]{1,0:T(8,128)(2,1)S(1)}, bf16[256,2048]{1,0:T(8,128)(2,1)}, u32[]{:S(2)}, u32[]{:S(2)}) collective-permute-start(bf16[256,2048]{1,0:T(8,128)(2,1)S(1)} %convert_element_type.354.a_ref), channel_id=1, source_target_pairs={{0,4},{1,5},{2,6},{3,7},{4,0},{5,1},{6,2},{7,3},{8,12},{9,13},{10,... | collective-permute-start | bytes 3145736 | tf_op jit(solution)/shard_map/cond/branch_1_fun/ppermute | solution.py:42
  395.3 23.7 %collective-permute-start.4 = (bf16[256,2048]{1,0:T(8,128)(2,1)S(1)}, bf16[256,2048]{1,0:T(8,128)(2,1)S(1)}, u32[]{:S(2)}, u32[]{:S(2)}) collective-permute-start(bf16[256,2048]{1,0:T(8,128)(2,1)S(1)} %convert_element_type.354.a_ref), channel_id=1, source_target_pairs={{0,1},{1,0},{2,3},{3,2},{4,5},{5,4},{6,7},{7,6},{8,9},{9,8},{10,11... | collective-permute-start | bytes 3145736 | tf_op jit(solution)/shard_map/cond/branch_1_fun/ppermute | solution.py:42
  424.6 14.0 %collective-permute-start.5 = (bf16[128,2048]{1,0:T(8,128)(2,1)S(1)}, bf16[128,2048]{1,0:T(8,128)(2,1)S(1)}, u32[]{:S(2)}, u32[]{:S(2)}) collective-permute-start(bf16[128,2048]{1,0:T(8,128)(2,1)S(1)} %slice.132), channel_id=1, source_target_pairs={{0,4},{1,5},{2,6},{3,7},{4,0},{5,1},{6,2},{7,3},{8,12},{9,13},{10,... | collective-permute-start | bytes 1572872 | tf_op jit(solution)/shard_map/cond/branch_1_fun/ppermute | solution.py:42
  427.2 13.7 %collective-permute-start.6 = (bf16[128,2048]{1,0:T(8,128)(2,1)S(1)}, bf16[128,2048]{1,0:T(8,128)(2,1)S(1)}, u32[]{:S(2)}, u32[]{:S(2)}) collective-permute-start(bf16[128,2048]{1,0:T(8,128)(2,1)S(1)} %slice.133), channel_id=1, source_target_pairs={{0,2},{1,3},{2,0},{3,1},{4,6},{5,7},{6,4},{7,5},{8,10},{9,11},{10,... | collective-permute-start | bytes 1572872 | tf_op jit(solution)/shard_map/cond/branch_1_fun/ppermute | solution.py:42
  454.9 53.7 %all-to-all-start.3 = ((bf16[8,704,256]{2,1,0:T(8,128)(2,1)}), bf16[8,704,256]{2,1,0:T(8,128)(2,1)}, u32[]{:S(2)}, u32[]{:S(2)}) async-start(bf16[8,704,256]{2,1,0:T(8,128)(2,1)} %bitcast.205), calls=%async_computation.3 | async-start | bytes 5767168 | tf_op jit(solution)/shard_map/all_to_all | solution.py:803
  459.7 29.1 %collective-permute-start.25 = (bf16[256,2048]{1,0:T(8,128)(2,1)}, bf16[256,2048]{1,0:T(8,128)(2,1)S(1)}, u32[]{:S(2)}, u32[]{:S(2)}) collective-permute-start(bf16[256,2048]{1,0:T(8,128)(2,1)} %get-tuple-element.383), channel_id=1, source_target_pairs={{0,1},{1,0},{2,3},{3,2},{4,5},{5,4},{6,7},{7,6},{8,9},{9,8},{10,11... | collective-permute-start | bytes 3145736 | tf_op jit(solution)/shard_map/cond/branch_1_fun/ppermute | solution.py:42
  460.2 36.9 %collective-permute-start.23 = (bf16[256,2048]{1,0:T(8,128)(2,1)}, bf16[256,2048]{1,0:T(8,128)(2,1)S(1)}, u32[]{:S(2)}, u32[]{:S(2)}) collective-permute-start(bf16[256,2048]{1,0:T(8,128)(2,1)} %get-tuple-element.379), channel_id=1, source_target_pairs={{0,1},{1,0},{2,3},{3,2},{4,5},{5,4},{6,7},{7,6},{8,9},{9,8},{10,11... | collective-permute-start | bytes 3145736 | tf_op jit(solution)/shard_map/cond/branch_1_fun/ppermute | solution.py:42
  460.3 33.6 %collective-permute-start.24 = (bf16[256,2048]{1,0:T(8,128)(2,1)}, bf16[256,2048]{1,0:T(8,128)(2,1)S(1)}, u32[]{:S(2)}, u32[]{:S(2)}) collective-permute-start(bf16[256,2048]{1,0:T(8,128)(2,1)} %get-tuple-element.381), channel_id=1, source_target_pairs={{0,1},{1,0},{2,3},{3,2},{4,5},{5,4},{6,7},{7,6},{8,9},{9,8},{10,11... | collective-permute-start | bytes 3145736 | tf_op jit(solution)/shard_map/cond/branch_1_fun/ppermute | solution.py:42
  460.7 34.8 %collective-permute-start.28 = (bf16[256,2048]{1,0:T(8,128)(2,1)}, bf16[256,2048]{1,0:T(8,128)(2,1)S(1)}, u32[]{:S(2)}, u32[]{:S(2)}) collective-permute-start(bf16[256,2048]{1,0:T(8,128)(2,1)} %get-tuple-element.386), channel_id=1, source_target_pairs={{0,1},{1,0},{2,3},{3,2},{4,5},{5,4},{6,7},{7,6},{8,9},{9,8},{10,11... | collective-permute-start | bytes 3145736 | tf_op jit(solution)/shard_map/cond/branch_1_fun/ppermute | solution.py:42
  490.4 14.3 %collective-permute-start.26 = (bf16[128,2048]{1,0:T(8,128)(2,1)S(1)}, bf16[128,2048]{1,0:T(8,128)(2,1)S(1)}, u32[]{:S(2)}, u32[]{:S(2)}) collective-permute-start(bf16[128,2048]{1,0:T(8,128)(2,1)S(1)} %get-tuple-element.775), channel_id=1, source_target_pairs={{0,2},{1,3},{2,0},{3,1},{4,6},{5,7},{6,4},{7,5},{8,10},{9,11},{10,... | collective-permute-start | bytes 1572872 | tf_op jit(solution)/shard_map/cond/branch_1_fun/ppermute | solution.py:42
  492.3 13.7 %collective-permute-start.27 = (bf16[128,2048]{1,0:T(8,128)(2,1)S(1)}, bf16[128,2048]{1,0:T(8,128)(2,1)S(1)}, u32[]{:S(2)}, u32[]{:S(2)}) collective-permute-start(bf16[128,2048]{1,0:T(8,128)(2,1)S(1)} %get-tuple-element.774), channel_id=1, source_target_pairs={{0,4},{1,5},{2,6},{3,7},{4,0},{5,1},{6,2},{7,3},{8,12},{9,13},{10,... | collective-permute-start | bytes 1572872 | tf_op jit(solution)/shard_map/cond/branch_1_fun/ppermute | solution.py:42
  510.9 85.7 %all-to-all-start.4 = ((bf16[8,256,256]{2,1,0:T(8,128)(2,1)}), bf16[8,256,256]{2,1,0:T(8,128)(2,1)}, u32[]{:S(2)}, u32[]{:S(2)}) async-start(bf16[8,256,256]{2,1,0:T(8,128)(2,1)} %bitcast.80), calls=%async_computation.4 | async-start | bytes 2097152 | tf_op jit(solution)/shard_map/all_to_all | solution.py:1040
  515.4 177.9 %all-reduce.10.cloned.1.call-start = ((), (), s32[]{:S(2)}) async-start(), calls=%async_computation.7 | async-start | bytes 4472832 | tf_op jit(solution)/shard_map/psum | solution.py:1062
  525.4 10.0 %collective-permute-start.36 = (bf16[2,256,256]{2,1,0:T(8,128)(2,1)}, bf16[2,256,256]{2,1,0:T(8,128)(2,1)S(1)}, u32[]{:S(2)}, u32[]{:S(2)}) collective-permute-start(bf16[2,256,256]{2,1,0:T(8,128)(2,1)} %fusion.10), channel_id=1, source_target_pairs={{0,2},{1,3},{2,0},{3,1},{4,6},{5,7},{6,4},{7,5},{8,10},{9,11},{10,... | collective-permute-start | bytes 786440 | tf_op jit(solution)/shard_map/cond/branch_1_fun/ppermute | solution.py:42
  527.3 14.5 %collective-permute-start.31 = (bf16[256,2048]{1,0:T(8,128)(2,1)}, bf16[256,2048]{1,0:T(8,128)(2,1)S(1)}, u32[]{:S(2)}, u32[]{:S(2)}) collective-permute-start(bf16[256,2048]{1,0:T(8,128)(2,1)} %get-tuple-element.421), channel_id=1, source_target_pairs={{0,1},{1,0},{2,3},{3,2},{4,5},{5,4},{6,7},{7,6},{8,9},{9,8},{10,11... | collective-permute-start | bytes 3145736 | tf_op jit(solution)/shard_map/cond/branch_1_fun/ppermute | solution.py:42
  538.1 10.8 %collective-permute-start.29 = (bf16[256,2048]{1,0:T(8,128)(2,1)}, bf16[256,2048]{1,0:T(8,128)(2,1)S(1)}, u32[]{:S(2)}, u32[]{:S(2)}) collective-permute-start(bf16[256,2048]{1,0:T(8,128)(2,1)} %get-tuple-element.417), channel_id=1, source_target_pairs={{0,1},{1,0},{2,3},{3,2},{4,5},{5,4},{6,7},{7,6},{8,9},{9,8},{10,11... | collective-permute-start | bytes 3145736 | tf_op jit(solution)/shard_map/cond/branch_1_fun/ppermute | solution.py:42
  538.6 8.6 %collective-permute-start.34 = (bf16[256,2048]{1,0:T(8,128)(2,1)}, bf16[256,2048]{1,0:T(8,128)(2,1)S(1)}, u32[]{:S(2)}, u32[]{:S(2)}) collective-permute-start(bf16[256,2048]{1,0:T(8,128)(2,1)} %get-tuple-element.424), channel_id=1, source_target_pairs={{0,1},{1,0},{2,3},{3,2},{4,5},{5,4},{6,7},{7,6},{8,9},{9,8},{10,11... | collective-permute-start | bytes 3145736 | tf_op jit(solution)/shard_map/cond/branch_1_fun/ppermute | solution.py:42
  543.6 12.9 %collective-permute-start.32 = (bf16[128,2048]{1,0:T(8,128)(2,1)S(1)}, bf16[128,2048]{1,0:T(8,128)(2,1)S(1)}, u32[]{:S(2)}, u32[]{:S(2)}) collective-permute-start(bf16[128,2048]{1,0:T(8,128)(2,1)S(1)} %get-tuple-element.777), channel_id=1, source_target_pairs={{0,2},{1,3},{2,0},{3,1},{4,6},{5,7},{6,4},{7,5},{8,10},{9,11},{10,... | collective-permute-start | bytes 1572872 | tf_op jit(solution)/shard_map/cond/branch_1_fun/ppermute | solution.py:42
  543.9 12.6 %collective-permute-start.33 = (bf16[128,2048]{1,0:T(8,128)(2,1)S(1)}, bf16[128,2048]{1,0:T(8,128)(2,1)S(1)}, u32[]{:S(2)}, u32[]{:S(2)}) collective-permute-start(bf16[128,2048]{1,0:T(8,128)(2,1)S(1)} %get-tuple-element.776), channel_id=1, source_target_pairs={{0,4},{1,5},{2,6},{3,7},{4,0},{5,1},{6,2},{7,3},{8,12},{9,13},{10,... | collective-permute-start | bytes 1572872 | tf_op jit(solution)/shard_map/cond/branch_1_fun/ppermute | solution.py:42
  559.1 23.4 %collective-permute-start.13 = (bf16[256,2048]{1,0:T(8,128)(2,1)}, bf16[256,2048]{1,0:T(8,128)(2,1)S(1)}, u32[]{:S(2)}, u32[]{:S(2)}) collective-permute-start(bf16[256,2048]{1,0:T(8,128)(2,1)} %get-tuple-element.430), channel_id=1, source_target_pairs={{0,4},{1,5},{2,6},{3,7},{4,0},{5,1},{6,2},{7,3},{8,12},{9,13},{10,... | collective-permute-start | bytes 3145736 | tf_op jit(solution)/shard_map/cond/branch_1_fun/ppermute | solution.py:42
  560.6 23.2 %collective-permute-start.12 = (bf16[256,2048]{1,0:T(8,128)(2,1)}, bf16[256,2048]{1,0:T(8,128)(2,1)}, u32[]{:S(2)}, u32[]{:S(2)}) collective-permute-start(bf16[256,2048]{1,0:T(8,128)(2,1)} %get-tuple-element.429), channel_id=1, source_target_pairs={{0,2},{1,3},{2,0},{3,1},{4,6},{5,7},{6,4},{7,5},{8,10},{9,11},{10,... | collective-permute-start | bytes 3145736 | tf_op jit(solution)/shard_map/cond/branch_1_fun/ppermute | solution.py:42
  602.3 62.8 %all-to-all-start = ((bf16[8,704,256]{2,1,0:T(8,128)(2,1)}), bf16[8,704,256]{2,1,0:T(8,128)(2,1)}, u32[]{:S(2)}, u32[]{:S(2)}) async-start(bf16[8,704,256]{2,1,0:T(8,128)(2,1)} %bitcast.206), calls=%async_computation | async-start | bytes 5767168 | tf_op jit(solution)/shard_map/cond/branch_1_fun/all_to_all | solution.py:803
  606.7 56.5 %collective-permute-start.9 = (bf16[256,2048]{1,0:T(8,128)(2,1)}, bf16[256,2048]{1,0:T(8,128)(2,1)S(1)}, u32[]{:S(2)}, u32[]{:S(2)}) collective-permute-start(bf16[256,2048]{1,0:T(8,128)(2,1)} %get-tuple-element.444), channel_id=1, source_target_pairs={{0,4},{1,5},{2,6},{3,7},{4,0},{5,1},{6,2},{7,3},{8,12},{9,13},{10,... | collective-permute-start | bytes 3145736 | tf_op jit(solution)/shard_map/cond/branch_1_fun/ppermute | solution.py:42
  608.7 54.7 %collective-permute-start.8 = (bf16[256,2048]{1,0:T(8,128)(2,1)}, bf16[256,2048]{1,0:T(8,128)(2,1)S(1)}, u32[]{:S(2)}, u32[]{:S(2)}) collective-permute-start(bf16[256,2048]{1,0:T(8,128)(2,1)} %get-tuple-element.443), channel_id=1, source_target_pairs={{0,2},{1,3},{2,0},{3,1},{4,6},{5,7},{6,4},{7,5},{8,10},{9,11},{10,... | collective-permute-start | bytes 3145736 | tf_op jit(solution)/shard_map/cond/branch_1_fun/ppermute | solution.py:42
  (77 other events, 660.1 us)
Sparse Core Ops, SparseCore 0:
  82.0 106.9 all-gather.2
  277.4 112.9 all-reduce.7
  393.4 205.2 all-reduce.11
  601.7 91.4 all-reduce.9
